TPU v7x, 32 devices: a whole 2x2x4 slice. The times are simulated.
32 devices in a mesh: rows: 4 (over z), cols: 8 (over y, x, core).
Axes of the slice: x: 2, y: 2, z: 4, core: 2. Of those that a mesh axis runs over, the one named last changes fastest.
Arguments:
- features: bfloat16 [64, 512, 180], P('rows', 'cols'), may hold values from -8 to 8
- gain_one: float32 [180], replicated, may hold values from 0.1 to 1.9
- qkv_weight: bfloat16 [180, 540], replicated, may hold values from -4 to 4
- bias_table: float32 [1521, 6], replicated, may hold values from -4 to 4
- proj_weight: bfloat16 [180, 180], replicated, may hold values from -0.4375 to 0.4375
- gain_two: float32 [180], replicated, may hold values from 0.1 to 1.9
- hidden_weight: bfloat16 [180, 360], replicated, may hold values from -0.4375 to 0.4375
- output_weight: bfloat16 [360, 180], replicated, may hold values from -0.3125 to 0.3125
- group_conv: bfloat16 [3, 3, 180, 180], replicated, may hold values from -0.15625 to 0.15625
- before_conv: bfloat16 [3, 3, 180, 64], replicated, may hold values from -0.15625 to 0.15625
- upsample_conv: bfloat16 [3, 3, 64, 256], replicated, may hold values from -0.25 to 0.25
Outputs:
- upscaled: bfloat16 [64, 128, 1024], P(None, 'rows', 'cols')
All inputs are finite; a program needn't handle non-finite values.
Results may differ from a plain program's by a relative error of at most 0.017.
Values may be sent and summed in bfloat16 or wider, within the bound.
No kernel may reach another device: no remote copies, remote signals or barrier semaphores. Data moves between devices by JAX's collectives and lax.ppermute only.
A program may use at most 128 MiB of HBM per device.

v0:
```python
import jax
import jax.numpy as jnp
import numpy as np
from jax import lax
from jax.sharding import PartitionSpec as P

HEADS = 6
WIN = 16
KWIN = 24


def padded_2(block, sides, width):
    for axis, dim in sides:
        count = lax.axis_size(axis)
        forward = [(i, i + 1) for i in range(count - 1)]
        backward = [(target, source) for source, target in forward]
        low = lax.ppermute(
            lax.slice_in_dim(block, block.shape[dim] - width, None, axis=dim), axis, forward
        )
        high = lax.ppermute(lax.slice_in_dim(block, 0, width, axis=dim), axis, backward)
        block = jnp.concatenate([low, block, high], axis=dim)
    return block


def layer_norm(values, gain):
    center = values - jnp.mean(values, axis=-1, keepdims=True)
    spread = jnp.mean(center * center, axis=-1, keepdims=True)
    return center * lax.rsqrt(spread + 1e-05) * gain


def offset_selector():
    side = WIN + KWIN - 1
    query_pos = np.arange(WIN)[:, None, None]
    key_pos = np.arange(KWIN)[None, :, None]
    entry = np.arange(side)[None, None, :]
    return (entry == key_pos - query_pos + WIN - 1).astype(np.float32)


def build_bias(bias_table):
    side = WIN + KWIN - 1
    grid = bias_table.reshape(side, side, HEADS)
    selector = jnp.asarray(offset_selector())
    partial_rows = jnp.einsum("ipa,abh->hipb", selector, grid, precision=lax.Precision.HIGHEST)
    full = jnp.einsum("jqb,hipb->hijpq", selector, partial_rows, precision=lax.Precision.HIGHEST)
    return full.reshape(HEADS, WIN * WIN, KWIN * KWIN)


def query_windows(values):
    height, width, chans = values.shape
    blocks = values.reshape(height // WIN, WIN, width // WIN, WIN, chans)
    return blocks.transpose(0, 2, 1, 3, 4).reshape(-1, WIN * WIN, chans)


def undo_windows(values, height, width):
    chans = values.shape[-1]
    blocks = values.reshape(height // WIN, width // WIN, WIN, WIN, chans)
    return blocks.transpose(0, 2, 1, 3, 4).reshape(height, width, chans)


def key_windows(padded):
    span = KWIN - WIN
    height, width, chans = padded.shape
    nbr = height // span
    nbc = width // span
    blocks = padded.reshape(nbr, span, nbc, span, chans)
    stacked = jnp.stack([blocks[0 : nbr - 1 : 2], blocks[1:nbr:2], blocks[2:nbr:2]], axis=1)
    stacked = jnp.stack(
        [stacked[:, :, :, 0 : nbc - 1 : 2], stacked[:, :, :, 1:nbc:2], stacked[:, :, :, 2:nbc:2]],
        axis=4,
    )
    stacked = stacked.transpose(0, 3, 1, 2, 4, 5, 6)
    return stacked.reshape(-1, KWIN * KWIN, chans)


def attend_group(query_block, keyval_block, bias):
    groups = query_block.shape[0]
    chans = query_block.shape[-1]
    head_size = chans // HEADS
    qs = query_block.reshape(groups, WIN * WIN, HEADS, head_size)
    keys = keyval_block[..., :chans].reshape(groups, KWIN * KWIN, HEADS, head_size)
    vals = keyval_block[..., chans:].reshape(groups, KWIN * KWIN, HEADS, head_size)
    scores = (
        jnp.einsum("gqhd,gkhd->ghqk", qs, keys, preferred_element_type=jnp.float32)
        / jnp.sqrt(jnp.float32(head_size))
        + bias[None]
    )
    probs = jax.nn.softmax(scores, axis=-1).astype(jnp.bfloat16)
    result = jnp.einsum("ghqk,gkhd->gqhd", probs, vals, preferred_element_type=jnp.float32)
    return result.reshape(groups, WIN * WIN, chans).astype(jnp.bfloat16)


def conv_last(padded, weight):
    height = padded.shape[0] - 2
    width = padded.shape[1] - 2
    total = jnp.zeros((height, width, weight.shape[3]), jnp.float32)
    for tap_r in range(3):
        for tap_c in range(3):
            total = total + jnp.dot(
                padded[tap_r : tap_r + height, tap_c : tap_c + width],
                weight[tap_r, tap_c],
                preferred_element_type=jnp.float32,
            )
    return total


def conv_to_first(padded, weight):
    height = padded.shape[0] - 2
    width = padded.shape[1] - 2
    total = jnp.zeros((weight.shape[3], height, width), jnp.float32)
    for tap_r in range(3):
        for tap_c in range(3):
            total = total + jnp.einsum(
                "hwc,co->ohw",
                padded[tap_r : tap_r + height, tap_c : tap_c + width],
                weight[tap_r, tap_c],
                preferred_element_type=jnp.float32,
            )
    return total


def conv_first(padded, weight):
    height = padded.shape[1] - 2
    width = padded.shape[2] - 2
    total = jnp.zeros((weight.shape[3], height, width), jnp.float32)
    for tap_r in range(3):
        for tap_c in range(3):
            total = total + jnp.einsum(
                "chw,co->ohw",
                padded[:, tap_r : tap_r + height, tap_c : tap_c + width],
                weight[tap_r, tap_c],
                preferred_element_type=jnp.float32,
            )
    return total


def shuffle(expanded):
    chans4, height, width = expanded.shape
    chans = chans4 // 4
    parts = expanded.reshape(chans, 2, 2, height, width).transpose(0, 3, 1, 4, 2)
    return parts.reshape(chans, 2 * height, 2 * width)


def on_device(
    features,
    gain_one,
    qkv_weight,
    bias_table,
    proj_weight,
    gain_two,
    hidden_weight,
    output_weight,
    group_conv,
    before_conv,
    upsample_conv,
):
    height, width, chans = features.shape
    rim = (KWIN - WIN) // 2
    base = features.astype(jnp.float32)
    normed = layer_norm(base, gain_one).astype(jnp.bfloat16)
    projected = jnp.dot(normed, qkv_weight, preferred_element_type=jnp.float32)
    queries = projected[..., :chans].astype(jnp.bfloat16)
    keyvals = projected[..., chans:].astype(jnp.bfloat16)
    padded = padded_2(keyvals, (("rows", 0), ("cols", 1)), rim)
    bias = build_bias(bias_table)
    query_win = query_windows(queries)
    keyval_win = key_windows(padded)
    count = query_win.shape[0]
    group = 4
    attended = lax.map(
        lambda pair: attend_group(pair[0], pair[1], bias),
        (
            query_win.reshape(count // group, group, WIN * WIN, chans),
            keyval_win.reshape(count // group, group, KWIN * KWIN, 2 * chans),
        ),
    )
    attended = undo_windows(attended.reshape(count, WIN * WIN, chans), height, width)
    first = base + jnp.dot(attended, proj_weight, preferred_element_type=jnp.float32)
    second_norm = layer_norm(first, gain_two).astype(jnp.bfloat16)
    inner = jax.nn.gelu(
        jnp.dot(second_norm, hidden_weight, preferred_element_type=jnp.float32), approximate=False
    ).astype(jnp.bfloat16)
    mixed = (first + jnp.dot(inner, output_weight, preferred_element_type=jnp.float32)).astype(
        jnp.bfloat16
    )
    mixed_pad = padded_2(mixed, (("rows", 0), ("cols", 1)), 1)
    grouped = (base + conv_last(mixed_pad, group_conv)).astype(jnp.bfloat16)
    grouped_pad = padded_2(grouped, (("rows", 0), ("cols", 1)), 1)
    lowfeat = jax.nn.leaky_relu(conv_to_first(grouped_pad, before_conv), 0.01).astype(jnp.bfloat16)
    lowfeat_pad = padded_2(lowfeat, (("rows", 1), ("cols", 2)), 1)
    expanded = conv_first(lowfeat_pad, upsample_conv)
    return shuffle(expanded).astype(jnp.bfloat16)


def solution(mesh):
    placed = (P("rows", "cols", None), P(), P(), P(), P(), P(), P(), P(), P(), P(), P())
    return jax.shard_map(
        on_device, mesh=mesh, in_specs=placed, out_specs=P(None, "rows", "cols"), check_vma=False
    )
```

profile of v0, /device:TPU:3, one launch (start us, length us, event | category | flops | bytes accessed | tf_op | source)
XLA Modules:
  0.0 176.1 jit_solution(13212975307266474251)
XLA Ops:
  0.0 1.3 convert_reduce_fusion
  1.3 1.4 fusion.43
  2.8 1.8 %convolution_convert_fusion = bf16[16,64,540]{2,1,0:T(8,128)(2,1)S(1)} fusion(bf16[16,64,180]{2,1,0:T(8,128)(2,1)} %param.12, f32[180]{0:T(256)} %param.13, f32[16,64]{1,0:T(8,128)S(1)} %add_rsqrt_fusion.1, f32[16,64]{1,0:T(8,128)S(1)} %broadcast_multiply_fusion.1, bf16[180,540]{1,0:T(8,128)(2,1)S(1)} %copy-done), kind=kOutput, calls=%fused_computation.15 | convolution fusion | flops 200540160 | bytes 1677872 | tf_op jit(solution)/shard_map/dot_general | solution.py:160
  4.8 3.2 %collective-permute-start = (bf16[4,64,360]{2,1,0:T(8,128)(2,1)S(1)}, bf16[4,64,360]{2,1,0:T(8,128)(2,1)S(1)}, u32[]{:S(2)}, u32[]{:S(2)}) collective-permute-start(bf16[4,64,360]{2,1,0:T(8,128)(2,1)S(1)} %get-tuple-element.30), channel_id=1, source_target_pairs={{0,8},{8,16},{16,24},{1,9},{9,17},{17,25},{2,10},{10,18},{18,26},{... | collective-permute-start | bytes 552968 | tf_op jit(solution)/shard_map/ppermute | solution.py:17
  8.0 1.3 collective-permute-start.1
  9.3 0.3 slice.345
  9.8 1.1 convolution_bitcast_fusion.1
  10.9 0.7 collective-permute-done
  11.6 3.8 %collective-permute-done.1 = bf16[4,64,360]{2,1,0:T(8,128)(2,1)S(1)} collective-permute-done((bf16[4,64,360]{2,1,0:T(8,128)(2,1)S(1)}, bf16[4,64,360]{2,1,0:T(8,128)(2,1)S(1)}, u32[]{:S(2)}, u32[]{:S(2)}) %collective-permute-start.1) | collective-permute-done | bytes 184352 | tf_op jit(solution)/shard_map/ppermute | solution.py:20
  15.4 4.9 %collective-permute-start.2 = (bf16[24,4,360]{2,1,0:T(4,128)(2,1)S(1)}, bf16[24,4,360]{2,1,0:T(4,128)(2,1)S(1)}, u32[]{:S(2)}, u32[]{:S(2)}) collective-permute-start(bf16[24,4,360]{2,1,0:T(4,128)(2,1)S(1)} %get-tuple-element.32), channel_id=1, source_target_pairs={{0,1},{1,2},{2,3},{3,4},{4,5},{5,6},{6,7},{8,9},{9,10},{10,11},{11... | collective-permute-start | bytes 207368 | tf_op jit(solution)/shard_map/ppermute | solution.py:17
  20.3 2.1 %collective-permute-start.3 = (bf16[24,4,360]{2,1,0:T(4,128)(2,1)S(1)}, bf16[24,4,360]{2,1,0:T(4,128)(2,1)}, u32[]{:S(2)}, u32[]{:S(2)}) collective-permute-start(bf16[24,4,360]{2,1,0:T(4,128)(2,1)S(1)} %get-tuple-element.33), channel_id=1, source_target_pairs={{1,0},{2,1},{3,2},{4,3},{5,4},{6,5},{7,6},{9,8},{10,9},{11,10},{12... | collective-permute-start | bytes 207368 | tf_op jit(solution)/shard_map/ppermute | solution.py:20
  22.4 18.2 %convolution_bitcast_fusion = f32[6,16,16,24,24]{4,3,2,1,0:T(8,128)} fusion(f32[6,16,24,39,1]{3,2,4,1,0:T(8,128)S(1)} %convolution_bitcast_fusion.1, f32[16,24,39,1,1]{2,1,0,4,3:T(8,128)S(1)} %copy-done.7), kind=kOutput, calls=%fused_computation.5 | convolution fusion | flops 414056448 | bytes 3958272 | tf_op jit(solution)/shard_map/jqb,hipb->hijpq/dot_general | solution.py:44
  40.7 0.8 copy.68
  41.6 2.7 %reshape.80 = bf16[4,256,6,30]{3,2,1,0:T(8,128)(2,1)S(1)} reshape(bf16[1,4,16,16,180]{4,3,2,1,0:T(8,128)(2,1)} %bitcast.226) | data formatting | bytes 737280 | tf_op jit(solution)/shard_map/while/body/eval_jaxpr/reshape | solution.py:79
  44.3 13.5 %add.126 = f32[6,256,576]{2,1,0:T(8,128)} reshape(f32[6,16,16,24,24]{4,3,2,1,0:T(8,128)} %convolution_bitcast_fusion) | data formatting | bytes 7077888 | tf_op jit(solution)/shard_map/while/body/eval_jaxpr/add | solution.py:83
  57.7 5.3 %copy.43 = f32[6,256,576]{1,2,0:T(8,128)} copy(f32[6,256,576]{2,1,0:T(8,128)} %add.126) | data formatting | bytes 7077888 | tf_op jit(solution)/shard_map/while/body/eval_jaxpr/add | solution.py:83
  63.0 1.6 pad_maximum_fusion.1
  65.5 0.4 pad_maximum_fusion
  65.9 1.5 fusion.247
  67.5 2.1 %copy.38 = bf16[4,576,180]{1,0,2:T(4,128)(2,1)} copy(bf16[4,576,180]{2,1,0:T(8,128)(2,1)S(1)} %get-tuple-element.20) | data formatting | bytes 1658880 | tf_op jit(solution)/shard_map/while/body/eval_jaxpr/slice | solution.py:81
  69.5 2.7 %copy.40 = bf16[4,576,180]{1,0,2:T(4,128)(2,1)S(1)} copy(bf16[4,576,180]{2,1,0:T(8,128)(2,1)} %get-tuple-element.22) | data formatting | bytes 1658880 | tf_op jit(solution)/shard_map/while/body/eval_jaxpr/slice | solution.py:80
  72.2 7.1 %fusion.8 = f32[4,6,256,576]{2,3,1,0:T(8,128)} fusion(bf16[4,256,6,30]{3,2,1,0:T(8,128)(2,1)S(1)} %reshape.80, bf16[4,576,6,30]{1,0,3,2:T(4,128)(2,1)S(1)} %bitcast.222), kind=kOutput, calls=%fused_computation.24 | convolution fusion | flops 212336640 | bytes 15353856 | tf_op jit(solution)/shard_map/while/body/eval_jaxpr/gqhd,gkhd->ghqk/dot_general | solution.py:83
  79.4 19.1 %fusion.253 = (f32[4,6,256]{2,1,0:T(8,128)S(1)}, f32[4,6,256,576]{2,3,1,0:T(8,128)}) fusion(f32[4,6,256,576]{2,3,1,0:T(8,128)} %fusion.8, f32[6,256,576]{1,2,0:T(8,128)} %copy.43), kind=kOutput, calls=%fused_computation.316 | output fusion | flops 21234240 | bytes 31875072 | tf_op jit(solution)/shard_map/while/body/eval_jaxpr/sub | solution.py:87
  98.5 6.3 %fusion.42 = bf16[4,256,6,30]{1,3,2,0:T(8,128)(2,1)S(1)} fusion(f32[4,6,256,576]{2,3,1,0:T(8,128)} %get-tuple-element.53, f32[4,6,256]{2,1,0:T(8,128)S(1)} %get-tuple-element.52, bf16[4,576,6,30]{1,0,3,2:T(4,128)(2,1)S(1)} %bitcast.230), kind=kOutput, calls=%fused_computation.76 | convolution fusion | flops 219598848 | bytes 15378432 | tf_op jit(solution)/shard_map/while/body/eval_jaxpr/ghqk,gkhd->gqhd/dot_general | solution.py:88
  104.8 1.3 copy.45
  106.1 1.2 convert_element_type.61
  107.4 0.4 fusion.254
  107.8 0.4 multiply_reduce_fusion
  108.3 0.9 fusion.82
  109.2 3.8 %fusion.28 = bf16[16,64,180]{2,1,0:T(8,128)(2,1)S(1)} fusion(f32[16,64,180]{2,1,0:T(8,128)S(1)} %get-tuple-element.55, f32[16,64,360]{2,1,0:T(8,128)S(1)} %get-tuple-element.56, u16[64,360]{1,0:T(8,128)(2,1)S(1)} %get-tuple-element.14, u16[64,360]{1,0:T(8,128)(2,1)S(1)} %get-tuple-element.13, bf16[360,180]{0,1:T(8,128)(2,1)S(1)} %copy-done.12), kind=kOutput, calls=%fused_computation.60 | convolution fusion | flops 158883840 | bytes 2802240 | tf_op jit(solution)/shard_map/dot_general | solution.py:182
  113.1 3.2 %collective-permute-start.4 = (bf16[1,64,180]{2,1,0:T(8,128)(2,1)S(1)}, bf16[1,64,180]{2,1,0:T(8,128)(2,1)S(1)}, u32[]{:S(2)}, u32[]{:S(2)}) collective-permute-start(bf16[1,64,180]{2,1,0:T(8,128)(2,1)S(1)} %get-tuple-element.44), channel_id=1, source_target_pairs={{0,8},{8,16},{16,24},{1,9},{9,17},{17,25},{2,10},{10,18},{18,26},{... | collective-permute-start | bytes 69128 | tf_op jit(solution)/shard_map/ppermute | solution.py:17
  116.3 1.3 collective-permute-start.5
  117.9 3.1 %collective-permute-done.5 = bf16[1,64,180]{2,1,0:T(8,128)(2,1)S(1)} collective-permute-done((bf16[1,64,180]{2,1,0:T(8,128)(2,1)S(1)}, bf16[1,64,180]{2,1,0:T(8,128)(2,1)S(1)}, u32[]{:S(2)}, u32[]{:S(2)}) %collective-permute-start.5) | collective-permute-done | bytes 23072 | tf_op jit(solution)/shard_map/ppermute | solution.py:20
  121.0 6.0 %collective-permute-start.6 = (bf16[18,1,180]{2,1,0:T(2,128)(2,1)S(1)}, bf16[18,1,180]{2,1,0:T(2,128)(2,1)S(1)}, u32[]{:S(2)}, u32[]{:S(2)}) collective-permute-start(bf16[18,1,180]{2,1,0:T(2,128)(2,1)S(1)} %get-tuple-element.40), channel_id=1, source_target_pairs={{0,1},{1,2},{2,3},{3,4},{4,5},{5,6},{6,7},{8,9},{9,10},{10,11},{11... | collective-permute-start | bytes 19448 | tf_op jit(solution)/shard_map/ppermute | solution.py:17
  127.0 1.9 %collective-permute-start.7 = (bf16[18,1,180]{2,1,0:T(2,128)(2,1)S(1)}, bf16[18,1,180]{2,1,0:T(2,128)(2,1)S(1)}, u32[]{:S(2)}, u32[]{:S(2)}) collective-permute-start(bf16[18,1,180]{2,1,0:T(2,128)(2,1)S(1)} %get-tuple-element.41), channel_id=1, source_target_pairs={{1,0},{2,1},{3,2},{4,3},{5,4},{6,5},{7,6},{9,8},{10,9},{11,10},{12... | collective-permute-start | bytes 19448 | tf_op jit(solution)/shard_map/ppermute | solution.py:20
  128.9 0.3 fusion.87
  129.2 0.3 fusion.83
  129.5 3.5 %collective-permute-done.7 = bf16[18,1,180]{2,1,0:T(2,128)(2,1)S(1)} collective-permute-done((bf16[18,1,180]{2,1,0:T(2,128)(2,1)S(1)}, bf16[18,1,180]{2,1,0:T(2,128)(2,1)S(1)}, u32[]{:S(2)}, u32[]{:S(2)}) %collective-permute-start.7) | collective-permute-done | bytes 6512 | tf_op jit(solution)/shard_map/ppermute | solution.py:20
  133.8 0.3 fusion.111
  134.1 0.3 fusion.118
  134.4 0.3 fusion.27
  134.8 0.5 fusion.30
  135.3 3.2 %collective-permute-start.8 = (bf16[1,64,180]{2,1,0:T(8,128)(2,1)S(1)}, bf16[1,64,180]{2,1,0:T(8,128)(2,1)S(1)}, u32[]{:S(2)}, u32[]{:S(2)}) collective-permute-start(bf16[1,64,180]{2,1,0:T(8,128)(2,1)S(1)} %get-tuple-element.42), channel_id=1, source_target_pairs={{0,8},{8,16},{16,24},{1,9},{9,17},{17,25},{2,10},{10,18},{18,26},{... | collective-permute-start | bytes 69128 | tf_op jit(solution)/shard_map/ppermute | solution.py:17
  138.5 1.3 collective-permute-start.9
  140.1 3.1 %collective-permute-done.9 = bf16[1,64,180]{2,1,0:T(8,128)(2,1)S(1)} collective-permute-done((bf16[1,64,180]{2,1,0:T(8,128)(2,1)S(1)}, bf16[1,64,180]{2,1,0:T(8,128)(2,1)S(1)}, u32[]{:S(2)}, u32[]{:S(2)}) %collective-permute-start.9) | collective-permute-done | bytes 23072 | tf_op jit(solution)/shard_map/ppermute | solution.py:20
  143.2 3.4 %collective-permute-start.10 = (bf16[18,1,180]{2,1,0:T(2,128)(2,1)S(1)}, bf16[18,1,180]{2,1,0:T(2,128)(2,1)S(1)}, u32[]{:S(2)}, u32[]{:S(2)}) collective-permute-start(bf16[18,1,180]{2,1,0:T(2,128)(2,1)S(1)} %get-tuple-element.36), channel_id=1, source_target_pairs={{0,1},{1,2},{2,3},{3,4},{4,5},{5,6},{6,7},{8,9},{9,10},{10,11},{11... | collective-permute-start | bytes 19448 | tf_op jit(solution)/shard_map/ppermute | solution.py:17
  146.5 2.2 %collective-permute-start.11 = (bf16[18,1,180]{2,1,0:T(2,128)(2,1)S(1)}, bf16[18,1,180]{2,1,0:T(2,128)(2,1)S(1)}, u32[]{:S(2)}, u32[]{:S(2)}) collective-permute-start(bf16[18,1,180]{2,1,0:T(2,128)(2,1)S(1)} %get-tuple-element.37), channel_id=1, source_target_pairs={{1,0},{2,1},{3,2},{4,3},{5,4},{6,5},{7,6},{9,8},{10,9},{11,10},{12... | collective-permute-start | bytes 19448 | tf_op jit(solution)/shard_map/ppermute | solution.py:20
  149.0 0.3 fusion.91
  149.3 3.2 %collective-permute-done.11 = bf16[18,1,180]{2,1,0:T(2,128)(2,1)S(1)} collective-permute-done((bf16[18,1,180]{2,1,0:T(2,128)(2,1)S(1)}, bf16[18,1,180]{2,1,0:T(2,128)(2,1)S(1)}, u32[]{:S(2)}, u32[]{:S(2)}) %collective-permute-start.11) | collective-permute-done | bytes 6512 | tf_op jit(solution)/shard_map/ppermute | solution.py:20
  153.4 0.3 fusion.101
  153.7 0.3 fusion.108
  154.0 0.4 fusion.41
  154.3 0.3 fusion.51
  154.7 1.6 collective-permute-start.12
  156.3 1.3 collective-permute-start.13
  157.9 2.9 %collective-permute-done.13 = bf16[64,1,64]{0,2,1:T(8,128)(2,1)S(1)} collective-permute-done((bf16[64,1,64]{0,2,1:T(8,128)(2,1)S(1)}, bf16[64,1,64]{0,2,1:T(8,128)(2,1)S(1)}, u32[]{:S(2)}, u32[]{:S(2)}) %collective-permute-start.13) | collective-permute-done | bytes 8224 | tf_op jit(solution)/shard_map/ppermute | solution.py:20
  160.9 3.4 %collective-permute-start.14 = (bf16[64,18,1]{0,2,1:T(2,128)(2,1)S(1)}, bf16[64,18,1]{0,2,1:T(2,128)(2,1)S(1)}, u32[]{:S(2)}, u32[]{:S(2)}) collective-permute-start(bf16[64,18,1]{0,2,1:T(2,128)(2,1)S(1)} %get-tuple-element.48), channel_id=1, source_target_pairs={{0,1},{1,2},{2,3},{3,4},{4,5},{5,6},{6,7},{8,9},{9,10},{10,11},{11... | collective-permute-start | bytes 6920 | tf_op jit(solution)/shard_map/ppermute | solution.py:17
  164.2 1.9 %collective-permute-start.15 = (bf16[64,18,1]{0,2,1:T(2,128)(2,1)S(1)}, bf16[64,18,1]{0,2,1:T(2,128)(2,1)S(1)}, u32[]{:S(2)}, u32[]{:S(2)}) collective-permute-start(bf16[64,18,1]{0,2,1:T(2,128)(2,1)S(1)} %get-tuple-element.49), channel_id=1, source_target_pairs={{1,0},{2,1},{3,2},{4,3},{5,4},{6,5},{7,6},{9,8},{10,9},{11,10},{12... | collective-permute-start | bytes 6920 | tf_op jit(solution)/shard_map/ppermute | solution.py:20
  166.7 3.4 %collective-permute-done.15 = bf16[64,18,1]{0,2,1:T(2,128)(2,1)S(1)} collective-permute-done((bf16[64,18,1]{0,2,1:T(2,128)(2,1)S(1)}, bf16[64,18,1]{0,2,1:T(2,128)(2,1)S(1)}, u32[]{:S(2)}, u32[]{:S(2)}) %collective-permute-start.15) | collective-permute-done | bytes 2336 | tf_op jit(solution)/shard_map/ppermute | solution.py:20
  171.4 0.4 fusion.21
  171.8 0.3 fusion.34
  172.1 1.0 copy.47
  173.1 1.4 copy.48
  174.5 1.7 copy.49
  (73 shorter events, 6.3 us)
Async XLA Ops:
  0.0 2.8 %copy-start = (bf16[180,540]{1,0:T(8,128)(2,1)S(1)}, bf16[180,540]{1,0:T(8,128)(2,1)}, u32[]{:S(2)}) copy-start(bf16[180,540]{1,0:T(8,128)(2,1)} %param.14) | copy-start | bytes 583204
  4.6 5.1 %copy-start.10 = (f32[1521,6]{0,1:T(8,128)S(1)}, f32[1521,6]{0,1:T(8,128)}, u32[]{:S(2)}) copy-start(f32[1521,6]{0,1:T(8,128)} %param.15) | copy-start | bytes 109516
  4.6 5.2 %copy-start.8 = (f32[16,24,39,1]{2,1,0,3:T(8,128)S(1)}, f32[16,24,39,1]{2,1,0,3:T(8,128)}, u32[]{:S(2)}) copy-start(f32[16,24,39,1]{2,1,0,3:T(8,128)} %constant.98) | copy-start | bytes 179716
  4.8 6.8 %collective-permute-start = (bf16[4,64,360]{2,1,0:T(8,128)(2,1)S(1)}, bf16[4,64,360]{2,1,0:T(8,128)(2,1)S(1)}, u32[]{:S(2)}, u32[]{:S(2)}) collective-permute-start(bf16[4,64,360]{2,1,0:T(8,128)(2,1)S(1)} %get-tuple-element.30), channel_id=1, source_target_pairs={{0,8},{8,16},{16,24},{1,9},{9,17},{17,25},{2,10},{10,18},{18,26},{... | collective-permute-start | bytes 552968 | tf_op jit(solution)/shard_map/ppermute | solution.py:17
  8.0 7.3 %collective-permute-start.1 = (bf16[4,64,360]{2,1,0:T(8,128)(2,1)S(1)}, bf16[4,64,360]{2,1,0:T(8,128)(2,1)S(1)}, u32[]{:S(2)}, u32[]{:S(2)}) collective-permute-start(bf16[4,64,360]{2,1,0:T(8,128)(2,1)S(1)} %get-tuple-element.31), channel_id=1, source_target_pairs={{8,0},{16,8},{24,16},{9,1},{17,9},{25,17},{10,2},{18,10},{26,18},{... | collective-permute-start | bytes 552968 | tf_op jit(solution)/shard_map/ppermute | solution.py:20
  9.7 12.8 %copy-start.7 = (f32[16,24,39,1,1]{2,1,0,4,3:T(8,128)S(1)}, f32[16,24,39,1,1]{2,1,0,4,3:T(8,128)}, u32[]{:S(2)}) copy-start(f32[16,24,39,1,1]{2,1,0,4,3:T(8,128)} %constant.99) | copy-start | bytes 179716
  15.4 47.6 %collective-permute-start.2 = (bf16[24,4,360]{2,1,0:T(4,128)(2,1)S(1)}, bf16[24,4,360]{2,1,0:T(4,128)(2,1)S(1)}, u32[]{:S(2)}, u32[]{:S(2)}) collective-permute-start(bf16[24,4,360]{2,1,0:T(4,128)(2,1)S(1)} %get-tuple-element.32), channel_id=1, source_target_pairs={{0,1},{1,2},{2,3},{3,4},{4,5},{5,6},{6,7},{8,9},{9,10},{10,11},{11... | collective-permute-start | bytes 207368 | tf_op jit(solution)/shard_map/ppermute | solution.py:17
  20.3 42.7 %collective-permute-start.3 = (bf16[24,4,360]{2,1,0:T(4,128)(2,1)S(1)}, bf16[24,4,360]{2,1,0:T(4,128)(2,1)}, u32[]{:S(2)}, u32[]{:S(2)}) collective-permute-start(bf16[24,4,360]{2,1,0:T(4,128)(2,1)S(1)} %get-tuple-element.33), channel_id=1, source_target_pairs={{1,0},{2,1},{3,2},{4,3},{5,4},{6,5},{7,6},{9,8},{10,9},{11,10},{12... | collective-permute-start | bytes 207368 | tf_op jit(solution)/shard_map/ppermute | solution.py:20
  79.4 19.1 %copy-start.3 = (bf16[4,576,180]{1,0,2:T(4,128)(2,1)S(1)}, bf16[4,576,180]{1,0,2:T(4,128)(2,1)}, u32[]{:S(2)}) copy-start(bf16[4,576,180]{1,0,2:T(4,128)(2,1)} %copy.38) | copy-start | bytes 2488324
  106.1 1.3 copy-start.2
  106.1 1.3 copy-start.9
  107.4 0.9 copy-start.11
  107.4 0.9 copy-start.13
  108.3 0.9 copy-start.12
  109.2 8.4 %copy-start.4 = (bf16[3,3,180,180]{3,2,1,0:T(8,128)(2,1)S(1)}, bf16[3,3,180,180]{3,2,1,0:T(8,128)(2,1)}, u32[]{:S(2)}) copy-start(bf16[3,3,180,180]{3,2,1,0:T(8,128)(2,1)} %param.20) | copy-start | bytes 1749604
  113.1 4.8 %collective-permute-start.4 = (bf16[1,64,180]{2,1,0:T(8,128)(2,1)S(1)}, bf16[1,64,180]{2,1,0:T(8,128)(2,1)S(1)}, u32[]{:S(2)}, u32[]{:S(2)}) collective-permute-start(bf16[1,64,180]{2,1,0:T(8,128)(2,1)S(1)} %get-tuple-element.44), channel_id=1, source_target_pairs={{0,8},{8,16},{16,24},{1,9},{9,17},{17,25},{2,10},{10,18},{18,26},{... | collective-permute-start | bytes 69128 | tf_op jit(solution)/shard_map/ppermute | solution.py:17
  116.3 4.7 %collective-permute-start.5 = (bf16[1,64,180]{2,1,0:T(8,128)(2,1)S(1)}, bf16[1,64,180]{2,1,0:T(8,128)(2,1)S(1)}, u32[]{:S(2)}, u32[]{:S(2)}) collective-permute-start(bf16[1,64,180]{2,1,0:T(8,128)(2,1)S(1)} %get-tuple-element.45), channel_id=1, source_target_pairs={{8,0},{16,8},{24,16},{9,1},{17,9},{25,17},{10,2},{18,10},{26,18},{... | collective-permute-start | bytes 69128 | tf_op jit(solution)/shard_map/ppermute | solution.py:20
  121.0 8.5 %collective-permute-start.6 = (bf16[18,1,180]{2,1,0:T(2,128)(2,1)S(1)}, bf16[18,1,180]{2,1,0:T(2,128)(2,1)S(1)}, u32[]{:S(2)}, u32[]{:S(2)}) collective-permute-start(bf16[18,1,180]{2,1,0:T(2,128)(2,1)S(1)} %get-tuple-element.40), channel_id=1, source_target_pairs={{0,1},{1,2},{2,3},{3,4},{4,5},{5,6},{6,7},{8,9},{9,10},{10,11},{11... | collective-permute-start | bytes 19448 | tf_op jit(solution)/shard_map/ppermute | solution.py:17
  127.0 6.0 %collective-permute-start.7 = (bf16[18,1,180]{2,1,0:T(2,128)(2,1)S(1)}, bf16[18,1,180]{2,1,0:T(2,128)(2,1)S(1)}, u32[]{:S(2)}, u32[]{:S(2)}) collective-permute-start(bf16[18,1,180]{2,1,0:T(2,128)(2,1)S(1)} %get-tuple-element.41), channel_id=1, source_target_pairs={{1,0},{2,1},{3,2},{4,3},{5,4},{6,5},{7,6},{9,8},{10,9},{11,10},{12... | collective-permute-start | bytes 19448 | tf_op jit(solution)/shard_map/ppermute | solution.py:20
  134.8 5.0 %copy-start.5 = (bf16[3,3,180,64]{2,3,1,0:T(8,128)(2,1)S(1)}, bf16[3,3,180,64]{2,3,1,0:T(8,128)(2,1)}, u32[]{:S(2)}) copy-start(bf16[3,3,180,64]{2,3,1,0:T(8,128)(2,1)} %param.21) | copy-start | bytes 622084
  135.3 4.8 %collective-permute-start.8 = (bf16[1,64,180]{2,1,0:T(8,128)(2,1)S(1)}, bf16[1,64,180]{2,1,0:T(8,128)(2,1)S(1)}, u32[]{:S(2)}, u32[]{:S(2)}) collective-permute-start(bf16[1,64,180]{2,1,0:T(8,128)(2,1)S(1)} %get-tuple-element.42), channel_id=1, source_target_pairs={{0,8},{8,16},{16,24},{1,9},{9,17},{17,25},{2,10},{10,18},{18,26},{... | collective-permute-start | bytes 69128 | tf_op jit(solution)/shard_map/ppermute | solution.py:17
  138.5 4.7 %collective-permute-start.9 = (bf16[1,64,180]{2,1,0:T(8,128)(2,1)S(1)}, bf16[1,64,180]{2,1,0:T(8,128)(2,1)S(1)}, u32[]{:S(2)}, u32[]{:S(2)}) collective-permute-start(bf16[1,64,180]{2,1,0:T(8,128)(2,1)S(1)} %get-tuple-element.43), channel_id=1, source_target_pairs={{8,0},{16,8},{24,16},{9,1},{17,9},{25,17},{10,2},{18,10},{26,18},{... | collective-permute-start | bytes 69128 | tf_op jit(solution)/shard_map/ppermute | solution.py:20
  143.2 6.2 %collective-permute-start.10 = (bf16[18,1,180]{2,1,0:T(2,128)(2,1)S(1)}, bf16[18,1,180]{2,1,0:T(2,128)(2,1)S(1)}, u32[]{:S(2)}, u32[]{:S(2)}) collective-permute-start(bf16[18,1,180]{2,1,0:T(2,128)(2,1)S(1)} %get-tuple-element.36), channel_id=1, source_target_pairs={{0,1},{1,2},{2,3},{3,4},{4,5},{5,6},{6,7},{8,9},{9,10},{10,11},{11... | collective-permute-start | bytes 19448 | tf_op jit(solution)/shard_map/ppermute | solution.py:17
  146.5 6.0 %collective-permute-start.11 = (bf16[18,1,180]{2,1,0:T(2,128)(2,1)S(1)}, bf16[18,1,180]{2,1,0:T(2,128)(2,1)S(1)}, u32[]{:S(2)}, u32[]{:S(2)}) collective-permute-start(bf16[18,1,180]{2,1,0:T(2,128)(2,1)S(1)} %get-tuple-element.37), channel_id=1, source_target_pairs={{1,0},{2,1},{3,2},{4,3},{5,4},{6,5},{7,6},{9,8},{10,9},{11,10},{12... | collective-permute-start | bytes 19448 | tf_op jit(solution)/shard_map/ppermute | solution.py:20
  154.3 3.3 %copy-start.6 = (bf16[3,3,64,256]{3,2,1,0:T(8,128)(2,1)S(1)}, bf16[3,3,64,256]{3,2,1,0:T(8,128)(2,1)}, u32[]{:S(2)}) copy-start(bf16[3,3,64,256]{3,2,1,0:T(8,128)(2,1)} %param.22) | copy-start | bytes 884740
  154.7 3.2 %collective-permute-start.12 = (bf16[64,1,64]{0,2,1:T(8,128)(2,1)S(1)}, bf16[64,1,64]{0,2,1:T(8,128)(2,1)S(1)}, u32[]{:S(2)}, u32[]{:S(2)}) collective-permute-start(bf16[64,1,64]{0,2,1:T(8,128)(2,1)S(1)} %get-tuple-element.50), channel_id=1, source_target_pairs={{0,8},{8,16},{16,24},{1,9},{9,17},{17,25},{2,10},{10,18},{18,26},{... | collective-permute-start | bytes 24584 | tf_op jit(solution)/shard_map/ppermute | solution.py:17
  156.3 4.5 %collective-permute-start.13 = (bf16[64,1,64]{0,2,1:T(8,128)(2,1)S(1)}, bf16[64,1,64]{0,2,1:T(8,128)(2,1)S(1)}, u32[]{:S(2)}, u32[]{:S(2)}) collective-permute-start(bf16[64,1,64]{0,2,1:T(8,128)(2,1)S(1)} %get-tuple-element.51), channel_id=1, source_target_pairs={{8,0},{16,8},{24,16},{9,1},{17,9},{25,17},{10,2},{18,10},{26,18},{... | collective-permute-start | bytes 24584 | tf_op jit(solution)/shard_map/ppermute | solution.py:20
  160.9 5.9 %collective-permute-start.14 = (bf16[64,18,1]{0,2,1:T(2,128)(2,1)S(1)}, bf16[64,18,1]{0,2,1:T(2,128)(2,1)S(1)}, u32[]{:S(2)}, u32[]{:S(2)}) collective-permute-start(bf16[64,18,1]{0,2,1:T(2,128)(2,1)S(1)} %get-tuple-element.48), channel_id=1, source_target_pairs={{0,1},{1,2},{2,3},{3,4},{4,5},{5,6},{6,7},{8,9},{9,10},{10,11},{11... | collective-permute-start | bytes 6920 | tf_op jit(solution)/shard_map/ppermute | solution.py:17
  164.2 5.9 %collective-permute-start.15 = (bf16[64,18,1]{0,2,1:T(2,128)(2,1)S(1)}, bf16[64,18,1]{0,2,1:T(2,128)(2,1)S(1)}, u32[]{:S(2)}, u32[]{:S(2)}) collective-permute-start(bf16[64,18,1]{0,2,1:T(2,128)(2,1)S(1)} %get-tuple-element.49), channel_id=1, source_target_pairs={{1,0},{2,1},{3,2},{4,3},{5,4},{6,5},{7,6},{9,8},{10,9},{11,10},{12... | collective-permute-start | bytes 6920 | tf_op jit(solution)/shard_map/ppermute | solution.py:20
  173.1 3.1 %copy-start.1 = (bf16[180,540]{1,0:T(8,128)(2,1)S(1)}, bf16[180,540]{1,0:T(8,128)(2,1)}, u32[]{:S(2)}) copy-start(bf16[180,540]{1,0:T(8,128)(2,1)} %param.14) | copy-start | bytes 583204
where the time goes:
time: 177 us; the launch traced here: 176 us
  matrix products  47.9 us (27%)
  starting transfers between devices  42.1 us (24%)
  local copies, waits for them, and re-layouts  36.6 us (21%)
  other arithmetic  25.4 us (14%)
  waiting for transfers between devices  23.5 us (13%)
    ppermute x8, starting transfers between devices, padded_2(): lax.ppermute(lax.slice_in_dim(block, block.shape[dim] - width, None, axis...  28.8 us
    ppermute x8, waiting for transfers between devices, padded_2(): lax.ppermute(lax.slice_in_dim(block, 0, width, axis=dim), axis, backward)  22.8 us
    sub x1, other arithmetic, attend_group(): probs = jax.nn.softmax(scores, axis=-1).astype(jnp.bfloat16)  19.1 us
    add x2, local copies, waits for them, and re-layouts, attend_group(): jnp.einsum('gqhd,gkhd->ghqk', qs, keys, preferred_element_type=jnp.float32)  18.8 us
    dot_general x1, matrix products, build_bias(): jnp.einsum('jqb,hipb->hijpq', selector, partial_rows, precision=lax.Preci...  18.2 us
    ppermute x8, starting transfers between devices, padded_2(): lax.ppermute(lax.slice_in_dim(block, 0, width, axis=dim), axis, backward)  13.3 us
    dot_general x1, matrix products, attend_group(): jnp.einsum('gqhd,gkhd->ghqk', qs, keys, preferred_element_type=jnp.float32)  7.14 us
    dot_general x1, matrix products, attend_group(): jnp.einsum('ghqk,gkhd->gqhd', probs, vals, preferred_element_type=jnp.flo...  6.31 us
  transfers between devices with their start and end apart: 16, of which 8 were waited for; matrix products, arithmetic and copies ran while one was open for 25% of the time, Pallas kernels for 0%

commit v1 on v0

v1 whole, which is shorter than its diff:
```python
import functools

import jax
import jax.numpy as jnp
import numpy as np
from jax import lax
from jax.experimental import pallas as pl
from jax.experimental.pallas import tpu as pltpu
from jax.sharding import PartitionSpec as P

HEADS = 6
HD = 30
HP = 32
WIN = 16
KWIN = 24
KEYS = KWIN * KWIN
CHUNKS = 3
CHUNK = KEYS // CHUNKS
SIDE = WIN + KWIN - 1
RIM = (KWIN - WIN) // 2
EDGE = WIN + 2 * RIM
STRIP = 8
LOG2E = 1.4426950408889634
F32 = jnp.float32
BF16 = jnp.bfloat16
NT = (((1,), (1,)), ((), ()))
TN = (((0,), (0,)), ((), ()))


def dot(a, b):
    return jnp.dot(a, b, preferred_element_type=F32)


def dot_nt(a, b):
    return lax.dot_general(a, b, NT, preferred_element_type=F32)


def layer_norm(values, gain):
    center = values - jnp.mean(values, axis=-1, keepdims=True)
    spread = jnp.mean(center * center, axis=-1, keepdims=True)
    return center * lax.rsqrt(spread + 1e-05) * gain


def call(kernel, out_shape, scratch, flops, bytes_accessed, smem=0):
    def run(*args):
        specs = [pl.BlockSpec(memory_space=pltpu.VMEM)] * len(args)
        for index in range(smem):
            specs[index] = pl.BlockSpec(memory_space=pltpu.SMEM)
        return pl.pallas_call(
            kernel,
            out_shape=out_shape,
            in_specs=specs,
            scratch_shapes=scratch,
            compiler_params=pltpu.CompilerParams(vmem_limit_bytes=24 * 2**20),
            cost_estimate=pl.CostEstimate(
                flops=flops, bytes_accessed=bytes_accessed, transcendentals=0
            ),
        )(*args)

    return run


def bias_kernel(table_ref, left_ref, border_ref, right_ref, middle_ref, t_scr, e_scr, w_scr, x_scr):
    for d in range(SIDE):
        t_scr[8 * d : 8 * d + HEADS, 0:SIDE] = jnp.exp(table_ref[:, SIDE * d : SIDE * (d + 1)])

    def head(h, carry):
        values = t_scr[pl.ds(h, SIDE, stride=8), 0:SIDE].astype(BF16)

        def expand(cols, first):
            width = -(-SIDE * cols // 128) * 128
            spot = lax.broadcasted_iota(jnp.int32, (SIDE, width), 1) // cols
            row = lax.broadcasted_iota(jnp.int32, (SIDE, width), 0)
            pick = (spot == SIDE - 1 - row).astype(F32).astype(BF16)
            e_scr[0:SIDE, 0:width] = lax.dot_general(values, pick, TN, preferred_element_type=F32)
            lane = lax.broadcasted_iota(jnp.int32, (KWIN, width), 1) % cols
            out = jnp.zeros((KWIN, width), F32)
            for jj in range(cols):
                start = WIN - 1 - first - jj
                out = jnp.where(lane == jj, e_scr[start : start + KWIN, 0:width], out)
            w_scr[:, 0:width] = out

        lanes = lax.broadcasted_iota(jnp.int32, (KWIN, 128), 1)
        expand(WIN, 0)
        for p in range(KWIN):
            rows = slice(p * KWIN, (p + 1) * KWIN)
            low = w_scr[:, (23 - p) * WIN : (23 - p) * WIN + 128]
            high = w_scr[:, (31 - p) * WIN : (31 - p) * WIN + 128]
            x_scr[0, rows] = jnp.where(lanes < 64, low, high)
            x_scr[1, rows] = w_scr[:, (27 - p) * WIN : (27 - p) * WIN + 128]
        border_ref[h] = x_scr[0].astype(BF16)
        middle_ref[h] = x_scr[1].astype(BF16)
        for out_ref, first in ((left_ref, WIN - STRIP), (right_ref, 0)):
            expand(STRIP, first)
            for p in range(KWIN):
                rows = slice(p * KWIN, (p + 1) * KWIN)
                x_scr[0, rows] = w_scr[:, (23 - p) * STRIP : (23 - p) * STRIP + 128]
            out_ref[h] = x_scr[0].astype(BF16)
        return carry

    lax.fori_loop(0, HEADS, head, 0)


def build_bias(bias_table):
    return call(
        bias_kernel,
        [jax.ShapeDtypeStruct((HEADS, KEYS, 128), BF16)] * 4,
        [
            pltpu.VMEM((8 * SIDE, 128), F32),
            pltpu.VMEM((SIDE + 1, 640), F32),
            pltpu.VMEM((KWIN, 640), F32),
            pltpu.VMEM((2, KEYS, 128), F32),
        ],
        4_000_000_000,
        4_000_000,
    )(bias_table.T)


def one_hot(shape, row_of, col_of):
    row = lax.broadcasted_iota(jnp.int32, shape, 0)
    col = lax.broadcasted_iota(jnp.int32, shape, 1)
    return (row_of(row) == col_of(col)).astype(F32).astype(BF16)


def spread_head(place):
    return jnp.where(place % HP < HD, place // HP * HD + place % HP, -1)


def weights_into(qkv_ref, proj_ref, wk_ref, wqv_ref, wp_ref):
    chans = qkv_ref.shape[0]
    width = HEADS * HP
    qkv = qkv_ref[...]
    pick = one_hot(
        (3 * chans, 3 * 128),
        lambda row: row,
        lambda col: jnp.where(
            (col % 128 < 2 * HP) & (col % HP < HD),
            chans + (col // 128 * 2 + col % 128 // HP) * HD + col % HP,
            -1,
        ),
    )
    wk_ref[...] = dot(qkv, pick).astype(BF16)
    pick = one_hot(
        (2 * width, 3 * chans),
        lambda row: jnp.where(
            row % HP < HD, row // HP * HD + row % HP + jnp.where(row < width, 0, chans), -1
        ),
        lambda col: col,
    )
    wqv_ref[...] = dot_nt(pick, qkv).astype(BF16)
    pick = one_hot((width, chans), spread_head, lambda col: col)
    wp_ref[...] = dot(pick, proj_ref[...]).astype(BF16)


def set_queries(q_scr, wqv_ref, groups):
    scale = LOG2E / np.sqrt(HD)
    rows = jnp.concatenate([rows.reshape(128, rows.shape[2]) for rows in groups], axis=0)
    queries = (dot_nt(wqv_ref[0 : HEADS * HP], rows.astype(BF16)) * scale).astype(BF16)
    none = jnp.zeros((HP, 128), BF16)
    for g in range(len(groups)):
        lanes = slice(128 * g, 128 * g + 128)
        for t in range(HEADS // 2):
            one = queries[2 * t * HP : (2 * t + 1) * HP, lanes]
            two = queries[(2 * t + 1) * HP : (2 * t + 2) * HP, lanes]
            q_scr[g, t, 0:HP] = jnp.concatenate([one, none], axis=1)
            q_scr[g, t, HP : 2 * HP] = jnp.concatenate([none, two], axis=1)


class BiasCopies:
    def __init__(self, bias_refs, bias_scr, sem):
        self.copies = [
            pltpu.make_async_copy(ref, bias_scr.at[index], sem.at[index])
            for index, ref in enumerate(bias_refs)
        ]

    def start(self):
        for copy in self.copies:
            copy.start()

    def wait(self):
        for copy in self.copies:
            copy.wait()


def lookup(g, values):
    out = values[0]
    for index in range(1, len(values)):
        out = jnp.where(g >= index, values[index], out)
    return out


def attention(kinds, windows, q_scr, k_ref, v_ref, bias_ref, wp_ref, p_scr, a_scr, o_scr):
    groups = len(windows)
    pairs = HEADS // 2
    stages = [(c, t) for c in range(CHUNKS) for t in range(pairs)]

    def sum_values(g, c, t, slot):
        part = dot(v_ref[lookup(g, windows), c, 2 * t * HP : 2 * (t + 1) * HP], p_scr[slot])
        o_scr[g, t] = part if c == 0 else o_scr[g, t] * a_scr[slot] + part

    p_scr[(len(stages) - 1) % 3] = jnp.zeros((CHUNK, 256), BF16)
    a_scr[(len(stages) - 1) % 3] = jnp.zeros((1, 256), F32)
    o_scr[0, pairs - 1] = jnp.zeros((2 * HP, 256), F32)

    def attend(g, carry):
        window = lookup(g, windows)
        tops = [None] * pairs
        for n, (c, t) in enumerate(stages):
            rows = slice(CHUNK * c, CHUNK * (c + 1))
            s = dot(k_ref[window, rows, 128 * t : 128 * t + 2 * HP], q_scr[g, t])
            top = jnp.max(jnp.max(s.reshape(CHUNK // 8, 8, 256), axis=0), axis=0, keepdims=True)
            if c > 0:
                top = jnp.maximum(top, tops[t])
            if n == 0:
                sum_values(jnp.maximum(g - 1, 0), *stages[-1], (len(stages) - 1) % 3)
            else:
                sum_values(g, *stages[n - 1], (n - 1) % 3)
            if c > 0:
                a_scr[n % 3] = jnp.exp2(tops[t] - top)
            tops[t] = top
            prob = jnp.exp2(s - top).astype(BF16)
            for half in range(2):
                lanes = slice(128 * half, 128 * half + 128)
                head = 2 * t + half
                bias = bias_ref[head, rows] if kinds is None else bias_ref[lookup(g, kinds), head, rows]
                p_scr[n % 3, :, lanes] = prob[:, lanes] * bias
        return carry

    lax.fori_loop(0, groups, attend, 0)
    sum_values(groups - 1, *stages[-1], (len(stages) - 1) % 3)
    attended = []
    for g in range(groups):
        parts = []
        for t in range(pairs):
            for half in range(2):
                lanes = slice(128 * half, 128 * half + 128)
                one = o_scr[g, t, half * HP : (half + 1) * HP, lanes]
                parts.append((one * (1.0 / one[HD : HD + 1])).astype(BF16))
        attended.append(jnp.concatenate(parts, axis=0))
    attended = jnp.concatenate(attended, axis=1)
    return lax.dot_general(attended, wp_ref[...], TN, preferred_element_type=F32)


def feed_forward(first, gain, hidden_ref, output_ref):
    normed = layer_norm(first, gain).astype(BF16)
    inner = dot(normed, hidden_ref[...])
    inner = (0.5 * inner * (1.0 + lax.erf(inner * np.float32(np.sqrt(0.5))))).astype(BF16)
    return first + dot_nt(inner, output_ref[...])


def project(keys, wk_ref, wqv_ref, k_ref, v_ref, index):
    width = HEADS * HP
    one_row = (lax.broadcasted_iota(jnp.int32, (width, 1), 0) % HP == HD).astype(F32)
    keys = keys.reshape(KEYS, keys.shape[2]).astype(BF16)
    k_ref[index] = dot(keys, wk_ref[...]).astype(BF16)
    for c in range(CHUNKS):
        part = keys[CHUNK * c : CHUNK * (c + 1)]
        v_ref[index, c] = (dot_nt(wqv_ref[width : 2 * width], part) + one_row).astype(BF16)


def from_sides(even, first, second):
    first, second = first.astype(F32), second.astype(F32)
    return jnp.where(even, second, first), jnp.where(even, first, second)


def border_rows(ref, c0):
    return jnp.concatenate([ref[0:4, c0 : c0 + WIN], ref[12:16, c0 : c0 + WIN]], axis=0)


def inner_kernel(
    flags,
    own_ref,
    row_one_ref,
    row_two_ref,
    gain_one_ref,
    qkv_ref,
    proj_ref,
    border_bias_ref,
    middle_bias_ref,
    gain_two_ref,
    hidden_ref,
    output_ref,
    nrm_ref,
    wk_ref,
    wqv_ref,
    wp_ref,
    k_ref,
    v_ref,
    border_ref,
    mid_ref,
    q_scr,
    p_scr,
    a_scr,
    o_scr,
    bias_scr,
    sem,
):
    height, cols, chans = own_ref.shape
    inner = cols // WIN - 2
    copies = BiasCopies((border_bias_ref, middle_bias_ref), bias_scr, sem)
    copies.start()
    weights_into(qkv_ref, proj_ref, wk_ref, wqv_ref, wp_ref)
    gain_one = gain_one_ref[...]
    for r in range(RIM):
        above, below = from_sides(flags[4] > 0, row_one_ref[r], row_two_ref[r])
        nrm_ref[r] = layer_norm(above, gain_one)
        nrm_ref[RIM + height + r] = layer_norm(below, gain_one)
    for r in range(height):
        nrm_ref[RIM + r] = layer_norm(own_ref[r].astype(F32), gain_one)
    kinds, windows, first, queries = [], [], [], []
    for w in range(inner):
        c0 = WIN * (w + 1)
        project(nrm_ref[:, c0 - RIM : c0 - RIM + KWIN], wk_ref, wqv_ref, k_ref, v_ref, w)
        first.append(border_rows(own_ref, c0).reshape(128, chans))
        queries.append(border_rows(nrm_ref.at[RIM : RIM + height], c0))
        kinds.append(0)
        windows.append(w)
    for w in range(inner - 1):
        c0 = WIN * (w + 1)
        first.append(own_ref[4:12, c0 : c0 + WIN].reshape(128, chans))
        queries.append(nrm_ref[RIM + 4 : RIM + 12, c0 : c0 + WIN])
        kinds.append(1)
        windows.append(w)
    groups = len(kinds)
    set_queries(q_scr, wqv_ref, queries)
    copies.wait()
    first = jnp.concatenate(first, axis=0).astype(F32) + attention(
        kinds, windows, q_scr, k_ref, v_ref, bias_scr, wp_ref, p_scr, a_scr, o_scr
    )
    mixed = feed_forward(first, gain_two_ref[...], hidden_ref, output_ref)
    mixed = mixed.reshape(groups, 8, WIN, chans)
    for g in range(groups):
        if g < inner:
            border_ref[:, WIN * g : WIN * (g + 1)] = mixed[g]
        else:
            mid_ref[:, WIN * (g - inner) : WIN * (g - inner + 1)] = mixed[g]


def outer_kernel(
    flags,
    own_ref,
    nrm_ref,
    col_one_ref,
    col_two_ref,
    gain_one_ref,
    wk_ref,
    wqv_ref,
    wp_ref,
    inner_k_ref,
    inner_v_ref,
    inner_border_ref,
    left_bias_ref,
    border_bias_ref,
    right_bias_ref,
    gain_two_ref,
    hidden_ref,
    output_ref,
    pay_one_ref,
    pay_two_ref,
    edge_ref,
    side_ref,
    k_ref,
    v_ref,
    side_scr,
    x_scr,
    q_scr,
    p_scr,
    a_scr,
    o_scr,
    bias_scr,
    sem,
    image,
):
    height, cols, chans = own_ref.shape
    inner = cols // WIN - 2
    copies = BiasCopies((left_bias_ref, border_bias_ref, right_bias_ref), bias_scr, sem)
    copies.start()
    gain_one = gain_one_ref[...]
    for r in range(height + 2 * RIM):
        both = from_sides(flags[5] > 0, col_one_ref[r], col_two_ref[r])
        for side in range(2):
            if RIM <= r < RIM + height:
                x_scr[side, r - RIM] = both[side]
            side_scr[side, r, side * EDGE : (side + 1) * EDGE] = layer_norm(both[side], gain_one)
    side_scr[0, :, EDGE : 2 * EDGE] = nrm_ref[:, 0:EDGE]
    side_scr[1, :, 0:EDGE] = nrm_ref[:, cols - EDGE : cols]
    k_ref[2] = inner_k_ref[inner - 1]
    v_ref[2] = inner_v_ref[inner - 1]
    for index, side, c0 in ((0, 0, RIM), (1, 0, RIM + WIN), (3, 1, RIM), (4, 1, RIM + WIN)):
        project(side_scr[side, :, c0 : c0 + KWIN], wk_ref, wqv_ref, k_ref, v_ref, index)
    spots = (EDGE - STRIP, 0, cols - WIN, EDGE)
    first, queries = [], []
    for g in range(4):
        side, c0 = g // 2, spots[g]
        if g in (0, 3):
            x = x_scr[side, :, c0 - side * EDGE : c0 - side * EDGE + STRIP]
            queries.append(side_scr[side, RIM : RIM + height, c0 : c0 + STRIP])
        else:
            x = border_rows(own_ref, c0).astype(F32)
            queries.append(border_rows(nrm_ref.at[RIM : RIM + height], c0))
        first.append(x.reshape(128, chans))
    set_queries(q_scr, wqv_ref, queries)
    copies.wait()
    first = jnp.concatenate(first, axis=0) + attention(
        [0, 1, 1, 2], [0, 1, 3, 4], q_scr, k_ref, v_ref, bias_scr, wp_ref, p_scr, a_scr, o_scr
    )
    image[0:4, STRIP + WIN : STRIP + cols - WIN] = inner_border_ref[0:4]
    image[12:16, STRIP + WIN : STRIP + cols - WIN] = inner_border_ref[4:8]
    for pair in range(2):
        mixed = feed_forward(first[256 * pair : 256 * pair + 256], gain_two_ref[...], hidden_ref, output_ref)
        for s in range(2):
            g = 2 * pair + s
            one = mixed[s * 128 : (s + 1) * 128]
            if g in (0, 3):
                one = jnp.where(flags[g // 3] > 0, 0.0, one).reshape(height, STRIP, chans)
                c0 = 0 if g == 0 else STRIP + cols
                image[:, c0 : c0 + STRIP] = one
            else:
                one = one.reshape(8, WIN, chans)
                c0 = STRIP + spots[g]
                image[0:4, c0 : c0 + WIN] = one[0:4]
                image[12:16, c0 : c0 + WIN] = one[4:8]
    even = flags[4] > 0
    pay_one_ref[...] = jnp.where(even, image[13:16], image[0:3]).astype(BF16)
    pay_two_ref[...] = jnp.where(even, image[0:3], image[13:16]).astype(BF16)
    edge_ref[0:4] = image[0:4]
    edge_ref[4:8] = image[12:16]
    side_ref[:, 0:STRIP] = image[4:12, 0:STRIP]
    side_ref[:, STRIP : 2 * STRIP] = image[4:12, STRIP + cols :]


def middle_kernel(
    own_ref,
    nrm_ref,
    k_ref,
    v_ref,
    wqv_ref,
    wp_ref,
    inner_mid_ref,
    middle_bias_ref,
    gain_two_ref,
    hidden_ref,
    output_ref,
    mid_ref,
    q_scr,
    p_scr,
    a_scr,
    o_scr,
):
    height, cols, chans = own_ref.shape
    spots = (0, cols - 2 * WIN, cols - WIN)
    set_queries(q_scr, wqv_ref, [nrm_ref[RIM + 4 : RIM + 12, c0 : c0 + WIN] for c0 in spots])
    first = [own_ref[4:12, c0 : c0 + WIN].reshape(128, chans) for c0 in spots]
    first = jnp.concatenate(first, axis=0).astype(F32) + attention(
        None, [1, 2, 3], q_scr, k_ref, v_ref, middle_bias_ref, wp_ref, p_scr, a_scr, o_scr
    )
    mixed = feed_forward(first, gain_two_ref[...], hidden_ref, output_ref)
    mixed = mixed.reshape(3, 8, WIN, chans)
    mid_ref[:, WIN : cols - 2 * WIN] = inner_mid_ref[...]
    for g in range(3):
        mid_ref[:, spots[g] : spots[g] + WIN] = mixed[g]


def attention_scratch(groups, kinds):
    scratch = [
        pltpu.VMEM((groups, HEADS // 2, 2 * HP, 256), BF16),
        pltpu.VMEM((3, CHUNK, 256), BF16),
        pltpu.VMEM((3, 1, 256), F32),
        pltpu.VMEM((groups, HEADS // 2, 2 * HP, 256), F32),
    ]
    if kinds:
        scratch.append(pltpu.VMEM((kinds, HEADS, KEYS, 128), BF16))
        scratch.append(pltpu.SemaphoreType.DMA((kinds,)))
    return scratch


def inner_block(*args):
    height, cols, chans = args[1].shape
    inner = cols // WIN - 2
    width = HEADS * HP
    groups = 2 * inner - 1
    return call(
        inner_kernel,
        (
            jax.ShapeDtypeStruct((height + 2 * RIM, cols, chans), F32),
            jax.ShapeDtypeStruct((chans, 3 * 128), BF16),
            jax.ShapeDtypeStruct((2 * width, chans), BF16),
            jax.ShapeDtypeStruct((width, chans), BF16),
            jax.ShapeDtypeStruct((inner, KEYS, 3 * 128), BF16),
            jax.ShapeDtypeStruct((inner, CHUNKS, width, CHUNK), BF16),
            jax.ShapeDtypeStruct((8, WIN * inner, chans), F32),
            jax.ShapeDtypeStruct((8, WIN * (inner - 1), chans), F32),
        ),
        attention_scratch(groups, 2),
        5_000_000_000,
        4_000_000,
        smem=1,
    )(*args)


def outer_block(*args):
    height, cols, chans = args[1].shape
    span = cols + 2 * STRIP
    return call(
        outer_kernel,
        (
            jax.ShapeDtypeStruct((3, span, chans), BF16),
            jax.ShapeDtypeStruct((3, span, chans), BF16),
            jax.ShapeDtypeStruct((8, span, chans), F32),
            jax.ShapeDtypeStruct((8, 2 * STRIP, chans), F32),
            jax.ShapeDtypeStruct((5, KEYS, 3 * 128), BF16),
            jax.ShapeDtypeStruct((5, CHUNKS, HEADS * HP, CHUNK), BF16),
        ),
        [
            pltpu.VMEM((2, height + 2 * RIM, 2 * EDGE, chans), F32),
            pltpu.VMEM((2, height, EDGE, chans), F32),
            *attention_scratch(4, 3),
            pltpu.VMEM((height, span, chans), F32),
        ],
        5_000_000_000,
        4_000_000,
        smem=1,
    )(*args)


def middle_block(*args):
    height, cols, chans = args[0].shape
    return call(
        middle_kernel,
        jax.ShapeDtypeStruct((8, cols, chans), F32),
        attention_scratch(3, 0),
        5_000_000_000,
        4_000_000,
    )(*args)


def conv_kernel(
    flags,
    own_ref,
    row_one_ref,
    row_two_ref,
    col_one_ref,
    col_two_ref,
    back_one_ref,
    back_two_ref,
    edge_ref,
    side_ref,
    mid_ref,
    group_ref,
    before_ref,
    upsample_ref,
    out_ref,
    base,
    image,
    taps,
    grouped,
    sums,
    lowfeat,
    low_taps,
    out_scr,
    wg_scr,
    wb_scr,
    wu_scr,
):
    height, cols, chans = own_ref.shape
    span = cols + 2 * STRIP
    at_left, at_right, at_top, at_bottom = (flags[i] > 0 for i in range(4))
    even_row, even_col = flags[4] > 0, flags[5] > 0

    feats = before_ref.shape[2]
    pad = chans // 16 * 16
    for a in range(3):
        wb_scr[256 * a + pad : 256 * (a + 1)] = jnp.zeros((256 - pad, 3 * feats), BF16)
        wu_scr[256 * a + 3 * feats : 256 * (a + 1)] = jnp.zeros((256 - 3 * feats, 4 * feats), BF16)
        for b in range(3):
            wg_scr[256 * (3 * a + b) + pad : 256 * (3 * a + b + 1)] = jnp.zeros((256 - pad, chans), BF16)
            wg_scr[256 * (3 * a + b) : 256 * (3 * a + b) + chans] = group_ref[a, b]
    same = one_hot((chans, chans), lambda row: row, lambda col: col)
    order = one_hot(
        (4 * feats, 4 * feats), lambda row: row, lambda col: col % feats * 4 + col // feats
    )
    for a in range(3):
        part = before_ref[a].reshape(3 * feats, chans)
        wb_scr[256 * a : 256 * a + chans] = dot_nt(same, part).astype(BF16)
        part = upsample_ref[a].reshape(3 * feats, 4 * feats)
        wu_scr[256 * a : 256 * a + 3 * feats] = dot(part, order).astype(BF16)

    above, below = from_sides(even_row, row_one_ref[...], row_two_ref[...])
    base[0:2, STRIP : STRIP + cols] = above[2:4]
    base[2 : 2 + height, STRIP : STRIP + cols] = own_ref[...].astype(F32)
    base[2 + height : 4 + height, STRIP : STRIP + cols] = below[0:2]
    rows = slice(2, height + 6)
    before_side, after_side = from_sides(even_col, col_one_ref[rows], col_two_ref[rows])
    base[:, 0:STRIP] = before_side[:, EDGE - STRIP :]
    base[:, STRIP + cols : span] = after_side[:, 0:STRIP]
    base[:, span:] = jnp.zeros((height + 4, STRIP, chans), F32)
    image[:, span:] = jnp.zeros((height + 6, STRIP, chans), F32)
    above, below = from_sides(even_row, back_one_ref[...], back_two_ref[...])
    image[0:3, 0:span] = above
    image[3:7, 0:span] = edge_ref[0:4]
    image[7:15, 0:STRIP] = side_ref[:, 0:STRIP]
    image[7:15, STRIP : STRIP + cols] = mid_ref[...]
    image[7:15, STRIP + cols : span] = side_ref[:, STRIP : 2 * STRIP]
    image[15:19, 0:span] = edge_ref[4:8]
    image[19:22, 0:span] = below
    taps[...] = jnp.zeros(taps.shape, BF16)
    grouped[...] = jnp.zeros(grouped.shape, BF16)
    part = 4
    col = lax.broadcasted_iota(jnp.int32, (span, chans), 0) - 2
    keep_grouped = (col < cols + 2) & ((col >= 0) | jnp.logical_not(at_left))
    keep_grouped = keep_grouped & ((col < cols) | jnp.logical_not(at_right))
    low_span = cols + 8
    col = lax.broadcasted_iota(jnp.int32, (low_span, 128), 0) - 1
    keep_low = (col <= cols) & ((col >= 0) | jnp.logical_not(at_left))
    keep_low = keep_low & ((col < cols) | jnp.logical_not(at_right))
    left_half = lax.broadcasted_iota(jnp.int32, (cols, 128), 1) < feats
    spot = lax.broadcasted_iota(jnp.int32, (256, 256), 0)
    place = lax.broadcasted_iota(jnp.int32, (256, 256), 1)
    spread = (spot % 128 // cols == place // 128) & (
        spot % cols * 2 + spot // 128 == place % 128
    )
    spread = spread.astype(F32).astype(BF16)

    def fill_taps(first, last):
        for b in range(3):
            start = STRIP - 3 + b
            taps[first:last, :, 256 * b : 256 * b + chans] = image[
                first:last, start : start + span, :
            ].astype(BF16)

    def group(h):
        lhs = jnp.concatenate(
            [taps[h + a : h + a + part].reshape(part * span, 768) for a in range(3)], axis=1
        )
        total = dot(lhs, wg_scr[...]).reshape(part, span, chans)
        total = total + base[h : h + part, STRIP - 2 : STRIP - 2 + span, :]
        for r in range(part):
            mask = keep_grouped
            if h + r < 2:
                mask = mask & jnp.logical_not(at_top)
            if h + r >= height + 2:
                mask = mask & jnp.logical_not(at_bottom)
            grouped[h + r, 0:span, 0:chans] = jnp.where(mask, total[r], 0.0).astype(BF16)

    def narrow(h, count):
        lhs = jnp.concatenate(
            [grouped[h + a : h + a + count].reshape(count * span, 256) for a in range(3)], axis=1
        )
        slot = h // part % 2
        sums[slot, 0:count, :, 0 : 3 * feats] = dot(lhs, wb_scr[...]).reshape(count, span, 3 * feats)
        for r in range(count):
            total = sums[slot, r, 0:low_span, 0:128]
            total = total + pltpu.roll(sums[slot, r, 1 : low_span + 1, 0:128], feats, 1)
            total = total + sums[slot, r, 2 : low_span + 2, 128:256]
            mask = keep_low
            if h + r == 0:
                mask = mask & jnp.logical_not(at_top)
            if h + r == height + 1:
                mask = mask & jnp.logical_not(at_bottom)
            lowfeat[h + r] = jnp.where(mask, jnp.where(total >= 0, total, 0.01 * total), 0.0)
            low_taps[h + r, :, 0:128] = jnp.where(
                left_half, lowfeat[h + r, 0:cols], pltpu.roll(lowfeat[h + r, 1 : cols + 1], feats, 1)
            ).astype(BF16)
            low_taps[h + r, :, 128:256] = jnp.where(
                left_half, lowfeat[h + r, 2 : cols + 2], 0.0
            ).astype(BF16)

    def expand(h):
        lhs = jnp.concatenate(
            [low_taps[h + a : h + a + part].reshape(part * cols, 256) for a in range(3)], axis=1
        )
        total = dot(lhs, wu_scr[...])
        for pair in range(part // 2):
            turned = total[2 * cols * pair : 2 * cols * (pair + 1)].T.astype(BF16)
            lhs = [
                jnp.concatenate(
                    [turned[(2 * a + b) * feats : (2 * a + b + 1) * feats] for b in range(2)], axis=1
                )
                for a in range(2)
            ]
            final = dot(jnp.concatenate(lhs, axis=0), spread)
            for r in range(2):
                for a in range(2):
                    row = 2 * (h + 2 * pair + r) + a
                    out_scr[pl.ds(row, feats, stride=2 * height), :] = final[
                        a * feats : (a + 1) * feats, 128 * r : 128 * (r + 1)
                    ]

    fill_taps(0, part + 2)
    narrowed = expanded = done = 0
    while expanded < height:
        expand_to, narrow_to = min(narrowed - 2, height), min(done - 2, height + 2)
        if done < height + 4:
            if done + part < height + 4:
                fill_taps(done + part + 2, done + 2 * part + 2)
            group(done)
            done += part
        while narrowed < narrow_to:
            count = min(part, height + 2 - narrowed)
            if narrowed + count > narrow_to:
                break
            narrow(narrowed, count)
            narrowed += count
        while expanded + part <= expand_to:
            expand(expanded)
            expanded += part
    out_ref[...] = out_scr[...].reshape(feats, 2 * height, 128).astype(BF16)


def convs(*args):
    height, cols, chans = args[1].shape
    span = cols + 2 * STRIP
    feats = args[-2].shape[2]
    return call(
        conv_kernel,
        jax.ShapeDtypeStruct((feats, 2 * height, 2 * cols), BF16),
        [
            pltpu.VMEM((height + 4, span + STRIP, chans), F32),
            pltpu.VMEM((height + 6, span + STRIP, chans), F32),
            pltpu.VMEM((height + 6, span, 768), BF16),
            pltpu.VMEM((height + 4, span, 256), BF16),
            pltpu.VMEM((2, 4, span, 256), F32),
            pltpu.VMEM((height + 2, cols + 8, 128), F32),
            pltpu.VMEM((height + 2, cols, 256), BF16),
            pltpu.VMEM((feats * 2 * height, 128), F32),
            pltpu.VMEM((9 * 256, chans), BF16),
            pltpu.VMEM((3 * 256, 3 * feats), BF16),
            pltpu.VMEM((3 * 256, 4 * feats), BF16),
        ],
        8_000_000_000,
        4_000_000,
        smem=1,
    )(*args)


def swapped(axis, first, second):
    count = lax.axis_size(axis)
    out = []
    for start, payload in ((0, first), (1, second)):
        pairs = [(i, i + 1) for i in range(start, count - 1, 2)]
        pairs = pairs + [(b, a) for a, b in pairs]
        out.append(lax.ppermute(payload, axis, pairs))
    return out


def on_device(
    features,
    gain_one,
    qkv_weight,
    bias_table,
    proj_weight,
    gain_two,
    hidden_weight,
    output_weight,
    group_conv,
    before_conv,
    upsample_conv,
):
    height, cols, chans = features.shape
    row, column = lax.axis_index("rows"), lax.axis_index("cols")
    even_row, even_col = row % 2 == 0, column % 2 == 0
    flags = jnp.stack(
        [
            column == 0,
            column == lax.axis_size("cols") - 1,
            row == 0,
            row == lax.axis_size("rows") - 1,
            even_row,
            even_col,
        ]
    ).astype(jnp.int32)

    low, high = features[:RIM], features[height - RIM :]
    row_one, row_two = swapped(
        "rows", jnp.where(even_row, high, low), jnp.where(even_row, low, high)
    )
    above, below = jnp.where(even_row, row_two, row_one), jnp.where(even_row, row_one, row_two)
    low, high = (
        jnp.concatenate([part[:, span] for part in (above, features, below)], axis=0)
        for span in (slice(0, EDGE), slice(cols - EDGE, cols))
    )
    col_one, col_two = swapped(
        "cols", jnp.where(even_col, high, low), jnp.where(even_col, low, high)
    )

    left_bias, border_bias, right_bias, middle_bias = build_bias(bias_table)
    gain_one, gain_two = gain_one.reshape(1, chans), gain_two.reshape(1, chans)
    post = (gain_two, hidden_weight, output_weight.T)
    nrm, wk, wqv, wp, inner_k, inner_v, inner_border, inner_mid = inner_block(
        flags,
        features,
        row_one,
        row_two,
        gain_one,
        qkv_weight,
        proj_weight,
        border_bias,
        middle_bias,
        *post,
    )
    back_one, back_two, edge, side, keys, values = outer_block(
        flags,
        features,
        nrm,
        col_one,
        col_two,
        gain_one,
        wk,
        wqv,
        wp,
        inner_k,
        inner_v,
        inner_border,
        left_bias,
        border_bias,
        right_bias,
        *post,
    )
    back_one, back_two = swapped("rows", back_one, back_two)
    mid = middle_block(features, nrm, keys, values, wqv, wp, inner_mid, middle_bias, *post)
    return convs(
        flags,
        features,
        row_one,
        row_two,
        col_one,
        col_two,
        back_one,
        back_two,
        edge,
        side,
        mid,
        group_conv,
        before_conv.transpose(0, 1, 3, 2),
        upsample_conv,
    )


def solution(mesh):
    placed = (P("rows", "cols", None), P(), P(), P(), P(), P(), P(), P(), P(), P(), P())
    return jax.shard_map(
        on_device, mesh=mesh, in_specs=placed, out_specs=P(None, "rows", "cols"), check_vma=False
    )
```

time: 177 us -> 51.5 us (0.29)
  the two profiles are of different devices: /device:TPU:3 before, /device:TPU:20 now
where the time goes in v1:
time: 51.5 us; the launch traced here: 51.2 us
  Pallas kernels  32.3 us (63%)
  starting transfers between devices  11.7 us (23%)
  local copies, waits for them, and re-layouts  3.57 us (7%)
  other arithmetic  2.8 us (5%)
  waiting for transfers between devices  0.62 us (1%)
    pallas_call x5, Pallas kernels, run(): pl.pallas_call(kernel, out_shape=out_shape, in_specs=specs, scratch_shape...  32.3 us
    ppermute x6, starting transfers between devices, swapped(): out.append(lax.ppermute(payload, axis, pairs))  11.7 us
    unnamed x30, local copies, waits for them, and re-layouts  2.74 us
    select_n x1, other arithmetic, on_device(): jnp.where(even_row, low, high)  1.64 us
    select_n x1, other arithmetic, on_device(): jnp.where(even_col, low, high)  1.14 us
  transfers between devices with their start and end apart: 6, of which 1 were waited for; matrix products, arithmetic and copies ran while one was open for 2% of the time, Pallas kernels for 32%

profile of v1, /device:TPU:20, one launch (start us, length us, event | category | flops | bytes accessed | tf_op | source)
XLA Modules:
  0.0 51.2 jit_solution(2338229730483792607)
XLA Ops:
  0.0 1.6 %broadcast_select_fusion.4 = (bf16[4,64,180]{2,1,0:T(8,128)(2,1)}, bf16[4,64,180]{2,1,0:T(8,128)(2,1)S(1)}) fusion(pred[]{:T(512)} %eq.25, bf16[16,64,180]{2,1,0:T(8,128)(2,1)} %own_ref.7), kind=kLoop, calls=%fused_computation.6 | loop fusion | flops 92160 | bytes 368641 | tf_op jit(solution)/shard_map/jit(_where)/select_n | solution.py:775
  1.6 2.3 %collective-permute-start.1 = (bf16[4,64,180]{2,1,0:T(8,128)(2,1)}, bf16[4,64,180]{2,1,0:T(8,128)(2,1)S(1)}, u32[]{:S(2)}, u32[]{:S(2)}) collective-permute-start(bf16[4,64,180]{2,1,0:T(8,128)(2,1)} %get-tuple-element.45), channel_id=1, source_target_pairs={{8,16},{16,8},{9,17},{17,9},{10,18},{18,10},{11,19},{19,11},{12,20... | collective-permute-start | bytes 276488 | tf_op jit(solution)/shard_map/ppermute | solution.py:742
  4.0 0.1 collective-permute-start
  4.1 0.0 copy-start.8
  4.1 0.8 %copy-done.8 = f32[1521,6]{0,1:T(8,128)S(1)} copy-done((f32[1521,6]{0,1:T(8,128)S(1)}, f32[1521,6]{0,1:T(8,128)}, u32[]{:S(2)}) %copy-start.8) | copy-done | bytes 36528
  4.9 0.0 copy-start
  4.9 4.6 %shard_map.109 = (bf16[6,576,128]{2,1,0:T(8,128)(2,1)S(1)}, bf16[6,576,128]{2,1,0:T(8,128)(2,1)S(1)}, bf16[6,576,128]{2,1,0:T(8,128)(2,1)S(1)}, bf16[6,576,128]{2,1,0:T(8,128)(2,1)S(1)}) custom-call(f32[6,1521]{1,0:T(8,128)S(1)} %bitcast.15), custom_call_target="tpu_custom_call" | custom-call | flops 4000000000 | bytes 4000000 | tf_op jit(solution)/shard_map/pallas_call | solution.py:49
  9.5 0.0 copy-start.11
  9.5 0.9 %copy-done.11 = bf16[6,576,128]{2,1,0:T(8,128)(2,1)} copy-done((bf16[6,576,128]{2,1,0:T(8,128)(2,1)}, bf16[6,576,128]{2,1,0:T(8,128)(2,1)S(1)}, u32[]{:S(2)}) %copy-start.11) | copy-done | bytes 884760
  10.4 0.0 copy-start.13
  10.4 1.0 %copy-done.13 = bf16[6,576,128]{2,1,0:T(8,128)(2,1)} copy-done((bf16[6,576,128]{2,1,0:T(8,128)(2,1)}, bf16[6,576,128]{2,1,0:T(8,128)(2,1)S(1)}, u32[]{:S(2)}) %copy-start.13) | copy-done | bytes 884760
  11.4 0.0 copy-done
  11.4 0.0 copy-start.4
  11.4 0.0 copy-start.5
  11.4 0.0 copy-start.6
  11.4 0.0 copy-start.7
  11.4 0.0 copy-start.9
  11.4 0.0 copy-start.10
  11.4 0.7 %fusion = (bf16[16,24,180]{2,1,0:T(8,128)(2,1)S(1)}, bf16[16,24,180]{2,1,0:T(8,128)(2,1)}) fusion(bf16[16,64,180]{2,1,0:T(8,128)(2,1)S(1)} %copy-done), kind=kLoop, calls=%fused_computation.8 | loop fusion | bytes 552960 | tf_op jit(solution)/shard_map/slice | solution.py:779
  12.2 0.1 stack.27
  12.3 0.0 copy-start.12
  12.3 0.0 collective-permute-done.1.row_two_ref
  12.3 0.0 collective-permute-done.row_one_ref
  12.3 1.1 %broadcast_select_fusion = (bf16[24,24,180]{2,1,0:T(8,128)(2,1)S(1)}, bf16[24,24,180]{2,1,0:T(8,128)(2,1)S(1)}) fusion(pred[]{:T(512)} %eq.26, bf16[4,24,180]{2,1,0:T(8,128)(2,1)S(1)} %get-tuple-element.53, bf16[16,24,180]{2,1,0:T(8,128)(2,1)} %get-tuple-element.44, bf16[4,24,180]{2,1,0:T(8,128)(2,1)S(1)} %get-tuple-element.50, ...), kind=kLoop, calls=%fused_computation.2 | loop fusion | flops 622080 | bytes 829441 | tf_op jit(solution)/shard_map/jit(_where)/select_n | solution.py:783
  13.5 2.5 %collective-permute-start.3 = (bf16[24,24,180]{2,1,0:T(8,128)(2,1)S(1)}, bf16[24,24,180]{2,1,0:T(8,128)(2,1)S(1)}, u32[]{:S(2)}, u32[]{:S(2)}) collective-permute-start(bf16[24,24,180]{2,1,0:T(8,128)(2,1)S(1)} %get-tuple-element.41), channel_id=1, source_target_pairs={{1,2},{3,4},{5,6},{2,1},{4,3},{6,5},{9,10},{11,12},{13,14},{10,9},... | collective-permute-start | bytes 622088 | tf_op jit(solution)/shard_map/ppermute | solution.py:742
  16.0 1.1 %collective-permute-start.2 = (bf16[24,24,180]{2,1,0:T(8,128)(2,1)S(1)}, bf16[24,24,180]{2,1,0:T(8,128)(2,1)S(1)}, u32[]{:S(2)}, u32[]{:S(2)}) collective-permute-start(bf16[24,24,180]{2,1,0:T(8,128)(2,1)S(1)} %get-tuple-element.42), channel_id=1, source_target_pairs={{0,1},{2,3},{4,5},{6,7},{1,0},{3,2},{5,4},{7,6},{8,9},{10,11},{12,... | collective-permute-start | bytes 622088 | tf_op jit(solution)/shard_map/ppermute | solution.py:742
  17.1 0.0 copy-done.4
  17.1 0.0 copy-done.5
  17.1 0.0 copy-done.6
  17.1 0.0 copy-done.7
  17.1 0.0 copy-done.9
  17.1 0.0 copy-done.10
  17.1 0.0 copy-done.12
  17.1 0.0 copy-start.14
  17.1 6.9 %shard_map.110 = (f32[24,64,180]{2,1,0:T(8,128)S(1)}, bf16[180,384]{1,0:T(8,128)(2,1)S(1)}, bf16[384,180]{1,0:T(8,128)(2,1)S(1)}, bf16[192,180]{1,0:T(8,128)(2,1...) custom-call(s32[6]{0:T(128)S(1)} %convert_element_type.3.flags, ...), custom_call_target="tpu_custom_call" | custom-call | flops 5000000000 | bytes 4000000 | tf_op jit(solution)/shard_map/pallas_call | solution.py:49
  24.1 0.6 %collective-permute-done.3.col_two_ref = bf16[24,24,180]{2,1,0:T(8,128)(2,1)S(1)} collective-permute-done((bf16[24,24,180]{2,1,0:T(8,128)(2,1)S(1)}, bf16[24,24,180]{2,1,0:T(8,128)(2,1)S(1)}, u32[]{:S(2)}, u32[]{:S(2)}) %collective-permute-start.3) | collective-permute-done | bytes 207392 | tf_op jit(solution)/shard_map/ppermute | solution.py:742
  24.7 0.0 collective-permute-done.2.col_one_ref
  24.7 0.0 copy-done.14
  24.7 8.9 %shard_map.111 = (bf16[3,80,180]{2,1,0:T(8,128)(2,1)S(1)}, bf16[3,80,180]{2,1,0:T(8,128)(2,1)S(1)}, f32[8,80,180]{2,1,0:T(8,128)S(1)}, f32[8,16,180]{2,1,0:T(8,1...) custom-call(s32[6]{0:T(128)S(1)} %convert_element_type.3.flags, ...), custom_call_target="tpu_custom_call" | custom-call | flops 5000000000 | bytes 4000000 | tf_op jit(solution)/shard_map/pallas_call | solution.py:49
  33.6 2.1 %collective-permute-start.4 = (bf16[3,80,180]{2,1,0:T(8,128)(2,1)S(1)}, bf16[3,80,180]{2,1,0:T(8,128)(2,1)S(1)}, u32[]{:S(2)}, u32[]{:S(2)}) collective-permute-start(bf16[3,80,180]{2,1,0:T(8,128)(2,1)S(1)} %get-tuple-element.34), channel_id=1, source_target_pairs={{0,8},{16,24},{8,0},{24,16},{1,9},{17,25},{9,1},{25,17},{2,10},{18... | collective-permute-start | bytes 259208 | tf_op jit(solution)/shard_map/ppermute | solution.py:742
  35.6 3.7 %collective-permute-start.5 = (bf16[3,80,180]{2,1,0:T(8,128)(2,1)S(1)}, bf16[3,80,180]{2,1,0:T(8,128)(2,1)S(1)}, u32[]{:S(2)}, u32[]{:S(2)}) collective-permute-start(bf16[3,80,180]{2,1,0:T(8,128)(2,1)S(1)} %get-tuple-element.35), channel_id=1, source_target_pairs={{8,16},{16,8},{9,17},{17,9},{10,18},{18,10},{11,19},{19,11},{12,20... | collective-permute-start | bytes 259208 | tf_op jit(solution)/shard_map/ppermute | solution.py:742
  39.3 0.0 copy-start.1
  39.3 0.0 copy-start.2
  39.3 0.0 copy-start.3
  39.3 4.9 %shard_map.112.mid_ref = f32[8,64,180]{2,1,0:T(8,128)S(1)} custom-call(bf16[16,64,180]{2,1,0:T(8,128)(2,1)S(1)} %copy-done, f32[24,64,180]{2,1,0:T(8,128)S(1)} %get-tuple-element.25.nrm_ref, bf16[5,576,384]{2,1,0:T(8,128)(2,1)S(1)} %get-tuple-element.38.k_ref, bf16[5,3,192,192]{3,2,1,0:T(8,128)(2,1)S(1)} %get-tuple-element.39.v_ref, ...), custom_call_target="tpu_custom_call" | custom-call | flops 5000000000 | bytes 4000000 | tf_op jit(solution)/shard_map/pallas_call | solution.py:49
  44.2 0.0 collective-permute-done.4.back_one_ref
  44.2 0.0 collective-permute-done.5.back_two_ref
  44.2 0.0 copy-done.1
  44.2 0.0 copy-done.2
  44.3 0.0 copy-done.3
  44.3 7.0 %shard_map.113 = bf16[64,32,128]{2,1,0:T(8,128)(2,1)} custom-call(s32[6]{0:T(128)S(1)} %convert_element_type.3.flags, bf16[16,64,180]{2,1,0:T(8,128)(2,1)S(1)} %copy-done, bf16[4,64,180]{2,1,0:T(8,128)(2,1)S(1)} %collective-permute-done.row_one_ref, bf16[4,64,180]{2,1,0:T(8,128)(2,1)S(1)} %collective-permute-done.1.row_two_ref, ...), custom_call_target="tpu_custom_call" | custom-call | flops 8000000000 | bytes 4000000 | tf_op jit(solution)/shard_map/pallas_call | solution.py:49
  (3 shorter events, 0.0 us)
Async XLA Ops:
  1.6 10.6 %collective-permute-start.1 = (bf16[4,64,180]{2,1,0:T(8,128)(2,1)}, bf16[4,64,180]{2,1,0:T(8,128)(2,1)S(1)}, u32[]{:S(2)}, u32[]{:S(2)}) collective-permute-start(bf16[4,64,180]{2,1,0:T(8,128)(2,1)} %get-tuple-element.45), channel_id=1, source_target_pairs={{8,16},{16,8},{9,17},{17,9},{10,18},{18,10},{11,19},{19,11},{12,20... | collective-permute-start | bytes 276488 | tf_op jit(solution)/shard_map/ppermute | solution.py:742
  4.0 8.3 %collective-permute-start = (bf16[4,64,180]{2,1,0:T(8,128)(2,1)S(1)}, bf16[4,64,180]{2,1,0:T(8,128)(2,1)S(1)}, u32[]{:S(2)}, u32[]{:S(2)}) collective-permute-start(bf16[4,64,180]{2,1,0:T(8,128)(2,1)S(1)} %get-tuple-element.46), channel_id=1, source_target_pairs={{0,8},{16,24},{8,0},{24,16},{1,9},{17,25},{9,1},{25,17},{2,10},{18... | collective-permute-start | bytes 276488 | tf_op jit(solution)/shard_map/ppermute | solution.py:742
  4.1 0.8 %copy-start.8 = (f32[1521,6]{0,1:T(8,128)S(1)}, f32[1521,6]{0,1:T(8,128)}, u32[]{:S(2)}) copy-start(f32[1521,6]{0,1:T(8,128)} %param.14) | copy-start | bytes 109516
  4.9 6.5 %copy-start = (bf16[16,64,180]{2,1,0:T(8,128)(2,1)S(1)}, bf16[16,64,180]{2,1,0:T(8,128)(2,1)}, u32[]{:S(2)}) copy-start(bf16[16,64,180]{2,1,0:T(8,128)(2,1)} %own_ref.7) | copy-start | bytes 1105924
  9.5 0.9 %copy-start.11 = (bf16[6,576,128]{2,1,0:T(8,128)(2,1)}, bf16[6,576,128]{2,1,0:T(8,128)(2,1)S(1)}, u32[]{:S(2)}) copy-start(bf16[6,576,128]{2,1,0:T(8,128)(2,1)S(1)} %get-tuple-element.23.border_bias_ref) | copy-start | bytes 2654212
  10.4 1.0 %copy-start.13 = (bf16[6,576,128]{2,1,0:T(8,128)(2,1)}, bf16[6,576,128]{2,1,0:T(8,128)(2,1)S(1)}, u32[]{:S(2)}) copy-start(bf16[6,576,128]{2,1,0:T(8,128)(2,1)S(1)} %get-tuple-element.33.right_bias_ref) | copy-start | bytes 2654212
  11.4 5.7 %copy-start.4 = (bf16[180,540]{1,0:T(8,128)(2,1)S(1)}, bf16[180,540]{1,0:T(8,128)(2,1)}, u32[]{:S(2)}) copy-start(bf16[180,540]{1,0:T(8,128)(2,1)} %qkv_ref.1) | copy-start | bytes 583204
  11.4 5.7 %copy-start.5 = (bf16[180,360]{1,0:T(8,128)(2,1)S(1)}, bf16[180,360]{1,0:T(8,128)(2,1)}, u32[]{:S(2)}) copy-start(bf16[180,360]{1,0:T(8,128)(2,1)} %hidden_ref.5) | copy-start | bytes 388804
  11.4 5.7 %copy-start.6 = (bf16[360,180]{0,1:T(8,128)(2,1)S(1)}, bf16[360,180]{0,1:T(8,128)(2,1)}, u32[]{:S(2)}) copy-start(bf16[360,180]{0,1:T(8,128)(2,1)} %param.18) | copy-start | bytes 388804
  11.4 5.7 %copy-start.7 = (bf16[180,180]{1,0:T(8,128)(2,1)S(1)}, bf16[180,180]{1,0:T(8,128)(2,1)}, u32[]{:S(2)}) copy-start(bf16[180,180]{1,0:T(8,128)(2,1)} %proj_ref.1) | copy-start | bytes 194404
  11.4 5.7 %copy-start.9 = (f32[180]{0:T(256)S(1)}, f32[180]{0:T(256)}, u32[]{:S(2)}) copy-start(f32[180]{0:T(256)} %param.12) | copy-start | bytes 2164
  11.4 5.7 %copy-start.10 = (f32[180]{0:T(256)S(1)}, f32[180]{0:T(256)}, u32[]{:S(2)}) copy-start(f32[180]{0:T(256)} %param.16) | copy-start | bytes 2164
  12.3 4.8 %copy-start.12 = (bf16[6,576,128]{2,1,0:T(8,128)(2,1)S(1)}, bf16[6,576,128]{2,1,0:T(8,128)(2,1)}, u32[]{:S(2)}) copy-start(bf16[6,576,128]{2,1,0:T(8,128)(2,1)} %copy-done.11) | copy-start | bytes 2654212
  13.5 11.2 %collective-permute-start.3 = (bf16[24,24,180]{2,1,0:T(8,128)(2,1)S(1)}, bf16[24,24,180]{2,1,0:T(8,128)(2,1)S(1)}, u32[]{:S(2)}, u32[]{:S(2)}) collective-permute-start(bf16[24,24,180]{2,1,0:T(8,128)(2,1)S(1)} %get-tuple-element.41), channel_id=1, source_target_pairs={{1,2},{3,4},{5,6},{2,1},{4,3},{6,5},{9,10},{11,12},{13,14},{10,9},... | collective-permute-start | bytes 622088 | tf_op jit(solution)/shard_map/ppermute | solution.py:742
  16.0 8.7 %collective-permute-start.2 = (bf16[24,24,180]{2,1,0:T(8,128)(2,1)S(1)}, bf16[24,24,180]{2,1,0:T(8,128)(2,1)S(1)}, u32[]{:S(2)}, u32[]{:S(2)}) collective-permute-start(bf16[24,24,180]{2,1,0:T(8,128)(2,1)S(1)} %get-tuple-element.42), channel_id=1, source_target_pairs={{0,1},{2,3},{4,5},{6,7},{1,0},{3,2},{5,4},{7,6},{8,9},{10,11},{12,... | collective-permute-start | bytes 622088 | tf_op jit(solution)/shard_map/ppermute | solution.py:742
  17.1 7.6 %copy-start.14 = (bf16[6,576,128]{2,1,0:T(8,128)(2,1)S(1)}, bf16[6,576,128]{2,1,0:T(8,128)(2,1)}, u32[]{:S(2)}) copy-start(bf16[6,576,128]{2,1,0:T(8,128)(2,1)} %copy-done.13) | copy-start | bytes 2654212
  33.6 10.7 %collective-permute-start.4 = (bf16[3,80,180]{2,1,0:T(8,128)(2,1)S(1)}, bf16[3,80,180]{2,1,0:T(8,128)(2,1)S(1)}, u32[]{:S(2)}, u32[]{:S(2)}) collective-permute-start(bf16[3,80,180]{2,1,0:T(8,128)(2,1)S(1)} %get-tuple-element.34), channel_id=1, source_target_pairs={{0,8},{16,24},{8,0},{24,16},{1,9},{17,25},{9,1},{25,17},{2,10},{18... | collective-permute-start | bytes 259208 | tf_op jit(solution)/shard_map/ppermute | solution.py:742
  35.6 8.6 %collective-permute-start.5 = (bf16[3,80,180]{2,1,0:T(8,128)(2,1)S(1)}, bf16[3,80,180]{2,1,0:T(8,128)(2,1)S(1)}, u32[]{:S(2)}, u32[]{:S(2)}) collective-permute-start(bf16[3,80,180]{2,1,0:T(8,128)(2,1)S(1)} %get-tuple-element.35), channel_id=1, source_target_pairs={{8,16},{16,8},{9,17},{17,9},{10,18},{18,10},{11,19},{19,11},{12,20... | collective-permute-start | bytes 259208 | tf_op jit(solution)/shard_map/ppermute | solution.py:742
  39.3 4.9 %copy-start.1 = (bf16[3,3,180,180]{3,2,1,0:T(8,128)(2,1)S(1)}, bf16[3,3,180,180]{3,2,1,0:T(8,128)(2,1)}, u32[]{:S(2)}) copy-start(bf16[3,3,180,180]{3,2,1,0:T(8,128)(2,1)} %group_ref.1) | copy-start | bytes 1749604
  39.3 4.9 %copy-start.2 = (bf16[3,3,180,64]{2,3,1,0:T(8,128)(2,1)S(1)}, bf16[3,3,180,64]{2,3,1,0:T(8,128)(2,1)}, u32[]{:S(2)}) copy-start(bf16[3,3,180,64]{2,3,1,0:T(8,128)(2,1)} %param.20) | copy-start | bytes 622084
  39.3 4.9 %copy-start.3 = (bf16[3,3,64,256]{3,2,1,0:T(8,128)(2,1)S(1)}, bf16[3,3,64,256]{3,2,1,0:T(8,128)(2,1)}, u32[]{:S(2)}) copy-start(bf16[3,3,64,256]{3,2,1,0:T(8,128)(2,1)} %upsample_ref.1) | copy-start | bytes 884740

commit v2 on v1

--- a/solution.py
+++ b/solution.py
@@ -14,8 +14,6 @@
 WIN = 16
 KWIN = 24
 KEYS = KWIN * KWIN
-CHUNKS = 3
-CHUNK = KEYS // CHUNKS
 SIDE = WIN + KWIN - 1
 RIM = (KWIN - WIN) // 2
 EDGE = WIN + 2 * RIM
@@ -41,26 +39,19 @@
     return center * lax.rsqrt(spread + 1e-05) * gain
 
 
-def call(kernel, out_shape, scratch, flops, bytes_accessed, smem=0):
-    def run(*args):
-        specs = [pl.BlockSpec(memory_space=pltpu.VMEM)] * len(args)
-        for index in range(smem):
-            specs[index] = pl.BlockSpec(memory_space=pltpu.SMEM)
-        return pl.pallas_call(
-            kernel,
-            out_shape=out_shape,
-            in_specs=specs,
-            scratch_shapes=scratch,
-            compiler_params=pltpu.CompilerParams(vmem_limit_bytes=24 * 2**20),
-            cost_estimate=pl.CostEstimate(
-                flops=flops, bytes_accessed=bytes_accessed, transcendentals=0
-            ),
-        )(*args)
-
-    return run
-
-
-def bias_kernel(table_ref, left_ref, border_ref, right_ref, middle_ref, t_scr, e_scr, w_scr, x_scr):
+def call(kernel, out_shape, scratch, flops, bytes_accessed):
+    return pl.pallas_call(
+        kernel,
+        out_shape=out_shape,
+        scratch_shapes=scratch,
+        compiler_params=pltpu.CompilerParams(vmem_limit_bytes=24 * 2**20),
+        cost_estimate=pl.CostEstimate(
+            flops=flops, bytes_accessed=bytes_accessed, transcendentals=0
+        ),
+    )
+
+
+def bias_kernel(table_ref, out_ref, t_scr, e_scr, w_scr, x_scr):
     for d in range(SIDE):
         t_scr[8 * d : 8 * d + HEADS, 0:SIDE] = jnp.exp(table_ref[:, SIDE * d : SIDE * (d + 1)])
 
@@ -88,14 +79,14 @@
             high = w_scr[:, (31 - p) * WIN : (31 - p) * WIN + 128]
             x_scr[0, rows] = jnp.where(lanes < 64, low, high)
             x_scr[1, rows] = w_scr[:, (27 - p) * WIN : (27 - p) * WIN + 128]
-        border_ref[h] = x_scr[0].astype(BF16)
-        middle_ref[h] = x_scr[1].astype(BF16)
-        for out_ref, first in ((left_ref, WIN - STRIP), (right_ref, 0)):
+        out_ref[1, h] = x_scr[0].astype(BF16)
+        out_ref[3, h] = x_scr[1].astype(BF16)
+        for kind, first in ((0, WIN - STRIP), (2, 0)):
             expand(STRIP, first)
             for p in range(KWIN):
                 rows = slice(p * KWIN, (p + 1) * KWIN)
                 x_scr[0, rows] = w_scr[:, (23 - p) * STRIP : (23 - p) * STRIP + 128]
-            out_ref[h] = x_scr[0].astype(BF16)
+            out_ref[kind, h] = x_scr[0].astype(BF16)
         return carry
 
     lax.fori_loop(0, HEADS, head, 0)
@@ -104,7 +95,7 @@
 def build_bias(bias_table):
     return call(
         bias_kernel,
-        [jax.ShapeDtypeStruct((HEADS, KEYS, 128), BF16)] * 4,
+        jax.ShapeDtypeStruct((4, HEADS, KEYS, 128), BF16),
         [
             pltpu.VMEM((8 * SIDE, 128), F32),
             pltpu.VMEM((SIDE + 1, 640), F32),
@@ -166,22 +157,6 @@
             q_scr[g, t, HP : 2 * HP] = jnp.concatenate([none, two], axis=1)
 
 
-class BiasCopies:
-    def __init__(self, bias_refs, bias_scr, sem):
-        self.copies = [
-            pltpu.make_async_copy(ref, bias_scr.at[index], sem.at[index])
-            for index, ref in enumerate(bias_refs)
-        ]
-
-    def start(self):
-        for copy in self.copies:
-            copy.start()
-
-    def wait(self):
-        for copy in self.copies:
-            copy.wait()
-
-
 def lookup(g, values):
     out = values[0]
     for index in range(1, len(values)):
@@ -189,45 +164,52 @@
     return out
 
 
-def attention(kinds, windows, q_scr, k_ref, v_ref, bias_ref, wp_ref, p_scr, a_scr, o_scr):
-    groups = len(windows)
+def attention(kinds, windows, q_scr, k_ref, v_ref, bias_ref, wp_ref, s_scr, m_scr, p_scr, o_scr):
+    groups = len(kinds)
     pairs = HEADS // 2
-    stages = [(c, t) for c in range(CHUNKS) for t in range(pairs)]
-
-    def sum_values(g, c, t, slot):
-        part = dot(v_ref[lookup(g, windows), c, 2 * t * HP : 2 * (t + 1) * HP], p_scr[slot])
-        o_scr[g, t] = part if c == 0 else o_scr[g, t] * a_scr[slot] + part
-
-    p_scr[(len(stages) - 1) % 3] = jnp.zeros((CHUNK, 256), BF16)
-    a_scr[(len(stages) - 1) % 3] = jnp.zeros((1, 256), F32)
-    o_scr[0, pairs - 1] = jnp.zeros((2 * HP, 256), F32)
+    step = 192
+
+    def keep(g, t, k0, top):
+        keys = k_ref[lookup(g, windows), k0 : k0 + step, 128 * t : 128 * t + 2 * HP]
+        one = dot(keys, q_scr[g, t])
+        s_scr[t, k0 : k0 + step] = one
+        part = jnp.max(one.reshape(step // 8, 8, 256), axis=0)
+        return part if top is None else jnp.maximum(top, part)
+
+    def sum_values(g, t):
+        o_scr[g, t] = dot(v_ref[lookup(g, windows), 2 * t * HP : 2 * (t + 1) * HP], p_scr[t])
+
+    top = None
+    for k0 in range(0, KEYS, step):
+        top = keep(0, 0, k0, top)
+    m_scr[...] = top
+    p_scr[pairs - 1] = jnp.zeros((KEYS, 256), BF16)
 
     def attend(g, carry):
-        window = lookup(g, windows)
-        tops = [None] * pairs
-        for n, (c, t) in enumerate(stages):
-            rows = slice(CHUNK * c, CHUNK * (c + 1))
-            s = dot(k_ref[window, rows, 128 * t : 128 * t + 2 * HP], q_scr[g, t])
-            top = jnp.max(jnp.max(s.reshape(CHUNK // 8, 8, 256), axis=0), axis=0, keepdims=True)
-            if c > 0:
-                top = jnp.maximum(top, tops[t])
-            if n == 0:
-                sum_values(jnp.maximum(g - 1, 0), *stages[-1], (len(stages) - 1) % 3)
+        kind = lookup(g, kinds)
+        top = m_scr[...]
+        for t in range(pairs):
+            top = jnp.max(top, axis=0, keepdims=True)
+            if t == 0:
+                sum_values(jnp.maximum(g - 1, 0), pairs - 1)
             else:
-                sum_values(g, *stages[n - 1], (n - 1) % 3)
-            if c > 0:
-                a_scr[n % 3] = jnp.exp2(tops[t] - top)
-            tops[t] = top
-            prob = jnp.exp2(s - top).astype(BF16)
-            for half in range(2):
-                lanes = slice(128 * half, 128 * half + 128)
-                head = 2 * t + half
-                bias = bias_ref[head, rows] if kinds is None else bias_ref[lookup(g, kinds), head, rows]
-                p_scr[n % 3, :, lanes] = prob[:, lanes] * bias
+                sum_values(g, t - 1)
+            following = g if t + 1 < pairs else jnp.minimum(g + 1, groups - 1)
+            later = None
+            for k0 in range(0, KEYS, step):
+                prob = jnp.exp2(s_scr[t, k0 : k0 + step] - top).astype(BF16)
+                for half in range(2):
+                    lanes = slice(128 * half, 128 * half + 128)
+                    p_scr[t, k0 : k0 + step, lanes] = (
+                        prob[:, lanes] * bias_ref[kind, 2 * t + half, k0 : k0 + step]
+                    )
+                later = keep(following, (t + 1) % pairs, k0, later)
+            top = later
+        m_scr[...] = top
         return carry
 
     lax.fori_loop(0, groups, attend, 0)
-    sum_values(groups - 1, *stages[-1], (len(stages) - 1) % 3)
+    sum_values(groups - 1, pairs - 1)
     attended = []
     for g in range(groups):
         parts = []
@@ -248,14 +230,29 @@
     return first + dot_nt(inner, output_ref[...])
 
 
+def feed_groups(first, gain, hidden_ref, output_ref):
+    groups = range(first.shape[0] // 128)
+    return [feed_forward(first[128 * g : 128 * (g + 1)], gain, hidden_ref, output_ref) for g in groups]
+
+
 def project(keys, wk_ref, wqv_ref, k_ref, v_ref, index):
     width = HEADS * HP
     one_row = (lax.broadcasted_iota(jnp.int32, (width, 1), 0) % HP == HD).astype(F32)
     keys = keys.reshape(KEYS, keys.shape[2]).astype(BF16)
     k_ref[index] = dot(keys, wk_ref[...]).astype(BF16)
-    for c in range(CHUNKS):
-        part = keys[CHUNK * c : CHUNK * (c + 1)]
-        v_ref[index, c] = (dot_nt(wqv_ref[width : 2 * width], part) + one_row).astype(BF16)
+    v_ref[index] = (dot_nt(wqv_ref[width : 2 * width], keys) + one_row).astype(BF16)
+
+
+def at_edges():
+    row, column = lax.axis_index("rows"), lax.axis_index("cols")
+    return (
+        column == 0,
+        column == lax.axis_size("cols") - 1,
+        row == 0,
+        row == lax.axis_size("rows") - 1,
+        row % 2 == 0,
+        column % 2 == 0,
+    )
 
 
 def from_sides(even, first, second):
@@ -267,16 +264,34 @@
     return jnp.concatenate([ref[0:4, c0 : c0 + WIN], ref[12:16, c0 : c0 + WIN]], axis=0)
 
 
+def pack_kernel(own_ref, row_one_ref, row_two_ref, pay_one_ref, pay_two_ref):
+    height, cols, chans = own_ref.shape
+    even_row, even_col = at_edges()[4:]
+    above, below = from_sides(even_row, row_one_ref[...], row_two_ref[...])
+    for rows, part in (
+        (slice(0, RIM), above),
+        (slice(RIM, RIM + height), own_ref[...].astype(F32)),
+        (slice(RIM + height, 2 * RIM + height), below),
+    ):
+        low, high = part[:, 0:EDGE], part[:, cols - EDGE : cols]
+        pay_one_ref[rows] = jnp.where(even_col, high, low).astype(BF16)
+        pay_two_ref[rows] = jnp.where(even_col, low, high).astype(BF16)
+
+
+def pack(own, row_one, row_two):
+    height, cols, chans = own.shape
+    pay = jax.ShapeDtypeStruct((height + 2 * RIM, EDGE, chans), BF16)
+    return call(pack_kernel, (pay, pay), [], 1_000_000, 1_000_000)(own, row_one, row_two)
+
+
 def inner_kernel(
-    flags,
     own_ref,
     row_one_ref,
     row_two_ref,
     gain_one_ref,
     qkv_ref,
     proj_ref,
-    border_bias_ref,
-    middle_bias_ref,
+    bias_ref,
     gain_two_ref,
     hidden_ref,
     output_ref,
@@ -289,20 +304,18 @@
     border_ref,
     mid_ref,
     q_scr,
+    s_scr,
+    m_scr,
     p_scr,
-    a_scr,
     o_scr,
-    bias_scr,
-    sem,
 ):
     height, cols, chans = own_ref.shape
     inner = cols // WIN - 2
-    copies = BiasCopies((border_bias_ref, middle_bias_ref), bias_scr, sem)
-    copies.start()
+    flags = at_edges()
     weights_into(qkv_ref, proj_ref, wk_ref, wqv_ref, wp_ref)
     gain_one = gain_one_ref[...]
     for r in range(RIM):
-        above, below = from_sides(flags[4] > 0, row_one_ref[r], row_two_ref[r])
+        above, below = from_sides(flags[4], row_one_ref[r], row_two_ref[r])
         nrm_ref[r] = layer_norm(above, gain_one)
         nrm_ref[RIM + height + r] = layer_norm(below, gain_one)
     for r in range(height):
@@ -313,31 +326,29 @@
         project(nrm_ref[:, c0 - RIM : c0 - RIM + KWIN], wk_ref, wqv_ref, k_ref, v_ref, w)
         first.append(border_rows(own_ref, c0).reshape(128, chans))
         queries.append(border_rows(nrm_ref.at[RIM : RIM + height], c0))
-        kinds.append(0)
+        kinds.append(1)
         windows.append(w)
     for w in range(inner - 1):
         c0 = WIN * (w + 1)
         first.append(own_ref[4:12, c0 : c0 + WIN].reshape(128, chans))
         queries.append(nrm_ref[RIM + 4 : RIM + 12, c0 : c0 + WIN])
-        kinds.append(1)
+        kinds.append(3)
         windows.append(w)
     groups = len(kinds)
     set_queries(q_scr, wqv_ref, queries)
-    copies.wait()
     first = jnp.concatenate(first, axis=0).astype(F32) + attention(
-        kinds, windows, q_scr, k_ref, v_ref, bias_scr, wp_ref, p_scr, a_scr, o_scr
-    )
-    mixed = feed_forward(first, gain_two_ref[...], hidden_ref, output_ref)
-    mixed = mixed.reshape(groups, 8, WIN, chans)
+        kinds, windows, q_scr, k_ref, v_ref, bias_ref, wp_ref, s_scr, m_scr, p_scr, o_scr
+    )
+    mixed = feed_groups(first, gain_two_ref[...], hidden_ref, output_ref)
     for g in range(groups):
+        one = mixed[g].reshape(8, WIN, chans)
         if g < inner:
-            border_ref[:, WIN * g : WIN * (g + 1)] = mixed[g]
+            border_ref[:, WIN * g : WIN * (g + 1)] = one
         else:
-            mid_ref[:, WIN * (g - inner) : WIN * (g - inner + 1)] = mixed[g]
+            mid_ref[:, WIN * (g - inner) : WIN * (g - inner + 1)] = one
 
 
 def outer_kernel(
-    flags,
     own_ref,
     nrm_ref,
     col_one_ref,
@@ -349,9 +360,7 @@
     inner_k_ref,
     inner_v_ref,
     inner_border_ref,
-    left_bias_ref,
-    border_bias_ref,
-    right_bias_ref,
+    bias_ref,
     gain_two_ref,
     hidden_ref,
     output_ref,
@@ -364,20 +373,18 @@
     side_scr,
     x_scr,
     q_scr,
+    s_scr,
+    m_scr,
     p_scr,
-    a_scr,
     o_scr,
-    bias_scr,
-    sem,
     image,
 ):
     height, cols, chans = own_ref.shape
     inner = cols // WIN - 2
-    copies = BiasCopies((left_bias_ref, border_bias_ref, right_bias_ref), bias_scr, sem)
-    copies.start()
+    flags = at_edges()
     gain_one = gain_one_ref[...]
     for r in range(height + 2 * RIM):
-        both = from_sides(flags[5] > 0, col_one_ref[r], col_two_ref[r])
+        both = from_sides(flags[5], col_one_ref[r], col_two_ref[r])
         for side in range(2):
             if RIM <= r < RIM + height:
                 x_scr[side, r - RIM] = both[side]
@@ -400,27 +407,23 @@
             queries.append(border_rows(nrm_ref.at[RIM : RIM + height], c0))
         first.append(x.reshape(128, chans))
     set_queries(q_scr, wqv_ref, queries)
-    copies.wait()
     first = jnp.concatenate(first, axis=0) + attention(
-        [0, 1, 1, 2], [0, 1, 3, 4], q_scr, k_ref, v_ref, bias_scr, wp_ref, p_scr, a_scr, o_scr
+        [0, 1, 1, 2], [0, 1, 3, 4], q_scr, k_ref, v_ref, bias_ref, wp_ref, s_scr, m_scr, p_scr, o_scr
     )
     image[0:4, STRIP + WIN : STRIP + cols - WIN] = inner_border_ref[0:4]
     image[12:16, STRIP + WIN : STRIP + cols - WIN] = inner_border_ref[4:8]
-    for pair in range(2):
-        mixed = feed_forward(first[256 * pair : 256 * pair + 256], gain_two_ref[...], hidden_ref, output_ref)
-        for s in range(2):
-            g = 2 * pair + s
-            one = mixed[s * 128 : (s + 1) * 128]
-            if g in (0, 3):
-                one = jnp.where(flags[g // 3] > 0, 0.0, one).reshape(height, STRIP, chans)
-                c0 = 0 if g == 0 else STRIP + cols
-                image[:, c0 : c0 + STRIP] = one
-            else:
-                one = one.reshape(8, WIN, chans)
-                c0 = STRIP + spots[g]
-                image[0:4, c0 : c0 + WIN] = one[0:4]
-                image[12:16, c0 : c0 + WIN] = one[4:8]
-    even = flags[4] > 0
+    mixed = feed_groups(first, gain_two_ref[...], hidden_ref, output_ref)
+    for g in range(4):
+        if g in (0, 3):
+            one = jnp.where(flags[g // 3], 0.0, mixed[g]).reshape(height, STRIP, chans)
+            c0 = 0 if g == 0 else STRIP + cols
+            image[:, c0 : c0 + STRIP] = one
+        else:
+            one = mixed[g].reshape(8, WIN, chans)
+            c0 = STRIP + spots[g]
+            image[0:4, c0 : c0 + WIN] = one[0:4]
+            image[12:16, c0 : c0 + WIN] = one[4:8]
+    even = flags[4]
     pay_one_ref[...] = jnp.where(even, image[13:16], image[0:3]).astype(BF16)
     pay_two_ref[...] = jnp.where(even, image[0:3], image[13:16]).astype(BF16)
     edge_ref[0:4] = image[0:4]
@@ -437,14 +440,15 @@
     wqv_ref,
     wp_ref,
     inner_mid_ref,
-    middle_bias_ref,
+    bias_ref,
     gain_two_ref,
     hidden_ref,
     output_ref,
     mid_ref,
     q_scr,
+    s_scr,
+    m_scr,
     p_scr,
-    a_scr,
     o_scr,
 ):
     height, cols, chans = own_ref.shape
@@ -452,30 +456,26 @@
     set_queries(q_scr, wqv_ref, [nrm_ref[RIM + 4 : RIM + 12, c0 : c0 + WIN] for c0 in spots])
     first = [own_ref[4:12, c0 : c0 + WIN].reshape(128, chans) for c0 in spots]
     first = jnp.concatenate(first, axis=0).astype(F32) + attention(
-        None, [1, 2, 3], q_scr, k_ref, v_ref, middle_bias_ref, wp_ref, p_scr, a_scr, o_scr
-    )
-    mixed = feed_forward(first, gain_two_ref[...], hidden_ref, output_ref)
-    mixed = mixed.reshape(3, 8, WIN, chans)
+        [3, 3, 3], [1, 2, 3], q_scr, k_ref, v_ref, bias_ref, wp_ref, s_scr, m_scr, p_scr, o_scr
+    )
+    mixed = feed_groups(first, gain_two_ref[...], hidden_ref, output_ref)
     mid_ref[:, WIN : cols - 2 * WIN] = inner_mid_ref[...]
     for g in range(3):
-        mid_ref[:, spots[g] : spots[g] + WIN] = mixed[g]
-
-
-def attention_scratch(groups, kinds):
-    scratch = [
+        mid_ref[:, spots[g] : spots[g] + WIN] = mixed[g].reshape(8, WIN, chans)
+
+
+def attention_scratch(groups):
+    return [
         pltpu.VMEM((groups, HEADS // 2, 2 * HP, 256), BF16),
-        pltpu.VMEM((3, CHUNK, 256), BF16),
-        pltpu.VMEM((3, 1, 256), F32),
+        pltpu.VMEM((HEADS // 2, KEYS, 256), F32),
+        pltpu.VMEM((8, 256), F32),
+        pltpu.VMEM((HEADS // 2, KEYS, 256), BF16),
         pltpu.VMEM((groups, HEADS // 2, 2 * HP, 256), F32),
     ]
-    if kinds:
-        scratch.append(pltpu.VMEM((kinds, HEADS, KEYS, 128), BF16))
-        scratch.append(pltpu.SemaphoreType.DMA((kinds,)))
-    return scratch
 
 
 def inner_block(*args):
-    height, cols, chans = args[1].shape
+    height, cols, chans = args[0].shape
     inner = cols // WIN - 2
     width = HEADS * HP
     groups = 2 * inner - 1
@@ -487,19 +487,18 @@
             jax.ShapeDtypeStruct((2 * width, chans), BF16),
             jax.ShapeDtypeStruct((width, chans), BF16),
             jax.ShapeDtypeStruct((inner, KEYS, 3 * 128), BF16),
-            jax.ShapeDtypeStruct((inner, CHUNKS, width, CHUNK), BF16),
+            jax.ShapeDtypeStruct((inner, width, KEYS), BF16),
             jax.ShapeDtypeStruct((8, WIN * inner, chans), F32),
             jax.ShapeDtypeStruct((8, WIN * (inner - 1), chans), F32),
         ),
-        attention_scratch(groups, 2),
+        attention_scratch(groups),
         5_000_000_000,
         4_000_000,
-        smem=1,
     )(*args)
 
 
 def outer_block(*args):
-    height, cols, chans = args[1].shape
+    height, cols, chans = args[0].shape
     span = cols + 2 * STRIP
     return call(
         outer_kernel,
@@ -509,17 +508,16 @@
             jax.ShapeDtypeStruct((8, span, chans), F32),
             jax.ShapeDtypeStruct((8, 2 * STRIP, chans), F32),
             jax.ShapeDtypeStruct((5, KEYS, 3 * 128), BF16),
-            jax.ShapeDtypeStruct((5, CHUNKS, HEADS * HP, CHUNK), BF16),
+            jax.ShapeDtypeStruct((5, HEADS * HP, KEYS), BF16),
         ),
         [
             pltpu.VMEM((2, height + 2 * RIM, 2 * EDGE, chans), F32),
             pltpu.VMEM((2, height, EDGE, chans), F32),
-            *attention_scratch(4, 3),
+            *attention_scratch(4),
             pltpu.VMEM((height, span, chans), F32),
         ],
         5_000_000_000,
         4_000_000,
-        smem=1,
     )(*args)
 
 
@@ -528,14 +526,13 @@
     return call(
         middle_kernel,
         jax.ShapeDtypeStruct((8, cols, chans), F32),
-        attention_scratch(3, 0),
+        attention_scratch(3),
         5_000_000_000,
         4_000_000,
     )(*args)
 
 
 def conv_kernel(
-    flags,
     own_ref,
     row_one_ref,
     row_two_ref,
@@ -564,8 +561,7 @@
 ):
     height, cols, chans = own_ref.shape
     span = cols + 2 * STRIP
-    at_left, at_right, at_top, at_bottom = (flags[i] > 0 for i in range(4))
-    even_row, even_col = flags[4] > 0, flags[5] > 0
+    at_left, at_right, at_top, at_bottom, even_row, even_col = at_edges()
 
     feats = before_ref.shape[2]
     pad = chans // 16 * 16
@@ -708,7 +704,7 @@
 
 
 def convs(*args):
-    height, cols, chans = args[1].shape
+    height, cols, chans = args[0].shape
     span = cols + 2 * STRIP
     feats = args[-2].shape[2]
     return call(
@@ -729,7 +725,6 @@
         ],
         8_000_000_000,
         4_000_000,
-        smem=1,
     )(*args)
 
 
@@ -757,49 +752,27 @@
     upsample_conv,
 ):
     height, cols, chans = features.shape
-    row, column = lax.axis_index("rows"), lax.axis_index("cols")
-    even_row, even_col = row % 2 == 0, column % 2 == 0
-    flags = jnp.stack(
-        [
-            column == 0,
-            column == lax.axis_size("cols") - 1,
-            row == 0,
-            row == lax.axis_size("rows") - 1,
-            even_row,
-            even_col,
-        ]
-    ).astype(jnp.int32)
-
+    even_row = lax.axis_index("rows") % 2 == 0
     low, high = features[:RIM], features[height - RIM :]
     row_one, row_two = swapped(
         "rows", jnp.where(even_row, high, low), jnp.where(even_row, low, high)
     )
-    above, below = jnp.where(even_row, row_two, row_one), jnp.where(even_row, row_one, row_two)
-    low, high = (
-        jnp.concatenate([part[:, span] for part in (above, features, below)], axis=0)
-        for span in (slice(0, EDGE), slice(cols - EDGE, cols))
-    )
-    col_one, col_two = swapped(
-        "cols", jnp.where(even_col, high, low), jnp.where(even_col, low, high)
-    )
-
-    left_bias, border_bias, right_bias, middle_bias = build_bias(bias_table)
+    col_one, col_two = swapped("cols", *pack(features, row_one, row_two))
+
+    bias = build_bias(bias_table)
     gain_one, gain_two = gain_one.reshape(1, chans), gain_two.reshape(1, chans)
     post = (gain_two, hidden_weight, output_weight.T)
     nrm, wk, wqv, wp, inner_k, inner_v, inner_border, inner_mid = inner_block(
-        flags,
         features,
         row_one,
         row_two,
         gain_one,
         qkv_weight,
         proj_weight,
-        border_bias,
-        middle_bias,
+        bias,
         *post,
     )
     back_one, back_two, edge, side, keys, values = outer_block(
-        flags,
         features,
         nrm,
         col_one,
@@ -811,15 +784,12 @@
         inner_k,
         inner_v,
         inner_border,
-        left_bias,
-        border_bias,
-        right_bias,
+        bias,
         *post,
     )
     back_one, back_two = swapped("rows", back_one, back_two)
-    mid = middle_block(features, nrm, keys, values, wqv, wp, inner_mid, middle_bias, *post)
+    mid = middle_block(features, nrm, keys, values, wqv, wp, inner_mid, bias, *post)
     return convs(
-        flags,
         features,
         row_one,
         row_two,

time: 51.5 us -> 43.5 us (0.84)
  the two profiles are of different devices: /device:TPU:20 before, /device:TPU:12 now
where the time goes in v2:
time: 43.5 us; the launch traced here: 43.3 us
  Pallas kernels  25.3 us (58%)
  starting transfers between devices  11.7 us (27%)
  waiting for transfers between devices  4.25 us (10%)
  other arithmetic  0.99 us (2%)
  local copies, waits for them, and re-layouts  0.85 us (2%)
    ppermute x6, starting transfers between devices, swapped(): out.append(lax.ppermute(payload, axis, pairs))  11.7 us
    pallas_call x1, Pallas kernels, convs(): call(conv_kernel, jax.ShapeDtypeStruct((feats, 2 * height, 2 * cols), BF1...  6.47 us
    pallas_call x1, Pallas kernels, outer_block(): call(outer_kernel, (jax.ShapeDtypeStruct((3, span, chans), BF16), jax.Sha...  5.81 us
    pallas_call x1, Pallas kernels, inner_block(): call(inner_kernel, (jax.ShapeDtypeStruct((height + 2 * RIM, cols, chans),...  4.64 us
    pallas_call x1, Pallas kernels, build_bias(): call(bias_kernel, jax.ShapeDtypeStruct((4, HEADS, KEYS, 128), BF16), [plt...  4.62 us
    ppermute x6, waiting for transfers between devices, swapped(): out.append(lax.ppermute(payload, axis, pairs))  4.25 us
    pallas_call x1, Pallas kernels, middle_block(): call(middle_kernel, jax.ShapeDtypeStruct((8, cols, chans), F32), attentio...  3.58 us
    select_n x1, other arithmetic, on_device(): jnp.where(even_row, low, high)  0.99 us
  transfers between devices with their start and end apart: 6, of which 2 were waited for; matrix products, arithmetic and copies ran while one was open for 0% of the time, Pallas kernels for 30%

profile of v2, /device:TPU:12, one launch (start us, length us, event | category | flops | bytes accessed | tf_op | source)
XLA Modules:
  0.0 43.3 jit_solution(18026092718808783278)
XLA Ops:
  0.0 1.0 %broadcast_select_fusion = (bf16[4,64,180]{2,1,0:T(8,128)(2,1)S(1)}, bf16[4,64,180]{2,1,0:T(8,128)(2,1)S(1)}) fusion(pred[]{:T(512)S(6)} %eq.5, bf16[16,64,180]{2,1,0:T(8,128)(2,1)} %own_ref.9), kind=kLoop, calls=%fused_computation | loop fusion | flops 92160 | bytes 368641 | tf_op jit(solution)/shard_map/jit(_where)/select_n | solution.py:758
  1.0 3.5 %collective-permute-start.1 = (bf16[4,64,180]{2,1,0:T(8,128)(2,1)S(1)}, bf16[4,64,180]{2,1,0:T(8,128)(2,1)S(1)}, u32[]{:S(2)}, u32[]{:S(2)}) collective-permute-start(bf16[4,64,180]{2,1,0:T(8,128)(2,1)S(1)} %get-tuple-element.37), channel_id=1, source_target_pairs={{8,16},{16,8},{9,17},{17,9},{10,18},{18,10},{11,19},{19,11},{12,20... | collective-permute-start | bytes 276488 | tf_op jit(solution)/shard_map/ppermute | solution.py:737
  4.5 0.1 collective-permute-start
  4.6 0.0 copy-start.8
  4.6 0.8 %copy-done.8 = f32[1521,6]{0,1:T(8,128)S(1)} copy-done((f32[1521,6]{0,1:T(8,128)S(1)}, f32[1521,6]{0,1:T(8,128)}, u32[]{:S(2)}) %copy-start.8) | copy-done | bytes 36528
  5.4 0.0 copy-start
  5.4 0.0 copy-start.4
  5.4 0.0 copy-start.5
  5.4 0.0 copy-start.6
  5.4 0.0 copy-start.7
  5.4 0.0 copy-start.9
  5.4 0.0 copy-start.10
  5.4 4.6 %shard_map.110.bias_ref = bf16[4,6,576,128]{3,2,1,0:T(8,128)(2,1)S(1)} custom-call(f32[6,1521]{1,0:T(8,128)S(1)} %bitcast.9), custom_call_target="tpu_custom_call" | custom-call | flops 4000000000 | bytes 4000000 | tf_op jit(solution)/shard_map/pallas_call | solution.py:96
  10.0 0.0 collective-permute-done.1.row_two_ref
  10.1 0.0 collective-permute-done.row_one_ref
  10.1 0.0 copy-done
  10.1 0.2 shard_map.109
  10.3 0.1 collective-permute-start.2
  10.3 3.4 %collective-permute-start.3 = (bf16[24,24,180]{2,1,0:T(8,128)(2,1)S(1)}, bf16[24,24,180]{2,1,0:T(8,128)(2,1)S(1)}, u32[]{:S(2)}, u32[]{:S(2)}) collective-permute-start(bf16[24,24,180]{2,1,0:T(8,128)(2,1)S(1)} %get-tuple-element.22), channel_id=1, source_target_pairs={{1,2},{3,4},{5,6},{2,1},{4,3},{6,5},{9,10},{11,12},{13,14},{10,9},... | collective-permute-start | bytes 622088 | tf_op jit(solution)/shard_map/ppermute | solution.py:737
  13.8 0.0 copy-done.4
  13.8 0.0 copy-done.5
  13.8 0.0 copy-done.6
  13.8 0.0 copy-done.7
  13.8 0.0 copy-done.9
  13.8 0.0 copy-done.10
  13.8 4.6 %shard_map.111 = (f32[24,64,180]{2,1,0:T(8,128)S(1)}, bf16[180,384]{1,0:T(8,128)(2,1)S(1)}, bf16[384,180]{1,0:T(8,128)(2,1)S(1)}, bf16[192,180]{1,0:T(8,128)(2,1...) custom-call(bf16[16,64,180]{2,1,0:T(8,128)(2,1)S(1)} %copy-done, ...), custom_call_target="tpu_custom_call" | custom-call | flops 5000000000 | bytes 4000000 | tf_op jit(solution)/shard_map/pallas_call | solution.py:482
  18.5 0.0 collective-permute-done.2.col_one_ref
  18.5 3.6 %collective-permute-done.3.col_two_ref = bf16[24,24,180]{2,1,0:T(8,128)(2,1)S(1)} collective-permute-done((bf16[24,24,180]{2,1,0:T(8,128)(2,1)S(1)}, bf16[24,24,180]{2,1,0:T(8,128)(2,1)S(1)}, u32[]{:S(2)}, u32[]{:S(2)}) %collective-permute-start.3) | collective-permute-done | bytes 207392 | tf_op jit(solution)/shard_map/ppermute | solution.py:737
  22.1 5.8 %shard_map.112 = (bf16[3,80,180]{2,1,0:T(8,128)(2,1)S(1)}, bf16[3,80,180]{2,1,0:T(8,128)(2,1)S(1)}, f32[8,80,180]{2,1,0:T(8,128)S(1)}, f32[8,16,180]{2,1,0:T(8,1...) custom-call(bf16[16,64,180]{2,1,0:T(8,128)(2,1)S(1)} %copy-done, ...), custom_call_target="tpu_custom_call" | custom-call | flops 5000000000 | bytes 4000000 | tf_op jit(solution)/shard_map/pallas_call | solution.py:503
  28.0 2.1 %collective-permute-start.4 = (bf16[3,80,180]{2,1,0:T(8,128)(2,1)S(1)}, bf16[3,80,180]{2,1,0:T(8,128)(2,1)S(1)}, u32[]{:S(2)}, u32[]{:S(2)}) collective-permute-start(bf16[3,80,180]{2,1,0:T(8,128)(2,1)S(1)} %get-tuple-element.30), channel_id=1, source_target_pairs={{0,8},{16,24},{8,0},{24,16},{1,9},{17,25},{9,1},{25,17},{2,10},{18... | collective-permute-start | bytes 259208 | tf_op jit(solution)/shard_map/ppermute | solution.py:737
  30.0 2.5 %collective-permute-start.5 = (bf16[3,80,180]{2,1,0:T(8,128)(2,1)S(1)}, bf16[3,80,180]{2,1,0:T(8,128)(2,1)S(1)}, u32[]{:S(2)}, u32[]{:S(2)}) collective-permute-start(bf16[3,80,180]{2,1,0:T(8,128)(2,1)S(1)} %get-tuple-element.31), channel_id=1, source_target_pairs={{8,16},{16,8},{9,17},{17,9},{10,18},{18,10},{11,19},{19,11},{12,20... | collective-permute-start | bytes 259208 | tf_op jit(solution)/shard_map/ppermute | solution.py:737
  32.6 0.0 copy-start.1
  32.6 0.0 copy-start.2
  32.6 0.0 copy-start.3
  32.6 3.6 %shard_map.113.mid_ref = f32[8,64,180]{2,1,0:T(8,128)S(1)} custom-call(bf16[16,64,180]{2,1,0:T(8,128)(2,1)S(1)} %copy-done, f32[24,64,180]{2,1,0:T(8,128)S(1)} %get-tuple-element.23.nrm_ref, bf16[5,576,384]{2,1,0:T(8,128)(2,1)S(1)} %get-tuple-element.34.k_ref, bf16[5,192,576]{2,1,0:T(8,128)(2,1)S(1)} %get-tuple-element.35.v_ref, ...), custom_call_target="tpu_custom_call" | custom-call | flops 5000000000 | bytes 4000000 | tf_op jit(solution)/shard_map/pallas_call | solution.py:526
  36.2 0.0 collective-permute-done.4.back_one_ref
  36.2 0.6 %collective-permute-done.5.back_two_ref = bf16[3,80,180]{2,1,0:T(8,128)(2,1)S(1)} collective-permute-done((bf16[3,80,180]{2,1,0:T(8,128)(2,1)S(1)}, bf16[3,80,180]{2,1,0:T(8,128)(2,1)S(1)}, u32[]{:S(2)}, u32[]{:S(2)}) %collective-permute-start.5) | collective-permute-done | bytes 86432 | tf_op jit(solution)/shard_map/ppermute | solution.py:737
  36.8 0.0 copy-done.1
  36.8 0.0 copy-done.2
  36.8 0.0 copy-done.3
  36.8 6.5 %shard_map.114 = bf16[64,32,128]{2,1,0:T(8,128)(2,1)} custom-call(bf16[16,64,180]{2,1,0:T(8,128)(2,1)S(1)} %copy-done, bf16[4,64,180]{2,1,0:T(8,128)(2,1)S(1)} %collective-permute-done.row_one_ref, bf16[4,64,180]{2,1,0:T(8,128)(2,1)S(1)} %collective-permute-done.1.row_two_ref, bf16[24,24,180]{2,1,0:T(8,128)(2,1)S(1)} %collective-permute-done.2.col_one_ref, ...), custom_call_target="tpu_custom_call" | custom-call | flops 8000000000 | bytes 4000000 | tf_op jit(solution)/shard_map/pallas_call | solution.py:710
Async XLA Ops:
  1.0 9.1 %collective-permute-start.1 = (bf16[4,64,180]{2,1,0:T(8,128)(2,1)S(1)}, bf16[4,64,180]{2,1,0:T(8,128)(2,1)S(1)}, u32[]{:S(2)}, u32[]{:S(2)}) collective-permute-start(bf16[4,64,180]{2,1,0:T(8,128)(2,1)S(1)} %get-tuple-element.37), channel_id=1, source_target_pairs={{8,16},{16,8},{9,17},{17,9},{10,18},{18,10},{11,19},{19,11},{12,20... | collective-permute-start | bytes 276488 | tf_op jit(solution)/shard_map/ppermute | solution.py:737
  4.5 5.6 %collective-permute-start = (bf16[4,64,180]{2,1,0:T(8,128)(2,1)S(1)}, bf16[4,64,180]{2,1,0:T(8,128)(2,1)S(1)}, u32[]{:S(2)}, u32[]{:S(2)}) collective-permute-start(bf16[4,64,180]{2,1,0:T(8,128)(2,1)S(1)} %get-tuple-element.38), channel_id=1, source_target_pairs={{0,8},{16,24},{8,0},{24,16},{1,9},{17,25},{9,1},{25,17},{2,10},{18... | collective-permute-start | bytes 276488 | tf_op jit(solution)/shard_map/ppermute | solution.py:737
  4.6 0.8 %copy-start.8 = (f32[1521,6]{0,1:T(8,128)S(1)}, f32[1521,6]{0,1:T(8,128)}, u32[]{:S(2)}) copy-start(f32[1521,6]{0,1:T(8,128)} %param.14) | copy-start | bytes 109516
  5.4 4.7 %copy-start = (bf16[16,64,180]{2,1,0:T(8,128)(2,1)S(1)}, bf16[16,64,180]{2,1,0:T(8,128)(2,1)}, u32[]{:S(2)}) copy-start(bf16[16,64,180]{2,1,0:T(8,128)(2,1)} %own_ref.9) | copy-start | bytes 1105924
  5.4 8.4 %copy-start.4 = (bf16[180,540]{1,0:T(8,128)(2,1)S(1)}, bf16[180,540]{1,0:T(8,128)(2,1)}, u32[]{:S(2)}) copy-start(bf16[180,540]{1,0:T(8,128)(2,1)} %qkv_ref.1) | copy-start | bytes 583204
  5.4 8.4 %copy-start.5 = (bf16[180,360]{1,0:T(8,128)(2,1)S(1)}, bf16[180,360]{1,0:T(8,128)(2,1)}, u32[]{:S(2)}) copy-start(bf16[180,360]{1,0:T(8,128)(2,1)} %hidden_ref.5) | copy-start | bytes 388804
  5.4 8.4 %copy-start.6 = (bf16[360,180]{0,1:T(8,128)(2,1)S(1)}, bf16[360,180]{0,1:T(8,128)(2,1)}, u32[]{:S(2)}) copy-start(bf16[360,180]{0,1:T(8,128)(2,1)} %param.18) | copy-start | bytes 388804
  5.4 8.4 %copy-start.7 = (bf16[180,180]{1,0:T(8,128)(2,1)S(1)}, bf16[180,180]{1,0:T(8,128)(2,1)}, u32[]{:S(2)}) copy-start(bf16[180,180]{1,0:T(8,128)(2,1)} %proj_ref.1) | copy-start | bytes 194404
  5.4 8.4 %copy-start.9 = (f32[180]{0:T(256)S(1)}, f32[180]{0:T(256)}, u32[]{:S(2)}) copy-start(f32[180]{0:T(256)} %param.12) | copy-start | bytes 2164
  5.4 8.4 %copy-start.10 = (f32[180]{0:T(256)S(1)}, f32[180]{0:T(256)}, u32[]{:S(2)}) copy-start(f32[180]{0:T(256)} %param.16) | copy-start | bytes 2164
  10.3 8.2 %collective-permute-start.2 = (bf16[24,24,180]{2,1,0:T(8,128)(2,1)S(1)}, bf16[24,24,180]{2,1,0:T(8,128)(2,1)S(1)}, u32[]{:S(2)}, u32[]{:S(2)}) collective-permute-start(bf16[24,24,180]{2,1,0:T(8,128)(2,1)S(1)} %get-tuple-element.21), channel_id=1, source_target_pairs={{0,1},{2,3},{4,5},{6,7},{1,0},{3,2},{5,4},{7,6},{8,9},{10,11},{12,... | collective-permute-start | bytes 622088 | tf_op jit(solution)/shard_map/ppermute | solution.py:737
  10.3 11.8 %collective-permute-start.3 = (bf16[24,24,180]{2,1,0:T(8,128)(2,1)S(1)}, bf16[24,24,180]{2,1,0:T(8,128)(2,1)S(1)}, u32[]{:S(2)}, u32[]{:S(2)}) collective-permute-start(bf16[24,24,180]{2,1,0:T(8,128)(2,1)S(1)} %get-tuple-element.22), channel_id=1, source_target_pairs={{1,2},{3,4},{5,6},{2,1},{4,3},{6,5},{9,10},{11,12},{13,14},{10,9},... | collective-permute-start | bytes 622088 | tf_op jit(solution)/shard_map/ppermute | solution.py:737
  28.0 8.2 %collective-permute-start.4 = (bf16[3,80,180]{2,1,0:T(8,128)(2,1)S(1)}, bf16[3,80,180]{2,1,0:T(8,128)(2,1)S(1)}, u32[]{:S(2)}, u32[]{:S(2)}) collective-permute-start(bf16[3,80,180]{2,1,0:T(8,128)(2,1)S(1)} %get-tuple-element.30), channel_id=1, source_target_pairs={{0,8},{16,24},{8,0},{24,16},{1,9},{17,25},{9,1},{25,17},{2,10},{18... | collective-permute-start | bytes 259208 | tf_op jit(solution)/shard_map/ppermute | solution.py:737
  30.0 6.8 %collective-permute-start.5 = (bf16[3,80,180]{2,1,0:T(8,128)(2,1)S(1)}, bf16[3,80,180]{2,1,0:T(8,128)(2,1)S(1)}, u32[]{:S(2)}, u32[]{:S(2)}) collective-permute-start(bf16[3,80,180]{2,1,0:T(8,128)(2,1)S(1)} %get-tuple-element.31), channel_id=1, source_target_pairs={{8,16},{16,8},{9,17},{17,9},{10,18},{18,10},{11,19},{19,11},{12,20... | collective-permute-start | bytes 259208 | tf_op jit(solution)/shard_map/ppermute | solution.py:737
  32.6 4.2 %copy-start.1 = (bf16[3,3,180,180]{3,2,1,0:T(8,128)(2,1)S(1)}, bf16[3,3,180,180]{3,2,1,0:T(8,128)(2,1)}, u32[]{:S(2)}) copy-start(bf16[3,3,180,180]{3,2,1,0:T(8,128)(2,1)} %group_ref.1) | copy-start | bytes 1749604
  32.6 4.2 %copy-start.2 = (bf16[3,3,180,64]{2,3,1,0:T(8,128)(2,1)S(1)}, bf16[3,3,180,64]{2,3,1,0:T(8,128)(2,1)}, u32[]{:S(2)}) copy-start(bf16[3,3,180,64]{2,3,1,0:T(8,128)(2,1)} %param.20) | copy-start | bytes 622084
  32.6 4.2 %copy-start.3 = (bf16[3,3,64,256]{3,2,1,0:T(8,128)(2,1)S(1)}, bf16[3,3,64,256]{3,2,1,0:T(8,128)(2,1)}, u32[]{:S(2)}) copy-start(bf16[3,3,64,256]{3,2,1,0:T(8,128)(2,1)} %upsample_ref.1) | copy-start | bytes 884740

commit v3 on v2

--- a/solution.py
+++ b/solution.py
@@ -264,24 +264,56 @@
     return jnp.concatenate([ref[0:4, c0 : c0 + WIN], ref[12:16, c0 : c0 + WIN]], axis=0)
 
 
-def pack_kernel(own_ref, row_one_ref, row_two_ref, pay_one_ref, pay_two_ref):
+def halves(wide, count):
+    left = lax.broadcasted_iota(jnp.int32, (1, 128), 1) < 64
+    rest = wide.shape[0] - count
+    out = jnp.where(left, wide[0:rest], pltpu.roll(wide[count:], 64, 1))
+    return out if rest == count else jnp.concatenate([out, wide[rest:count]], axis=0)
+
+
+def unhalve(packed, rows):
+    count = packed.shape[0]
+    return jnp.concatenate([packed, pltpu.roll(packed[0 : rows - count], 64, 1)], axis=0)
+
+
+def pack_kernel(own_ref, row_one_ref, row_two_ref, pay_one_ref, pay_two_ref, x_scr, flat):
     height, cols, chans = own_ref.shape
     even_row, even_col = at_edges()[4:]
     above, below = from_sides(even_row, row_one_ref[...], row_two_ref[...])
-    for rows, part in (
-        (slice(0, RIM), above),
-        (slice(RIM, RIM + height), own_ref[...].astype(F32)),
-        (slice(RIM + height, 2 * RIM + height), below),
-    ):
-        low, high = part[:, 0:EDGE], part[:, cols - EDGE : cols]
-        pay_one_ref[rows] = jnp.where(even_col, high, low).astype(BF16)
-        pay_two_ref[rows] = jnp.where(even_col, low, high).astype(BF16)
+    x_scr[0:RIM] = above
+    x_scr[RIM : RIM + height] = own_ref[...].astype(F32)
+    x_scr[RIM + height :] = below
+    for side, near, far in ((0, 0, WIN), (1, cols - WIN, cols - WIN - RIM)):
+        for r in range(height + 2 * RIM):
+            flat[side, WIN * r : WIN * (r + 1), 0:chans] = x_scr[r, near : near + WIN]
+            place = WIN * (height + 2 * RIM) + RIM * r
+            flat[side, place : place + RIM, 0:chans] = x_scr[r, far : far + RIM]
+    count = flat.shape[1]
+    for lanes in (slice(0, 128), slice(128, 256)):
+        low, high = flat[0, :, lanes], flat[1, :, lanes]
+        one, two = jnp.where(even_col, high, low), jnp.where(even_col, low, high)
+        rows = slice(0, count)
+        if lanes.start:
+            one, two = halves(one, count // 2), halves(two, count // 2)
+            rows = slice(count, count + count // 2)
+        pay_one_ref[rows] = one.astype(BF16)
+        pay_two_ref[rows] = two.astype(BF16)
 
 
 def pack(own, row_one, row_two):
     height, cols, chans = own.shape
-    pay = jax.ShapeDtypeStruct((height + 2 * RIM, EDGE, chans), BF16)
-    return call(pack_kernel, (pay, pay), [], 1_000_000, 1_000_000)(own, row_one, row_two)
+    pixels = (height + 2 * RIM) * (WIN + RIM)
+    pay = jax.ShapeDtypeStruct((pixels * 3 // 2, 128), BF16)
+    return call(
+        pack_kernel,
+        (pay, pay),
+        [
+            pltpu.VMEM((height + 2 * RIM, cols, chans), F32),
+            pltpu.VMEM((2, pixels, 256), F32),
+        ],
+        1_000_000,
+        1_000_000,
+    )(own, row_one, row_two)
 
 
 def inner_kernel(
@@ -351,8 +383,8 @@
 def outer_kernel(
     own_ref,
     nrm_ref,
+    col_two_ref,
     col_one_ref,
-    col_two_ref,
     gain_one_ref,
     wk_ref,
     wqv_ref,
@@ -368,10 +400,13 @@
     pay_two_ref,
     edge_ref,
     side_ref,
+    strip_ref,
     k_ref,
     v_ref,
     side_scr,
     x_scr,
+    n_scr,
+    b_scr,
     q_scr,
     s_scr,
     m_scr,
@@ -383,12 +418,21 @@
     inner = cols // WIN - 2
     flags = at_edges()
     gain_one = gain_one_ref[...]
-    for r in range(height + 2 * RIM):
-        both = from_sides(flags[5], col_one_ref[r], col_two_ref[r])
-        for side in range(2):
-            if RIM <= r < RIM + height:
-                x_scr[side, r - RIM] = both[side]
-            side_scr[side, r, side * EDGE : (side + 1) * EDGE] = layer_norm(both[side], gain_one)
+    rows = height + 2 * RIM
+    pixels = rows * (WIN + RIM)
+    both = from_sides(flags[5], col_one_ref[...], col_two_ref[...])
+    for side in range(2):
+        x_scr[side, :, 0:128] = both[side][0:pixels]
+        x_scr[side, :, 128:256] = unhalve(both[side][pixels:], pixels)
+        n_scr[...] = layer_norm(x_scr[side, :, 0:chans], gain_one)
+        near, far = (EDGE - WIN, EDGE - WIN - RIM) if side == 0 else (EDGE, EDGE + WIN)
+        for r in range(rows):
+            side_scr[side, r, near : near + WIN] = n_scr[WIN * r : WIN * (r + 1)]
+            place = WIN * rows + RIM * r
+            side_scr[side, r, far : far + RIM] = n_scr[place : place + RIM]
+        c0 = WIN - STRIP if side == 0 else 0
+        x = x_scr[side, 0 : WIN * rows, 0:chans].reshape(rows, WIN, chans)
+        strip_ref[side] = x[:, c0 : c0 + STRIP]
     side_scr[0, :, EDGE : 2 * EDGE] = nrm_ref[:, 0:EDGE]
     side_scr[1, :, 0:EDGE] = nrm_ref[:, cols - EDGE : cols]
     k_ref[2] = inner_k_ref[inner - 1]
@@ -400,7 +444,7 @@
     for g in range(4):
         side, c0 = g // 2, spots[g]
         if g in (0, 3):
-            x = x_scr[side, :, c0 - side * EDGE : c0 - side * EDGE + STRIP]
+            x = strip_ref[side, RIM : RIM + height]
             queries.append(side_scr[side, RIM : RIM + height, c0 : c0 + STRIP])
         else:
             x = border_rows(own_ref, c0).astype(F32)
@@ -424,8 +468,14 @@
             image[0:4, c0 : c0 + WIN] = one[0:4]
             image[12:16, c0 : c0 + WIN] = one[4:8]
     even = flags[4]
-    pay_one_ref[...] = jnp.where(even, image[13:16], image[0:3]).astype(BF16)
-    pay_two_ref[...] = jnp.where(even, image[0:3], image[13:16]).astype(BF16)
+    count = 3 * image.shape[1]
+    for pay_ref, rows in (
+        (pay_one_ref, jnp.where(even, image[13:16], image[0:3])),
+        (pay_two_ref, jnp.where(even, image[0:3], image[13:16])),
+    ):
+        b_scr[:, 0:chans] = rows.reshape(count, chans)
+        pay_ref[0:count] = b_scr[:, 0:128].astype(BF16)
+        pay_ref[count:] = halves(b_scr[:, 128:256], 128).astype(BF16)
     edge_ref[0:4] = image[0:4]
     edge_ref[4:8] = image[12:16]
     side_ref[:, 0:STRIP] = image[4:12, 0:STRIP]
@@ -503,16 +553,19 @@
     return call(
         outer_kernel,
         (
-            jax.ShapeDtypeStruct((3, span, chans), BF16),
-            jax.ShapeDtypeStruct((3, span, chans), BF16),
+            jax.ShapeDtypeStruct((3 * span + 128, 128), BF16),
+            jax.ShapeDtypeStruct((3 * span + 128, 128), BF16),
             jax.ShapeDtypeStruct((8, span, chans), F32),
             jax.ShapeDtypeStruct((8, 2 * STRIP, chans), F32),
+            jax.ShapeDtypeStruct((2, height + 2 * RIM, STRIP, chans), F32),
             jax.ShapeDtypeStruct((5, KEYS, 3 * 128), BF16),
             jax.ShapeDtypeStruct((5, HEADS * HP, KEYS), BF16),
         ),
         [
             pltpu.VMEM((2, height + 2 * RIM, 2 * EDGE, chans), F32),
-            pltpu.VMEM((2, height, EDGE, chans), F32),
+            pltpu.VMEM((2, (height + 2 * RIM) * (WIN + RIM), 256), F32),
+            pltpu.VMEM(((height + 2 * RIM) * (WIN + RIM), chans), F32),
+            pltpu.VMEM((3 * span, 256), F32),
             *attention_scratch(4),
             pltpu.VMEM((height, span, chans), F32),
         ],
@@ -536,8 +589,7 @@
     own_ref,
     row_one_ref,
     row_two_ref,
-    col_one_ref,
-    col_two_ref,
+    strip_ref,
     back_one_ref,
     back_two_ref,
     edge_ref,
@@ -561,7 +613,7 @@
 ):
     height, cols, chans = own_ref.shape
     span = cols + 2 * STRIP
-    at_left, at_right, at_top, at_bottom, even_row, even_col = at_edges()
+    at_left, at_right, at_top, at_bottom, even_row, _ = at_edges()
 
     feats = before_ref.shape[2]
     pad = chans // 16 * 16
@@ -586,19 +638,20 @@
     base[2 : 2 + height, STRIP : STRIP + cols] = own_ref[...].astype(F32)
     base[2 + height : 4 + height, STRIP : STRIP + cols] = below[0:2]
     rows = slice(2, height + 6)
-    before_side, after_side = from_sides(even_col, col_one_ref[rows], col_two_ref[rows])
-    base[:, 0:STRIP] = before_side[:, EDGE - STRIP :]
-    base[:, STRIP + cols : span] = after_side[:, 0:STRIP]
+    base[:, 0:STRIP] = strip_ref[0, rows]
+    base[:, STRIP + cols : span] = strip_ref[1, rows]
     base[:, span:] = jnp.zeros((height + 4, STRIP, chans), F32)
     image[:, span:] = jnp.zeros((height + 6, STRIP, chans), F32)
     above, below = from_sides(even_row, back_one_ref[...], back_two_ref[...])
-    image[0:3, 0:span] = above
+    for rows, packed in ((slice(0, 3), above), (slice(19, 22), below)):
+        image[rows, 0:span, 0:128] = packed[0 : 3 * span].reshape(3, span, 128)
+        rest = unhalve(packed[3 * span :], 3 * span).reshape(3, span, 128)
+        image[rows, 0:span, 128:chans] = rest[:, :, 0 : chans - 128]
     image[3:7, 0:span] = edge_ref[0:4]
     image[7:15, 0:STRIP] = side_ref[:, 0:STRIP]
     image[7:15, STRIP : STRIP + cols] = mid_ref[...]
     image[7:15, STRIP + cols : span] = side_ref[:, STRIP : 2 * STRIP]
     image[15:19, 0:span] = edge_ref[4:8]
-    image[19:22, 0:span] = below
     taps[...] = jnp.zeros(taps.shape, BF16)
     grouped[...] = jnp.zeros(grouped.shape, BF16)
     part = 4
@@ -731,11 +784,11 @@
 def swapped(axis, first, second):
     count = lax.axis_size(axis)
     out = []
-    for start, payload in ((0, first), (1, second)):
+    for start, payload in ((1, second), (0, first)):
         pairs = [(i, i + 1) for i in range(start, count - 1, 2)]
         pairs = pairs + [(b, a) for a, b in pairs]
         out.append(lax.ppermute(payload, axis, pairs))
-    return out
+    return out[::-1]
 
 
 def on_device(
@@ -772,11 +825,11 @@
         bias,
         *post,
     )
-    back_one, back_two, edge, side, keys, values = outer_block(
+    back_one, back_two, edge, side, strips, keys, values = outer_block(
         features,
         nrm,
+        col_two,
         col_one,
-        col_two,
         gain_one,
         wk,
         wqv,
@@ -793,8 +846,7 @@
         features,
         row_one,
         row_two,
-        col_one,
-        col_two,
+        strips,
         back_one,
         back_two,
         edge,

time: 43.5 us -> 40.6 us (0.933)
  waiting for transfers between devices: 4.25 us -> 0.72 us
  Pallas kernels: 25.3 us -> 25.9 us
    ppermute x6, waiting for transfers between devices: 4.25 us -> 0.72 us  [swapped(): out.append(lax.ppermute(payload, axis, pairs))]
  transfers between devices with their start and end apart: 6 -> 6, of which waited for: 2 -> 2; matrix products, arithmetic and copies ran while one was open for 0% -> 0% of each run, Pallas kernels for 30% -> 32%
where the time goes in v3:
time: 40.6 us; the launch traced here: 40.3 us
  Pallas kernels  25.9 us (64%)
  starting transfers between devices  11.7 us (29%)
  other arithmetic  0.99 us (2%)
  local copies, waits for them, and re-layouts  0.85 us (2%)
  waiting for transfers between devices  0.72 us (2%)
    ppermute x6, starting transfers between devices, swapped(): out.append(lax.ppermute(payload, axis, pairs))  11.7 us
    pallas_call x1, Pallas kernels, convs(): call(conv_kernel, jax.ShapeDtypeStruct((feats, 2 * height, 2 * cols), BF1...  6.5 us
    pallas_call x1, Pallas kernels, outer_block(): call(outer_kernel, (jax.ShapeDtypeStruct((3 * span + 128, 128), BF16), ja...  6.16 us
    pallas_call x1, Pallas kernels, inner_block(): call(inner_kernel, (jax.ShapeDtypeStruct((height + 2 * RIM, cols, chans),...  4.74 us
    pallas_call x1, Pallas kernels, build_bias(): call(bias_kernel, jax.ShapeDtypeStruct((4, HEADS, KEYS, 128), BF16), [plt...  4.62 us
    pallas_call x1, Pallas kernels, middle_block(): call(middle_kernel, jax.ShapeDtypeStruct((8, cols, chans), F32), attentio...  3.61 us
    select_n x1, other arithmetic, on_device(): jnp.where(even_row, low, high)  0.99 us
    unnamed x22, local copies, waits for them, and re-layouts  0.85 us
  transfers between devices with their start and end apart: 6, of which 2 were waited for; matrix products, arithmetic and copies ran while one was open for 0% of the time, Pallas kernels for 32%

profile of v3, /device:TPU:12, one launch (start us, length us, event | category | flops | bytes accessed | tf_op | source)
XLA Modules:
  0.0 40.3 jit_solution(13359175734770079417)
XLA Ops:
  0.0 1.0 %broadcast_select_fusion = (bf16[4,64,180]{2,1,0:T(8,128)(2,1)S(1)}, bf16[4,64,180]{2,1,0:T(8,128)(2,1)S(1)}) fusion(pred[]{:T(512)S(6)} %eq.5, bf16[16,64,180]{2,1,0:T(8,128)(2,1)} %own_ref.9), kind=kLoop, calls=%fused_computation | loop fusion | flops 92160 | bytes 368641 | tf_op jit(solution)/shard_map/jit(_where)/select_n | solution.py:811
  1.0 3.5 %collective-permute-start.1 = (bf16[4,64,180]{2,1,0:T(8,128)(2,1)S(1)}, bf16[4,64,180]{2,1,0:T(8,128)(2,1)S(1)}, u32[]{:S(2)}, u32[]{:S(2)}) collective-permute-start(bf16[4,64,180]{2,1,0:T(8,128)(2,1)S(1)} %get-tuple-element.39), channel_id=1, source_target_pairs={{8,16},{16,8},{9,17},{17,9},{10,18},{18,10},{11,19},{19,11},{12,20... | collective-permute-start | bytes 276488 | tf_op jit(solution)/shard_map/ppermute | solution.py:790
  4.5 0.1 collective-permute-start
  4.6 0.0 copy-start.8
  4.6 0.8 %copy-done.8 = f32[1521,6]{0,1:T(8,128)S(1)} copy-done((f32[1521,6]{0,1:T(8,128)S(1)}, f32[1521,6]{0,1:T(8,128)}, u32[]{:S(2)}) %copy-start.8) | copy-done | bytes 36528
  5.4 0.0 copy-start
  5.4 0.0 copy-start.4
  5.4 0.0 copy-start.5
  5.4 0.0 copy-start.6
  5.4 0.0 copy-start.7
  5.4 0.0 copy-start.9
  5.4 0.0 copy-start.10
  5.4 4.6 %shard_map.109.bias_ref = bf16[4,6,576,128]{3,2,1,0:T(8,128)(2,1)S(1)} custom-call(f32[6,1521]{1,0:T(8,128)S(1)} %bitcast.9), custom_call_target="tpu_custom_call" | custom-call | flops 4000000000 | bytes 4000000 | tf_op jit(solution)/shard_map/pallas_call | solution.py:96
  10.0 0.0 collective-permute-done.1.row_two_ref
  10.1 0.0 collective-permute-done.row_one_ref
  10.1 0.0 copy-done
  10.1 0.2 shard_map.111
  10.3 2.5 %collective-permute-start.2 = (bf16[720,128]{1,0:T(8,128)(2,1)S(1)}, bf16[720,128]{1,0:T(8,128)(2,1)S(1)}, u32[]{:S(2)}, u32[]{:S(2)}) collective-permute-start(bf16[720,128]{1,0:T(8,128)(2,1)S(1)} %get-tuple-element.23), channel_id=1, source_target_pairs={{1,2},{3,4},{5,6},{2,1},{4,3},{6,5},{9,10},{11,12},{13,14},{10,9},... | collective-permute-start | bytes 552968 | tf_op jit(solution)/shard_map/ppermute | solution.py:790
  12.8 1.1 %collective-permute-start.3 = (bf16[720,128]{1,0:T(8,128)(2,1)S(1)}, bf16[720,128]{1,0:T(8,128)(2,1)S(1)}, u32[]{:S(2)}, u32[]{:S(2)}) collective-permute-start(bf16[720,128]{1,0:T(8,128)(2,1)S(1)} %get-tuple-element.24), channel_id=1, source_target_pairs={{0,1},{2,3},{4,5},{6,7},{1,0},{3,2},{5,4},{7,6},{8,9},{10,11},{12,... | collective-permute-start | bytes 552968 | tf_op jit(solution)/shard_map/ppermute | solution.py:790
  13.9 0.0 copy-done.4
  13.9 0.0 copy-done.5
  13.9 0.0 copy-done.6
  13.9 0.0 copy-done.7
  13.9 0.0 copy-done.9
  13.9 0.0 copy-done.10
  13.9 4.7 %shard_map.110 = (f32[24,64,180]{2,1,0:T(8,128)S(1)}, bf16[180,384]{1,0:T(8,128)(2,1)S(1)}, bf16[384,180]{1,0:T(8,128)(2,1)S(1)}, bf16[192,180]{1,0:T(8,128)(2,1...) custom-call(bf16[16,64,180]{2,1,0:T(8,128)(2,1)S(1)} %copy-done, ...), custom_call_target="tpu_custom_call" | custom-call | flops 5000000000 | bytes 4000000 | tf_op jit(solution)/shard_map/pallas_call | solution.py:532
  18.7 0.5 %collective-permute-done.2.col_two_ref = bf16[720,128]{1,0:T(8,128)(2,1)S(1)} collective-permute-done((bf16[720,128]{1,0:T(8,128)(2,1)S(1)}, bf16[720,128]{1,0:T(8,128)(2,1)S(1)}, u32[]{:S(2)}, u32[]{:S(2)}) %collective-permute-start.2) | collective-permute-done | bytes 184352 | tf_op jit(solution)/shard_map/ppermute | solution.py:790
  19.1 0.0 collective-permute-done.3.col_one_ref
  19.1 6.2 %shard_map.112 = (bf16[368,128]{1,0:T(8,128)(2,1)S(1)}, bf16[368,128]{1,0:T(8,128)(2,1)S(1)}, f32[8,80,180]{2,1,0:T(8,128)S(1)}, f32[8,16,180]{2,1,0:T(8,128)S(1...) custom-call(bf16[16,64,180]{2,1,0:T(8,128)(2,1)S(1)} %copy-done, ...), custom_call_target="tpu_custom_call" | custom-call | flops 5000000000 | bytes 4000000 | tf_op jit(solution)/shard_map/pallas_call | solution.py:553
  25.3 2.1 %collective-permute-start.4 = (bf16[368,128]{1,0:T(8,128)(2,1)S(1)}, bf16[368,128]{1,0:T(8,128)(2,1)S(1)}, u32[]{:S(2)}, u32[]{:S(2)}) collective-permute-start(bf16[368,128]{1,0:T(8,128)(2,1)S(1)} %get-tuple-element.32), channel_id=1, source_target_pairs={{0,8},{16,24},{8,0},{24,16},{1,9},{17,25},{9,1},{25,17},{2,10},{18... | collective-permute-start | bytes 282632 | tf_op jit(solution)/shard_map/ppermute | solution.py:790
  27.4 2.5 %collective-permute-start.5 = (bf16[368,128]{1,0:T(8,128)(2,1)S(1)}, bf16[368,128]{1,0:T(8,128)(2,1)S(1)}, u32[]{:S(2)}, u32[]{:S(2)}) collective-permute-start(bf16[368,128]{1,0:T(8,128)(2,1)S(1)} %get-tuple-element.33), channel_id=1, source_target_pairs={{8,16},{16,8},{9,17},{17,9},{10,18},{18,10},{11,19},{19,11},{12,20... | collective-permute-start | bytes 282632 | tf_op jit(solution)/shard_map/ppermute | solution.py:790
  29.9 0.0 copy-start.1
  29.9 0.0 copy-start.2
  29.9 0.0 copy-start.3
  29.9 3.6 %shard_map.113.mid_ref = f32[8,64,180]{2,1,0:T(8,128)S(1)} custom-call(bf16[16,64,180]{2,1,0:T(8,128)(2,1)S(1)} %copy-done, f32[24,64,180]{2,1,0:T(8,128)S(1)} %get-tuple-element.22.nrm_ref, bf16[5,576,384]{2,1,0:T(8,128)(2,1)S(1)} %get-tuple-element.36.k_ref, bf16[5,192,576]{2,1,0:T(8,128)(2,1)S(1)} %get-tuple-element.37.v_ref, ...), custom_call_target="tpu_custom_call" | custom-call | flops 5000000000 | bytes 4000000 | tf_op jit(solution)/shard_map/pallas_call | solution.py:579
  33.6 0.0 collective-permute-done.4.back_one_ref
  33.6 0.3 collective-permute-done.5.back_two_ref
  33.8 0.0 copy-done.1
  33.8 0.0 copy-done.2
  33.8 0.0 copy-done.3
  33.8 6.5 %shard_map.114 = bf16[64,32,128]{2,1,0:T(8,128)(2,1)} custom-call(bf16[16,64,180]{2,1,0:T(8,128)(2,1)S(1)} %copy-done, bf16[4,64,180]{2,1,0:T(8,128)(2,1)S(1)} %collective-permute-done.row_one_ref, bf16[4,64,180]{2,1,0:T(8,128)(2,1)S(1)} %collective-permute-done.1.row_two_ref, f32[2,24,8,180]{3,2,1,0:T(8,128)S(1)} %get-tuple-element.31.strip_ref, ...), custom_call_target="tpu_custom_call" | custom-call | flops 8000000000 | bytes 4000000 | tf_op jit(solution)/shard_map/pallas_call | solution.py:763
Async XLA Ops:
  1.0 9.1 %collective-permute-start.1 = (bf16[4,64,180]{2,1,0:T(8,128)(2,1)S(1)}, bf16[4,64,180]{2,1,0:T(8,128)(2,1)S(1)}, u32[]{:S(2)}, u32[]{:S(2)}) collective-permute-start(bf16[4,64,180]{2,1,0:T(8,128)(2,1)S(1)} %get-tuple-element.39), channel_id=1, source_target_pairs={{8,16},{16,8},{9,17},{17,9},{10,18},{18,10},{11,19},{19,11},{12,20... | collective-permute-start | bytes 276488 | tf_op jit(solution)/shard_map/ppermute | solution.py:790
  4.5 5.6 %collective-permute-start = (bf16[4,64,180]{2,1,0:T(8,128)(2,1)S(1)}, bf16[4,64,180]{2,1,0:T(8,128)(2,1)S(1)}, u32[]{:S(2)}, u32[]{:S(2)}) collective-permute-start(bf16[4,64,180]{2,1,0:T(8,128)(2,1)S(1)} %get-tuple-element.40), channel_id=1, source_target_pairs={{0,8},{16,24},{8,0},{24,16},{1,9},{17,25},{9,1},{25,17},{2,10},{18... | collective-permute-start | bytes 276488 | tf_op jit(solution)/shard_map/ppermute | solution.py:790
  4.6 0.8 %copy-start.8 = (f32[1521,6]{0,1:T(8,128)S(1)}, f32[1521,6]{0,1:T(8,128)}, u32[]{:S(2)}) copy-start(f32[1521,6]{0,1:T(8,128)} %param.14) | copy-start | bytes 109516
  5.4 4.7 %copy-start = (bf16[16,64,180]{2,1,0:T(8,128)(2,1)S(1)}, bf16[16,64,180]{2,1,0:T(8,128)(2,1)}, u32[]{:S(2)}) copy-start(bf16[16,64,180]{2,1,0:T(8,128)(2,1)} %own_ref.9) | copy-start | bytes 1105924
  5.4 8.5 %copy-start.4 = (bf16[180,540]{1,0:T(8,128)(2,1)S(1)}, bf16[180,540]{1,0:T(8,128)(2,1)}, u32[]{:S(2)}) copy-start(bf16[180,540]{1,0:T(8,128)(2,1)} %qkv_ref.1) | copy-start | bytes 583204
  5.4 8.5 %copy-start.5 = (bf16[180,360]{1,0:T(8,128)(2,1)S(1)}, bf16[180,360]{1,0:T(8,128)(2,1)}, u32[]{:S(2)}) copy-start(bf16[180,360]{1,0:T(8,128)(2,1)} %hidden_ref.5) | copy-start | bytes 388804
  5.4 8.5 %copy-start.6 = (bf16[360,180]{0,1:T(8,128)(2,1)S(1)}, bf16[360,180]{0,1:T(8,128)(2,1)}, u32[]{:S(2)}) copy-start(bf16[360,180]{0,1:T(8,128)(2,1)} %param.18) | copy-start | bytes 388804
  5.4 8.5 %copy-start.7 = (bf16[180,180]{1,0:T(8,128)(2,1)S(1)}, bf16[180,180]{1,0:T(8,128)(2,1)}, u32[]{:S(2)}) copy-start(bf16[180,180]{1,0:T(8,128)(2,1)} %proj_ref.1) | copy-start | bytes 194404
  5.4 8.5 %copy-start.9 = (f32[180]{0:T(256)S(1)}, f32[180]{0:T(256)}, u32[]{:S(2)}) copy-start(f32[180]{0:T(256)} %param.12) | copy-start | bytes 2164
  5.4 8.5 %copy-start.10 = (f32[180]{0:T(256)S(1)}, f32[180]{0:T(256)}, u32[]{:S(2)}) copy-start(f32[180]{0:T(256)} %param.16) | copy-start | bytes 2164
  10.3 8.8 %collective-permute-start.2 = (bf16[720,128]{1,0:T(8,128)(2,1)S(1)}, bf16[720,128]{1,0:T(8,128)(2,1)S(1)}, u32[]{:S(2)}, u32[]{:S(2)}) collective-permute-start(bf16[720,128]{1,0:T(8,128)(2,1)S(1)} %get-tuple-element.23), channel_id=1, source_target_pairs={{1,2},{3,4},{5,6},{2,1},{4,3},{6,5},{9,10},{11,12},{13,14},{10,9},... | collective-permute-start | bytes 552968 | tf_op jit(solution)/shard_map/ppermute | solution.py:790
  12.8 6.3 %collective-permute-start.3 = (bf16[720,128]{1,0:T(8,128)(2,1)S(1)}, bf16[720,128]{1,0:T(8,128)(2,1)S(1)}, u32[]{:S(2)}, u32[]{:S(2)}) collective-permute-start(bf16[720,128]{1,0:T(8,128)(2,1)S(1)} %get-tuple-element.24), channel_id=1, source_target_pairs={{0,1},{2,3},{4,5},{6,7},{1,0},{3,2},{5,4},{7,6},{8,9},{10,11},{12,... | collective-permute-start | bytes 552968 | tf_op jit(solution)/shard_map/ppermute | solution.py:790
  25.3 8.3 %collective-permute-start.4 = (bf16[368,128]{1,0:T(8,128)(2,1)S(1)}, bf16[368,128]{1,0:T(8,128)(2,1)S(1)}, u32[]{:S(2)}, u32[]{:S(2)}) collective-permute-start(bf16[368,128]{1,0:T(8,128)(2,1)S(1)} %get-tuple-element.32), channel_id=1, source_target_pairs={{0,8},{16,24},{8,0},{24,16},{1,9},{17,25},{9,1},{25,17},{2,10},{18... | collective-permute-start | bytes 282632 | tf_op jit(solution)/shard_map/ppermute | solution.py:790
  27.4 6.5 %collective-permute-start.5 = (bf16[368,128]{1,0:T(8,128)(2,1)S(1)}, bf16[368,128]{1,0:T(8,128)(2,1)S(1)}, u32[]{:S(2)}, u32[]{:S(2)}) collective-permute-start(bf16[368,128]{1,0:T(8,128)(2,1)S(1)} %get-tuple-element.33), channel_id=1, source_target_pairs={{8,16},{16,8},{9,17},{17,9},{10,18},{18,10},{11,19},{19,11},{12,20... | collective-permute-start | bytes 282632 | tf_op jit(solution)/shard_map/ppermute | solution.py:790
  29.9 3.9 %copy-start.1 = (bf16[3,3,180,180]{3,2,1,0:T(8,128)(2,1)S(1)}, bf16[3,3,180,180]{3,2,1,0:T(8,128)(2,1)}, u32[]{:S(2)}) copy-start(bf16[3,3,180,180]{3,2,1,0:T(8,128)(2,1)} %group_ref.1) | copy-start | bytes 1749604
  29.9 3.9 %copy-start.2 = (bf16[3,3,180,64]{2,3,1,0:T(8,128)(2,1)S(1)}, bf16[3,3,180,64]{2,3,1,0:T(8,128)(2,1)}, u32[]{:S(2)}) copy-start(bf16[3,3,180,64]{2,3,1,0:T(8,128)(2,1)} %param.20) | copy-start | bytes 622084
  29.9 3.9 %copy-start.3 = (bf16[3,3,64,256]{3,2,1,0:T(8,128)(2,1)S(1)}, bf16[3,3,64,256]{3,2,1,0:T(8,128)(2,1)}, u32[]{:S(2)}) copy-start(bf16[3,3,64,256]{3,2,1,0:T(8,128)(2,1)} %upsample_ref.1) | copy-start | bytes 884740

commit v4 on v3

--- a/solution.py
+++ b/solution.py
@@ -39,10 +39,12 @@
     return center * lax.rsqrt(spread + 1e-05) * gain
 
 
-def call(kernel, out_shape, scratch, flops, bytes_accessed):
+def call(kernel, out_shape, scratch, flops, bytes_accessed, in_specs=None):
+    more = {} if in_specs is None else {"in_specs": in_specs}
     return pl.pallas_call(
         kernel,
         out_shape=out_shape,
+        **more,
         scratch_shapes=scratch,
         compiler_params=pltpu.CompilerParams(vmem_limit_bytes=24 * 2**20),
         cost_estimate=pl.CostEstimate(
@@ -73,12 +75,18 @@
 
         lanes = lax.broadcasted_iota(jnp.int32, (KWIN, 128), 1)
         expand(WIN, 0)
-        for p in range(KWIN):
-            rows = slice(p * KWIN, (p + 1) * KWIN)
-            low = w_scr[:, (23 - p) * WIN : (23 - p) * WIN + 128]
-            high = w_scr[:, (31 - p) * WIN : (31 - p) * WIN + 128]
-            x_scr[0, rows] = jnp.where(lanes < 64, low, high)
-            x_scr[1, rows] = w_scr[:, (27 - p) * WIN : (27 - p) * WIN + 128]
+        whole = w_scr[...]
+        for phase in range(8):
+            turned = whole if phase == 0 else pltpu.roll(whole, 640 - WIN * phase, 1)
+            for p in range(KWIN):
+                rows = slice(p * KWIN, (p + 1) * KWIN)
+                if (23 - p) % 8 == phase:
+                    at = (23 - p) // 8 * 128
+                    low, high = turned[:, at : at + 128], turned[:, at + 128 : at + 256]
+                    x_scr[0, rows] = jnp.where(lanes < 64, low, high)
+                if (27 - p) % 8 == phase:
+                    at = (27 - p) // 8 * 128
+                    x_scr[1, rows] = turned[:, at : at + 128]
         out_ref[1, h] = x_scr[0].astype(BF16)
         out_ref[3, h] = x_scr[1].astype(BF16)
         for kind, first in ((0, WIN - STRIP), (2, 0)):
@@ -157,70 +165,55 @@
             q_scr[g, t, HP : 2 * HP] = jnp.concatenate([none, two], axis=1)
 
 
-def lookup(g, values):
-    out = values[0]
-    for index in range(1, len(values)):
-        out = jnp.where(g >= index, values[index], out)
-    return out
-
-
-def attention(kinds, windows, q_scr, k_ref, v_ref, bias_ref, wp_ref, s_scr, m_scr, p_scr, o_scr):
-    groups = len(kinds)
+def attention(groups, q_scr, k_ref, v_ref, bias_ref, wp_ref, s_scr, p_scr, o_scr, finish):
     pairs = HEADS // 2
     step = 192
-
-    def keep(g, t, k0, top):
-        keys = k_ref[lookup(g, windows), k0 : k0 + step, 128 * t : 128 * t + 2 * HP]
+    stages = [(g, t) for g in range(len(groups)) for t in range(pairs)]
+
+    def keep(n, k0, top):
+        g, t = stages[n]
+        keys = k_ref[groups[g][1], k0 : k0 + step, 128 * t : 128 * t + 2 * HP]
         one = dot(keys, q_scr[g, t])
-        s_scr[t, k0 : k0 + step] = one
+        s_scr[n % 2, k0 : k0 + step] = one
         part = jnp.max(one.reshape(step // 8, 8, 256), axis=0)
         return part if top is None else jnp.maximum(top, part)
 
-    def sum_values(g, t):
-        o_scr[g, t] = dot(v_ref[lookup(g, windows), 2 * t * HP : 2 * (t + 1) * HP], p_scr[t])
-
-    top = None
-    for k0 in range(0, KEYS, step):
-        top = keep(0, 0, k0, top)
-    m_scr[...] = top
-    p_scr[pairs - 1] = jnp.zeros((KEYS, 256), BF16)
-
-    def attend(g, carry):
-        kind = lookup(g, kinds)
-        top = m_scr[...]
-        for t in range(pairs):
-            top = jnp.max(top, axis=0, keepdims=True)
-            if t == 0:
-                sum_values(jnp.maximum(g - 1, 0), pairs - 1)
-            else:
-                sum_values(g, t - 1)
-            following = g if t + 1 < pairs else jnp.minimum(g + 1, groups - 1)
-            later = None
-            for k0 in range(0, KEYS, step):
-                prob = jnp.exp2(s_scr[t, k0 : k0 + step] - top).astype(BF16)
-                for half in range(2):
-                    lanes = slice(128 * half, 128 * half + 128)
-                    p_scr[t, k0 : k0 + step, lanes] = (
-                        prob[:, lanes] * bias_ref[kind, 2 * t + half, k0 : k0 + step]
-                    )
-                later = keep(following, (t + 1) % pairs, k0, later)
-            top = later
-        m_scr[...] = top
-        return carry
-
-    lax.fori_loop(0, groups, attend, 0)
-    sum_values(groups - 1, pairs - 1)
-    attended = []
-    for g in range(groups):
+    def sum_values(n):
+        g, t = stages[n]
+        o_scr[n % 6] = dot(v_ref[groups[g][1], 2 * t * HP : 2 * (t + 1) * HP], p_scr[n % 2])
+
+    def project_group(g):
         parts = []
         for t in range(pairs):
             for half in range(2):
                 lanes = slice(128 * half, 128 * half + 128)
-                one = o_scr[g, t, half * HP : (half + 1) * HP, lanes]
+                one = o_scr[(pairs * g + t) % 6, half * HP : (half + 1) * HP, lanes]
                 parts.append((one * (1.0 / one[HD : HD + 1])).astype(BF16))
-        attended.append(jnp.concatenate(parts, axis=0))
-    attended = jnp.concatenate(attended, axis=1)
-    return lax.dot_general(attended, wp_ref[...], TN, preferred_element_type=F32)
+        attended = jnp.concatenate(parts, axis=0)
+        finish(g, lax.dot_general(attended, wp_ref[...], TN, preferred_element_type=F32))
+
+    top = None
+    for k0 in range(0, KEYS, step):
+        top = keep(0, k0, top)
+    for n, (g, t) in enumerate(stages):
+        top = jnp.max(top, axis=0, keepdims=True)
+        if n > 0:
+            sum_values(n - 1)
+        later = None
+        for k0 in range(0, KEYS, step):
+            prob = jnp.exp2(s_scr[n % 2, k0 : k0 + step] - top).astype(BF16)
+            for half in range(2):
+                lanes = slice(128 * half, 128 * half + 128)
+                p_scr[n % 2, k0 : k0 + step, lanes] = (
+                    prob[:, lanes] * bias_ref[groups[g][0], 2 * t + half, k0 : k0 + step]
+                )
+            if n + 1 < len(stages):
+                later = keep(n + 1, k0, later)
+        top = later
+        if t == 0 and g > 0:
+            project_group(g - 1)
+    sum_values(len(stages) - 1)
+    project_group(len(groups) - 1)
 
 
 def feed_forward(first, gain, hidden_ref, output_ref):
@@ -228,11 +221,6 @@
     inner = dot(normed, hidden_ref[...])
     inner = (0.5 * inner * (1.0 + lax.erf(inner * np.float32(np.sqrt(0.5))))).astype(BF16)
     return first + dot_nt(inner, output_ref[...])
-
-
-def feed_groups(first, gain, hidden_ref, output_ref):
-    groups = range(first.shape[0] // 128)
-    return [feed_forward(first[128 * g : 128 * (g + 1)], gain, hidden_ref, output_ref) for g in groups]
 
 
 def project(keys, wk_ref, wqv_ref, k_ref, v_ref, index):
@@ -276,7 +264,29 @@
     return jnp.concatenate([packed, pltpu.roll(packed[0 : rows - count], 64, 1)], axis=0)
 
 
-def pack_kernel(own_ref, row_one_ref, row_two_ref, pay_one_ref, pay_two_ref, x_scr, flat):
+def split_kernel(own_ref, pay_one_ref, pay_two_ref, sem):
+    even_row = at_edges()[4]
+    high = own_ref.shape[0] - RIM
+    one, two = jnp.where(even_row, high, 0), jnp.where(even_row, 0, high)
+    copies = [
+        pltpu.make_async_copy(own_ref.at[pl.ds(start, RIM)], pay_ref, sem.at[index])
+        for index, (start, pay_ref) in enumerate(((two, pay_two_ref), (one, pay_one_ref)))
+    ]
+    for copy in copies:
+        copy.start()
+    for copy in copies:
+        copy.wait()
+
+
+def split(own):
+    height, cols, chans = own.shape
+    pay = jax.ShapeDtypeStruct((RIM, cols, chans), BF16)
+    return call(
+        split_kernel, (pay, pay), [pltpu.SemaphoreType.DMA((2,))], 1000, 1000, [pl.BlockSpec(memory_space=pl.ANY)]
+    )(own)
+
+
+def pack_kernel(own_ref, row_two_ref, row_one_ref, pay_one_ref, pay_two_ref, x_scr, flat):
     height, cols, chans = own_ref.shape
     even_row, even_col = at_edges()[4:]
     above, below = from_sides(even_row, row_one_ref[...], row_two_ref[...])
@@ -313,13 +323,13 @@
         ],
         1_000_000,
         1_000_000,
-    )(own, row_one, row_two)
+    )(own, row_two, row_one)
 
 
 def inner_kernel(
     own_ref,
+    row_two_ref,
     row_one_ref,
-    row_two_ref,
     gain_one_ref,
     qkv_ref,
     proj_ref,
@@ -337,7 +347,6 @@
     mid_ref,
     q_scr,
     s_scr,
-    m_scr,
     p_scr,
     o_scr,
 ):
@@ -352,32 +361,29 @@
         nrm_ref[RIM + height + r] = layer_norm(below, gain_one)
     for r in range(height):
         nrm_ref[RIM + r] = layer_norm(own_ref[r].astype(F32), gain_one)
-    kinds, windows, first, queries = [], [], [], []
+    groups, first, queries = [], [], []
     for w in range(inner):
         c0 = WIN * (w + 1)
         project(nrm_ref[:, c0 - RIM : c0 - RIM + KWIN], wk_ref, wqv_ref, k_ref, v_ref, w)
-        first.append(border_rows(own_ref, c0).reshape(128, chans))
+        first.append(border_rows(own_ref, c0))
         queries.append(border_rows(nrm_ref.at[RIM : RIM + height], c0))
-        kinds.append(1)
-        windows.append(w)
+        groups.append((1, w))
     for w in range(inner - 1):
         c0 = WIN * (w + 1)
-        first.append(own_ref[4:12, c0 : c0 + WIN].reshape(128, chans))
+        first.append(own_ref[4:12, c0 : c0 + WIN])
         queries.append(nrm_ref[RIM + 4 : RIM + 12, c0 : c0 + WIN])
-        kinds.append(3)
-        windows.append(w)
-    groups = len(kinds)
+        groups.append((3, w))
     set_queries(q_scr, wqv_ref, queries)
-    first = jnp.concatenate(first, axis=0).astype(F32) + attention(
-        kinds, windows, q_scr, k_ref, v_ref, bias_ref, wp_ref, s_scr, m_scr, p_scr, o_scr
-    )
-    mixed = feed_groups(first, gain_two_ref[...], hidden_ref, output_ref)
-    for g in range(groups):
-        one = mixed[g].reshape(8, WIN, chans)
+
+    def finish(g, attended):
+        one = first[g].astype(F32).reshape(128, chans) + attended
+        one = feed_forward(one, gain_two_ref[...], hidden_ref, output_ref).reshape(8, WIN, chans)
         if g < inner:
             border_ref[:, WIN * g : WIN * (g + 1)] = one
         else:
             mid_ref[:, WIN * (g - inner) : WIN * (g - inner + 1)] = one
+
+    attention(groups, q_scr, k_ref, v_ref, bias_ref, wp_ref, s_scr, p_scr, o_scr, finish)
 
 
 def outer_kernel(
@@ -409,7 +415,6 @@
     b_scr,
     q_scr,
     s_scr,
-    m_scr,
     p_scr,
     o_scr,
     image,
@@ -451,22 +456,23 @@
             queries.append(border_rows(nrm_ref.at[RIM : RIM + height], c0))
         first.append(x.reshape(128, chans))
     set_queries(q_scr, wqv_ref, queries)
-    first = jnp.concatenate(first, axis=0) + attention(
-        [0, 1, 1, 2], [0, 1, 3, 4], q_scr, k_ref, v_ref, bias_ref, wp_ref, s_scr, m_scr, p_scr, o_scr
-    )
     image[0:4, STRIP + WIN : STRIP + cols - WIN] = inner_border_ref[0:4]
     image[12:16, STRIP + WIN : STRIP + cols - WIN] = inner_border_ref[4:8]
-    mixed = feed_groups(first, gain_two_ref[...], hidden_ref, output_ref)
-    for g in range(4):
+
+    def finish(g, attended):
+        one = feed_forward(first[g] + attended, gain_two_ref[...], hidden_ref, output_ref)
         if g in (0, 3):
-            one = jnp.where(flags[g // 3], 0.0, mixed[g]).reshape(height, STRIP, chans)
+            one = jnp.where(flags[g // 3], 0.0, one).reshape(height, STRIP, chans)
             c0 = 0 if g == 0 else STRIP + cols
             image[:, c0 : c0 + STRIP] = one
         else:
-            one = mixed[g].reshape(8, WIN, chans)
+            one = one.reshape(8, WIN, chans)
             c0 = STRIP + spots[g]
             image[0:4, c0 : c0 + WIN] = one[0:4]
             image[12:16, c0 : c0 + WIN] = one[4:8]
+
+    groups = [(0, 0), (1, 1), (1, 3), (2, 4)]
+    attention(groups, q_scr, k_ref, v_ref, bias_ref, wp_ref, s_scr, p_scr, o_scr, finish)
     even = flags[4]
     count = 3 * image.shape[1]
     for pay_ref, rows in (
@@ -497,30 +503,30 @@
     mid_ref,
     q_scr,
     s_scr,
-    m_scr,
     p_scr,
     o_scr,
 ):
     height, cols, chans = own_ref.shape
     spots = (0, cols - 2 * WIN, cols - WIN)
     set_queries(q_scr, wqv_ref, [nrm_ref[RIM + 4 : RIM + 12, c0 : c0 + WIN] for c0 in spots])
-    first = [own_ref[4:12, c0 : c0 + WIN].reshape(128, chans) for c0 in spots]
-    first = jnp.concatenate(first, axis=0).astype(F32) + attention(
-        [3, 3, 3], [1, 2, 3], q_scr, k_ref, v_ref, bias_ref, wp_ref, s_scr, m_scr, p_scr, o_scr
-    )
-    mixed = feed_groups(first, gain_two_ref[...], hidden_ref, output_ref)
     mid_ref[:, WIN : cols - 2 * WIN] = inner_mid_ref[...]
-    for g in range(3):
-        mid_ref[:, spots[g] : spots[g] + WIN] = mixed[g].reshape(8, WIN, chans)
+
+    def finish(g, attended):
+        c0 = spots[g]
+        one = own_ref[4:12, c0 : c0 + WIN].astype(F32).reshape(128, chans) + attended
+        one = feed_forward(one, gain_two_ref[...], hidden_ref, output_ref)
+        mid_ref[:, c0 : c0 + WIN] = one.reshape(8, WIN, chans)
+
+    groups = [(3, 1), (3, 2), (3, 3)]
+    attention(groups, q_scr, k_ref, v_ref, bias_ref, wp_ref, s_scr, p_scr, o_scr, finish)
 
 
 def attention_scratch(groups):
     return [
         pltpu.VMEM((groups, HEADS // 2, 2 * HP, 256), BF16),
-        pltpu.VMEM((HEADS // 2, KEYS, 256), F32),
-        pltpu.VMEM((8, 256), F32),
-        pltpu.VMEM((HEADS // 2, KEYS, 256), BF16),
-        pltpu.VMEM((groups, HEADS // 2, 2 * HP, 256), F32),
+        pltpu.VMEM((2, KEYS, 256), F32),
+        pltpu.VMEM((2, KEYS, 256), BF16),
+        pltpu.VMEM((6, 2 * HP, 256), F32),
     ]
 
 
@@ -587,11 +593,11 @@
 
 def conv_kernel(
     own_ref,
+    row_two_ref,
     row_one_ref,
-    row_two_ref,
     strip_ref,
+    back_two_ref,
     back_one_ref,
-    back_two_ref,
     edge_ref,
     side_ref,
     mid_ref,
@@ -804,12 +810,8 @@
     before_conv,
     upsample_conv,
 ):
-    height, cols, chans = features.shape
-    even_row = lax.axis_index("rows") % 2 == 0
-    low, high = features[:RIM], features[height - RIM :]
-    row_one, row_two = swapped(
-        "rows", jnp.where(even_row, high, low), jnp.where(even_row, low, high)
-    )
+    chans = features.shape[2]
+    row_one, row_two = swapped("rows", *split(features))
     col_one, col_two = swapped("cols", *pack(features, row_one, row_two))
 
     bias = build_bias(bias_table)
@@ -817,8 +819,8 @@
     post = (gain_two, hidden_weight, output_weight.T)
     nrm, wk, wqv, wp, inner_k, inner_v, inner_border, inner_mid = inner_block(
         features,
+        row_two,
         row_one,
-        row_two,
         gain_one,
         qkv_weight,
         proj_weight,
@@ -844,11 +846,11 @@
     mid = middle_block(features, nrm, keys, values, wqv, wp, inner_mid, bias, *post)
     return convs(
         features,
+        row_two,
         row_one,
-        row_two,
         strips,
+        back_two,
         back_one,
-        back_two,
         edge,
         side,
         mid,

time: 40.6 us -> 42.6 us (1.049)
  the two profiles are of different devices: /device:TPU:12 before, /device:TPU:0 now
where the time goes in v4:
time: 42.6 us; the launch traced here: 42.4 us
  Pallas kernels  27.2 us (64%)
  starting transfers between devices  13.1 us (31%)
  local copies, waits for them, and re-layouts  1.88 us (4%)
    ppermute x6, starting transfers between devices, swapped(): out.append(lax.ppermute(payload, axis, pairs))  13.1 us
    pallas_call x1, Pallas kernels, outer_block(): call(outer_kernel, (jax.ShapeDtypeStruct((3 * span + 128, 128), BF16), ja...  6.98 us
    pallas_call x1, Pallas kernels, convs(): call(conv_kernel, jax.ShapeDtypeStruct((feats, 2 * height, 2 * cols), BF1...  6.49 us
    pallas_call x1, Pallas kernels, inner_block(): call(inner_kernel, (jax.ShapeDtypeStruct((height + 2 * RIM, cols, chans),...  5.33 us
    pallas_call x1, Pallas kernels, middle_block(): call(middle_kernel, jax.ShapeDtypeStruct((8, cols, chans), F32), attentio...  4.1 us
    pallas_call x1, Pallas kernels, build_bias(): call(bias_kernel, jax.ShapeDtypeStruct((4, HEADS, KEYS, 128), BF16), [plt...  3.75 us
    unnamed x24, local copies, waits for them, and re-layouts  1.88 us
  transfers between devices with their start and end apart: 6, of which 0 were waited for; matrix products, arithmetic and copies ran while one was open for 0% of the time, Pallas kernels for 31%

profile of v4, /device:TPU:0, one launch (start us, length us, event | category | flops | bytes accessed | tf_op | source)
XLA Modules:
  0.0 42.4 jit_solution(878885034284976900)
XLA Ops:
  0.0 0.0 copy-start
  0.0 1.0 %copy-done = bf16[16,64,180]{2,1,0:T(8,128)(2,1)S(1)} copy-done((bf16[16,64,180]{2,1,0:T(8,128)(2,1)S(1)}, bf16[16,64,180]{2,1,0:T(8,128)(2,1)}, u32[]{:S(2)}) %copy-start) | copy-done | bytes 368664
  1.0 0.3 shard_map.109
  1.4 0.7 %collective-permute-start = (bf16[4,64,180]{2,1,0:T(8,128)(2,1)S(1)}, bf16[4,64,180]{2,1,0:T(8,128)(2,1)S(1)}, u32[]{:S(2)}, u32[]{:S(2)}) collective-permute-start(bf16[4,64,180]{2,1,0:T(8,128)(2,1)S(1)} %get-tuple-element.24), channel_id=1, source_target_pairs={{8,16},{16,8},{9,17},{17,9},{10,18},{18,10},{11,19},{19,11},{12,20... | collective-permute-start | bytes 276488 | tf_op jit(solution)/shard_map/ppermute | solution.py:796
  2.1 5.9 %collective-permute-start.1 = (bf16[4,64,180]{2,1,0:T(8,128)(2,1)S(1)}, bf16[4,64,180]{2,1,0:T(8,128)(2,1)S(1)}, u32[]{:S(2)}, u32[]{:S(2)}) collective-permute-start(bf16[4,64,180]{2,1,0:T(8,128)(2,1)S(1)} %get-tuple-element.25), channel_id=1, source_target_pairs={{0,8},{16,24},{8,0},{24,16},{1,9},{17,25},{9,1},{25,17},{2,10},{18... | collective-permute-start | bytes 276488 | tf_op jit(solution)/shard_map/ppermute | solution.py:796
  8.0 0.0 copy-start.9
  8.0 0.8 %copy-done.9 = f32[1521,6]{0,1:T(8,128)S(1)} copy-done((f32[1521,6]{0,1:T(8,128)S(1)}, f32[1521,6]{0,1:T(8,128)}, u32[]{:S(2)}) %copy-start.9) | copy-done | bytes 36528
  8.8 0.0 copy-start.1
  8.8 0.0 copy-start.5
  8.8 0.0 copy-start.6
  8.8 0.0 copy-start.7
  8.8 0.0 copy-start.8
  8.8 0.0 copy-start.10
  8.8 0.0 copy-start.11
  8.8 3.7 %shard_map.110.bias_ref = bf16[4,6,576,128]{3,2,1,0:T(8,128)(2,1)S(1)} custom-call(f32[6,1521]{1,0:T(8,128)S(1)} %bitcast.9), custom_call_target="tpu_custom_call" | custom-call | flops 4000000000 | bytes 4000000 | tf_op jit(solution)/shard_map/pallas_call | solution.py:104
  12.6 0.0 collective-permute-done.row_two_ref
  12.6 0.0 collective-permute-done.1.row_one_ref
  12.6 0.0 copy-done.1
  12.6 0.2 shard_map.112
  12.8 0.7 %collective-permute-start.2 = (bf16[720,128]{1,0:T(8,128)(2,1)S(1)}, bf16[720,128]{1,0:T(8,128)(2,1)S(1)}, u32[]{:S(2)}, u32[]{:S(2)}) collective-permute-start(bf16[720,128]{1,0:T(8,128)(2,1)S(1)} %get-tuple-element.27), channel_id=1, source_target_pairs={{1,2},{3,4},{5,6},{2,1},{4,3},{6,5},{9,10},{11,12},{13,14},{10,9},... | collective-permute-start | bytes 552968 | tf_op jit(solution)/shard_map/ppermute | solution.py:796
  13.5 2.9 %collective-permute-start.3 = (bf16[720,128]{1,0:T(8,128)(2,1)S(1)}, bf16[720,128]{1,0:T(8,128)(2,1)S(1)}, u32[]{:S(2)}, u32[]{:S(2)}) collective-permute-start(bf16[720,128]{1,0:T(8,128)(2,1)S(1)} %get-tuple-element.28), channel_id=1, source_target_pairs={{0,1},{2,3},{4,5},{6,7},{1,0},{3,2},{5,4},{7,6},{8,9},{10,11},{12,... | collective-permute-start | bytes 552968 | tf_op jit(solution)/shard_map/ppermute | solution.py:796
  16.4 0.0 copy-done.5
  16.4 0.0 copy-done.6
  16.4 0.0 copy-done.7
  16.4 0.0 copy-done.8
  16.4 0.0 copy-done.10
  16.4 0.0 copy-done.11
  16.4 5.3 %shard_map.111 = (f32[24,64,180]{2,1,0:T(8,128)S(1)}, bf16[180,384]{1,0:T(8,128)(2,1)S(1)}, bf16[384,180]{1,0:T(8,128)(2,1)S(1)}, bf16[192,180]{1,0:T(8,128)(2,1...) custom-call(bf16[16,64,180]{2,1,0:T(8,128)(2,1)S(1)} %copy-done.1, ...), custom_call_target="tpu_custom_call" | custom-call | flops 5000000000 | bytes 4000000 | tf_op jit(solution)/shard_map/pallas_call | solution.py:538
  21.8 0.0 collective-permute-done.2.col_two_ref
  21.8 0.0 collective-permute-done.3.col_one_ref
  21.8 7.0 %shard_map.113 = (bf16[368,128]{1,0:T(8,128)(2,1)S(1)}, bf16[368,128]{1,0:T(8,128)(2,1)S(1)}, f32[8,80,180]{2,1,0:T(8,128)S(1)}, f32[8,16,180]{2,1,0:T(8,128)S(1...) custom-call(bf16[16,64,180]{2,1,0:T(8,128)(2,1)S(1)} %copy-done.1, ...), custom_call_target="tpu_custom_call" | custom-call | flops 5000000000 | bytes 4000000 | tf_op jit(solution)/shard_map/pallas_call | solution.py:559
  28.8 0.8 %collective-permute-start.4 = (bf16[368,128]{1,0:T(8,128)(2,1)S(1)}, bf16[368,128]{1,0:T(8,128)(2,1)S(1)}, u32[]{:S(2)}, u32[]{:S(2)}) collective-permute-start(bf16[368,128]{1,0:T(8,128)(2,1)S(1)} %get-tuple-element.36), channel_id=1, source_target_pairs={{8,16},{16,8},{9,17},{17,9},{10,18},{18,10},{11,19},{19,11},{12,20... | collective-permute-start | bytes 282632 | tf_op jit(solution)/shard_map/ppermute | solution.py:796
  29.6 2.1 %collective-permute-start.5 = (bf16[368,128]{1,0:T(8,128)(2,1)S(1)}, bf16[368,128]{1,0:T(8,128)(2,1)S(1)}, u32[]{:S(2)}, u32[]{:S(2)}) collective-permute-start(bf16[368,128]{1,0:T(8,128)(2,1)S(1)} %get-tuple-element.37), channel_id=1, source_target_pairs={{0,8},{16,24},{8,0},{24,16},{1,9},{17,25},{9,1},{25,17},{2,10},{18... | collective-permute-start | bytes 282632 | tf_op jit(solution)/shard_map/ppermute | solution.py:796
  31.7 0.0 copy-start.2
  31.7 0.0 copy-start.3
  31.7 0.0 copy-start.4
  31.7 4.1 %shard_map.114.mid_ref = f32[8,64,180]{2,1,0:T(8,128)S(1)} custom-call(bf16[16,64,180]{2,1,0:T(8,128)(2,1)S(1)} %copy-done.1, f32[24,64,180]{2,1,0:T(8,128)S(1)} %get-tuple-element.26.nrm_ref, bf16[5,576,384]{2,1,0:T(8,128)(2,1)S(1)} %get-tuple-element.40.k_ref, bf16[5,192,576]{2,1,0:T(8,128)(2,1)S(1)} %get-tuple-element.41.v_ref, ...), custom_call_target="tpu_custom_call" | custom-call | flops 5000000000 | bytes 4000000 | tf_op jit(solution)/shard_map/pallas_call | solution.py:585
  35.8 0.0 collective-permute-done.4.back_two_ref
  35.9 0.0 collective-permute-done.5.back_one_ref
  35.9 0.0 copy-done.2
  35.9 0.0 copy-done.3
  35.9 0.0 copy-done.4
  35.9 6.5 %shard_map.115 = bf16[64,32,128]{2,1,0:T(8,128)(2,1)} custom-call(bf16[16,64,180]{2,1,0:T(8,128)(2,1)S(1)} %copy-done.1, bf16[4,64,180]{2,1,0:T(8,128)(2,1)S(1)} %collective-permute-done.row_two_ref, bf16[4,64,180]{2,1,0:T(8,128)(2,1)S(1)} %collective-permute-done.1.row_one_ref, f32[2,24,8,180]{3,2,1,0:T(8,128)S(1)} %get-tuple-element.35.strip_ref, ...), custom_call_target="tpu_custom_call" | custom-call | flops 8000000000 | bytes 4000000 | tf_op jit(solution)/shard_map/pallas_call | solution.py:769
Async XLA Ops:
  0.0 1.0 %copy-start = (bf16[16,64,180]{2,1,0:T(8,128)(2,1)S(1)}, bf16[16,64,180]{2,1,0:T(8,128)(2,1)}, u32[]{:S(2)}) copy-start(bf16[16,64,180]{2,1,0:T(8,128)(2,1)} %own_ref.11) | copy-start | bytes 1105924
  1.4 11.2 %collective-permute-start = (bf16[4,64,180]{2,1,0:T(8,128)(2,1)S(1)}, bf16[4,64,180]{2,1,0:T(8,128)(2,1)S(1)}, u32[]{:S(2)}, u32[]{:S(2)}) collective-permute-start(bf16[4,64,180]{2,1,0:T(8,128)(2,1)S(1)} %get-tuple-element.24), channel_id=1, source_target_pairs={{8,16},{16,8},{9,17},{17,9},{10,18},{18,10},{11,19},{19,11},{12,20... | collective-permute-start | bytes 276488 | tf_op jit(solution)/shard_map/ppermute | solution.py:796
  2.1 10.5 %collective-permute-start.1 = (bf16[4,64,180]{2,1,0:T(8,128)(2,1)S(1)}, bf16[4,64,180]{2,1,0:T(8,128)(2,1)S(1)}, u32[]{:S(2)}, u32[]{:S(2)}) collective-permute-start(bf16[4,64,180]{2,1,0:T(8,128)(2,1)S(1)} %get-tuple-element.25), channel_id=1, source_target_pairs={{0,8},{16,24},{8,0},{24,16},{1,9},{17,25},{9,1},{25,17},{2,10},{18... | collective-permute-start | bytes 276488 | tf_op jit(solution)/shard_map/ppermute | solution.py:796
  8.0 0.8 %copy-start.9 = (f32[1521,6]{0,1:T(8,128)S(1)}, f32[1521,6]{0,1:T(8,128)}, u32[]{:S(2)}) copy-start(f32[1521,6]{0,1:T(8,128)} %param.14) | copy-start | bytes 109516
  8.8 3.8 %copy-start.1 = (bf16[16,64,180]{2,1,0:T(8,128)(2,1)S(1)}, bf16[16,64,180]{2,1,0:T(8,128)(2,1)}, u32[]{:S(2)}) copy-start(bf16[16,64,180]{2,1,0:T(8,128)(2,1)} %own_ref.11) | copy-start | bytes 1105924
  8.8 7.7 %copy-start.5 = (bf16[180,540]{1,0:T(8,128)(2,1)S(1)}, bf16[180,540]{1,0:T(8,128)(2,1)}, u32[]{:S(2)}) copy-start(bf16[180,540]{1,0:T(8,128)(2,1)} %qkv_ref.1) | copy-start | bytes 583204
  8.8 7.7 %copy-start.6 = (bf16[180,360]{1,0:T(8,128)(2,1)S(1)}, bf16[180,360]{1,0:T(8,128)(2,1)}, u32[]{:S(2)}) copy-start(bf16[180,360]{1,0:T(8,128)(2,1)} %hidden_ref.5) | copy-start | bytes 388804
  8.8 7.7 %copy-start.7 = (bf16[360,180]{0,1:T(8,128)(2,1)S(1)}, bf16[360,180]{0,1:T(8,128)(2,1)}, u32[]{:S(2)}) copy-start(bf16[360,180]{0,1:T(8,128)(2,1)} %param.18) | copy-start | bytes 388804
  8.8 7.7 %copy-start.8 = (bf16[180,180]{1,0:T(8,128)(2,1)S(1)}, bf16[180,180]{1,0:T(8,128)(2,1)}, u32[]{:S(2)}) copy-start(bf16[180,180]{1,0:T(8,128)(2,1)} %proj_ref.1) | copy-start | bytes 194404
  8.8 7.6 %copy-start.10 = (f32[180]{0:T(256)S(1)}, f32[180]{0:T(256)}, u32[]{:S(2)}) copy-start(f32[180]{0:T(256)} %param.12) | copy-start | bytes 2164
  8.8 7.6 %copy-start.11 = (f32[180]{0:T(256)S(1)}, f32[180]{0:T(256)}, u32[]{:S(2)}) copy-start(f32[180]{0:T(256)} %param.16) | copy-start | bytes 2164
  12.8 9.0 %collective-permute-start.2 = (bf16[720,128]{1,0:T(8,128)(2,1)S(1)}, bf16[720,128]{1,0:T(8,128)(2,1)S(1)}, u32[]{:S(2)}, u32[]{:S(2)}) collective-permute-start(bf16[720,128]{1,0:T(8,128)(2,1)S(1)} %get-tuple-element.27), channel_id=1, source_target_pairs={{1,2},{3,4},{5,6},{2,1},{4,3},{6,5},{9,10},{11,12},{13,14},{10,9},... | collective-permute-start | bytes 552968 | tf_op jit(solution)/shard_map/ppermute | solution.py:796
  13.5 8.3 %collective-permute-start.3 = (bf16[720,128]{1,0:T(8,128)(2,1)S(1)}, bf16[720,128]{1,0:T(8,128)(2,1)S(1)}, u32[]{:S(2)}, u32[]{:S(2)}) collective-permute-start(bf16[720,128]{1,0:T(8,128)(2,1)S(1)} %get-tuple-element.28), channel_id=1, source_target_pairs={{0,1},{2,3},{4,5},{6,7},{1,0},{3,2},{5,4},{7,6},{8,9},{10,11},{12,... | collective-permute-start | bytes 552968 | tf_op jit(solution)/shard_map/ppermute | solution.py:796
  28.8 7.1 %collective-permute-start.4 = (bf16[368,128]{1,0:T(8,128)(2,1)S(1)}, bf16[368,128]{1,0:T(8,128)(2,1)S(1)}, u32[]{:S(2)}, u32[]{:S(2)}) collective-permute-start(bf16[368,128]{1,0:T(8,128)(2,1)S(1)} %get-tuple-element.36), channel_id=1, source_target_pairs={{8,16},{16,8},{9,17},{17,9},{10,18},{18,10},{11,19},{19,11},{12,20... | collective-permute-start | bytes 282632 | tf_op jit(solution)/shard_map/ppermute | solution.py:796
  29.6 6.2 %collective-permute-start.5 = (bf16[368,128]{1,0:T(8,128)(2,1)S(1)}, bf16[368,128]{1,0:T(8,128)(2,1)S(1)}, u32[]{:S(2)}, u32[]{:S(2)}) collective-permute-start(bf16[368,128]{1,0:T(8,128)(2,1)S(1)} %get-tuple-element.37), channel_id=1, source_target_pairs={{0,8},{16,24},{8,0},{24,16},{1,9},{17,25},{9,1},{25,17},{2,10},{18... | collective-permute-start | bytes 282632 | tf_op jit(solution)/shard_map/ppermute | solution.py:796
  31.7 4.1 %copy-start.2 = (bf16[3,3,180,180]{3,2,1,0:T(8,128)(2,1)S(1)}, bf16[3,3,180,180]{3,2,1,0:T(8,128)(2,1)}, u32[]{:S(2)}) copy-start(bf16[3,3,180,180]{3,2,1,0:T(8,128)(2,1)} %group_ref.1) | copy-start | bytes 1749604
  31.7 4.1 %copy-start.3 = (bf16[3,3,180,64]{2,3,1,0:T(8,128)(2,1)S(1)}, bf16[3,3,180,64]{2,3,1,0:T(8,128)(2,1)}, u32[]{:S(2)}) copy-start(bf16[3,3,180,64]{2,3,1,0:T(8,128)(2,1)} %param.20) | copy-start | bytes 622084
  31.7 4.2 %copy-start.4 = (bf16[3,3,64,256]{3,2,1,0:T(8,128)(2,1)S(1)}, bf16[3,3,64,256]{3,2,1,0:T(8,128)(2,1)}, u32[]{:S(2)}) copy-start(bf16[3,3,64,256]{3,2,1,0:T(8,128)(2,1)} %upsample_ref.1) | copy-start | bytes 884740

commit v5 on v3

--- a/solution.py
+++ b/solution.py
@@ -73,12 +73,18 @@
 
         lanes = lax.broadcasted_iota(jnp.int32, (KWIN, 128), 1)
         expand(WIN, 0)
-        for p in range(KWIN):
-            rows = slice(p * KWIN, (p + 1) * KWIN)
-            low = w_scr[:, (23 - p) * WIN : (23 - p) * WIN + 128]
-            high = w_scr[:, (31 - p) * WIN : (31 - p) * WIN + 128]
-            x_scr[0, rows] = jnp.where(lanes < 64, low, high)
-            x_scr[1, rows] = w_scr[:, (27 - p) * WIN : (27 - p) * WIN + 128]
+        whole = w_scr[...]
+        for phase in range(8):
+            turned = whole if phase == 0 else pltpu.roll(whole, 640 - WIN * phase, 1)
+            for p in range(KWIN):
+                rows = slice(p * KWIN, (p + 1) * KWIN)
+                if (23 - p) % 8 == phase:
+                    at = (23 - p) // 8 * 128
+                    low, high = turned[:, at : at + 128], turned[:, at + 128 : at + 256]
+                    x_scr[0, rows] = jnp.where(lanes < 64, low, high)
+                if (27 - p) % 8 == phase:
+                    at = (27 - p) // 8 * 128
+                    x_scr[1, rows] = turned[:, at : at + 128]
         out_ref[1, h] = x_scr[0].astype(BF16)
         out_ref[3, h] = x_scr[1].astype(BF16)
         for kind, first in ((0, WIN - STRIP), (2, 0)):
@@ -179,22 +185,22 @@
     def sum_values(g, t):
         o_scr[g, t] = dot(v_ref[lookup(g, windows), 2 * t * HP : 2 * (t + 1) * HP], p_scr[t])
 
-    top = None
-    for k0 in range(0, KEYS, step):
-        top = keep(0, 0, k0, top)
-    m_scr[...] = top
+    for t in range(2):
+        later = None
+        for k0 in range(0, KEYS, step):
+            later = keep(0, t, k0, later)
+        m_scr[t] = jnp.broadcast_to(jnp.max(later, axis=0, keepdims=True), later.shape) if t == 0 else later
     p_scr[pairs - 1] = jnp.zeros((KEYS, 256), BF16)
 
     def attend(g, carry):
         kind = lookup(g, kinds)
-        top = m_scr[...]
+        top, coming = m_scr[0, 0:1], m_scr[1]
         for t in range(pairs):
-            top = jnp.max(top, axis=0, keepdims=True)
             if t == 0:
                 sum_values(jnp.maximum(g - 1, 0), pairs - 1)
             else:
                 sum_values(g, t - 1)
-            following = g if t + 1 < pairs else jnp.minimum(g + 1, groups - 1)
+            following = g if t + 2 < pairs else jnp.minimum(g + 1, groups - 1)
             later = None
             for k0 in range(0, KEYS, step):
                 prob = jnp.exp2(s_scr[t, k0 : k0 + step] - top).astype(BF16)
@@ -203,9 +209,10 @@
                     p_scr[t, k0 : k0 + step, lanes] = (
                         prob[:, lanes] * bias_ref[kind, 2 * t + half, k0 : k0 + step]
                     )
-                later = keep(following, (t + 1) % pairs, k0, later)
-            top = later
-        m_scr[...] = top
+                later = keep(following, (t + 2) % pairs, k0, later)
+            top, coming = jnp.max(coming, axis=0, keepdims=True), later
+        m_scr[0] = jnp.broadcast_to(top, coming.shape)
+        m_scr[1] = coming
         return carry
 
     lax.fori_loop(0, groups, attend, 0)
@@ -230,9 +237,12 @@
     return first + dot_nt(inner, output_ref[...])
 
 
-def feed_groups(first, gain, hidden_ref, output_ref):
-    groups = range(first.shape[0] // 128)
-    return [feed_forward(first[128 * g : 128 * (g + 1)], gain, hidden_ref, output_ref) for g in groups]
+def feed_groups(first, gain, hidden_ref, output_ref, batch):
+    out = []
+    for start in range(0, first.shape[0], 128 * batch):
+        mixed = feed_forward(first[start : start + 128 * batch], gain, hidden_ref, output_ref)
+        out += [mixed[128 * g : 128 * (g + 1)] for g in range(batch)]
+    return out
 
 
 def project(keys, wk_ref, wqv_ref, k_ref, v_ref, index):
@@ -371,7 +381,7 @@
     first = jnp.concatenate(first, axis=0).astype(F32) + attention(
         kinds, windows, q_scr, k_ref, v_ref, bias_ref, wp_ref, s_scr, m_scr, p_scr, o_scr
     )
-    mixed = feed_groups(first, gain_two_ref[...], hidden_ref, output_ref)
+    mixed = feed_groups(first, gain_two_ref[...], hidden_ref, output_ref, len(kinds))
     for g in range(groups):
         one = mixed[g].reshape(8, WIN, chans)
         if g < inner:
@@ -456,7 +466,7 @@
     )
     image[0:4, STRIP + WIN : STRIP + cols - WIN] = inner_border_ref[0:4]
     image[12:16, STRIP + WIN : STRIP + cols - WIN] = inner_border_ref[4:8]
-    mixed = feed_groups(first, gain_two_ref[...], hidden_ref, output_ref)
+    mixed = feed_groups(first, gain_two_ref[...], hidden_ref, output_ref, 1)
     for g in range(4):
         if g in (0, 3):
             one = jnp.where(flags[g // 3], 0.0, mixed[g]).reshape(height, STRIP, chans)
@@ -508,7 +518,7 @@
     first = jnp.concatenate(first, axis=0).astype(F32) + attention(
         [3, 3, 3], [1, 2, 3], q_scr, k_ref, v_ref, bias_ref, wp_ref, s_scr, m_scr, p_scr, o_scr
     )
-    mixed = feed_groups(first, gain_two_ref[...], hidden_ref, output_ref)
+    mixed = feed_groups(first, gain_two_ref[...], hidden_ref, output_ref, 3)
     mid_ref[:, WIN : cols - 2 * WIN] = inner_mid_ref[...]
     for g in range(3):
         mid_ref[:, spots[g] : spots[g] + WIN] = mixed[g].reshape(8, WIN, chans)
@@ -518,7 +528,7 @@
     return [
         pltpu.VMEM((groups, HEADS // 2, 2 * HP, 256), BF16),
         pltpu.VMEM((HEADS // 2, KEYS, 256), F32),
-        pltpu.VMEM((8, 256), F32),
+        pltpu.VMEM((2, 8, 256), F32),
         pltpu.VMEM((HEADS // 2, KEYS, 256), BF16),
         pltpu.VMEM((groups, HEADS // 2, 2 * HP, 256), F32),
     ]
@@ -590,8 +600,8 @@
     row_one_ref,
     row_two_ref,
     strip_ref,
+    back_two_ref,
     back_one_ref,
-    back_two_ref,
     edge_ref,
     side_ref,
     mid_ref,
@@ -652,8 +662,9 @@
     image[7:15, STRIP : STRIP + cols] = mid_ref[...]
     image[7:15, STRIP + cols : span] = side_ref[:, STRIP : 2 * STRIP]
     image[15:19, 0:span] = edge_ref[4:8]
-    taps[...] = jnp.zeros(taps.shape, BF16)
-    grouped[...] = jnp.zeros(grouped.shape, BF16)
+    grouped[:, :, 128:256] = jnp.zeros((height + 4, span, 128), BF16)
+    for b in range(3):
+        taps[:, :, 256 * b + 128 : 256 * b + 256] = jnp.zeros((height + 6, span, 128), BF16)
     part = 4
     col = lax.broadcasted_iota(jnp.int32, (span, chans), 0) - 2
     keep_grouped = (col < cols + 2) & ((col >= 0) | jnp.logical_not(at_left))
@@ -847,8 +858,8 @@
         row_one,
         row_two,
         strips,
+        back_two,
         back_one,
-        back_two,
         edge,
         side,
         mid,

time: 40.6 us -> 40.2 us (level)
  the two profiles are of different devices: /device:TPU:12 before, /device:TPU:0 now
where the time goes in v5:
time: 40.2 us; the launch traced here: 40 us
  Pallas kernels  24.9 us (62%)
  starting transfers between devices  13.1 us (33%)
  other arithmetic  0.99 us (2%)
  local copies, waits for them, and re-layouts  0.84 us (2%)
    ppermute x6, starting transfers between devices, swapped(): out.append(lax.ppermute(payload, axis, pairs))  13.1 us
    pallas_call x1, Pallas kernels, convs(): call(conv_kernel, jax.ShapeDtypeStruct((feats, 2 * height, 2 * cols), BF1...  6.49 us
    pallas_call x1, Pallas kernels, outer_block(): call(outer_kernel, (jax.ShapeDtypeStruct((3 * span + 128, 128), BF16), ja...  6.28 us
    pallas_call x1, Pallas kernels, inner_block(): call(inner_kernel, (jax.ShapeDtypeStruct((height + 2 * RIM, cols, chans),...  4.61 us
    pallas_call x1, Pallas kernels, build_bias(): call(bias_kernel, jax.ShapeDtypeStruct((4, HEADS, KEYS, 128), BF16), [plt...  3.75 us
    pallas_call x1, Pallas kernels, middle_block(): call(middle_kernel, jax.ShapeDtypeStruct((8, cols, chans), F32), attentio...  3.51 us
    select_n x1, other arithmetic, on_device(): jnp.where(even_row, low, high)  0.99 us
    unnamed x22, local copies, waits for them, and re-layouts  0.84 us
  transfers between devices with their start and end apart: 6, of which 0 were waited for; matrix products, arithmetic and copies ran while one was open for 0% of the time, Pallas kernels for 30%

profile of v5, /device:TPU:0, one launch (start us, length us, event | category | flops | bytes accessed | tf_op | source)
XLA Modules:
  0.0 40.0 jit_solution(15907634142864734893)
XLA Ops:
  0.0 1.0 %broadcast_select_fusion = (bf16[4,64,180]{2,1,0:T(8,128)(2,1)S(1)}, bf16[4,64,180]{2,1,0:T(8,128)(2,1)S(1)}) fusion(pred[]{:T(512)S(6)} %eq.5, bf16[16,64,180]{2,1,0:T(8,128)(2,1)} %own_ref.9), kind=kLoop, calls=%fused_computation | loop fusion | flops 92160 | bytes 368641 | tf_op jit(solution)/shard_map/jit(_where)/select_n | solution.py:822
  1.0 0.7 %collective-permute-start.1 = (bf16[4,64,180]{2,1,0:T(8,128)(2,1)S(1)}, bf16[4,64,180]{2,1,0:T(8,128)(2,1)S(1)}, u32[]{:S(2)}, u32[]{:S(2)}) collective-permute-start(bf16[4,64,180]{2,1,0:T(8,128)(2,1)S(1)} %get-tuple-element.39), channel_id=1, source_target_pairs={{8,16},{16,8},{9,17},{17,9},{10,18},{18,10},{11,19},{19,11},{12,20... | collective-permute-start | bytes 276488 | tf_op jit(solution)/shard_map/ppermute | solution.py:801
  1.7 5.9 %collective-permute-start = (bf16[4,64,180]{2,1,0:T(8,128)(2,1)S(1)}, bf16[4,64,180]{2,1,0:T(8,128)(2,1)S(1)}, u32[]{:S(2)}, u32[]{:S(2)}) collective-permute-start(bf16[4,64,180]{2,1,0:T(8,128)(2,1)S(1)} %get-tuple-element.40), channel_id=1, source_target_pairs={{0,8},{16,24},{8,0},{24,16},{1,9},{17,25},{9,1},{25,17},{2,10},{18... | collective-permute-start | bytes 276488 | tf_op jit(solution)/shard_map/ppermute | solution.py:801
  7.6 0.0 copy-start.8
  7.6 0.8 %copy-done.8 = f32[1521,6]{0,1:T(8,128)S(1)} copy-done((f32[1521,6]{0,1:T(8,128)S(1)}, f32[1521,6]{0,1:T(8,128)}, u32[]{:S(2)}) %copy-start.8) | copy-done | bytes 36528
  8.4 0.0 copy-start
  8.4 0.0 copy-start.4
  8.4 0.0 copy-start.5
  8.4 0.0 copy-start.6
  8.4 0.0 copy-start.7
  8.4 0.0 copy-start.9
  8.4 0.0 copy-start.10
  8.4 3.7 %shard_map.109.bias_ref = bf16[4,6,576,128]{3,2,1,0:T(8,128)(2,1)S(1)} custom-call(f32[6,1521]{1,0:T(8,128)S(1)} %bitcast.9), custom_call_target="tpu_custom_call" | custom-call | flops 4000000000 | bytes 4000000 | tf_op jit(solution)/shard_map/pallas_call | solution.py:102
  12.2 0.0 collective-permute-done.1.row_two_ref
  12.2 0.0 collective-permute-done.row_one_ref
  12.2 0.0 copy-done
  12.2 0.2 shard_map.111
  12.4 0.7 %collective-permute-start.2 = (bf16[720,128]{1,0:T(8,128)(2,1)S(1)}, bf16[720,128]{1,0:T(8,128)(2,1)S(1)}, u32[]{:S(2)}, u32[]{:S(2)}) collective-permute-start(bf16[720,128]{1,0:T(8,128)(2,1)S(1)} %get-tuple-element.23), channel_id=1, source_target_pairs={{1,2},{3,4},{5,6},{2,1},{4,3},{6,5},{9,10},{11,12},{13,14},{10,9},... | collective-permute-start | bytes 552968 | tf_op jit(solution)/shard_map/ppermute | solution.py:801
  13.1 2.9 %collective-permute-start.3 = (bf16[720,128]{1,0:T(8,128)(2,1)S(1)}, bf16[720,128]{1,0:T(8,128)(2,1)S(1)}, u32[]{:S(2)}, u32[]{:S(2)}) collective-permute-start(bf16[720,128]{1,0:T(8,128)(2,1)S(1)} %get-tuple-element.24), channel_id=1, source_target_pairs={{0,1},{2,3},{4,5},{6,7},{1,0},{3,2},{5,4},{7,6},{8,9},{10,11},{12,... | collective-permute-start | bytes 552968 | tf_op jit(solution)/shard_map/ppermute | solution.py:801
  16.0 0.0 copy-done.4
  16.0 0.0 copy-done.5
  16.0 0.0 copy-done.6
  16.0 0.0 copy-done.7
  16.0 0.0 copy-done.9
  16.1 0.0 copy-done.10
  16.1 4.6 %shard_map.110 = (f32[24,64,180]{2,1,0:T(8,128)S(1)}, bf16[180,384]{1,0:T(8,128)(2,1)S(1)}, bf16[384,180]{1,0:T(8,128)(2,1)S(1)}, bf16[192,180]{1,0:T(8,128)(2,1...) custom-call(bf16[16,64,180]{2,1,0:T(8,128)(2,1)S(1)} %copy-done, ...), custom_call_target="tpu_custom_call" | custom-call | flops 5000000000 | bytes 4000000 | tf_op jit(solution)/shard_map/pallas_call | solution.py:542
  20.7 0.0 collective-permute-done.2.col_two_ref
  20.7 0.0 collective-permute-done.3.col_one_ref
  20.7 6.3 %shard_map.112 = (bf16[368,128]{1,0:T(8,128)(2,1)S(1)}, bf16[368,128]{1,0:T(8,128)(2,1)S(1)}, f32[8,80,180]{2,1,0:T(8,128)S(1)}, f32[8,16,180]{2,1,0:T(8,128)S(1...) custom-call(bf16[16,64,180]{2,1,0:T(8,128)(2,1)S(1)} %copy-done, ...), custom_call_target="tpu_custom_call" | custom-call | flops 5000000000 | bytes 4000000 | tf_op jit(solution)/shard_map/pallas_call | solution.py:563
  27.0 0.8 %collective-permute-start.4 = (bf16[368,128]{1,0:T(8,128)(2,1)S(1)}, bf16[368,128]{1,0:T(8,128)(2,1)S(1)}, u32[]{:S(2)}, u32[]{:S(2)}) collective-permute-start(bf16[368,128]{1,0:T(8,128)(2,1)S(1)} %get-tuple-element.32), channel_id=1, source_target_pairs={{8,16},{16,8},{9,17},{17,9},{10,18},{18,10},{11,19},{19,11},{12,20... | collective-permute-start | bytes 282632 | tf_op jit(solution)/shard_map/ppermute | solution.py:801
  27.8 2.1 %collective-permute-start.5 = (bf16[368,128]{1,0:T(8,128)(2,1)S(1)}, bf16[368,128]{1,0:T(8,128)(2,1)S(1)}, u32[]{:S(2)}, u32[]{:S(2)}) collective-permute-start(bf16[368,128]{1,0:T(8,128)(2,1)S(1)} %get-tuple-element.33), channel_id=1, source_target_pairs={{0,8},{16,24},{8,0},{24,16},{1,9},{17,25},{9,1},{25,17},{2,10},{18... | collective-permute-start | bytes 282632 | tf_op jit(solution)/shard_map/ppermute | solution.py:801
  29.9 0.0 copy-start.1
  29.9 0.0 copy-start.2
  29.9 0.0 copy-start.3
  29.9 3.5 %shard_map.113.mid_ref = f32[8,64,180]{2,1,0:T(8,128)S(1)} custom-call(bf16[16,64,180]{2,1,0:T(8,128)(2,1)S(1)} %copy-done, f32[24,64,180]{2,1,0:T(8,128)S(1)} %get-tuple-element.22.nrm_ref, bf16[5,576,384]{2,1,0:T(8,128)(2,1)S(1)} %get-tuple-element.36.k_ref, bf16[5,192,576]{2,1,0:T(8,128)(2,1)S(1)} %get-tuple-element.37.v_ref, ...), custom_call_target="tpu_custom_call" | custom-call | flops 5000000000 | bytes 4000000 | tf_op jit(solution)/shard_map/pallas_call | solution.py:589
  33.4 0.0 collective-permute-done.4.back_two_ref
  33.5 0.0 collective-permute-done.5.back_one_ref
  33.5 0.0 copy-done.1
  33.5 0.0 copy-done.2
  33.5 0.0 copy-done.3
  33.5 6.5 %shard_map.114 = bf16[64,32,128]{2,1,0:T(8,128)(2,1)} custom-call(bf16[16,64,180]{2,1,0:T(8,128)(2,1)S(1)} %copy-done, bf16[4,64,180]{2,1,0:T(8,128)(2,1)S(1)} %collective-permute-done.row_one_ref, bf16[4,64,180]{2,1,0:T(8,128)(2,1)S(1)} %collective-permute-done.1.row_two_ref, f32[2,24,8,180]{3,2,1,0:T(8,128)S(1)} %get-tuple-element.31.strip_ref, ...), custom_call_target="tpu_custom_call" | custom-call | flops 8000000000 | bytes 4000000 | tf_op jit(solution)/shard_map/pallas_call | solution.py:774
Async XLA Ops:
  1.0 11.2 %collective-permute-start.1 = (bf16[4,64,180]{2,1,0:T(8,128)(2,1)S(1)}, bf16[4,64,180]{2,1,0:T(8,128)(2,1)S(1)}, u32[]{:S(2)}, u32[]{:S(2)}) collective-permute-start(bf16[4,64,180]{2,1,0:T(8,128)(2,1)S(1)} %get-tuple-element.39), channel_id=1, source_target_pairs={{8,16},{16,8},{9,17},{17,9},{10,18},{18,10},{11,19},{19,11},{12,20... | collective-permute-start | bytes 276488 | tf_op jit(solution)/shard_map/ppermute | solution.py:801
  1.7 10.5 %collective-permute-start = (bf16[4,64,180]{2,1,0:T(8,128)(2,1)S(1)}, bf16[4,64,180]{2,1,0:T(8,128)(2,1)S(1)}, u32[]{:S(2)}, u32[]{:S(2)}) collective-permute-start(bf16[4,64,180]{2,1,0:T(8,128)(2,1)S(1)} %get-tuple-element.40), channel_id=1, source_target_pairs={{0,8},{16,24},{8,0},{24,16},{1,9},{17,25},{9,1},{25,17},{2,10},{18... | collective-permute-start | bytes 276488 | tf_op jit(solution)/shard_map/ppermute | solution.py:801
  7.6 0.8 %copy-start.8 = (f32[1521,6]{0,1:T(8,128)S(1)}, f32[1521,6]{0,1:T(8,128)}, u32[]{:S(2)}) copy-start(f32[1521,6]{0,1:T(8,128)} %param.14) | copy-start | bytes 109516
  8.4 3.8 %copy-start = (bf16[16,64,180]{2,1,0:T(8,128)(2,1)S(1)}, bf16[16,64,180]{2,1,0:T(8,128)(2,1)}, u32[]{:S(2)}) copy-start(bf16[16,64,180]{2,1,0:T(8,128)(2,1)} %own_ref.9) | copy-start | bytes 1105924
  8.4 7.7 %copy-start.4 = (bf16[180,540]{1,0:T(8,128)(2,1)S(1)}, bf16[180,540]{1,0:T(8,128)(2,1)}, u32[]{:S(2)}) copy-start(bf16[180,540]{1,0:T(8,128)(2,1)} %qkv_ref.1) | copy-start | bytes 583204
  8.4 7.7 %copy-start.5 = (bf16[180,360]{1,0:T(8,128)(2,1)S(1)}, bf16[180,360]{1,0:T(8,128)(2,1)}, u32[]{:S(2)}) copy-start(bf16[180,360]{1,0:T(8,128)(2,1)} %hidden_ref.5) | copy-start | bytes 388804
  8.4 7.7 %copy-start.6 = (bf16[360,180]{0,1:T(8,128)(2,1)S(1)}, bf16[360,180]{0,1:T(8,128)(2,1)}, u32[]{:S(2)}) copy-start(bf16[360,180]{0,1:T(8,128)(2,1)} %param.18) | copy-start | bytes 388804
  8.4 7.7 %copy-start.7 = (bf16[180,180]{1,0:T(8,128)(2,1)S(1)}, bf16[180,180]{1,0:T(8,128)(2,1)}, u32[]{:S(2)}) copy-start(bf16[180,180]{1,0:T(8,128)(2,1)} %proj_ref.1) | copy-start | bytes 194404
  8.4 7.6 %copy-start.9 = (f32[180]{0:T(256)S(1)}, f32[180]{0:T(256)}, u32[]{:S(2)}) copy-start(f32[180]{0:T(256)} %param.12) | copy-start | bytes 2164
  8.4 7.6 %copy-start.10 = (f32[180]{0:T(256)S(1)}, f32[180]{0:T(256)}, u32[]{:S(2)}) copy-start(f32[180]{0:T(256)} %param.16) | copy-start | bytes 2164
  12.4 8.2 %collective-permute-start.2 = (bf16[720,128]{1,0:T(8,128)(2,1)S(1)}, bf16[720,128]{1,0:T(8,128)(2,1)S(1)}, u32[]{:S(2)}, u32[]{:S(2)}) collective-permute-start(bf16[720,128]{1,0:T(8,128)(2,1)S(1)} %get-tuple-element.23), channel_id=1, source_target_pairs={{1,2},{3,4},{5,6},{2,1},{4,3},{6,5},{9,10},{11,12},{13,14},{10,9},... | collective-permute-start | bytes 552968 | tf_op jit(solution)/shard_map/ppermute | solution.py:801
  13.1 7.6 %collective-permute-start.3 = (bf16[720,128]{1,0:T(8,128)(2,1)S(1)}, bf16[720,128]{1,0:T(8,128)(2,1)S(1)}, u32[]{:S(2)}, u32[]{:S(2)}) collective-permute-start(bf16[720,128]{1,0:T(8,128)(2,1)S(1)} %get-tuple-element.24), channel_id=1, source_target_pairs={{0,1},{2,3},{4,5},{6,7},{1,0},{3,2},{5,4},{7,6},{8,9},{10,11},{12,... | collective-permute-start | bytes 552968 | tf_op jit(solution)/shard_map/ppermute | solution.py:801
  27.0 6.5 %collective-permute-start.4 = (bf16[368,128]{1,0:T(8,128)(2,1)S(1)}, bf16[368,128]{1,0:T(8,128)(2,1)S(1)}, u32[]{:S(2)}, u32[]{:S(2)}) collective-permute-start(bf16[368,128]{1,0:T(8,128)(2,1)S(1)} %get-tuple-element.32), channel_id=1, source_target_pairs={{8,16},{16,8},{9,17},{17,9},{10,18},{18,10},{11,19},{19,11},{12,20... | collective-permute-start | bytes 282632 | tf_op jit(solution)/shard_map/ppermute | solution.py:801
  27.8 5.6 %collective-permute-start.5 = (bf16[368,128]{1,0:T(8,128)(2,1)S(1)}, bf16[368,128]{1,0:T(8,128)(2,1)S(1)}, u32[]{:S(2)}, u32[]{:S(2)}) collective-permute-start(bf16[368,128]{1,0:T(8,128)(2,1)S(1)} %get-tuple-element.33), channel_id=1, source_target_pairs={{0,8},{16,24},{8,0},{24,16},{1,9},{17,25},{9,1},{25,17},{2,10},{18... | collective-permute-start | bytes 282632 | tf_op jit(solution)/shard_map/ppermute | solution.py:801
  29.9 3.5 %copy-start.1 = (bf16[3,3,180,180]{3,2,1,0:T(8,128)(2,1)S(1)}, bf16[3,3,180,180]{3,2,1,0:T(8,128)(2,1)}, u32[]{:S(2)}) copy-start(bf16[3,3,180,180]{3,2,1,0:T(8,128)(2,1)} %group_ref.1) | copy-start | bytes 1749604
  29.9 3.5 %copy-start.2 = (bf16[3,3,180,64]{2,3,1,0:T(8,128)(2,1)S(1)}, bf16[3,3,180,64]{2,3,1,0:T(8,128)(2,1)}, u32[]{:S(2)}) copy-start(bf16[3,3,180,64]{2,3,1,0:T(8,128)(2,1)} %param.20) | copy-start | bytes 622084
  29.9 3.6 %copy-start.3 = (bf16[3,3,64,256]{3,2,1,0:T(8,128)(2,1)S(1)}, bf16[3,3,64,256]{3,2,1,0:T(8,128)(2,1)}, u32[]{:S(2)}) copy-start(bf16[3,3,64,256]{3,2,1,0:T(8,128)(2,1)} %upsample_ref.1) | copy-start | bytes 884740

commit v6 on v5

--- a/solution.py
+++ b/solution.py
@@ -173,7 +173,7 @@
 def attention(kinds, windows, q_scr, k_ref, v_ref, bias_ref, wp_ref, s_scr, m_scr, p_scr, o_scr):
     groups = len(kinds)
     pairs = HEADS // 2
-    step = 192
+    step = 144
 
     def keep(g, t, k0, top):
         keys = k_ref[lookup(g, windows), k0 : k0 + step, 128 * t : 128 * t + 2 * HP]
@@ -183,24 +183,27 @@
         return part if top is None else jnp.maximum(top, part)
 
     def sum_values(g, t):
-        o_scr[g, t] = dot(v_ref[lookup(g, windows), 2 * t * HP : 2 * (t + 1) * HP], p_scr[t])
-
-    for t in range(2):
-        later = None
-        for k0 in range(0, KEYS, step):
-            later = keep(0, t, k0, later)
-        m_scr[t] = jnp.broadcast_to(jnp.max(later, axis=0, keepdims=True), later.shape) if t == 0 else later
+        for half in range(2):
+            head = 2 * t + half
+            lanes = slice(128 * half, 128 * half + 128)
+            o_scr[g, head] = dot(v_ref[lookup(g, windows), head * HP : (head + 1) * HP], p_scr[t, :, lanes])
+
+    top = None
+    for k0 in range(0, KEYS, step):
+        top = keep(0, 0, k0, top)
+    m_scr[...] = top
     p_scr[pairs - 1] = jnp.zeros((KEYS, 256), BF16)
 
     def attend(g, carry):
         kind = lookup(g, kinds)
-        top, coming = m_scr[0, 0:1], m_scr[1]
+        top = m_scr[...]
         for t in range(pairs):
+            top = jnp.max(top, axis=0, keepdims=True)
             if t == 0:
                 sum_values(jnp.maximum(g - 1, 0), pairs - 1)
             else:
                 sum_values(g, t - 1)
-            following = g if t + 2 < pairs else jnp.minimum(g + 1, groups - 1)
+            following = g if t + 1 < pairs else jnp.minimum(g + 1, groups - 1)
             later = None
             for k0 in range(0, KEYS, step):
                 prob = jnp.exp2(s_scr[t, k0 : k0 + step] - top).astype(BF16)
@@ -209,10 +212,9 @@
                     p_scr[t, k0 : k0 + step, lanes] = (
                         prob[:, lanes] * bias_ref[kind, 2 * t + half, k0 : k0 + step]
                     )
-                later = keep(following, (t + 2) % pairs, k0, later)
-            top, coming = jnp.max(coming, axis=0, keepdims=True), later
-        m_scr[0] = jnp.broadcast_to(top, coming.shape)
-        m_scr[1] = coming
+                later = keep(following, (t + 1) % pairs, k0, later)
+            top = later
+        m_scr[...] = top
         return carry
 
     lax.fori_loop(0, groups, attend, 0)
@@ -220,11 +222,9 @@
     attended = []
     for g in range(groups):
         parts = []
-        for t in range(pairs):
-            for half in range(2):
-                lanes = slice(128 * half, 128 * half + 128)
-                one = o_scr[g, t, half * HP : (half + 1) * HP, lanes]
-                parts.append((one * (1.0 / one[HD : HD + 1])).astype(BF16))
+        for head in range(HEADS):
+            one = o_scr[g, head]
+            parts.append((one * (1.0 / one[HD : HD + 1])).astype(BF16))
         attended.append(jnp.concatenate(parts, axis=0))
     attended = jnp.concatenate(attended, axis=1)
     return lax.dot_general(attended, wp_ref[...], TN, preferred_element_type=F32)
@@ -466,7 +466,7 @@
     )
     image[0:4, STRIP + WIN : STRIP + cols - WIN] = inner_border_ref[0:4]
     image[12:16, STRIP + WIN : STRIP + cols - WIN] = inner_border_ref[4:8]
-    mixed = feed_groups(first, gain_two_ref[...], hidden_ref, output_ref, 1)
+    mixed = feed_groups(first, gain_two_ref[...], hidden_ref, output_ref, 2)
     for g in range(4):
         if g in (0, 3):
             one = jnp.where(flags[g // 3], 0.0, mixed[g]).reshape(height, STRIP, chans)
@@ -528,9 +528,9 @@
     return [
         pltpu.VMEM((groups, HEADS // 2, 2 * HP, 256), BF16),
         pltpu.VMEM((HEADS // 2, KEYS, 256), F32),
-        pltpu.VMEM((2, 8, 256), F32),
+        pltpu.VMEM((8, 256), F32),
         pltpu.VMEM((HEADS // 2, KEYS, 256), BF16),
-        pltpu.VMEM((groups, HEADS // 2, 2 * HP, 256), F32),
+        pltpu.VMEM((groups, HEADS, HP, 128), F32),
     ]
 
 
@@ -689,10 +689,13 @@
             ].astype(BF16)
 
     def group(h):
-        lhs = jnp.concatenate(
-            [taps[h + a : h + a + part].reshape(part * span, 768) for a in range(3)], axis=1
-        )
-        total = dot(lhs, wg_scr[...]).reshape(part, span, chans)
+        totals = []
+        for h2 in range(h, h + part, 2):
+            lhs = jnp.concatenate(
+                [taps[h2 + a : h2 + a + 2].reshape(2 * span, 768) for a in range(3)], axis=1
+            )
+            totals.append(dot(lhs, wg_scr[...]).reshape(2, span, chans))
+        total = jnp.concatenate(totals, axis=0)
         total = total + base[h : h + part, STRIP - 2 : STRIP - 2 + span, :]
         for r in range(part):
             mask = keep_grouped

time: 40.2 us -> 39.8 us (0.990)
  no operation moved by 1% of the time
where the time goes in v6:
time: 39.8 us; the launch traced here: 39.6 us
  Pallas kernels  24.5 us (62%)
  starting transfers between devices  13.1 us (33%)
  other arithmetic  0.99 us (2%)
  local copies, waits for them, and re-layouts  0.84 us (2%)
    ppermute x6, starting transfers between devices, swapped(): out.append(lax.ppermute(payload, axis, pairs))  13.1 us
    pallas_call x1, Pallas kernels, convs(): call(conv_kernel, jax.ShapeDtypeStruct((feats, 2 * height, 2 * cols), BF1...  6.32 us
    pallas_call x1, Pallas kernels, outer_block(): call(outer_kernel, (jax.ShapeDtypeStruct((3 * span + 128, 128), BF16), ja...  6.08 us
    pallas_call x1, Pallas kernels, inner_block(): call(inner_kernel, (jax.ShapeDtypeStruct((height + 2 * RIM, cols, chans),...  4.62 us
    pallas_call x1, Pallas kernels, build_bias(): call(bias_kernel, jax.ShapeDtypeStruct((4, HEADS, KEYS, 128), BF16), [plt...  3.75 us
    pallas_call x1, Pallas kernels, middle_block(): call(middle_kernel, jax.ShapeDtypeStruct((8, cols, chans), F32), attentio...  3.49 us
    select_n x1, other arithmetic, on_device(): jnp.where(even_row, low, high)  0.99 us
    unnamed x22, local copies, waits for them, and re-layouts  0.84 us
  transfers between devices with their start and end apart: 6, of which 0 were waited for; matrix products, arithmetic and copies ran while one was open for 0% of the time, Pallas kernels for 30%

profile of v6, /device:TPU:0, one launch (start us, length us, event | category | flops | bytes accessed | tf_op | source)
XLA Modules:
  0.0 39.6 jit_solution(2253154943401043168)
XLA Ops:
  0.0 1.0 %broadcast_select_fusion = (bf16[4,64,180]{2,1,0:T(8,128)(2,1)S(1)}, bf16[4,64,180]{2,1,0:T(8,128)(2,1)S(1)}) fusion(pred[]{:T(512)S(6)} %eq.5, bf16[16,64,180]{2,1,0:T(8,128)(2,1)} %own_ref.9), kind=kLoop, calls=%fused_computation | loop fusion | flops 92160 | bytes 368641 | tf_op jit(solution)/shard_map/jit(_where)/select_n | solution.py:825
  1.0 0.7 %collective-permute-start.1 = (bf16[4,64,180]{2,1,0:T(8,128)(2,1)S(1)}, bf16[4,64,180]{2,1,0:T(8,128)(2,1)S(1)}, u32[]{:S(2)}, u32[]{:S(2)}) collective-permute-start(bf16[4,64,180]{2,1,0:T(8,128)(2,1)S(1)} %get-tuple-element.39), channel_id=1, source_target_pairs={{8,16},{16,8},{9,17},{17,9},{10,18},{18,10},{11,19},{19,11},{12,20... | collective-permute-start | bytes 276488 | tf_op jit(solution)/shard_map/ppermute | solution.py:804
  1.7 5.9 %collective-permute-start = (bf16[4,64,180]{2,1,0:T(8,128)(2,1)S(1)}, bf16[4,64,180]{2,1,0:T(8,128)(2,1)S(1)}, u32[]{:S(2)}, u32[]{:S(2)}) collective-permute-start(bf16[4,64,180]{2,1,0:T(8,128)(2,1)S(1)} %get-tuple-element.40), channel_id=1, source_target_pairs={{0,8},{16,24},{8,0},{24,16},{1,9},{17,25},{9,1},{25,17},{2,10},{18... | collective-permute-start | bytes 276488 | tf_op jit(solution)/shard_map/ppermute | solution.py:804
  7.6 0.0 copy-start.8
  7.6 0.8 %copy-done.8 = f32[1521,6]{0,1:T(8,128)S(1)} copy-done((f32[1521,6]{0,1:T(8,128)S(1)}, f32[1521,6]{0,1:T(8,128)}, u32[]{:S(2)}) %copy-start.8) | copy-done | bytes 36528
  8.4 0.0 copy-start
  8.4 0.0 copy-start.4
  8.4 0.0 copy-start.5
  8.4 0.0 copy-start.6
  8.4 0.0 copy-start.7
  8.4 0.0 copy-start.9
  8.4 0.0 copy-start.10
  8.4 3.7 %shard_map.109.bias_ref = bf16[4,6,576,128]{3,2,1,0:T(8,128)(2,1)S(1)} custom-call(f32[6,1521]{1,0:T(8,128)S(1)} %bitcast.9), custom_call_target="tpu_custom_call" | custom-call | flops 4000000000 | bytes 4000000 | tf_op jit(solution)/shard_map/pallas_call | solution.py:102
  12.2 0.0 collective-permute-done.1.row_two_ref
  12.2 0.0 collective-permute-done.row_one_ref
  12.2 0.0 copy-done
  12.2 0.2 shard_map.111
  12.4 0.7 %collective-permute-start.2 = (bf16[720,128]{1,0:T(8,128)(2,1)S(1)}, bf16[720,128]{1,0:T(8,128)(2,1)S(1)}, u32[]{:S(2)}, u32[]{:S(2)}) collective-permute-start(bf16[720,128]{1,0:T(8,128)(2,1)S(1)} %get-tuple-element.23), channel_id=1, source_target_pairs={{1,2},{3,4},{5,6},{2,1},{4,3},{6,5},{9,10},{11,12},{13,14},{10,9},... | collective-permute-start | bytes 552968 | tf_op jit(solution)/shard_map/ppermute | solution.py:804
  13.1 2.9 %collective-permute-start.3 = (bf16[720,128]{1,0:T(8,128)(2,1)S(1)}, bf16[720,128]{1,0:T(8,128)(2,1)S(1)}, u32[]{:S(2)}, u32[]{:S(2)}) collective-permute-start(bf16[720,128]{1,0:T(8,128)(2,1)S(1)} %get-tuple-element.24), channel_id=1, source_target_pairs={{0,1},{2,3},{4,5},{6,7},{1,0},{3,2},{5,4},{7,6},{8,9},{10,11},{12,... | collective-permute-start | bytes 552968 | tf_op jit(solution)/shard_map/ppermute | solution.py:804
  16.0 0.0 copy-done.4
  16.0 0.0 copy-done.5
  16.0 0.0 copy-done.6
  16.0 0.0 copy-done.7
  16.0 0.0 copy-done.9
  16.1 0.0 copy-done.10
  16.1 4.6 %shard_map.110 = (f32[24,64,180]{2,1,0:T(8,128)S(1)}, bf16[180,384]{1,0:T(8,128)(2,1)S(1)}, bf16[384,180]{1,0:T(8,128)(2,1)S(1)}, bf16[192,180]{1,0:T(8,128)(2,1...) custom-call(bf16[16,64,180]{2,1,0:T(8,128)(2,1)S(1)} %copy-done, ...), custom_call_target="tpu_custom_call" | custom-call | flops 5000000000 | bytes 4000000 | tf_op jit(solution)/shard_map/pallas_call | solution.py:542
  20.7 0.0 collective-permute-done.2.col_two_ref
  20.7 0.0 collective-permute-done.3.col_one_ref
  20.7 6.1 %shard_map.112 = (bf16[368,128]{1,0:T(8,128)(2,1)S(1)}, bf16[368,128]{1,0:T(8,128)(2,1)S(1)}, f32[8,80,180]{2,1,0:T(8,128)S(1)}, f32[8,16,180]{2,1,0:T(8,128)S(1...) custom-call(bf16[16,64,180]{2,1,0:T(8,128)(2,1)S(1)} %copy-done, ...), custom_call_target="tpu_custom_call" | custom-call | flops 5000000000 | bytes 4000000 | tf_op jit(solution)/shard_map/pallas_call | solution.py:563
  26.8 0.8 %collective-permute-start.4 = (bf16[368,128]{1,0:T(8,128)(2,1)S(1)}, bf16[368,128]{1,0:T(8,128)(2,1)S(1)}, u32[]{:S(2)}, u32[]{:S(2)}) collective-permute-start(bf16[368,128]{1,0:T(8,128)(2,1)S(1)} %get-tuple-element.32), channel_id=1, source_target_pairs={{8,16},{16,8},{9,17},{17,9},{10,18},{18,10},{11,19},{19,11},{12,20... | collective-permute-start | bytes 282632 | tf_op jit(solution)/shard_map/ppermute | solution.py:804
  27.6 2.1 %collective-permute-start.5 = (bf16[368,128]{1,0:T(8,128)(2,1)S(1)}, bf16[368,128]{1,0:T(8,128)(2,1)S(1)}, u32[]{:S(2)}, u32[]{:S(2)}) collective-permute-start(bf16[368,128]{1,0:T(8,128)(2,1)S(1)} %get-tuple-element.33), channel_id=1, source_target_pairs={{0,8},{16,24},{8,0},{24,16},{1,9},{17,25},{9,1},{25,17},{2,10},{18... | collective-permute-start | bytes 282632 | tf_op jit(solution)/shard_map/ppermute | solution.py:804
  29.7 0.0 copy-start.1
  29.7 0.0 copy-start.2
  29.7 0.0 copy-start.3
  29.7 3.5 %shard_map.113.mid_ref = f32[8,64,180]{2,1,0:T(8,128)S(1)} custom-call(bf16[16,64,180]{2,1,0:T(8,128)(2,1)S(1)} %copy-done, f32[24,64,180]{2,1,0:T(8,128)S(1)} %get-tuple-element.22.nrm_ref, bf16[5,576,384]{2,1,0:T(8,128)(2,1)S(1)} %get-tuple-element.36.k_ref, bf16[5,192,576]{2,1,0:T(8,128)(2,1)S(1)} %get-tuple-element.37.v_ref, ...), custom_call_target="tpu_custom_call" | custom-call | flops 5000000000 | bytes 4000000 | tf_op jit(solution)/shard_map/pallas_call | solution.py:589
  33.2 0.0 collective-permute-done.4.back_two_ref
  33.2 0.0 collective-permute-done.5.back_one_ref
  33.3 0.0 copy-done.1
  33.3 0.0 copy-done.2
  33.3 0.0 copy-done.3
  33.3 6.3 %shard_map.114 = bf16[64,32,128]{2,1,0:T(8,128)(2,1)} custom-call(bf16[16,64,180]{2,1,0:T(8,128)(2,1)S(1)} %copy-done, bf16[4,64,180]{2,1,0:T(8,128)(2,1)S(1)} %collective-permute-done.row_one_ref, bf16[4,64,180]{2,1,0:T(8,128)(2,1)S(1)} %collective-permute-done.1.row_two_ref, f32[2,24,8,180]{3,2,1,0:T(8,128)S(1)} %get-tuple-element.31.strip_ref, ...), custom_call_target="tpu_custom_call" | custom-call | flops 8000000000 | bytes 4000000 | tf_op jit(solution)/shard_map/pallas_call | solution.py:777
Async XLA Ops:
  1.0 11.2 %collective-permute-start.1 = (bf16[4,64,180]{2,1,0:T(8,128)(2,1)S(1)}, bf16[4,64,180]{2,1,0:T(8,128)(2,1)S(1)}, u32[]{:S(2)}, u32[]{:S(2)}) collective-permute-start(bf16[4,64,180]{2,1,0:T(8,128)(2,1)S(1)} %get-tuple-element.39), channel_id=1, source_target_pairs={{8,16},{16,8},{9,17},{17,9},{10,18},{18,10},{11,19},{19,11},{12,20... | collective-permute-start | bytes 276488 | tf_op jit(solution)/shard_map/ppermute | solution.py:804
  1.7 10.5 %collective-permute-start = (bf16[4,64,180]{2,1,0:T(8,128)(2,1)S(1)}, bf16[4,64,180]{2,1,0:T(8,128)(2,1)S(1)}, u32[]{:S(2)}, u32[]{:S(2)}) collective-permute-start(bf16[4,64,180]{2,1,0:T(8,128)(2,1)S(1)} %get-tuple-element.40), channel_id=1, source_target_pairs={{0,8},{16,24},{8,0},{24,16},{1,9},{17,25},{9,1},{25,17},{2,10},{18... | collective-permute-start | bytes 276488 | tf_op jit(solution)/shard_map/ppermute | solution.py:804
  7.6 0.8 %copy-start.8 = (f32[1521,6]{0,1:T(8,128)S(1)}, f32[1521,6]{0,1:T(8,128)}, u32[]{:S(2)}) copy-start(f32[1521,6]{0,1:T(8,128)} %param.14) | copy-start | bytes 109516
  8.4 3.8 %copy-start = (bf16[16,64,180]{2,1,0:T(8,128)(2,1)S(1)}, bf16[16,64,180]{2,1,0:T(8,128)(2,1)}, u32[]{:S(2)}) copy-start(bf16[16,64,180]{2,1,0:T(8,128)(2,1)} %own_ref.9) | copy-start | bytes 1105924
  8.4 7.7 %copy-start.4 = (bf16[180,540]{1,0:T(8,128)(2,1)S(1)}, bf16[180,540]{1,0:T(8,128)(2,1)}, u32[]{:S(2)}) copy-start(bf16[180,540]{1,0:T(8,128)(2,1)} %qkv_ref.1) | copy-start | bytes 583204
  8.4 7.7 %copy-start.5 = (bf16[180,360]{1,0:T(8,128)(2,1)S(1)}, bf16[180,360]{1,0:T(8,128)(2,1)}, u32[]{:S(2)}) copy-start(bf16[180,360]{1,0:T(8,128)(2,1)} %hidden_ref.5) | copy-start | bytes 388804
  8.4 7.7 %copy-start.6 = (bf16[360,180]{0,1:T(8,128)(2,1)S(1)}, bf16[360,180]{0,1:T(8,128)(2,1)}, u32[]{:S(2)}) copy-start(bf16[360,180]{0,1:T(8,128)(2,1)} %param.18) | copy-start | bytes 388804
  8.4 7.7 %copy-start.7 = (bf16[180,180]{1,0:T(8,128)(2,1)S(1)}, bf16[180,180]{1,0:T(8,128)(2,1)}, u32[]{:S(2)}) copy-start(bf16[180,180]{1,0:T(8,128)(2,1)} %proj_ref.1) | copy-start | bytes 194404
  8.4 7.6 %copy-start.9 = (f32[180]{0:T(256)S(1)}, f32[180]{0:T(256)}, u32[]{:S(2)}) copy-start(f32[180]{0:T(256)} %param.12) | copy-start | bytes 2164
  8.4 7.6 %copy-start.10 = (f32[180]{0:T(256)S(1)}, f32[180]{0:T(256)}, u32[]{:S(2)}) copy-start(f32[180]{0:T(256)} %param.16) | copy-start | bytes 2164
  12.4 8.3 %collective-permute-start.2 = (bf16[720,128]{1,0:T(8,128)(2,1)S(1)}, bf16[720,128]{1,0:T(8,128)(2,1)S(1)}, u32[]{:S(2)}, u32[]{:S(2)}) collective-permute-start(bf16[720,128]{1,0:T(8,128)(2,1)S(1)} %get-tuple-element.23), channel_id=1, source_target_pairs={{1,2},{3,4},{5,6},{2,1},{4,3},{6,5},{9,10},{11,12},{13,14},{10,9},... | collective-permute-start | bytes 552968 | tf_op jit(solution)/shard_map/ppermute | solution.py:804
  13.1 7.6 %collective-permute-start.3 = (bf16[720,128]{1,0:T(8,128)(2,1)S(1)}, bf16[720,128]{1,0:T(8,128)(2,1)S(1)}, u32[]{:S(2)}, u32[]{:S(2)}) collective-permute-start(bf16[720,128]{1,0:T(8,128)(2,1)S(1)} %get-tuple-element.24), channel_id=1, source_target_pairs={{0,1},{2,3},{4,5},{6,7},{1,0},{3,2},{5,4},{7,6},{8,9},{10,11},{12,... | collective-permute-start | bytes 552968 | tf_op jit(solution)/shard_map/ppermute | solution.py:804
  26.8 6.4 %collective-permute-start.4 = (bf16[368,128]{1,0:T(8,128)(2,1)S(1)}, bf16[368,128]{1,0:T(8,128)(2,1)S(1)}, u32[]{:S(2)}, u32[]{:S(2)}) collective-permute-start(bf16[368,128]{1,0:T(8,128)(2,1)S(1)} %get-tuple-element.32), channel_id=1, source_target_pairs={{8,16},{16,8},{9,17},{17,9},{10,18},{18,10},{11,19},{19,11},{12,20... | collective-permute-start | bytes 282632 | tf_op jit(solution)/shard_map/ppermute | solution.py:804
  27.6 5.6 %collective-permute-start.5 = (bf16[368,128]{1,0:T(8,128)(2,1)S(1)}, bf16[368,128]{1,0:T(8,128)(2,1)S(1)}, u32[]{:S(2)}, u32[]{:S(2)}) collective-permute-start(bf16[368,128]{1,0:T(8,128)(2,1)S(1)} %get-tuple-element.33), channel_id=1, source_target_pairs={{0,8},{16,24},{8,0},{24,16},{1,9},{17,25},{9,1},{25,17},{2,10},{18... | collective-permute-start | bytes 282632 | tf_op jit(solution)/shard_map/ppermute | solution.py:804
  29.7 3.5 %copy-start.1 = (bf16[3,3,180,180]{3,2,1,0:T(8,128)(2,1)S(1)}, bf16[3,3,180,180]{3,2,1,0:T(8,128)(2,1)}, u32[]{:S(2)}) copy-start(bf16[3,3,180,180]{3,2,1,0:T(8,128)(2,1)} %group_ref.1) | copy-start | bytes 1749604
  29.7 3.5 %copy-start.2 = (bf16[3,3,180,64]{2,3,1,0:T(8,128)(2,1)S(1)}, bf16[3,3,180,64]{2,3,1,0:T(8,128)(2,1)}, u32[]{:S(2)}) copy-start(bf16[3,3,180,64]{2,3,1,0:T(8,128)(2,1)} %param.20) | copy-start | bytes 622084
  29.7 3.5 %copy-start.3 = (bf16[3,3,64,256]{3,2,1,0:T(8,128)(2,1)S(1)}, bf16[3,3,64,256]{3,2,1,0:T(8,128)(2,1)}, u32[]{:S(2)}) copy-start(bf16[3,3,64,256]{3,2,1,0:T(8,128)(2,1)} %upsample_ref.1) | copy-start | bytes 884740

commit v7 on v6

--- a/solution.py
+++ b/solution.py
@@ -492,6 +492,36 @@
     side_ref[:, STRIP : 2 * STRIP] = image[4:12, STRIP + cols :]
 
 
+def fill_taps(taps_ref, image, span):
+    chans = image.shape[2]
+    for b in range(3):
+        start = STRIP - 3 + b
+        lanes = slice(256 * b + 128, 256 * b + 256)
+        taps_ref[:, :, lanes] = jnp.zeros((taps_ref.shape[0], span, 128), BF16)
+        taps_ref[:, :, 256 * b : 256 * b + chans] = image[:, start : start + span].astype(BF16)
+
+
+def conv_weights(group_ref, before_ref, upsample_ref, wg_scr, wb_scr, wu_scr):
+    chans = group_ref.shape[2]
+    feats = before_ref.shape[2]
+    pad = chans // 16 * 16
+    for a in range(3):
+        wb_scr[256 * a + pad : 256 * (a + 1)] = jnp.zeros((256 - pad, 3 * feats), BF16)
+        wu_scr[256 * a + 3 * feats : 256 * (a + 1)] = jnp.zeros((256 - 3 * feats, 4 * feats), BF16)
+        for b in range(3):
+            wg_scr[256 * (3 * a + b) + pad : 256 * (3 * a + b + 1)] = jnp.zeros((256 - pad, chans), BF16)
+            wg_scr[256 * (3 * a + b) : 256 * (3 * a + b) + chans] = group_ref[a, b]
+    same = one_hot((chans, chans), lambda row: row, lambda col: col)
+    order = one_hot(
+        (4 * feats, 4 * feats), lambda row: row, lambda col: col % feats * 4 + col // feats
+    )
+    for a in range(3):
+        part = before_ref[a].reshape(3 * feats, chans)
+        wb_scr[256 * a : 256 * a + chans] = dot_nt(same, part).astype(BF16)
+        part = upsample_ref[a].reshape(3 * feats, 4 * feats)
+        wu_scr[256 * a : 256 * a + 3 * feats] = dot(part, order).astype(BF16)
+
+
 def middle_kernel(
     own_ref,
     nrm_ref,
@@ -500,16 +530,29 @@
     wqv_ref,
     wp_ref,
     inner_mid_ref,
+    edge_ref,
+    side_ref,
+    strip_ref,
+    row_two_ref,
+    row_one_ref,
+    group_ref,
+    before_ref,
+    upsample_ref,
     bias_ref,
     gain_two_ref,
     hidden_ref,
     output_ref,
-    mid_ref,
+    taps_ref,
+    base_ref,
+    wg_ref,
+    wb_ref,
+    wu_ref,
     q_scr,
     s_scr,
     m_scr,
     p_scr,
     o_scr,
+    image,
 ):
     height, cols, chans = own_ref.shape
     spots = (0, cols - 2 * WIN, cols - WIN)
@@ -519,9 +562,27 @@
         [3, 3, 3], [1, 2, 3], q_scr, k_ref, v_ref, bias_ref, wp_ref, s_scr, m_scr, p_scr, o_scr
     )
     mixed = feed_groups(first, gain_two_ref[...], hidden_ref, output_ref, 3)
-    mid_ref[:, WIN : cols - 2 * WIN] = inner_mid_ref[...]
+    span = cols + 2 * STRIP
+    image[:, span:] = jnp.zeros((height, STRIP, chans), F32)
+    image[0:4, 0:span] = edge_ref[0:4]
+    image[4:12, 0:STRIP] = side_ref[:, 0:STRIP]
+    image[4:12, STRIP + WIN : STRIP + cols - 2 * WIN] = inner_mid_ref[...]
     for g in range(3):
-        mid_ref[:, spots[g] : spots[g] + WIN] = mixed[g].reshape(8, WIN, chans)
+        c0 = STRIP + spots[g]
+        image[4:12, c0 : c0 + WIN] = mixed[g].reshape(8, WIN, chans)
+    image[4:12, STRIP + cols : span] = side_ref[:, STRIP : 2 * STRIP]
+    image[12:16, 0:span] = edge_ref[4:8]
+    fill_taps(taps_ref, image, span)
+    conv_weights(group_ref, before_ref, upsample_ref, wg_ref, wb_ref, wu_ref)
+    even_row = at_edges()[4]
+    above, below = from_sides(even_row, row_one_ref[...], row_two_ref[...])
+    base_ref[0:2, STRIP : STRIP + cols] = above[2:4]
+    base_ref[2 : 2 + height, STRIP : STRIP + cols] = own_ref[...].astype(F32)
+    base_ref[2 + height : 4 + height, STRIP : STRIP + cols] = below[0:2]
+    rows = slice(2, height + 6)
+    base_ref[:, 0:STRIP] = strip_ref[0, rows]
+    base_ref[:, STRIP + cols : span] = strip_ref[1, rows]
+    base_ref[:, span:] = jnp.zeros((height + 4, STRIP, chans), F32)
 
 
 def attention_scratch(groups):
@@ -586,85 +647,53 @@
 
 def middle_block(*args):
     height, cols, chans = args[0].shape
+    span = cols + 2 * STRIP
+    feats = args[-6].shape[2]
     return call(
         middle_kernel,
-        jax.ShapeDtypeStruct((8, cols, chans), F32),
-        attention_scratch(3),
+        (
+            jax.ShapeDtypeStruct((height, span, 768), BF16),
+            jax.ShapeDtypeStruct((height + 4, span + STRIP, chans), F32),
+            jax.ShapeDtypeStruct((9 * 256, chans), BF16),
+            jax.ShapeDtypeStruct((3 * 256, 3 * feats), BF16),
+            jax.ShapeDtypeStruct((3 * 256, 4 * feats), BF16),
+        ),
+        [*attention_scratch(3), pltpu.VMEM((height, span + STRIP, chans), F32)],
         5_000_000_000,
         4_000_000,
     )(*args)
 
 
 def conv_kernel(
-    own_ref,
-    row_one_ref,
-    row_two_ref,
-    strip_ref,
+    taps_ref,
+    base,
     back_two_ref,
     back_one_ref,
-    edge_ref,
-    side_ref,
-    mid_ref,
-    group_ref,
-    before_ref,
-    upsample_ref,
+    wg_scr,
+    wb_scr,
+    wu_scr,
     out_ref,
-    base,
     image,
-    taps,
+    halo_taps,
     grouped,
     sums,
     lowfeat,
     low_taps,
     out_scr,
-    wg_scr,
-    wb_scr,
-    wu_scr,
 ):
-    height, cols, chans = own_ref.shape
-    span = cols + 2 * STRIP
+    height, span = taps_ref.shape[:2]
+    cols = span - 2 * STRIP
+    chans = base.shape[2]
+    feats = out_ref.shape[0]
     at_left, at_right, at_top, at_bottom, even_row, _ = at_edges()
-
-    feats = before_ref.shape[2]
-    pad = chans // 16 * 16
-    for a in range(3):
-        wb_scr[256 * a + pad : 256 * (a + 1)] = jnp.zeros((256 - pad, 3 * feats), BF16)
-        wu_scr[256 * a + 3 * feats : 256 * (a + 1)] = jnp.zeros((256 - 3 * feats, 4 * feats), BF16)
-        for b in range(3):
-            wg_scr[256 * (3 * a + b) + pad : 256 * (3 * a + b + 1)] = jnp.zeros((256 - pad, chans), BF16)
-            wg_scr[256 * (3 * a + b) : 256 * (3 * a + b) + chans] = group_ref[a, b]
-    same = one_hot((chans, chans), lambda row: row, lambda col: col)
-    order = one_hot(
-        (4 * feats, 4 * feats), lambda row: row, lambda col: col % feats * 4 + col // feats
-    )
-    for a in range(3):
-        part = before_ref[a].reshape(3 * feats, chans)
-        wb_scr[256 * a : 256 * a + chans] = dot_nt(same, part).astype(BF16)
-        part = upsample_ref[a].reshape(3 * feats, 4 * feats)
-        wu_scr[256 * a : 256 * a + 3 * feats] = dot(part, order).astype(BF16)
-
-    above, below = from_sides(even_row, row_one_ref[...], row_two_ref[...])
-    base[0:2, STRIP : STRIP + cols] = above[2:4]
-    base[2 : 2 + height, STRIP : STRIP + cols] = own_ref[...].astype(F32)
-    base[2 + height : 4 + height, STRIP : STRIP + cols] = below[0:2]
-    rows = slice(2, height + 6)
-    base[:, 0:STRIP] = strip_ref[0, rows]
-    base[:, STRIP + cols : span] = strip_ref[1, rows]
-    base[:, span:] = jnp.zeros((height + 4, STRIP, chans), F32)
-    image[:, span:] = jnp.zeros((height + 6, STRIP, chans), F32)
-    above, below = from_sides(even_row, back_one_ref[...], back_two_ref[...])
-    for rows, packed in ((slice(0, 3), above), (slice(19, 22), below)):
+    image[:, span:] = jnp.zeros((6, STRIP, chans), F32)
+    sides = from_sides(even_row, back_one_ref[...], back_two_ref[...])
+    for rows, packed in ((slice(0, 3), sides[0]), (slice(3, 6), sides[1])):
         image[rows, 0:span, 0:128] = packed[0 : 3 * span].reshape(3, span, 128)
         rest = unhalve(packed[3 * span :], 3 * span).reshape(3, span, 128)
         image[rows, 0:span, 128:chans] = rest[:, :, 0 : chans - 128]
-    image[3:7, 0:span] = edge_ref[0:4]
-    image[7:15, 0:STRIP] = side_ref[:, 0:STRIP]
-    image[7:15, STRIP : STRIP + cols] = mid_ref[...]
-    image[7:15, STRIP + cols : span] = side_ref[:, STRIP : 2 * STRIP]
-    image[15:19, 0:span] = edge_ref[4:8]
+    fill_taps(halo_taps, image, span)
     grouped[:, :, 128:256] = jnp.zeros((height + 4, span, 128), BF16)
-    for b in range(3):
-        taps[:, :, 256 * b + 128 : 256 * b + 256] = jnp.zeros((height + 6, span, 128), BF16)
     part = 4
     col = lax.broadcasted_iota(jnp.int32, (span, chans), 0) - 2
     keep_grouped = (col < cols + 2) & ((col >= 0) | jnp.logical_not(at_left))
@@ -681,18 +710,20 @@
     )
     spread = spread.astype(F32).astype(BF16)
 
-    def fill_taps(first, last):
-        for b in range(3):
-            start = STRIP - 3 + b
-            taps[first:last, :, 256 * b : 256 * b + chans] = image[
-                first:last, start : start + span, :
-            ].astype(BF16)
+    def tap_row(row):
+        if 3 <= row < height + 3:
+            return taps_ref[row - 3]
+        return halo_taps[row if row < 3 else row - height]
 
     def group(h):
         totals = []
         for h2 in range(h, h + part, 2):
             lhs = jnp.concatenate(
-                [taps[h2 + a : h2 + a + 2].reshape(2 * span, 768) for a in range(3)], axis=1
+                [
+                    jnp.concatenate([tap_row(h2 + a), tap_row(h2 + a + 1)], axis=0)
+                    for a in range(3)
+                ],
+                axis=1,
             )
             totals.append(dot(lhs, wg_scr[...]).reshape(2, span, chans))
         total = jnp.concatenate(totals, axis=0)
@@ -749,13 +780,10 @@
                         a * feats : (a + 1) * feats, 128 * r : 128 * (r + 1)
                     ]
 
-    fill_taps(0, part + 2)
     narrowed = expanded = done = 0
     while expanded < height:
         expand_to, narrow_to = min(narrowed - 2, height), min(done - 2, height + 2)
         if done < height + 4:
-            if done + part < height + 4:
-                fill_taps(done + part + 2, done + 2 * part + 2)
             group(done)
             done += part
         while narrowed < narrow_to:
@@ -771,24 +799,21 @@
 
 
 def convs(*args):
-    height, cols, chans = args[0].shape
-    span = cols + 2 * STRIP
-    feats = args[-2].shape[2]
+    height, span = args[0].shape[:2]
+    chans = args[1].shape[2]
+    cols = span - 2 * STRIP
+    feats = args[-1].shape[1] // 4
     return call(
         conv_kernel,
         jax.ShapeDtypeStruct((feats, 2 * height, 2 * cols), BF16),
         [
-            pltpu.VMEM((height + 4, span + STRIP, chans), F32),
-            pltpu.VMEM((height + 6, span + STRIP, chans), F32),
-            pltpu.VMEM((height + 6, span, 768), BF16),
+            pltpu.VMEM((6, span + STRIP, chans), F32),
+            pltpu.VMEM((6, span, 768), BF16),
             pltpu.VMEM((height + 4, span, 256), BF16),
             pltpu.VMEM((2, 4, span, 256), F32),
             pltpu.VMEM((height + 2, cols + 8, 128), F32),
             pltpu.VMEM((height + 2, cols, 256), BF16),
             pltpu.VMEM((feats * 2 * height, 128), F32),
-            pltpu.VMEM((9 * 256, chans), BF16),
-            pltpu.VMEM((3 * 256, 3 * feats), BF16),
-            pltpu.VMEM((3 * 256, 4 * feats), BF16),
         ],
         8_000_000_000,
         4_000_000,
@@ -855,21 +880,26 @@
         *post,
     )
     back_one, back_two = swapped("rows", back_one, back_two)
-    mid = middle_block(features, nrm, keys, values, wqv, wp, inner_mid, bias, *post)
-    return convs(
+    taps, base, group, before, upsample = middle_block(
         features,
-        row_one,
-        row_two,
-        strips,
-        back_two,
-        back_one,
+        nrm,
+        keys,
+        values,
+        wqv,
+        wp,
+        inner_mid,
         edge,
         side,
-        mid,
+        strips,
+        row_two,
+        row_one,
         group_conv,
         before_conv.transpose(0, 1, 3, 2),
         upsample_conv,
-    )
+        bias,
+        *post,
+    )
+    return convs(taps, base, back_two, back_one, group, before, upsample)
 
 
 def solution(mesh):

time: 39.8 us -> 40.3 us (1.013)
  Pallas kernels: 24.5 us -> 25 us
    pallas_call x1, Pallas kernels: 3.49 us -> 4.37 us  [middle_block(): call(middle_kernel, (jax.ShapeDtypeStruct((height, span, 768), BF16), jax...]
  transfers between devices with their start and end apart: 6 -> 6, of which waited for: 0 -> 0; matrix products, arithmetic and copies ran while one was open for 0% -> 0% of each run, Pallas kernels for 30% -> 32%
where the time goes in v7:
time: 40.3 us; the launch traced here: 40.1 us
  Pallas kernels  25 us (62%)
  starting transfers between devices  13.1 us (33%)
  other arithmetic  0.99 us (2%)
  local copies, waits for them, and re-layouts  0.85 us (2%)
    ppermute x6, starting transfers between devices, swapped(): out.append(lax.ppermute(payload, axis, pairs))  13.1 us
    pallas_call x1, Pallas kernels, outer_block(): call(outer_kernel, (jax.ShapeDtypeStruct((3 * span + 128, 128), BF16), ja...  6.04 us
    pallas_call x1, Pallas kernels, convs(): call(conv_kernel, jax.ShapeDtypeStruct((feats, 2 * height, 2 * cols), BF1...  6.03 us
    pallas_call x1, Pallas kernels, inner_block(): call(inner_kernel, (jax.ShapeDtypeStruct((height + 2 * RIM, cols, chans),...  4.57 us
    pallas_call x1, Pallas kernels, middle_block(): call(middle_kernel, (jax.ShapeDtypeStruct((height, span, 768), BF16), jax...  4.37 us
    pallas_call x1, Pallas kernels, build_bias(): call(bias_kernel, jax.ShapeDtypeStruct((4, HEADS, KEYS, 128), BF16), [plt...  3.75 us
    select_n x1, other arithmetic, on_device(): jnp.where(even_row, low, high)  0.99 us
    unnamed x22, local copies, waits for them, and re-layouts  0.85 us
  transfers between devices with their start and end apart: 6, of which 0 were waited for; matrix products, arithmetic and copies ran while one was open for 0% of the time, Pallas kernels for 32%

profile of v7, /device:TPU:0, one launch (start us, length us, event | category | flops | bytes accessed | tf_op | source)
XLA Modules:
  0.0 40.1 jit_solution(10321080115869814520)
XLA Ops:
  0.0 1.0 %broadcast_select_fusion = (bf16[4,64,180]{2,1,0:T(8,128)(2,1)S(1)}, bf16[4,64,180]{2,1,0:T(8,128)(2,1)S(1)}) fusion(pred[]{:T(512)S(6)} %eq.5, bf16[16,64,180]{2,1,0:T(8,128)(2,1)} %own_ref.7), kind=kLoop, calls=%fused_computation | loop fusion | flops 92160 | bytes 368641 | tf_op jit(solution)/shard_map/jit(_where)/select_n | solution.py:850
  1.0 0.7 %collective-permute-start.1 = (bf16[4,64,180]{2,1,0:T(8,128)(2,1)S(1)}, bf16[4,64,180]{2,1,0:T(8,128)(2,1)S(1)}, u32[]{:S(2)}, u32[]{:S(2)}) collective-permute-start(bf16[4,64,180]{2,1,0:T(8,128)(2,1)S(1)} %get-tuple-element.49), channel_id=1, source_target_pairs={{8,16},{16,8},{9,17},{17,9},{10,18},{18,10},{11,19},{19,11},{12,20... | collective-permute-start | bytes 276488 | tf_op jit(solution)/shard_map/ppermute | solution.py:829
  1.7 5.9 %collective-permute-start = (bf16[4,64,180]{2,1,0:T(8,128)(2,1)S(1)}, bf16[4,64,180]{2,1,0:T(8,128)(2,1)S(1)}, u32[]{:S(2)}, u32[]{:S(2)}) collective-permute-start(bf16[4,64,180]{2,1,0:T(8,128)(2,1)S(1)} %get-tuple-element.50), channel_id=1, source_target_pairs={{0,8},{16,24},{8,0},{24,16},{1,9},{17,25},{9,1},{25,17},{2,10},{18... | collective-permute-start | bytes 276488 | tf_op jit(solution)/shard_map/ppermute | solution.py:829
  7.6 0.0 copy-start.8
  7.6 0.8 %copy-done.8 = f32[1521,6]{0,1:T(8,128)S(1)} copy-done((f32[1521,6]{0,1:T(8,128)S(1)}, f32[1521,6]{0,1:T(8,128)}, u32[]{:S(2)}) %copy-start.8) | copy-done | bytes 36528
  8.4 0.0 copy-start
  8.4 0.0 copy-start.4
  8.4 0.0 copy-start.5
  8.4 0.0 copy-start.6
  8.4 0.0 copy-start.7
  8.4 0.0 copy-start.9
  8.4 0.0 copy-start.10
  8.4 3.7 %shard_map.109.bias_ref = bf16[4,6,576,128]{3,2,1,0:T(8,128)(2,1)S(1)} custom-call(f32[6,1521]{1,0:T(8,128)S(1)} %bitcast.9), custom_call_target="tpu_custom_call" | custom-call | flops 4000000000 | bytes 4000000 | tf_op jit(solution)/shard_map/pallas_call | solution.py:102
  12.2 0.0 collective-permute-done.1.row_two_ref
  12.2 0.0 collective-permute-done.row_one_ref
  12.2 0.0 copy-done
  12.2 0.2 shard_map.111
  12.4 0.7 %collective-permute-start.2 = (bf16[720,128]{1,0:T(8,128)(2,1)S(1)}, bf16[720,128]{1,0:T(8,128)(2,1)S(1)}, u32[]{:S(2)}, u32[]{:S(2)}) collective-permute-start(bf16[720,128]{1,0:T(8,128)(2,1)S(1)} %get-tuple-element.28), channel_id=1, source_target_pairs={{1,2},{3,4},{5,6},{2,1},{4,3},{6,5},{9,10},{11,12},{13,14},{10,9},... | collective-permute-start | bytes 552968 | tf_op jit(solution)/shard_map/ppermute | solution.py:829
  13.1 2.9 %collective-permute-start.3 = (bf16[720,128]{1,0:T(8,128)(2,1)S(1)}, bf16[720,128]{1,0:T(8,128)(2,1)S(1)}, u32[]{:S(2)}, u32[]{:S(2)}) collective-permute-start(bf16[720,128]{1,0:T(8,128)(2,1)S(1)} %get-tuple-element.29), channel_id=1, source_target_pairs={{0,1},{2,3},{4,5},{6,7},{1,0},{3,2},{5,4},{7,6},{8,9},{10,11},{12,... | collective-permute-start | bytes 552968 | tf_op jit(solution)/shard_map/ppermute | solution.py:829
  16.0 0.0 copy-done.4
  16.0 0.0 copy-done.5
  16.0 0.0 copy-done.6
  16.0 0.0 copy-done.7
  16.0 0.0 copy-done.9
  16.0 0.0 copy-done.10
  16.1 4.6 %shard_map.110 = (f32[24,64,180]{2,1,0:T(8,128)S(1)}, bf16[180,384]{1,0:T(8,128)(2,1)S(1)}, bf16[384,180]{1,0:T(8,128)(2,1)S(1)}, bf16[192,180]{1,0:T(8,128)(2,1...) custom-call(bf16[16,64,180]{2,1,0:T(8,128)(2,1)S(1)} %copy-done, ...), custom_call_target="tpu_custom_call" | custom-call | flops 5000000000 | bytes 4000000 | tf_op jit(solution)/shard_map/pallas_call | solution.py:603
  20.6 0.0 collective-permute-done.2.col_two_ref
  20.6 0.0 collective-permute-done.3.col_one_ref
  20.7 0.0 copy-start.1
  20.7 0.0 copy-start.2
  20.7 0.0 copy-start.3
  20.7 6.0 %shard_map.112 = (bf16[368,128]{1,0:T(8,128)(2,1)S(1)}, bf16[368,128]{1,0:T(8,128)(2,1)S(1)}, f32[8,80,180]{2,1,0:T(8,128)S(1)}, f32[8,16,180]{2,1,0:T(8,128)S(1...) custom-call(bf16[16,64,180]{2,1,0:T(8,128)(2,1)S(1)} %copy-done, ...), custom_call_target="tpu_custom_call" | custom-call | flops 5000000000 | bytes 4000000 | tf_op jit(solution)/shard_map/pallas_call | solution.py:624
  26.7 0.8 %collective-permute-start.4 = (bf16[368,128]{1,0:T(8,128)(2,1)S(1)}, bf16[368,128]{1,0:T(8,128)(2,1)S(1)}, u32[]{:S(2)}, u32[]{:S(2)}) collective-permute-start(bf16[368,128]{1,0:T(8,128)(2,1)S(1)} %get-tuple-element.44), channel_id=1, source_target_pairs={{8,16},{16,8},{9,17},{17,9},{10,18},{18,10},{11,19},{19,11},{12,20... | collective-permute-start | bytes 282632 | tf_op jit(solution)/shard_map/ppermute | solution.py:829
  27.6 2.1 %collective-permute-start.5 = (bf16[368,128]{1,0:T(8,128)(2,1)S(1)}, bf16[368,128]{1,0:T(8,128)(2,1)S(1)}, u32[]{:S(2)}, u32[]{:S(2)}) collective-permute-start(bf16[368,128]{1,0:T(8,128)(2,1)S(1)} %get-tuple-element.45), channel_id=1, source_target_pairs={{0,8},{16,24},{8,0},{24,16},{1,9},{17,25},{9,1},{25,17},{2,10},{18... | collective-permute-start | bytes 282632 | tf_op jit(solution)/shard_map/ppermute | solution.py:829
  29.7 0.0 copy-done.1
  29.7 0.0 copy-done.2
  29.7 0.0 copy-done.3
  29.7 4.4 %shard_map.113 = (bf16[16,80,768]{2,1,0:T(8,128)(2,1)S(1)}, f32[20,88,180]{2,1,0:T(8,128)S(1)}, bf16[2304,180]{1,0:T(8,128)(2,1)S(1)}, bf16[768,192]{1,0:T(8,128)(2,1)S(1)}, bf16[768,256]{1,0:T(8,128)(2,1)S(1)}) custom-call(bf16[16,64,180]{2,1,0:T(8,128)(2,1)S(1)} %copy-done, f32[24,64,180]{2,1,0:T(8,128)S(1)} %get-tuple-element.27.nrm_ref, ...), custom_call_target="tpu_custom_call" | custom-call | flops 5000000000 | bytes 4000000 | tf_op jit(solution)/shard_map/pallas_call | solution.py:652
  34.1 0.0 collective-permute-done.4.back_two_ref
  34.1 0.0 collective-permute-done.5.back_one_ref
  34.1 6.0 %shard_map.114 = bf16[64,32,128]{2,1,0:T(8,128)(2,1)} custom-call(bf16[16,80,768]{2,1,0:T(8,128)(2,1)S(1)} %get-tuple-element.42.taps_ref, f32[20,88,180]{2,1,0:T(8,128)S(1)} %get-tuple-element.43.base, bf16[368,128]{1,0:T(8,128)(2,1)S(1)} %collective-permute-done.4.back_two_ref, bf16[368,128]{1,0:T(8,128)(2,1)S(1)} %collective-permute-done.5.back_one_ref, ...), custom_call_target="tpu_custom_call" | custom-call | flops 8000000000 | bytes 4000000 | tf_op jit(solution)/shard_map/pallas_call | solution.py:806
Async XLA Ops:
  1.0 11.2 %collective-permute-start.1 = (bf16[4,64,180]{2,1,0:T(8,128)(2,1)S(1)}, bf16[4,64,180]{2,1,0:T(8,128)(2,1)S(1)}, u32[]{:S(2)}, u32[]{:S(2)}) collective-permute-start(bf16[4,64,180]{2,1,0:T(8,128)(2,1)S(1)} %get-tuple-element.49), channel_id=1, source_target_pairs={{8,16},{16,8},{9,17},{17,9},{10,18},{18,10},{11,19},{19,11},{12,20... | collective-permute-start | bytes 276488 | tf_op jit(solution)/shard_map/ppermute | solution.py:829
  1.7 10.5 %collective-permute-start = (bf16[4,64,180]{2,1,0:T(8,128)(2,1)S(1)}, bf16[4,64,180]{2,1,0:T(8,128)(2,1)S(1)}, u32[]{:S(2)}, u32[]{:S(2)}) collective-permute-start(bf16[4,64,180]{2,1,0:T(8,128)(2,1)S(1)} %get-tuple-element.50), channel_id=1, source_target_pairs={{0,8},{16,24},{8,0},{24,16},{1,9},{17,25},{9,1},{25,17},{2,10},{18... | collective-permute-start | bytes 276488 | tf_op jit(solution)/shard_map/ppermute | solution.py:829
  7.6 0.8 %copy-start.8 = (f32[1521,6]{0,1:T(8,128)S(1)}, f32[1521,6]{0,1:T(8,128)}, u32[]{:S(2)}) copy-start(f32[1521,6]{0,1:T(8,128)} %param.14) | copy-start | bytes 109516
  8.4 3.8 %copy-start = (bf16[16,64,180]{2,1,0:T(8,128)(2,1)S(1)}, bf16[16,64,180]{2,1,0:T(8,128)(2,1)}, u32[]{:S(2)}) copy-start(bf16[16,64,180]{2,1,0:T(8,128)(2,1)} %own_ref.7) | copy-start | bytes 1105924
  8.4 7.7 %copy-start.4 = (bf16[180,540]{1,0:T(8,128)(2,1)S(1)}, bf16[180,540]{1,0:T(8,128)(2,1)}, u32[]{:S(2)}) copy-start(bf16[180,540]{1,0:T(8,128)(2,1)} %qkv_ref.1) | copy-start | bytes 583204
  8.4 7.7 %copy-start.5 = (bf16[180,360]{1,0:T(8,128)(2,1)S(1)}, bf16[180,360]{1,0:T(8,128)(2,1)}, u32[]{:S(2)}) copy-start(bf16[180,360]{1,0:T(8,128)(2,1)} %hidden_ref.5) | copy-start | bytes 388804
  8.4 7.7 %copy-start.6 = (bf16[360,180]{0,1:T(8,128)(2,1)S(1)}, bf16[360,180]{0,1:T(8,128)(2,1)}, u32[]{:S(2)}) copy-start(bf16[360,180]{0,1:T(8,128)(2,1)} %param.18) | copy-start | bytes 388804
  8.4 7.7 %copy-start.7 = (bf16[180,180]{1,0:T(8,128)(2,1)S(1)}, bf16[180,180]{1,0:T(8,128)(2,1)}, u32[]{:S(2)}) copy-start(bf16[180,180]{1,0:T(8,128)(2,1)} %proj_ref.1) | copy-start | bytes 194404
  8.4 7.6 %copy-start.9 = (f32[180]{0:T(256)S(1)}, f32[180]{0:T(256)}, u32[]{:S(2)}) copy-start(f32[180]{0:T(256)} %param.12) | copy-start | bytes 2164
  8.4 7.6 %copy-start.10 = (f32[180]{0:T(256)S(1)}, f32[180]{0:T(256)}, u32[]{:S(2)}) copy-start(f32[180]{0:T(256)} %param.16) | copy-start | bytes 2164
  12.4 8.2 %collective-permute-start.2 = (bf16[720,128]{1,0:T(8,128)(2,1)S(1)}, bf16[720,128]{1,0:T(8,128)(2,1)S(1)}, u32[]{:S(2)}, u32[]{:S(2)}) collective-permute-start(bf16[720,128]{1,0:T(8,128)(2,1)S(1)} %get-tuple-element.28), channel_id=1, source_target_pairs={{1,2},{3,4},{5,6},{2,1},{4,3},{6,5},{9,10},{11,12},{13,14},{10,9},... | collective-permute-start | bytes 552968 | tf_op jit(solution)/shard_map/ppermute | solution.py:829
  13.1 7.5 %collective-permute-start.3 = (bf16[720,128]{1,0:T(8,128)(2,1)S(1)}, bf16[720,128]{1,0:T(8,128)(2,1)S(1)}, u32[]{:S(2)}, u32[]{:S(2)}) collective-permute-start(bf16[720,128]{1,0:T(8,128)(2,1)S(1)} %get-tuple-element.29), channel_id=1, source_target_pairs={{0,1},{2,3},{4,5},{6,7},{1,0},{3,2},{5,4},{7,6},{8,9},{10,11},{12,... | collective-permute-start | bytes 552968 | tf_op jit(solution)/shard_map/ppermute | solution.py:829
  20.7 9.0 %copy-start.1 = (bf16[3,3,180,180]{3,2,1,0:T(8,128)(2,1)S(1)}, bf16[3,3,180,180]{3,2,1,0:T(8,128)(2,1)}, u32[]{:S(2)}) copy-start(bf16[3,3,180,180]{3,2,1,0:T(8,128)(2,1)} %group_ref.1) | copy-start | bytes 1749604
  20.7 9.0 %copy-start.2 = (bf16[3,3,180,64]{2,3,1,0:T(8,128)(2,1)S(1)}, bf16[3,3,180,64]{2,3,1,0:T(8,128)(2,1)}, u32[]{:S(2)}) copy-start(bf16[3,3,180,64]{2,3,1,0:T(8,128)(2,1)} %param.20) | copy-start | bytes 622084
  20.7 9.0 %copy-start.3 = (bf16[3,3,64,256]{3,2,1,0:T(8,128)(2,1)S(1)}, bf16[3,3,64,256]{3,2,1,0:T(8,128)(2,1)}, u32[]{:S(2)}) copy-start(bf16[3,3,64,256]{3,2,1,0:T(8,128)(2,1)} %upsample_ref.1) | copy-start | bytes 884740
  26.7 7.3 %collective-permute-start.4 = (bf16[368,128]{1,0:T(8,128)(2,1)S(1)}, bf16[368,128]{1,0:T(8,128)(2,1)S(1)}, u32[]{:S(2)}, u32[]{:S(2)}) collective-permute-start(bf16[368,128]{1,0:T(8,128)(2,1)S(1)} %get-tuple-element.44), channel_id=1, source_target_pairs={{8,16},{16,8},{9,17},{17,9},{10,18},{18,10},{11,19},{19,11},{12,20... | collective-permute-start | bytes 282632 | tf_op jit(solution)/shard_map/ppermute | solution.py:829
  27.6 6.5 %collective-permute-start.5 = (bf16[368,128]{1,0:T(8,128)(2,1)S(1)}, bf16[368,128]{1,0:T(8,128)(2,1)S(1)}, u32[]{:S(2)}, u32[]{:S(2)}) collective-permute-start(bf16[368,128]{1,0:T(8,128)(2,1)S(1)} %get-tuple-element.45), channel_id=1, source_target_pairs={{0,8},{16,24},{8,0},{24,16},{1,9},{17,25},{9,1},{25,17},{2,10},{18... | collective-permute-start | bytes 282632 | tf_op jit(solution)/shard_map/ppermute | solution.py:829

commit v8 on v7

--- a/solution.py
+++ b/solution.py
@@ -18,6 +18,7 @@
 RIM = (KWIN - WIN) // 2
 EDGE = WIN + 2 * RIM
 STRIP = 8
+SIDE_COLS = 4
 LOG2E = 1.4426950408889634
 F32 = jnp.float32
 BF16 = jnp.bfloat16
@@ -58,9 +59,9 @@
     def head(h, carry):
         values = t_scr[pl.ds(h, SIDE, stride=8), 0:SIDE].astype(BF16)
 
-        def expand(cols, first):
-            width = -(-SIDE * cols // 128) * 128
-            spot = lax.broadcasted_iota(jnp.int32, (SIDE, width), 1) // cols
+        def expand(cols, first, shift=0):
+            width = -(-(SIDE * cols + shift) // 128) * 128
+            spot = (lax.broadcasted_iota(jnp.int32, (SIDE, width), 1) - shift) // cols
             row = lax.broadcasted_iota(jnp.int32, (SIDE, width), 0)
             pick = (spot == SIDE - 1 - row).astype(F32).astype(BF16)
             e_scr[0:SIDE, 0:width] = lax.dot_general(values, pick, TN, preferred_element_type=F32)
@@ -86,13 +87,18 @@
                     at = (27 - p) // 8 * 128
                     x_scr[1, rows] = turned[:, at : at + 128]
         out_ref[1, h] = x_scr[0].astype(BF16)
-        out_ref[3, h] = x_scr[1].astype(BF16)
-        for kind, first in ((0, WIN - STRIP), (2, 0)):
-            expand(STRIP, first)
-            for p in range(KWIN):
-                rows = slice(p * KWIN, (p + 1) * KWIN)
-                x_scr[0, rows] = w_scr[:, (23 - p) * STRIP : (23 - p) * STRIP + 128]
-            out_ref[kind, h] = x_scr[0].astype(BF16)
+        out_ref[2, h] = x_scr[1].astype(BF16)
+        expand(SIDE_COLS, WIN - SIDE_COLS)
+        left = w_scr[:, 0:256]
+        expand(SIDE_COLS, 0, 64)
+        right = w_scr[:, 0:256]
+        whole = jnp.concatenate([left, right], axis=0)
+        for p in range(KWIN):
+            rows = slice(p * KWIN, (p + 1) * KWIN)
+            at = (23 - p) * SIDE_COLS
+            turned = whole if at == 0 else pltpu.roll(whole, 256 - at, 1)
+            x_scr[0, rows] = jnp.where(lanes < 64, turned[0:KWIN, 0:128], turned[KWIN:, 0:128])
+        out_ref[0, h] = x_scr[0].astype(BF16)
         return carry
 
     lax.fori_loop(0, HEADS, head, 0)
@@ -101,7 +107,7 @@
 def build_bias(bias_table):
     return call(
         bias_kernel,
-        jax.ShapeDtypeStruct((4, HEADS, KEYS, 128), BF16),
+        jax.ShapeDtypeStruct((3, HEADS, KEYS, 128), BF16),
         [
             pltpu.VMEM((8 * SIDE, 128), F32),
             pltpu.VMEM((SIDE + 1, 640), F32),
@@ -149,16 +155,23 @@
     wp_ref[...] = dot(pick, proj_ref[...]).astype(BF16)
 
 
-def set_queries(q_scr, wqv_ref, groups):
+def set_queries(q_scr, wqv_ref, groups, strips=None):
     scale = LOG2E / np.sqrt(HD)
-    rows = jnp.concatenate([rows.reshape(128, rows.shape[2]) for rows in groups], axis=0)
+    rows = jnp.concatenate([rows.reshape(128, rows.shape[-1]) for rows in groups], axis=0)
     queries = (dot_nt(wqv_ref[0 : HEADS * HP], rows.astype(BF16)) * scale).astype(BF16)
     none = jnp.zeros((HP, 128), BF16)
+    left = lax.broadcasted_iota(jnp.int32, (HP, 128), 1) < 64
     for g in range(len(groups)):
         lanes = slice(128 * g, 128 * g + 128)
         for t in range(HEADS // 2):
             one = queries[2 * t * HP : (2 * t + 1) * HP, lanes]
             two = queries[(2 * t + 1) * HP : (2 * t + 2) * HP, lanes]
+            if g == strips:
+                q_scr[g, t, 2 * HP : 3 * HP] = jnp.concatenate([jnp.where(left, none, one), none], axis=1)
+                q_scr[g, t, 3 * HP : 4 * HP] = jnp.concatenate([none, jnp.where(left, none, two)], axis=1)
+                one, two = jnp.where(left, one, none), jnp.where(left, two, none)
+            elif strips is not None:
+                q_scr[g, t, 2 * HP : 4 * HP] = jnp.zeros((2 * HP, 256), BF16)
             q_scr[g, t, 0:HP] = jnp.concatenate([one, none], axis=1)
             q_scr[g, t, HP : 2 * HP] = jnp.concatenate([none, two], axis=1)
 
@@ -170,13 +183,15 @@
     return out
 
 
-def attention(kinds, windows, q_scr, k_ref, v_ref, bias_ref, wp_ref, s_scr, m_scr, p_scr, o_scr):
+def attention(kinds, windows, q_scr, k_ref, v_ref, bias_ref, wp_ref, s_scr, m_scr, p_scr, o_scr, v_right=None):
     groups = len(kinds)
     pairs = HEADS // 2
     step = 144
+    depth = 2 * HP if v_right is None else 4 * HP
+    left = lax.broadcasted_iota(jnp.int32, (HP, 128), 1) < 64
 
     def keep(g, t, k0, top):
-        keys = k_ref[lookup(g, windows), k0 : k0 + step, 128 * t : 128 * t + 2 * HP]
+        keys = k_ref[lookup(g, windows), k0 : k0 + step, 128 * t : 128 * t + depth]
         one = dot(keys, q_scr[g, t])
         s_scr[t, k0 : k0 + step] = one
         part = jnp.max(one.reshape(step // 8, 8, 256), axis=0)
@@ -186,7 +201,14 @@
         for half in range(2):
             head = 2 * t + half
             lanes = slice(128 * half, 128 * half + 128)
-            o_scr[g, head] = dot(v_ref[lookup(g, windows), head * HP : (head + 1) * HP], p_scr[t, :, lanes])
+            window, rows = lookup(g, windows), slice(head * HP, (head + 1) * HP)
+            values = v_ref[window, rows]
+            if v_right is None:
+                o_scr[g, head] = dot(values, p_scr[t, :, lanes])
+            else:
+                values = jnp.concatenate([values, v_right[window, rows]], axis=0)
+                both = dot(values, p_scr[t, :, lanes])
+                o_scr[g, head] = jnp.where(left, both[0:HP], both[HP : 2 * HP])
 
     top = None
     for k0 in range(0, KEYS, step):
@@ -246,11 +268,15 @@
 
 
 def project(keys, wk_ref, wqv_ref, k_ref, v_ref, index):
+    keys = keys.reshape(KEYS, keys.shape[2]).astype(BF16)
+    k_ref[index] = dot(keys, wk_ref[...]).astype(BF16)
+    v_ref[index] = project_values(keys, wqv_ref)
+
+
+def project_values(keys, wqv_ref):
     width = HEADS * HP
     one_row = (lax.broadcasted_iota(jnp.int32, (width, 1), 0) % HP == HD).astype(F32)
-    keys = keys.reshape(KEYS, keys.shape[2]).astype(BF16)
-    k_ref[index] = dot(keys, wk_ref[...]).astype(BF16)
-    v_ref[index] = (dot_nt(wqv_ref[width : 2 * width], keys) + one_row).astype(BF16)
+    return (dot_nt(wqv_ref[width : 2 * width], keys) + one_row).astype(BF16)
 
 
 def at_edges():
@@ -374,7 +400,7 @@
         c0 = WIN * (w + 1)
         first.append(own_ref[4:12, c0 : c0 + WIN].reshape(128, chans))
         queries.append(nrm_ref[RIM + 4 : RIM + 12, c0 : c0 + WIN])
-        kinds.append(3)
+        kinds.append(2)
         windows.append(w)
     groups = len(kinds)
     set_queries(q_scr, wqv_ref, queries)
@@ -417,6 +443,8 @@
     x_scr,
     n_scr,
     b_scr,
+    strips,
+    v_right,
     q_scr,
     s_scr,
     m_scr,
@@ -447,36 +475,49 @@
     side_scr[1, :, 0:EDGE] = nrm_ref[:, cols - EDGE : cols]
     k_ref[2] = inner_k_ref[inner - 1]
     v_ref[2] = inner_v_ref[inner - 1]
-    for index, side, c0 in ((0, 0, RIM), (1, 0, RIM + WIN), (3, 1, RIM), (4, 1, RIM + WIN)):
+    for index, side, c0 in ((1, 0, RIM + WIN), (3, 1, RIM)):
         project(side_scr[side, :, c0 : c0 + KWIN], wk_ref, wqv_ref, k_ref, v_ref, index)
-    spots = (EDGE - STRIP, 0, cols - WIN, EDGE)
-    first, queries = [], []
-    for g in range(4):
-        side, c0 = g // 2, spots[g]
-        if g in (0, 3):
-            x = strip_ref[side, RIM : RIM + height]
-            queries.append(side_scr[side, RIM : RIM + height, c0 : c0 + STRIP])
-        else:
-            x = border_rows(own_ref, c0).astype(F32)
-            queries.append(border_rows(nrm_ref.at[RIM : RIM + height], c0))
-        first.append(x.reshape(128, chans))
-    set_queries(q_scr, wqv_ref, queries)
+        v_right[index] = v_ref[index]
+    strip_keys = [
+        side_scr[side, :, c0 : c0 + KWIN].reshape(KEYS, chans).astype(BF16)
+        for side, c0 in ((0, RIM), (1, RIM + WIN))
+    ]
+    moved = pltpu.roll(wk_ref[...].astype(F32), 2 * HP, 1).astype(BF16)
+    k_ref[0] = (dot(strip_keys[0], wk_ref[...]) + dot(strip_keys[1], moved)).astype(BF16)
+    v_ref[0] = project_values(strip_keys[0], wqv_ref)
+    v_right[0] = project_values(strip_keys[1], wqv_ref)
+    n = SIDE_COLS
+    for r in range(height):
+        for side, c0, c1 in ((0, STRIP - n, EDGE - n), (1, 0, EDGE)):
+            place = slice(64 * side + n * r, 64 * side + n * (r + 1))
+            strips[0, place] = strip_ref[side, RIM + r, c0 : c0 + n]
+            strips[1, place] = side_scr[side, RIM + r, c1 : c1 + n]
+    first, queries = [strips[0]], [strips[1]]
+    spots = (0, cols - WIN)
+    for c0 in spots:
+        first.append(border_rows(own_ref, c0).astype(F32).reshape(128, chans))
+        queries.append(border_rows(nrm_ref.at[RIM : RIM + height], c0))
+    set_queries(q_scr, wqv_ref, queries, 0)
     first = jnp.concatenate(first, axis=0) + attention(
-        [0, 1, 1, 2], [0, 1, 3, 4], q_scr, k_ref, v_ref, bias_ref, wp_ref, s_scr, m_scr, p_scr, o_scr
-    )
+        [0, 1, 1], [0, 1, 3], q_scr, k_ref, v_ref, bias_ref, wp_ref, s_scr, m_scr, p_scr, o_scr, v_right
+    )
+    image[:, 0:STRIP] = jnp.zeros((height, STRIP, chans), F32)
+    image[:, STRIP + cols :] = jnp.zeros((height, STRIP, chans), F32)
     image[0:4, STRIP + WIN : STRIP + cols - WIN] = inner_border_ref[0:4]
     image[12:16, STRIP + WIN : STRIP + cols - WIN] = inner_border_ref[4:8]
-    mixed = feed_groups(first, gain_two_ref[...], hidden_ref, output_ref, 2)
-    for g in range(4):
-        if g in (0, 3):
-            one = jnp.where(flags[g // 3], 0.0, mixed[g]).reshape(height, STRIP, chans)
-            c0 = 0 if g == 0 else STRIP + cols
-            image[:, c0 : c0 + STRIP] = one
-        else:
-            one = mixed[g].reshape(8, WIN, chans)
-            c0 = STRIP + spots[g]
-            image[0:4, c0 : c0 + WIN] = one[0:4]
-            image[12:16, c0 : c0 + WIN] = one[4:8]
+    mixed = feed_groups(first, gain_two_ref[...], hidden_ref, output_ref, 3)
+    row = lax.broadcasted_iota(jnp.int32, (128, chans), 0)
+    outside = (flags[0] & (row < 64)) | (flags[1] & (row >= 64))
+    strips[0] = jnp.where(outside, 0.0, mixed[0])
+    for r in range(height):
+        for side, c0 in ((0, STRIP - n), (1, STRIP + cols)):
+            place = 64 * side + n * r
+            image[r, c0 : c0 + n] = strips[0, place : place + n]
+    for g in range(2):
+        one = mixed[1 + g].reshape(8, WIN, chans)
+        c0 = STRIP + spots[g]
+        image[0:4, c0 : c0 + WIN] = one[0:4]
+        image[12:16, c0 : c0 + WIN] = one[4:8]
     even = flags[4]
     count = 3 * image.shape[1]
     for pay_ref, rows in (
@@ -559,7 +600,7 @@
     set_queries(q_scr, wqv_ref, [nrm_ref[RIM + 4 : RIM + 12, c0 : c0 + WIN] for c0 in spots])
     first = [own_ref[4:12, c0 : c0 + WIN].reshape(128, chans) for c0 in spots]
     first = jnp.concatenate(first, axis=0).astype(F32) + attention(
-        [3, 3, 3], [1, 2, 3], q_scr, k_ref, v_ref, bias_ref, wp_ref, s_scr, m_scr, p_scr, o_scr
+        [2, 2, 2], [1, 2, 3], q_scr, k_ref, v_ref, bias_ref, wp_ref, s_scr, m_scr, p_scr, o_scr
     )
     mixed = feed_groups(first, gain_two_ref[...], hidden_ref, output_ref, 3)
     span = cols + 2 * STRIP
@@ -585,9 +626,9 @@
     base_ref[:, span:] = jnp.zeros((height + 4, STRIP, chans), F32)
 
 
-def attention_scratch(groups):
+def attention_scratch(groups, depth=2 * HP):
     return [
-        pltpu.VMEM((groups, HEADS // 2, 2 * HP, 256), BF16),
+        pltpu.VMEM((groups, HEADS // 2, depth, 256), BF16),
         pltpu.VMEM((HEADS // 2, KEYS, 256), F32),
         pltpu.VMEM((8, 256), F32),
         pltpu.VMEM((HEADS // 2, KEYS, 256), BF16),
@@ -629,15 +670,17 @@
             jax.ShapeDtypeStruct((8, span, chans), F32),
             jax.ShapeDtypeStruct((8, 2 * STRIP, chans), F32),
             jax.ShapeDtypeStruct((2, height + 2 * RIM, STRIP, chans), F32),
-            jax.ShapeDtypeStruct((5, KEYS, 3 * 128), BF16),
-            jax.ShapeDtypeStruct((5, HEADS * HP, KEYS), BF16),
+            jax.ShapeDtypeStruct((4, KEYS, 3 * 128), BF16),
+            jax.ShapeDtypeStruct((4, HEADS * HP, KEYS), BF16),
         ),
         [
             pltpu.VMEM((2, height + 2 * RIM, 2 * EDGE, chans), F32),
             pltpu.VMEM((2, (height + 2 * RIM) * (WIN + RIM), 256), F32),
             pltpu.VMEM(((height + 2 * RIM) * (WIN + RIM), chans), F32),
             pltpu.VMEM((3 * span, 256), F32),
-            *attention_scratch(4),
+            pltpu.VMEM((2, 128, chans), F32),
+            pltpu.VMEM((4, HEADS * HP, KEYS), BF16),
+            *attention_scratch(3, 4 * HP),
             pltpu.VMEM((height, span, chans), F32),
         ],
         5_000_000_000,

time: 40.3 us -> 40 us (level)
  Pallas kernels: 25 us -> 24.5 us
where the time goes in v8:
time: 40 us; the launch traced here: 39.8 us
  Pallas kernels  24.5 us (61%)
  starting transfers between devices  13.2 us (33%)
  other arithmetic  0.99 us (2%)
  local copies, waits for them, and re-layouts  0.85 us (2%)
    ppermute x6, starting transfers between devices, swapped(): out.append(lax.ppermute(payload, axis, pairs))  13.2 us
    pallas_call x1, Pallas kernels, convs(): call(conv_kernel, jax.ShapeDtypeStruct((feats, 2 * height, 2 * cols), BF1...  5.99 us
    pallas_call x1, Pallas kernels, outer_block(): call(outer_kernel, (jax.ShapeDtypeStruct((3 * span + 128, 128), BF16), ja...  5.69 us
    pallas_call x1, Pallas kernels, inner_block(): call(inner_kernel, (jax.ShapeDtypeStruct((height + 2 * RIM, cols, chans),...  4.6 us
    pallas_call x1, Pallas kernels, middle_block(): call(middle_kernel, (jax.ShapeDtypeStruct((height, span, 768), BF16), jax...  4.35 us
    pallas_call x1, Pallas kernels, build_bias(): call(bias_kernel, jax.ShapeDtypeStruct((3, HEADS, KEYS, 128), BF16), [plt...  3.63 us
    select_n x1, other arithmetic, on_device(): jnp.where(even_row, low, high)  0.99 us
    unnamed x22, local copies, waits for them, and re-layouts  0.85 us
  transfers between devices with their start and end apart: 6, of which 0 were waited for; matrix products, arithmetic and copies ran while one was open for 0% of the time, Pallas kernels for 32%

profile of v8, /device:TPU:0, one launch (start us, length us, event | category | flops | bytes accessed | tf_op | source)
XLA Modules:
  0.0 39.8 jit_solution(6980651119089627139)
XLA Ops:
  0.0 1.0 %broadcast_select_fusion = (bf16[4,64,180]{2,1,0:T(8,128)(2,1)S(1)}, bf16[4,64,180]{2,1,0:T(8,128)(2,1)S(1)}) fusion(pred[]{:T(512)S(6)} %eq.5, bf16[16,64,180]{2,1,0:T(8,128)(2,1)} %own_ref.7), kind=kLoop, calls=%fused_computation | loop fusion | flops 92160 | bytes 368641 | tf_op jit(solution)/shard_map/jit(_where)/select_n | solution.py:893
  1.0 0.7 %collective-permute-start.1 = (bf16[4,64,180]{2,1,0:T(8,128)(2,1)S(1)}, bf16[4,64,180]{2,1,0:T(8,128)(2,1)S(1)}, u32[]{:S(2)}, u32[]{:S(2)}) collective-permute-start(bf16[4,64,180]{2,1,0:T(8,128)(2,1)S(1)} %get-tuple-element.49), channel_id=1, source_target_pairs={{8,16},{16,8},{9,17},{17,9},{10,18},{18,10},{11,19},{19,11},{12,20... | collective-permute-start | bytes 276488 | tf_op jit(solution)/shard_map/ppermute | solution.py:872
  1.7 5.9 %collective-permute-start = (bf16[4,64,180]{2,1,0:T(8,128)(2,1)S(1)}, bf16[4,64,180]{2,1,0:T(8,128)(2,1)S(1)}, u32[]{:S(2)}, u32[]{:S(2)}) collective-permute-start(bf16[4,64,180]{2,1,0:T(8,128)(2,1)S(1)} %get-tuple-element.50), channel_id=1, source_target_pairs={{0,8},{16,24},{8,0},{24,16},{1,9},{17,25},{9,1},{25,17},{2,10},{18... | collective-permute-start | bytes 276488 | tf_op jit(solution)/shard_map/ppermute | solution.py:872
  7.6 0.0 copy-start.8
  7.6 0.8 %copy-done.8 = f32[1521,6]{0,1:T(8,128)S(1)} copy-done((f32[1521,6]{0,1:T(8,128)S(1)}, f32[1521,6]{0,1:T(8,128)}, u32[]{:S(2)}) %copy-start.8) | copy-done | bytes 36528
  8.4 0.0 copy-start
  8.4 0.0 copy-start.4
  8.4 0.0 copy-start.5
  8.4 0.0 copy-start.6
  8.4 0.0 copy-start.7
  8.4 0.0 copy-start.9
  8.4 0.0 copy-start.10
  8.4 3.6 %shard_map.109.bias_ref = bf16[3,6,576,128]{3,2,1,0:T(8,128)(2,1)S(1)} custom-call(f32[6,1521]{1,0:T(8,128)S(1)} %bitcast.9), custom_call_target="tpu_custom_call" | custom-call | flops 4000000000 | bytes 4000000 | tf_op jit(solution)/shard_map/pallas_call | solution.py:108
  12.1 0.0 collective-permute-done.1.row_two_ref
  12.1 0.0 collective-permute-done.row_one_ref
  12.1 0.0 copy-done
  12.1 0.2 shard_map.111
  12.3 0.7 %collective-permute-start.2 = (bf16[720,128]{1,0:T(8,128)(2,1)S(1)}, bf16[720,128]{1,0:T(8,128)(2,1)S(1)}, u32[]{:S(2)}, u32[]{:S(2)}) collective-permute-start(bf16[720,128]{1,0:T(8,128)(2,1)S(1)} %get-tuple-element.28), channel_id=1, source_target_pairs={{1,2},{3,4},{5,6},{2,1},{4,3},{6,5},{9,10},{11,12},{13,14},{10,9},... | collective-permute-start | bytes 552968 | tf_op jit(solution)/shard_map/ppermute | solution.py:872
  13.0 2.9 %collective-permute-start.3 = (bf16[720,128]{1,0:T(8,128)(2,1)S(1)}, bf16[720,128]{1,0:T(8,128)(2,1)S(1)}, u32[]{:S(2)}, u32[]{:S(2)}) collective-permute-start(bf16[720,128]{1,0:T(8,128)(2,1)S(1)} %get-tuple-element.29), channel_id=1, source_target_pairs={{0,1},{2,3},{4,5},{6,7},{1,0},{3,2},{5,4},{7,6},{8,9},{10,11},{12,... | collective-permute-start | bytes 552968 | tf_op jit(solution)/shard_map/ppermute | solution.py:872
  15.9 0.0 copy-done.4
  15.9 0.0 copy-done.5
  15.9 0.0 copy-done.6
  15.9 0.0 copy-done.7
  15.9 0.0 copy-done.9
  15.9 0.0 copy-done.10
  15.9 4.6 %shard_map.110 = (f32[24,64,180]{2,1,0:T(8,128)S(1)}, bf16[180,384]{1,0:T(8,128)(2,1)S(1)}, bf16[384,180]{1,0:T(8,128)(2,1)S(1)}, bf16[192,180]{1,0:T(8,128)(2,1...) custom-call(bf16[16,64,180]{2,1,0:T(8,128)(2,1)S(1)} %copy-done, ...), custom_call_target="tpu_custom_call" | custom-call | flops 5000000000 | bytes 4000000 | tf_op jit(solution)/shard_map/pallas_call | solution.py:644
  20.6 0.0 collective-permute-done.2.col_two_ref
  20.6 0.0 collective-permute-done.3.col_one_ref
  20.6 0.0 copy-start.1
  20.6 0.0 copy-start.2
  20.6 0.0 copy-start.3
  20.6 5.7 %shard_map.112 = (bf16[368,128]{1,0:T(8,128)(2,1)S(1)}, bf16[368,128]{1,0:T(8,128)(2,1)S(1)}, f32[8,80,180]{2,1,0:T(8,128)S(1)}, f32[8,16,180]{2,1,0:T(8,128)S(1...) custom-call(bf16[16,64,180]{2,1,0:T(8,128)(2,1)S(1)} %copy-done, ...), custom_call_target="tpu_custom_call" | custom-call | flops 5000000000 | bytes 4000000 | tf_op jit(solution)/shard_map/pallas_call | solution.py:665
  26.3 0.8 %collective-permute-start.4 = (bf16[368,128]{1,0:T(8,128)(2,1)S(1)}, bf16[368,128]{1,0:T(8,128)(2,1)S(1)}, u32[]{:S(2)}, u32[]{:S(2)}) collective-permute-start(bf16[368,128]{1,0:T(8,128)(2,1)S(1)} %get-tuple-element.44), channel_id=1, source_target_pairs={{8,16},{16,8},{9,17},{17,9},{10,18},{18,10},{11,19},{19,11},{12,20... | collective-permute-start | bytes 282632 | tf_op jit(solution)/shard_map/ppermute | solution.py:872
  27.2 2.2 %collective-permute-start.5 = (bf16[368,128]{1,0:T(8,128)(2,1)S(1)}, bf16[368,128]{1,0:T(8,128)(2,1)S(1)}, u32[]{:S(2)}, u32[]{:S(2)}) collective-permute-start(bf16[368,128]{1,0:T(8,128)(2,1)S(1)} %get-tuple-element.45), channel_id=1, source_target_pairs={{0,8},{16,24},{8,0},{24,16},{1,9},{17,25},{9,1},{25,17},{2,10},{18... | collective-permute-start | bytes 282632 | tf_op jit(solution)/shard_map/ppermute | solution.py:872
  29.4 0.0 copy-done.1
  29.4 0.0 copy-done.2
  29.4 0.0 copy-done.3
  29.4 4.3 %shard_map.113 = (bf16[16,80,768]{2,1,0:T(8,128)(2,1)S(1)}, f32[20,88,180]{2,1,0:T(8,128)S(1)}, bf16[2304,180]{1,0:T(8,128)(2,1)S(1)}, bf16[768,192]{1,0:T(8,128)(2,1)S(1)}, bf16[768,256]{1,0:T(8,128)(2,1)S(1)}) custom-call(bf16[16,64,180]{2,1,0:T(8,128)(2,1)S(1)} %copy-done, f32[24,64,180]{2,1,0:T(8,128)S(1)} %get-tuple-element.27.nrm_ref, ...), custom_call_target="tpu_custom_call" | custom-call | flops 5000000000 | bytes 4000000 | tf_op jit(solution)/shard_map/pallas_call | solution.py:695
  33.7 0.0 collective-permute-done.4.back_two_ref
  33.7 0.0 collective-permute-done.5.back_one_ref
  33.8 6.0 %shard_map.114 = bf16[64,32,128]{2,1,0:T(8,128)(2,1)} custom-call(bf16[16,80,768]{2,1,0:T(8,128)(2,1)S(1)} %get-tuple-element.42.taps_ref, f32[20,88,180]{2,1,0:T(8,128)S(1)} %get-tuple-element.43.base, bf16[368,128]{1,0:T(8,128)(2,1)S(1)} %collective-permute-done.4.back_two_ref, bf16[368,128]{1,0:T(8,128)(2,1)S(1)} %collective-permute-done.5.back_one_ref, ...), custom_call_target="tpu_custom_call" | custom-call | flops 8000000000 | bytes 4000000 | tf_op jit(solution)/shard_map/pallas_call | solution.py:849
Async XLA Ops:
  1.0 11.1 %collective-permute-start.1 = (bf16[4,64,180]{2,1,0:T(8,128)(2,1)S(1)}, bf16[4,64,180]{2,1,0:T(8,128)(2,1)S(1)}, u32[]{:S(2)}, u32[]{:S(2)}) collective-permute-start(bf16[4,64,180]{2,1,0:T(8,128)(2,1)S(1)} %get-tuple-element.49), channel_id=1, source_target_pairs={{8,16},{16,8},{9,17},{17,9},{10,18},{18,10},{11,19},{19,11},{12,20... | collective-permute-start | bytes 276488 | tf_op jit(solution)/shard_map/ppermute | solution.py:872
  1.7 10.4 %collective-permute-start = (bf16[4,64,180]{2,1,0:T(8,128)(2,1)S(1)}, bf16[4,64,180]{2,1,0:T(8,128)(2,1)S(1)}, u32[]{:S(2)}, u32[]{:S(2)}) collective-permute-start(bf16[4,64,180]{2,1,0:T(8,128)(2,1)S(1)} %get-tuple-element.50), channel_id=1, source_target_pairs={{0,8},{16,24},{8,0},{24,16},{1,9},{17,25},{9,1},{25,17},{2,10},{18... | collective-permute-start | bytes 276488 | tf_op jit(solution)/shard_map/ppermute | solution.py:872
  7.6 0.8 %copy-start.8 = (f32[1521,6]{0,1:T(8,128)S(1)}, f32[1521,6]{0,1:T(8,128)}, u32[]{:S(2)}) copy-start(f32[1521,6]{0,1:T(8,128)} %param.14) | copy-start | bytes 109516
  8.4 3.7 %copy-start = (bf16[16,64,180]{2,1,0:T(8,128)(2,1)S(1)}, bf16[16,64,180]{2,1,0:T(8,128)(2,1)}, u32[]{:S(2)}) copy-start(bf16[16,64,180]{2,1,0:T(8,128)(2,1)} %own_ref.7) | copy-start | bytes 1105924
  8.4 7.5 %copy-start.4 = (bf16[180,540]{1,0:T(8,128)(2,1)S(1)}, bf16[180,540]{1,0:T(8,128)(2,1)}, u32[]{:S(2)}) copy-start(bf16[180,540]{1,0:T(8,128)(2,1)} %qkv_ref.1) | copy-start | bytes 583204
  8.4 7.5 %copy-start.5 = (bf16[180,360]{1,0:T(8,128)(2,1)S(1)}, bf16[180,360]{1,0:T(8,128)(2,1)}, u32[]{:S(2)}) copy-start(bf16[180,360]{1,0:T(8,128)(2,1)} %hidden_ref.5) | copy-start | bytes 388804
  8.4 7.5 %copy-start.6 = (bf16[360,180]{0,1:T(8,128)(2,1)S(1)}, bf16[360,180]{0,1:T(8,128)(2,1)}, u32[]{:S(2)}) copy-start(bf16[360,180]{0,1:T(8,128)(2,1)} %param.18) | copy-start | bytes 388804
  8.4 7.5 %copy-start.7 = (bf16[180,180]{1,0:T(8,128)(2,1)S(1)}, bf16[180,180]{1,0:T(8,128)(2,1)}, u32[]{:S(2)}) copy-start(bf16[180,180]{1,0:T(8,128)(2,1)} %proj_ref.1) | copy-start | bytes 194404
  8.4 7.5 %copy-start.9 = (f32[180]{0:T(256)S(1)}, f32[180]{0:T(256)}, u32[]{:S(2)}) copy-start(f32[180]{0:T(256)} %param.12) | copy-start | bytes 2164
  8.4 7.5 %copy-start.10 = (f32[180]{0:T(256)S(1)}, f32[180]{0:T(256)}, u32[]{:S(2)}) copy-start(f32[180]{0:T(256)} %param.16) | copy-start | bytes 2164
  12.3 8.2 %collective-permute-start.2 = (bf16[720,128]{1,0:T(8,128)(2,1)S(1)}, bf16[720,128]{1,0:T(8,128)(2,1)S(1)}, u32[]{:S(2)}, u32[]{:S(2)}) collective-permute-start(bf16[720,128]{1,0:T(8,128)(2,1)S(1)} %get-tuple-element.28), channel_id=1, source_target_pairs={{1,2},{3,4},{5,6},{2,1},{4,3},{6,5},{9,10},{11,12},{13,14},{10,9},... | collective-permute-start | bytes 552968 | tf_op jit(solution)/shard_map/ppermute | solution.py:872
  13.0 7.6 %collective-permute-start.3 = (bf16[720,128]{1,0:T(8,128)(2,1)S(1)}, bf16[720,128]{1,0:T(8,128)(2,1)S(1)}, u32[]{:S(2)}, u32[]{:S(2)}) collective-permute-start(bf16[720,128]{1,0:T(8,128)(2,1)S(1)} %get-tuple-element.29), channel_id=1, source_target_pairs={{0,1},{2,3},{4,5},{6,7},{1,0},{3,2},{5,4},{7,6},{8,9},{10,11},{12,... | collective-permute-start | bytes 552968 | tf_op jit(solution)/shard_map/ppermute | solution.py:872
  20.6 8.8 %copy-start.1 = (bf16[3,3,180,180]{3,2,1,0:T(8,128)(2,1)S(1)}, bf16[3,3,180,180]{3,2,1,0:T(8,128)(2,1)}, u32[]{:S(2)}) copy-start(bf16[3,3,180,180]{3,2,1,0:T(8,128)(2,1)} %group_ref.1) | copy-start | bytes 1749604
  20.6 8.8 %copy-start.2 = (bf16[3,3,180,64]{2,3,1,0:T(8,128)(2,1)S(1)}, bf16[3,3,180,64]{2,3,1,0:T(8,128)(2,1)}, u32[]{:S(2)}) copy-start(bf16[3,3,180,64]{2,3,1,0:T(8,128)(2,1)} %param.20) | copy-start | bytes 622084
  20.6 8.8 %copy-start.3 = (bf16[3,3,64,256]{3,2,1,0:T(8,128)(2,1)S(1)}, bf16[3,3,64,256]{3,2,1,0:T(8,128)(2,1)}, u32[]{:S(2)}) copy-start(bf16[3,3,64,256]{3,2,1,0:T(8,128)(2,1)} %upsample_ref.1) | copy-start | bytes 884740
  26.3 7.4 %collective-permute-start.4 = (bf16[368,128]{1,0:T(8,128)(2,1)S(1)}, bf16[368,128]{1,0:T(8,128)(2,1)S(1)}, u32[]{:S(2)}, u32[]{:S(2)}) collective-permute-start(bf16[368,128]{1,0:T(8,128)(2,1)S(1)} %get-tuple-element.44), channel_id=1, source_target_pairs={{8,16},{16,8},{9,17},{17,9},{10,18},{18,10},{11,19},{19,11},{12,20... | collective-permute-start | bytes 282632 | tf_op jit(solution)/shard_map/ppermute | solution.py:872
  27.2 6.6 %collective-permute-start.5 = (bf16[368,128]{1,0:T(8,128)(2,1)S(1)}, bf16[368,128]{1,0:T(8,128)(2,1)S(1)}, u32[]{:S(2)}, u32[]{:S(2)}) collective-permute-start(bf16[368,128]{1,0:T(8,128)(2,1)S(1)} %get-tuple-element.45), channel_id=1, source_target_pairs={{0,8},{16,24},{8,0},{24,16},{1,9},{17,25},{9,1},{25,17},{2,10},{18... | collective-permute-start | bytes 282632 | tf_op jit(solution)/shard_map/ppermute | solution.py:872

commit v9 on v8

--- a/solution.py
+++ b/solution.py
@@ -228,13 +228,13 @@
             following = g if t + 1 < pairs else jnp.minimum(g + 1, groups - 1)
             later = None
             for k0 in range(0, KEYS, step):
+                later = keep(following, (t + 1) % pairs, k0, later)
                 prob = jnp.exp2(s_scr[t, k0 : k0 + step] - top).astype(BF16)
                 for half in range(2):
                     lanes = slice(128 * half, 128 * half + 128)
                     p_scr[t, k0 : k0 + step, lanes] = (
                         prob[:, lanes] * bias_ref[kind, 2 * t + half, k0 : k0 + step]
                     )
-                later = keep(following, (t + 1) % pairs, k0, later)
             top = later
         m_scr[...] = top
         return carry
@@ -737,7 +737,7 @@
         image[rows, 0:span, 128:chans] = rest[:, :, 0 : chans - 128]
     fill_taps(halo_taps, image, span)
     grouped[:, :, 128:256] = jnp.zeros((height + 4, span, 128), BF16)
-    part = 4
+    part = 2
     col = lax.broadcasted_iota(jnp.int32, (span, chans), 0) - 2
     keep_grouped = (col < cols + 2) & ((col >= 0) | jnp.logical_not(at_left))
     keep_grouped = keep_grouped & ((col < cols) | jnp.logical_not(at_right))

time: 40 us -> 40.3 us (level)
  transfers between devices with their start and end apart: 6 -> 6, of which waited for: 0 -> 0; matrix products, arithmetic and copies ran while one was open for 0% -> 0% of each run, Pallas kernels for 32% -> 31%
where the time goes in v9:
time: 40.3 us; the launch traced here: 40.1 us
  Pallas kernels  24.8 us (62%)
  starting transfers between devices  13.2 us (33%)
  other arithmetic  0.99 us (2%)
  local copies, waits for them, and re-layouts  0.85 us (2%)
    ppermute x6, starting transfers between devices, swapped(): out.append(lax.ppermute(payload, axis, pairs))  13.2 us
    pallas_call x1, Pallas kernels, convs(): call(conv_kernel, jax.ShapeDtypeStruct((feats, 2 * height, 2 * cols), BF1...  6.38 us
    pallas_call x1, Pallas kernels, outer_block(): call(outer_kernel, (jax.ShapeDtypeStruct((3 * span + 128, 128), BF16), ja...  5.72 us
    pallas_call x1, Pallas kernels, inner_block(): call(inner_kernel, (jax.ShapeDtypeStruct((height + 2 * RIM, cols, chans),...  4.53 us
    pallas_call x1, Pallas kernels, middle_block(): call(middle_kernel, (jax.ShapeDtypeStruct((height, span, 768), BF16), jax...  4.32 us
    pallas_call x1, Pallas kernels, build_bias(): call(bias_kernel, jax.ShapeDtypeStruct((3, HEADS, KEYS, 128), BF16), [plt...  3.63 us
    select_n x1, other arithmetic, on_device(): jnp.where(even_row, low, high)  0.99 us
    unnamed x22, local copies, waits for them, and re-layouts  0.85 us
  transfers between devices with their start and end apart: 6, of which 0 were waited for; matrix products, arithmetic and copies ran while one was open for 0% of the time, Pallas kernels for 31%

profile of v9, /device:TPU:0, one launch (start us, length us, event | category | flops | bytes accessed | tf_op | source)
XLA Modules:
  0.0 40.1 jit_solution(7177091807249066310)
XLA Ops:
  0.0 1.0 %broadcast_select_fusion = (bf16[4,64,180]{2,1,0:T(8,128)(2,1)S(1)}, bf16[4,64,180]{2,1,0:T(8,128)(2,1)S(1)}) fusion(pred[]{:T(512)S(6)} %eq.5, bf16[16,64,180]{2,1,0:T(8,128)(2,1)} %own_ref.7), kind=kLoop, calls=%fused_computation | loop fusion | flops 92160 | bytes 368641 | tf_op jit(solution)/shard_map/jit(_where)/select_n | solution.py:893
  1.0 0.7 %collective-permute-start.1 = (bf16[4,64,180]{2,1,0:T(8,128)(2,1)S(1)}, bf16[4,64,180]{2,1,0:T(8,128)(2,1)S(1)}, u32[]{:S(2)}, u32[]{:S(2)}) collective-permute-start(bf16[4,64,180]{2,1,0:T(8,128)(2,1)S(1)} %get-tuple-element.49), channel_id=1, source_target_pairs={{8,16},{16,8},{9,17},{17,9},{10,18},{18,10},{11,19},{19,11},{12,20... | collective-permute-start | bytes 276488 | tf_op jit(solution)/shard_map/ppermute | solution.py:872
  1.7 5.9 %collective-permute-start = (bf16[4,64,180]{2,1,0:T(8,128)(2,1)S(1)}, bf16[4,64,180]{2,1,0:T(8,128)(2,1)S(1)}, u32[]{:S(2)}, u32[]{:S(2)}) collective-permute-start(bf16[4,64,180]{2,1,0:T(8,128)(2,1)S(1)} %get-tuple-element.50), channel_id=1, source_target_pairs={{0,8},{16,24},{8,0},{24,16},{1,9},{17,25},{9,1},{25,17},{2,10},{18... | collective-permute-start | bytes 276488 | tf_op jit(solution)/shard_map/ppermute | solution.py:872
  7.6 0.0 copy-start.8
  7.6 0.8 %copy-done.8 = f32[1521,6]{0,1:T(8,128)S(1)} copy-done((f32[1521,6]{0,1:T(8,128)S(1)}, f32[1521,6]{0,1:T(8,128)}, u32[]{:S(2)}) %copy-start.8) | copy-done | bytes 36528
  8.4 0.0 copy-start
  8.4 0.0 copy-start.4
  8.4 0.0 copy-start.5
  8.4 0.0 copy-start.6
  8.4 0.0 copy-start.7
  8.4 0.0 copy-start.9
  8.4 0.0 copy-start.10
  8.4 3.6 %shard_map.109.bias_ref = bf16[3,6,576,128]{3,2,1,0:T(8,128)(2,1)S(1)} custom-call(f32[6,1521]{1,0:T(8,128)S(1)} %bitcast.9), custom_call_target="tpu_custom_call" | custom-call | flops 4000000000 | bytes 4000000 | tf_op jit(solution)/shard_map/pallas_call | solution.py:108
  12.1 0.0 collective-permute-done.1.row_two_ref
  12.1 0.0 collective-permute-done.row_one_ref
  12.1 0.0 copy-done
  12.1 0.2 shard_map.111
  12.3 0.7 %collective-permute-start.2 = (bf16[720,128]{1,0:T(8,128)(2,1)S(1)}, bf16[720,128]{1,0:T(8,128)(2,1)S(1)}, u32[]{:S(2)}, u32[]{:S(2)}) collective-permute-start(bf16[720,128]{1,0:T(8,128)(2,1)S(1)} %get-tuple-element.28), channel_id=1, source_target_pairs={{1,2},{3,4},{5,6},{2,1},{4,3},{6,5},{9,10},{11,12},{13,14},{10,9},... | collective-permute-start | bytes 552968 | tf_op jit(solution)/shard_map/ppermute | solution.py:872
  13.0 2.9 %collective-permute-start.3 = (bf16[720,128]{1,0:T(8,128)(2,1)S(1)}, bf16[720,128]{1,0:T(8,128)(2,1)S(1)}, u32[]{:S(2)}, u32[]{:S(2)}) collective-permute-start(bf16[720,128]{1,0:T(8,128)(2,1)S(1)} %get-tuple-element.29), channel_id=1, source_target_pairs={{0,1},{2,3},{4,5},{6,7},{1,0},{3,2},{5,4},{7,6},{8,9},{10,11},{12,... | collective-permute-start | bytes 552968 | tf_op jit(solution)/shard_map/ppermute | solution.py:872
  15.9 0.0 copy-done.4
  15.9 0.0 copy-done.5
  15.9 0.0 copy-done.6
  15.9 0.0 copy-done.7
  15.9 0.0 copy-done.9
  15.9 0.0 copy-done.10
  15.9 4.5 %shard_map.110 = (f32[24,64,180]{2,1,0:T(8,128)S(1)}, bf16[180,384]{1,0:T(8,128)(2,1)S(1)}, bf16[384,180]{1,0:T(8,128)(2,1)S(1)}, bf16[192,180]{1,0:T(8,128)(2,1...) custom-call(bf16[16,64,180]{2,1,0:T(8,128)(2,1)S(1)} %copy-done, ...), custom_call_target="tpu_custom_call" | custom-call | flops 5000000000 | bytes 4000000 | tf_op jit(solution)/shard_map/pallas_call | solution.py:644
  20.5 0.0 collective-permute-done.2.col_two_ref
  20.5 0.0 collective-permute-done.3.col_one_ref
  20.5 0.0 copy-start.1
  20.5 0.0 copy-start.2
  20.5 0.0 copy-start.3
  20.5 5.7 %shard_map.112 = (bf16[368,128]{1,0:T(8,128)(2,1)S(1)}, bf16[368,128]{1,0:T(8,128)(2,1)S(1)}, f32[8,80,180]{2,1,0:T(8,128)S(1)}, f32[8,16,180]{2,1,0:T(8,128)S(1...) custom-call(bf16[16,64,180]{2,1,0:T(8,128)(2,1)S(1)} %copy-done, ...), custom_call_target="tpu_custom_call" | custom-call | flops 5000000000 | bytes 4000000 | tf_op jit(solution)/shard_map/pallas_call | solution.py:665
  26.3 0.8 %collective-permute-start.4 = (bf16[368,128]{1,0:T(8,128)(2,1)S(1)}, bf16[368,128]{1,0:T(8,128)(2,1)S(1)}, u32[]{:S(2)}, u32[]{:S(2)}) collective-permute-start(bf16[368,128]{1,0:T(8,128)(2,1)S(1)} %get-tuple-element.44), channel_id=1, source_target_pairs={{8,16},{16,8},{9,17},{17,9},{10,18},{18,10},{11,19},{19,11},{12,20... | collective-permute-start | bytes 282632 | tf_op jit(solution)/shard_map/ppermute | solution.py:872
  27.1 2.2 %collective-permute-start.5 = (bf16[368,128]{1,0:T(8,128)(2,1)S(1)}, bf16[368,128]{1,0:T(8,128)(2,1)S(1)}, u32[]{:S(2)}, u32[]{:S(2)}) collective-permute-start(bf16[368,128]{1,0:T(8,128)(2,1)S(1)} %get-tuple-element.45), channel_id=1, source_target_pairs={{0,8},{16,24},{8,0},{24,16},{1,9},{17,25},{9,1},{25,17},{2,10},{18... | collective-permute-start | bytes 282632 | tf_op jit(solution)/shard_map/ppermute | solution.py:872
  29.3 0.0 copy-done.1
  29.3 0.0 copy-done.2
  29.3 0.0 copy-done.3
  29.3 4.3 %shard_map.113 = (bf16[16,80,768]{2,1,0:T(8,128)(2,1)S(1)}, f32[20,88,180]{2,1,0:T(8,128)S(1)}, bf16[2304,180]{1,0:T(8,128)(2,1)S(1)}, bf16[768,192]{1,0:T(8,128)(2,1)S(1)}, bf16[768,256]{1,0:T(8,128)(2,1)S(1)}) custom-call(bf16[16,64,180]{2,1,0:T(8,128)(2,1)S(1)} %copy-done, f32[24,64,180]{2,1,0:T(8,128)S(1)} %get-tuple-element.27.nrm_ref, ...), custom_call_target="tpu_custom_call" | custom-call | flops 5000000000 | bytes 4000000 | tf_op jit(solution)/shard_map/pallas_call | solution.py:695
  33.7 0.0 collective-permute-done.4.back_two_ref
  33.7 0.0 collective-permute-done.5.back_one_ref
  33.7 6.4 %shard_map.114 = bf16[64,32,128]{2,1,0:T(8,128)(2,1)} custom-call(bf16[16,80,768]{2,1,0:T(8,128)(2,1)S(1)} %get-tuple-element.42.taps_ref, f32[20,88,180]{2,1,0:T(8,128)S(1)} %get-tuple-element.43.base, bf16[368,128]{1,0:T(8,128)(2,1)S(1)} %collective-permute-done.4.back_two_ref, bf16[368,128]{1,0:T(8,128)(2,1)S(1)} %collective-permute-done.5.back_one_ref, ...), custom_call_target="tpu_custom_call" | custom-call | flops 8000000000 | bytes 4000000 | tf_op jit(solution)/shard_map/pallas_call | solution.py:849
Async XLA Ops:
  1.0 11.1 %collective-permute-start.1 = (bf16[4,64,180]{2,1,0:T(8,128)(2,1)S(1)}, bf16[4,64,180]{2,1,0:T(8,128)(2,1)S(1)}, u32[]{:S(2)}, u32[]{:S(2)}) collective-permute-start(bf16[4,64,180]{2,1,0:T(8,128)(2,1)S(1)} %get-tuple-element.49), channel_id=1, source_target_pairs={{8,16},{16,8},{9,17},{17,9},{10,18},{18,10},{11,19},{19,11},{12,20... | collective-permute-start | bytes 276488 | tf_op jit(solution)/shard_map/ppermute | solution.py:872
  1.7 10.4 %collective-permute-start = (bf16[4,64,180]{2,1,0:T(8,128)(2,1)S(1)}, bf16[4,64,180]{2,1,0:T(8,128)(2,1)S(1)}, u32[]{:S(2)}, u32[]{:S(2)}) collective-permute-start(bf16[4,64,180]{2,1,0:T(8,128)(2,1)S(1)} %get-tuple-element.50), channel_id=1, source_target_pairs={{0,8},{16,24},{8,0},{24,16},{1,9},{17,25},{9,1},{25,17},{2,10},{18... | collective-permute-start | bytes 276488 | tf_op jit(solution)/shard_map/ppermute | solution.py:872
  7.6 0.8 %copy-start.8 = (f32[1521,6]{0,1:T(8,128)S(1)}, f32[1521,6]{0,1:T(8,128)}, u32[]{:S(2)}) copy-start(f32[1521,6]{0,1:T(8,128)} %param.14) | copy-start | bytes 109516
  8.4 3.7 %copy-start = (bf16[16,64,180]{2,1,0:T(8,128)(2,1)S(1)}, bf16[16,64,180]{2,1,0:T(8,128)(2,1)}, u32[]{:S(2)}) copy-start(bf16[16,64,180]{2,1,0:T(8,128)(2,1)} %own_ref.7) | copy-start | bytes 1105924
  8.4 7.5 %copy-start.4 = (bf16[180,540]{1,0:T(8,128)(2,1)S(1)}, bf16[180,540]{1,0:T(8,128)(2,1)}, u32[]{:S(2)}) copy-start(bf16[180,540]{1,0:T(8,128)(2,1)} %qkv_ref.1) | copy-start | bytes 583204
  8.4 7.5 %copy-start.5 = (bf16[180,360]{1,0:T(8,128)(2,1)S(1)}, bf16[180,360]{1,0:T(8,128)(2,1)}, u32[]{:S(2)}) copy-start(bf16[180,360]{1,0:T(8,128)(2,1)} %hidden_ref.5) | copy-start | bytes 388804
  8.4 7.5 %copy-start.6 = (bf16[360,180]{0,1:T(8,128)(2,1)S(1)}, bf16[360,180]{0,1:T(8,128)(2,1)}, u32[]{:S(2)}) copy-start(bf16[360,180]{0,1:T(8,128)(2,1)} %param.18) | copy-start | bytes 388804
  8.4 7.5 %copy-start.7 = (bf16[180,180]{1,0:T(8,128)(2,1)S(1)}, bf16[180,180]{1,0:T(8,128)(2,1)}, u32[]{:S(2)}) copy-start(bf16[180,180]{1,0:T(8,128)(2,1)} %proj_ref.1) | copy-start | bytes 194404
  8.4 7.5 %copy-start.9 = (f32[180]{0:T(256)S(1)}, f32[180]{0:T(256)}, u32[]{:S(2)}) copy-start(f32[180]{0:T(256)} %param.12) | copy-start | bytes 2164
  8.4 7.5 %copy-start.10 = (f32[180]{0:T(256)S(1)}, f32[180]{0:T(256)}, u32[]{:S(2)}) copy-start(f32[180]{0:T(256)} %param.16) | copy-start | bytes 2164
  12.3 8.2 %collective-permute-start.2 = (bf16[720,128]{1,0:T(8,128)(2,1)S(1)}, bf16[720,128]{1,0:T(8,128)(2,1)S(1)}, u32[]{:S(2)}, u32[]{:S(2)}) collective-permute-start(bf16[720,128]{1,0:T(8,128)(2,1)S(1)} %get-tuple-element.28), channel_id=1, source_target_pairs={{1,2},{3,4},{5,6},{2,1},{4,3},{6,5},{9,10},{11,12},{13,14},{10,9},... | collective-permute-start | bytes 552968 | tf_op jit(solution)/shard_map/ppermute | solution.py:872
  13.0 7.5 %collective-permute-start.3 = (bf16[720,128]{1,0:T(8,128)(2,1)S(1)}, bf16[720,128]{1,0:T(8,128)(2,1)S(1)}, u32[]{:S(2)}, u32[]{:S(2)}) collective-permute-start(bf16[720,128]{1,0:T(8,128)(2,1)S(1)} %get-tuple-element.29), channel_id=1, source_target_pairs={{0,1},{2,3},{4,5},{6,7},{1,0},{3,2},{5,4},{7,6},{8,9},{10,11},{12,... | collective-permute-start | bytes 552968 | tf_op jit(solution)/shard_map/ppermute | solution.py:872
  20.5 8.8 %copy-start.1 = (bf16[3,3,180,180]{3,2,1,0:T(8,128)(2,1)S(1)}, bf16[3,3,180,180]{3,2,1,0:T(8,128)(2,1)}, u32[]{:S(2)}) copy-start(bf16[3,3,180,180]{3,2,1,0:T(8,128)(2,1)} %group_ref.1) | copy-start | bytes 1749604
  20.5 8.8 %copy-start.2 = (bf16[3,3,180,64]{2,3,1,0:T(8,128)(2,1)S(1)}, bf16[3,3,180,64]{2,3,1,0:T(8,128)(2,1)}, u32[]{:S(2)}) copy-start(bf16[3,3,180,64]{2,3,1,0:T(8,128)(2,1)} %param.20) | copy-start | bytes 622084
  20.5 8.8 %copy-start.3 = (bf16[3,3,64,256]{3,2,1,0:T(8,128)(2,1)S(1)}, bf16[3,3,64,256]{3,2,1,0:T(8,128)(2,1)}, u32[]{:S(2)}) copy-start(bf16[3,3,64,256]{3,2,1,0:T(8,128)(2,1)} %upsample_ref.1) | copy-start | bytes 884740
  26.3 7.4 %collective-permute-start.4 = (bf16[368,128]{1,0:T(8,128)(2,1)S(1)}, bf16[368,128]{1,0:T(8,128)(2,1)S(1)}, u32[]{:S(2)}, u32[]{:S(2)}) collective-permute-start(bf16[368,128]{1,0:T(8,128)(2,1)S(1)} %get-tuple-element.44), channel_id=1, source_target_pairs={{8,16},{16,8},{9,17},{17,9},{10,18},{18,10},{11,19},{19,11},{12,20... | collective-permute-start | bytes 282632 | tf_op jit(solution)/shard_map/ppermute | solution.py:872
  27.1 6.6 %collective-permute-start.5 = (bf16[368,128]{1,0:T(8,128)(2,1)S(1)}, bf16[368,128]{1,0:T(8,128)(2,1)S(1)}, u32[]{:S(2)}, u32[]{:S(2)}) collective-permute-start(bf16[368,128]{1,0:T(8,128)(2,1)S(1)} %get-tuple-element.45), channel_id=1, source_target_pairs={{0,8},{16,24},{8,0},{24,16},{1,9},{17,25},{9,1},{25,17},{2,10},{18... | collective-permute-start | bytes 282632 | tf_op jit(solution)/shard_map/ppermute | solution.py:872

commit v10 on v9

--- a/solution.py
+++ b/solution.py
@@ -737,7 +737,6 @@
         image[rows, 0:span, 128:chans] = rest[:, :, 0 : chans - 128]
     fill_taps(halo_taps, image, span)
     grouped[:, :, 128:256] = jnp.zeros((height + 4, span, 128), BF16)
-    part = 2
     col = lax.broadcasted_iota(jnp.int32, (span, chans), 0) - 2
     keep_grouped = (col < cols + 2) & ((col >= 0) | jnp.logical_not(at_left))
     keep_grouped = keep_grouped & ((col < cols) | jnp.logical_not(at_right))
@@ -758,18 +757,15 @@
             return taps_ref[row - 3]
         return halo_taps[row if row < 3 else row - height]
 
-    def group(h):
-        totals = []
-        for h2 in range(h, h + part, 2):
-            lhs = jnp.concatenate(
-                [
-                    jnp.concatenate([tap_row(h2 + a), tap_row(h2 + a + 1)], axis=0)
-                    for a in range(3)
-                ],
-                axis=1,
-            )
-            totals.append(dot(lhs, wg_scr[...]).reshape(2, span, chans))
-        total = jnp.concatenate(totals, axis=0)
+    def group(h, part):
+        lhs = jnp.concatenate(
+            [
+                jnp.concatenate([tap_row(h + a + r) for r in range(part)], axis=0)
+                for a in range(3)
+            ],
+            axis=1,
+        )
+        total = dot(lhs, wg_scr[...]).reshape(part, span, chans)
         total = total + base[h : h + part, STRIP - 2 : STRIP - 2 + span, :]
         for r in range(part):
             mask = keep_grouped
@@ -783,7 +779,7 @@
         lhs = jnp.concatenate(
             [grouped[h + a : h + a + count].reshape(count * span, 256) for a in range(3)], axis=1
         )
-        slot = h // part % 2
+        slot = h // count % 2
         sums[slot, 0:count, :, 0 : 3 * feats] = dot(lhs, wb_scr[...]).reshape(count, span, 3 * feats)
         for r in range(count):
             total = sums[slot, r, 0:low_span, 0:128]
@@ -802,7 +798,7 @@
                 left_half, lowfeat[h + r, 2 : cols + 2], 0.0
             ).astype(BF16)
 
-    def expand(h):
+    def expand(h, part):
         lhs = jnp.concatenate(
             [low_taps[h + a : h + a + part].reshape(part * cols, 256) for a in range(3)], axis=1
         )
@@ -823,21 +819,14 @@
                         a * feats : (a + 1) * feats, 128 * r : 128 * (r + 1)
                     ]
 
-    narrowed = expanded = done = 0
-    while expanded < height:
-        expand_to, narrow_to = min(narrowed - 2, height), min(done - 2, height + 2)
-        if done < height + 4:
-            group(done)
-            done += part
-        while narrowed < narrow_to:
-            count = min(part, height + 2 - narrowed)
-            if narrowed + count > narrow_to:
-                break
-            narrow(narrowed, count)
-            narrowed += count
-        while expanded + part <= expand_to:
-            expand(expanded)
-            expanded += part
+    half, third = (height + 4) // 2, (height + 2) // 3
+    group(0, half)
+    group(half, half)
+    narrow(0, third)
+    narrow(third, third)
+    narrow(2 * third, third)
+    expand(0, height // 2)
+    expand(height // 2, height // 2)
     out_ref[...] = out_scr[...].reshape(feats, 2 * height, 128).astype(BF16)
 
 
@@ -853,7 +842,7 @@
             pltpu.VMEM((6, span + STRIP, chans), F32),
             pltpu.VMEM((6, span, 768), BF16),
             pltpu.VMEM((height + 4, span, 256), BF16),
-            pltpu.VMEM((2, 4, span, 256), F32),
+            pltpu.VMEM((2, 6, span, 256), F32),
             pltpu.VMEM((height + 2, cols + 8, 128), F32),
             pltpu.VMEM((height + 2, cols, 256), BF16),
             pltpu.VMEM((feats * 2 * height, 128), F32),

time: 40.3 us -> 39.4 us (0.978)
  Pallas kernels: 24.8 us -> 23.9 us
    pallas_call x1, Pallas kernels: 6.38 us -> 5.5 us  [convs(): call(conv_kernel, jax.ShapeDtypeStruct((feats, 2 * height, 2 * cols), BF1...]
  transfers between devices with their start and end apart: 6 -> 6, of which waited for: 0 -> 0; matrix products, arithmetic and copies ran while one was open for 0% -> 0% of each run, Pallas kernels for 31% -> 32%
where the time goes in v10:
time: 39.4 us; the launch traced here: 39.2 us
  Pallas kernels  23.9 us (61%)
  starting transfers between devices  13.2 us (34%)
  other arithmetic  0.99 us (3%)
  local copies, waits for them, and re-layouts  0.85 us (2%)
    ppermute x6, starting transfers between devices, swapped(): out.append(lax.ppermute(payload, axis, pairs))  13.2 us
    pallas_call x1, Pallas kernels, outer_block(): call(outer_kernel, (jax.ShapeDtypeStruct((3 * span + 128, 128), BF16), ja...  5.72 us
    pallas_call x1, Pallas kernels, convs(): call(conv_kernel, jax.ShapeDtypeStruct((feats, 2 * height, 2 * cols), BF1...  5.5 us
    pallas_call x1, Pallas kernels, inner_block(): call(inner_kernel, (jax.ShapeDtypeStruct((height + 2 * RIM, cols, chans),...  4.53 us
    pallas_call x1, Pallas kernels, middle_block(): call(middle_kernel, (jax.ShapeDtypeStruct((height, span, 768), BF16), jax...  4.32 us
    pallas_call x1, Pallas kernels, build_bias(): call(bias_kernel, jax.ShapeDtypeStruct((3, HEADS, KEYS, 128), BF16), [plt...  3.63 us
    select_n x1, other arithmetic, on_device(): jnp.where(even_row, low, high)  0.99 us
    unnamed x22, local copies, waits for them, and re-layouts  0.85 us
  transfers between devices with their start and end apart: 6, of which 0 were waited for; matrix products, arithmetic and copies ran while one was open for 0% of the time, Pallas kernels for 32%

profile of v10, /device:TPU:0, one launch (start us, length us, event | category | flops | bytes accessed | tf_op | source)
XLA Modules:
  0.0 39.2 jit_solution(1864330829194485089)
XLA Ops:
  0.0 1.0 %broadcast_select_fusion = (bf16[4,64,180]{2,1,0:T(8,128)(2,1)S(1)}, bf16[4,64,180]{2,1,0:T(8,128)(2,1)S(1)}) fusion(pred[]{:T(512)S(6)} %eq.5, bf16[16,64,180]{2,1,0:T(8,128)(2,1)} %own_ref.7), kind=kLoop, calls=%fused_computation | loop fusion | flops 92160 | bytes 368641 | tf_op jit(solution)/shard_map/jit(_where)/select_n | solution.py:882
  1.0 0.7 %collective-permute-start.1 = (bf16[4,64,180]{2,1,0:T(8,128)(2,1)S(1)}, bf16[4,64,180]{2,1,0:T(8,128)(2,1)S(1)}, u32[]{:S(2)}, u32[]{:S(2)}) collective-permute-start(bf16[4,64,180]{2,1,0:T(8,128)(2,1)S(1)} %get-tuple-element.49), channel_id=1, source_target_pairs={{8,16},{16,8},{9,17},{17,9},{10,18},{18,10},{11,19},{19,11},{12,20... | collective-permute-start | bytes 276488 | tf_op jit(solution)/shard_map/ppermute | solution.py:861
  1.7 5.9 %collective-permute-start = (bf16[4,64,180]{2,1,0:T(8,128)(2,1)S(1)}, bf16[4,64,180]{2,1,0:T(8,128)(2,1)S(1)}, u32[]{:S(2)}, u32[]{:S(2)}) collective-permute-start(bf16[4,64,180]{2,1,0:T(8,128)(2,1)S(1)} %get-tuple-element.50), channel_id=1, source_target_pairs={{0,8},{16,24},{8,0},{24,16},{1,9},{17,25},{9,1},{25,17},{2,10},{18... | collective-permute-start | bytes 276488 | tf_op jit(solution)/shard_map/ppermute | solution.py:861
  7.6 0.0 copy-start.8
  7.6 0.8 %copy-done.8 = f32[1521,6]{0,1:T(8,128)S(1)} copy-done((f32[1521,6]{0,1:T(8,128)S(1)}, f32[1521,6]{0,1:T(8,128)}, u32[]{:S(2)}) %copy-start.8) | copy-done | bytes 36528
  8.4 0.0 copy-start
  8.4 0.0 copy-start.4
  8.4 0.0 copy-start.5
  8.4 0.0 copy-start.6
  8.4 0.0 copy-start.7
  8.4 0.0 copy-start.9
  8.4 0.0 copy-start.10
  8.4 3.6 %shard_map.109.bias_ref = bf16[3,6,576,128]{3,2,1,0:T(8,128)(2,1)S(1)} custom-call(f32[6,1521]{1,0:T(8,128)S(1)} %bitcast.9), custom_call_target="tpu_custom_call" | custom-call | flops 4000000000 | bytes 4000000 | tf_op jit(solution)/shard_map/pallas_call | solution.py:108
  12.1 0.0 collective-permute-done.1.row_two_ref
  12.1 0.0 collective-permute-done.row_one_ref
  12.1 0.0 copy-done
  12.1 0.2 shard_map.111
  12.3 0.7 %collective-permute-start.2 = (bf16[720,128]{1,0:T(8,128)(2,1)S(1)}, bf16[720,128]{1,0:T(8,128)(2,1)S(1)}, u32[]{:S(2)}, u32[]{:S(2)}) collective-permute-start(bf16[720,128]{1,0:T(8,128)(2,1)S(1)} %get-tuple-element.28), channel_id=1, source_target_pairs={{1,2},{3,4},{5,6},{2,1},{4,3},{6,5},{9,10},{11,12},{13,14},{10,9},... | collective-permute-start | bytes 552968 | tf_op jit(solution)/shard_map/ppermute | solution.py:861
  13.0 2.9 %collective-permute-start.3 = (bf16[720,128]{1,0:T(8,128)(2,1)S(1)}, bf16[720,128]{1,0:T(8,128)(2,1)S(1)}, u32[]{:S(2)}, u32[]{:S(2)}) collective-permute-start(bf16[720,128]{1,0:T(8,128)(2,1)S(1)} %get-tuple-element.29), channel_id=1, source_target_pairs={{0,1},{2,3},{4,5},{6,7},{1,0},{3,2},{5,4},{7,6},{8,9},{10,11},{12,... | collective-permute-start | bytes 552968 | tf_op jit(solution)/shard_map/ppermute | solution.py:861
  15.9 0.0 copy-done.4
  15.9 0.0 copy-done.5
  15.9 0.0 copy-done.6
  15.9 0.0 copy-done.7
  15.9 0.0 copy-done.9
  15.9 0.0 copy-done.10
  15.9 4.5 %shard_map.110 = (f32[24,64,180]{2,1,0:T(8,128)S(1)}, bf16[180,384]{1,0:T(8,128)(2,1)S(1)}, bf16[384,180]{1,0:T(8,128)(2,1)S(1)}, bf16[192,180]{1,0:T(8,128)(2,1...) custom-call(bf16[16,64,180]{2,1,0:T(8,128)(2,1)S(1)} %copy-done, ...), custom_call_target="tpu_custom_call" | custom-call | flops 5000000000 | bytes 4000000 | tf_op jit(solution)/shard_map/pallas_call | solution.py:644
  20.5 0.0 collective-permute-done.2.col_two_ref
  20.5 0.0 collective-permute-done.3.col_one_ref
  20.5 0.0 copy-start.1
  20.5 0.0 copy-start.2
  20.5 0.0 copy-start.3
  20.5 5.7 %shard_map.112 = (bf16[368,128]{1,0:T(8,128)(2,1)S(1)}, bf16[368,128]{1,0:T(8,128)(2,1)S(1)}, f32[8,80,180]{2,1,0:T(8,128)S(1)}, f32[8,16,180]{2,1,0:T(8,128)S(1...) custom-call(bf16[16,64,180]{2,1,0:T(8,128)(2,1)S(1)} %copy-done, ...), custom_call_target="tpu_custom_call" | custom-call | flops 5000000000 | bytes 4000000 | tf_op jit(solution)/shard_map/pallas_call | solution.py:665
  26.3 0.8 %collective-permute-start.4 = (bf16[368,128]{1,0:T(8,128)(2,1)S(1)}, bf16[368,128]{1,0:T(8,128)(2,1)S(1)}, u32[]{:S(2)}, u32[]{:S(2)}) collective-permute-start(bf16[368,128]{1,0:T(8,128)(2,1)S(1)} %get-tuple-element.44), channel_id=1, source_target_pairs={{8,16},{16,8},{9,17},{17,9},{10,18},{18,10},{11,19},{19,11},{12,20... | collective-permute-start | bytes 282632 | tf_op jit(solution)/shard_map/ppermute | solution.py:861
  27.1 2.2 %collective-permute-start.5 = (bf16[368,128]{1,0:T(8,128)(2,1)S(1)}, bf16[368,128]{1,0:T(8,128)(2,1)S(1)}, u32[]{:S(2)}, u32[]{:S(2)}) collective-permute-start(bf16[368,128]{1,0:T(8,128)(2,1)S(1)} %get-tuple-element.45), channel_id=1, source_target_pairs={{0,8},{16,24},{8,0},{24,16},{1,9},{17,25},{9,1},{25,17},{2,10},{18... | collective-permute-start | bytes 282632 | tf_op jit(solution)/shard_map/ppermute | solution.py:861
  29.3 0.0 copy-done.1
  29.3 0.0 copy-done.2
  29.3 0.0 copy-done.3
  29.3 4.3 %shard_map.113 = (bf16[16,80,768]{2,1,0:T(8,128)(2,1)S(1)}, f32[20,88,180]{2,1,0:T(8,128)S(1)}, bf16[2304,180]{1,0:T(8,128)(2,1)S(1)}, bf16[768,192]{1,0:T(8,128)(2,1)S(1)}, bf16[768,256]{1,0:T(8,128)(2,1)S(1)}) custom-call(bf16[16,64,180]{2,1,0:T(8,128)(2,1)S(1)} %copy-done, f32[24,64,180]{2,1,0:T(8,128)S(1)} %get-tuple-element.27.nrm_ref, ...), custom_call_target="tpu_custom_call" | custom-call | flops 5000000000 | bytes 4000000 | tf_op jit(solution)/shard_map/pallas_call | solution.py:695
  33.7 0.0 collective-permute-done.4.back_two_ref
  33.7 0.0 collective-permute-done.5.back_one_ref
  33.7 5.5 %shard_map.114 = bf16[64,32,128]{2,1,0:T(8,128)(2,1)} custom-call(bf16[16,80,768]{2,1,0:T(8,128)(2,1)S(1)} %get-tuple-element.42.taps_ref, f32[20,88,180]{2,1,0:T(8,128)S(1)} %get-tuple-element.43.base, bf16[368,128]{1,0:T(8,128)(2,1)S(1)} %collective-permute-done.4.back_two_ref, bf16[368,128]{1,0:T(8,128)(2,1)S(1)} %collective-permute-done.5.back_one_ref, ...), custom_call_target="tpu_custom_call" | custom-call | flops 8000000000 | bytes 4000000 | tf_op jit(solution)/shard_map/pallas_call | solution.py:838
Async XLA Ops:
  1.0 11.1 %collective-permute-start.1 = (bf16[4,64,180]{2,1,0:T(8,128)(2,1)S(1)}, bf16[4,64,180]{2,1,0:T(8,128)(2,1)S(1)}, u32[]{:S(2)}, u32[]{:S(2)}) collective-permute-start(bf16[4,64,180]{2,1,0:T(8,128)(2,1)S(1)} %get-tuple-element.49), channel_id=1, source_target_pairs={{8,16},{16,8},{9,17},{17,9},{10,18},{18,10},{11,19},{19,11},{12,20... | collective-permute-start | bytes 276488 | tf_op jit(solution)/shard_map/ppermute | solution.py:861
  1.7 10.4 %collective-permute-start = (bf16[4,64,180]{2,1,0:T(8,128)(2,1)S(1)}, bf16[4,64,180]{2,1,0:T(8,128)(2,1)S(1)}, u32[]{:S(2)}, u32[]{:S(2)}) collective-permute-start(bf16[4,64,180]{2,1,0:T(8,128)(2,1)S(1)} %get-tuple-element.50), channel_id=1, source_target_pairs={{0,8},{16,24},{8,0},{24,16},{1,9},{17,25},{9,1},{25,17},{2,10},{18... | collective-permute-start | bytes 276488 | tf_op jit(solution)/shard_map/ppermute | solution.py:861
  7.6 0.8 %copy-start.8 = (f32[1521,6]{0,1:T(8,128)S(1)}, f32[1521,6]{0,1:T(8,128)}, u32[]{:S(2)}) copy-start(f32[1521,6]{0,1:T(8,128)} %param.14) | copy-start | bytes 109516
  8.4 3.7 %copy-start = (bf16[16,64,180]{2,1,0:T(8,128)(2,1)S(1)}, bf16[16,64,180]{2,1,0:T(8,128)(2,1)}, u32[]{:S(2)}) copy-start(bf16[16,64,180]{2,1,0:T(8,128)(2,1)} %own_ref.7) | copy-start | bytes 1105924
  8.4 7.5 %copy-start.4 = (bf16[180,540]{1,0:T(8,128)(2,1)S(1)}, bf16[180,540]{1,0:T(8,128)(2,1)}, u32[]{:S(2)}) copy-start(bf16[180,540]{1,0:T(8,128)(2,1)} %qkv_ref.1) | copy-start | bytes 583204
  8.4 7.5 %copy-start.5 = (bf16[180,360]{1,0:T(8,128)(2,1)S(1)}, bf16[180,360]{1,0:T(8,128)(2,1)}, u32[]{:S(2)}) copy-start(bf16[180,360]{1,0:T(8,128)(2,1)} %hidden_ref.5) | copy-start | bytes 388804
  8.4 7.5 %copy-start.6 = (bf16[360,180]{0,1:T(8,128)(2,1)S(1)}, bf16[360,180]{0,1:T(8,128)(2,1)}, u32[]{:S(2)}) copy-start(bf16[360,180]{0,1:T(8,128)(2,1)} %param.18) | copy-start | bytes 388804
  8.4 7.5 %copy-start.7 = (bf16[180,180]{1,0:T(8,128)(2,1)S(1)}, bf16[180,180]{1,0:T(8,128)(2,1)}, u32[]{:S(2)}) copy-start(bf16[180,180]{1,0:T(8,128)(2,1)} %proj_ref.1) | copy-start | bytes 194404
  8.4 7.5 %copy-start.9 = (f32[180]{0:T(256)S(1)}, f32[180]{0:T(256)}, u32[]{:S(2)}) copy-start(f32[180]{0:T(256)} %param.12) | copy-start | bytes 2164
  8.4 7.5 %copy-start.10 = (f32[180]{0:T(256)S(1)}, f32[180]{0:T(256)}, u32[]{:S(2)}) copy-start(f32[180]{0:T(256)} %param.16) | copy-start | bytes 2164
  12.3 8.2 %collective-permute-start.2 = (bf16[720,128]{1,0:T(8,128)(2,1)S(1)}, bf16[720,128]{1,0:T(8,128)(2,1)S(1)}, u32[]{:S(2)}, u32[]{:S(2)}) collective-permute-start(bf16[720,128]{1,0:T(8,128)(2,1)S(1)} %get-tuple-element.28), channel_id=1, source_target_pairs={{1,2},{3,4},{5,6},{2,1},{4,3},{6,5},{9,10},{11,12},{13,14},{10,9},... | collective-permute-start | bytes 552968 | tf_op jit(solution)/shard_map/ppermute | solution.py:861
  13.0 7.5 %collective-permute-start.3 = (bf16[720,128]{1,0:T(8,128)(2,1)S(1)}, bf16[720,128]{1,0:T(8,128)(2,1)S(1)}, u32[]{:S(2)}, u32[]{:S(2)}) collective-permute-start(bf16[720,128]{1,0:T(8,128)(2,1)S(1)} %get-tuple-element.29), channel_id=1, source_target_pairs={{0,1},{2,3},{4,5},{6,7},{1,0},{3,2},{5,4},{7,6},{8,9},{10,11},{12,... | collective-permute-start | bytes 552968 | tf_op jit(solution)/shard_map/ppermute | solution.py:861
  20.5 8.8 %copy-start.1 = (bf16[3,3,180,180]{3,2,1,0:T(8,128)(2,1)S(1)}, bf16[3,3,180,180]{3,2,1,0:T(8,128)(2,1)}, u32[]{:S(2)}) copy-start(bf16[3,3,180,180]{3,2,1,0:T(8,128)(2,1)} %group_ref.1) | copy-start | bytes 1749604
  20.5 8.8 %copy-start.2 = (bf16[3,3,180,64]{2,3,1,0:T(8,128)(2,1)S(1)}, bf16[3,3,180,64]{2,3,1,0:T(8,128)(2,1)}, u32[]{:S(2)}) copy-start(bf16[3,3,180,64]{2,3,1,0:T(8,128)(2,1)} %param.20) | copy-start | bytes 622084
  20.5 8.8 %copy-start.3 = (bf16[3,3,64,256]{3,2,1,0:T(8,128)(2,1)S(1)}, bf16[3,3,64,256]{3,2,1,0:T(8,128)(2,1)}, u32[]{:S(2)}) copy-start(bf16[3,3,64,256]{3,2,1,0:T(8,128)(2,1)} %upsample_ref.1) | copy-start | bytes 884740
  26.3 7.4 %collective-permute-start.4 = (bf16[368,128]{1,0:T(8,128)(2,1)S(1)}, bf16[368,128]{1,0:T(8,128)(2,1)S(1)}, u32[]{:S(2)}, u32[]{:S(2)}) collective-permute-start(bf16[368,128]{1,0:T(8,128)(2,1)S(1)} %get-tuple-element.44), channel_id=1, source_target_pairs={{8,16},{16,8},{9,17},{17,9},{10,18},{18,10},{11,19},{19,11},{12,20... | collective-permute-start | bytes 282632 | tf_op jit(solution)/shard_map/ppermute | solution.py:861
  27.1 6.6 %collective-permute-start.5 = (bf16[368,128]{1,0:T(8,128)(2,1)S(1)}, bf16[368,128]{1,0:T(8,128)(2,1)S(1)}, u32[]{:S(2)}, u32[]{:S(2)}) collective-permute-start(bf16[368,128]{1,0:T(8,128)(2,1)S(1)} %get-tuple-element.45), channel_id=1, source_target_pairs={{0,8},{16,24},{8,0},{24,16},{1,9},{17,25},{9,1},{25,17},{2,10},{18... | collective-permute-start | bytes 282632 | tf_op jit(solution)/shard_map/ppermute | solution.py:861

commit v11 on v10

--- a/solution.py
+++ b/solution.py
@@ -52,7 +52,9 @@
     )
 
 
-def bias_kernel(table_ref, out_ref, t_scr, e_scr, w_scr, x_scr):
+def bias_kernel(
+    table_ref, qkv_ref, proj_ref, out_ref, wk_ref, wqv_ref, wp_ref, t_scr, e_scr, w_scr, x_scr
+):
     for d in range(SIDE):
         t_scr[8 * d : 8 * d + HEADS, 0:SIDE] = jnp.exp(table_ref[:, SIDE * d : SIDE * (d + 1)])
 
@@ -102,12 +104,20 @@
         return carry
 
     lax.fori_loop(0, HEADS, head, 0)
-
-
-def build_bias(bias_table):
+    weights_into(qkv_ref, proj_ref, wk_ref, wqv_ref, wp_ref)
+
+
+def build_bias(bias_table, qkv_weight, proj_weight):
+    chans = qkv_weight.shape[0]
+    width = HEADS * HP
     return call(
         bias_kernel,
-        jax.ShapeDtypeStruct((3, HEADS, KEYS, 128), BF16),
+        (
+            jax.ShapeDtypeStruct((3, HEADS, KEYS, 128), BF16),
+            jax.ShapeDtypeStruct((chans, 3 * 128), BF16),
+            jax.ShapeDtypeStruct((2 * width, chans), BF16),
+            jax.ShapeDtypeStruct((width, chans), BF16),
+        ),
         [
             pltpu.VMEM((8 * SIDE, 128), F32),
             pltpu.VMEM((SIDE + 1, 640), F32),
@@ -116,7 +126,7 @@
         ],
         4_000_000_000,
         4_000_000,
-    )(bias_table.T)
+    )(bias_table.T, qkv_weight, proj_weight)
 
 
 def one_hot(shape, row_of, col_of):
@@ -357,16 +367,14 @@
     row_one_ref,
     row_two_ref,
     gain_one_ref,
-    qkv_ref,
-    proj_ref,
+    wk_ref,
+    wqv_ref,
+    wp_ref,
     bias_ref,
     gain_two_ref,
     hidden_ref,
     output_ref,
     nrm_ref,
-    wk_ref,
-    wqv_ref,
-    wp_ref,
     k_ref,
     v_ref,
     border_ref,
@@ -380,7 +388,6 @@
     height, cols, chans = own_ref.shape
     inner = cols // WIN - 2
     flags = at_edges()
-    weights_into(qkv_ref, proj_ref, wk_ref, wqv_ref, wp_ref)
     gain_one = gain_one_ref[...]
     for r in range(RIM):
         above, below = from_sides(flags[4], row_one_ref[r], row_two_ref[r])
@@ -645,9 +652,6 @@
         inner_kernel,
         (
             jax.ShapeDtypeStruct((height + 2 * RIM, cols, chans), F32),
-            jax.ShapeDtypeStruct((chans, 3 * 128), BF16),
-            jax.ShapeDtypeStruct((2 * width, chans), BF16),
-            jax.ShapeDtypeStruct((width, chans), BF16),
             jax.ShapeDtypeStruct((inner, KEYS, 3 * 128), BF16),
             jax.ShapeDtypeStruct((inner, width, KEYS), BF16),
             jax.ShapeDtypeStruct((8, WIN * inner, chans), F32),
@@ -824,8 +828,8 @@
     group(half, half)
     narrow(0, third)
     narrow(third, third)
+    expand(0, height // 2)
     narrow(2 * third, third)
-    expand(0, height // 2)
     expand(height // 2, height // 2)
     out_ref[...] = out_scr[...].reshape(feats, 2 * height, 128).astype(BF16)
 
@@ -883,16 +887,17 @@
     )
     col_one, col_two = swapped("cols", *pack(features, row_one, row_two))
 
-    bias = build_bias(bias_table)
+    bias, wk, wqv, wp = build_bias(bias_table, qkv_weight, proj_weight)
     gain_one, gain_two = gain_one.reshape(1, chans), gain_two.reshape(1, chans)
     post = (gain_two, hidden_weight, output_weight.T)
-    nrm, wk, wqv, wp, inner_k, inner_v, inner_border, inner_mid = inner_block(
+    nrm, inner_k, inner_v, inner_border, inner_mid = inner_block(
         features,
         row_one,
         row_two,
         gain_one,
-        qkv_weight,
-        proj_weight,
+        wk,
+        wqv,
+        wp,
         bias,
         *post,
     )

time: 39.4 us -> 41.8 us (1.061)
  local copies, waits for them, and re-layouts: 0.85 us -> 2.67 us
  Pallas kernels: 23.9 us -> 24.9 us
    unnamed x22, local copies, waits for them, and re-layouts: 0.85 us -> 2.67 us
    pallas_call x1, Pallas kernels: 3.63 us -> 4.15 us  [build_bias(): call(bias_kernel, (jax.ShapeDtypeStruct((3, HEADS, KEYS, 128), BF16), jax...]
    pallas_call x1, Pallas kernels: 5.5 us -> 6 us  [convs(): call(conv_kernel, jax.ShapeDtypeStruct((feats, 2 * height, 2 * cols), BF1...]
    ppermute x6, starting transfers between devices: 13.2 us -> 12.8 us  [swapped(): out.append(lax.ppermute(payload, axis, pairs))]
  transfers between devices with their start and end apart: 6 -> 6, of which waited for: 0 -> 0; matrix products, arithmetic and copies ran while one was open for 0% -> 0% of each run, Pallas kernels for 32% -> 31%
where the time goes in v11:
time: 41.8 us; the launch traced here: 41.6 us
  Pallas kernels  24.9 us (60%)
  starting transfers between devices  12.8 us (31%)
  local copies, waits for them, and re-layouts  2.67 us (6%)
  other arithmetic  0.99 us (2%)
    ppermute x6, starting transfers between devices, swapped(): out.append(lax.ppermute(payload, axis, pairs))  12.8 us
    pallas_call x1, Pallas kernels, convs(): call(conv_kernel, jax.ShapeDtypeStruct((feats, 2 * height, 2 * cols), BF1...  6 us
    pallas_call x1, Pallas kernels, outer_block(): call(outer_kernel, (jax.ShapeDtypeStruct((3 * span + 128, 128), BF16), ja...  5.71 us
    pallas_call x1, Pallas kernels, inner_block(): call(inner_kernel, (jax.ShapeDtypeStruct((height + 2 * RIM, cols, chans),...  4.52 us
    pallas_call x1, Pallas kernels, middle_block(): call(middle_kernel, (jax.ShapeDtypeStruct((height, span, 768), BF16), jax...  4.33 us
    pallas_call x1, Pallas kernels, build_bias(): call(bias_kernel, (jax.ShapeDtypeStruct((3, HEADS, KEYS, 128), BF16), jax...  4.15 us
    unnamed x22, local copies, waits for them, and re-layouts  2.67 us
    select_n x1, other arithmetic, on_device(): jnp.where(even_row, low, high)  0.99 us
  transfers between devices with their start and end apart: 6, of which 0 were waited for; matrix products, arithmetic and copies ran while one was open for 0% of the time, Pallas kernels for 31%

profile of v11, /device:TPU:0, one launch (start us, length us, event | category | flops | bytes accessed | tf_op | source)
XLA Modules:
  0.0 41.6 jit_solution(4397272646534170654)
XLA Ops:
  0.0 1.0 %broadcast_select_fusion = (bf16[4,64,180]{2,1,0:T(8,128)(2,1)S(1)}, bf16[4,64,180]{2,1,0:T(8,128)(2,1)S(1)}) fusion(pred[]{:T(512)S(6)} %eq.5, bf16[16,64,180]{2,1,0:T(8,128)(2,1)} %own_ref.7), kind=kLoop, calls=%fused_computation | loop fusion | flops 92160 | bytes 368641 | tf_op jit(solution)/shard_map/jit(_where)/select_n | solution.py:886
  1.0 0.7 %collective-permute-start.1 = (bf16[4,64,180]{2,1,0:T(8,128)(2,1)S(1)}, bf16[4,64,180]{2,1,0:T(8,128)(2,1)S(1)}, u32[]{:S(2)}, u32[]{:S(2)}) collective-permute-start(bf16[4,64,180]{2,1,0:T(8,128)(2,1)S(1)} %get-tuple-element.51), channel_id=1, source_target_pairs={{8,16},{16,8},{9,17},{17,9},{10,18},{18,10},{11,19},{19,11},{12,20... | collective-permute-start | bytes 276488 | tf_op jit(solution)/shard_map/ppermute | solution.py:865
  1.7 5.9 %collective-permute-start = (bf16[4,64,180]{2,1,0:T(8,128)(2,1)S(1)}, bf16[4,64,180]{2,1,0:T(8,128)(2,1)S(1)}, u32[]{:S(2)}, u32[]{:S(2)}) collective-permute-start(bf16[4,64,180]{2,1,0:T(8,128)(2,1)S(1)} %get-tuple-element.52), channel_id=1, source_target_pairs={{0,8},{16,24},{8,0},{24,16},{1,9},{17,25},{9,1},{25,17},{2,10},{18... | collective-permute-start | bytes 276488 | tf_op jit(solution)/shard_map/ppermute | solution.py:865
  7.6 0.0 copy-start.4
  7.6 0.9 %copy-done.4 = bf16[180,540]{1,0:T(8,128)(2,1)S(1)} copy-done((bf16[180,540]{1,0:T(8,128)(2,1)S(1)}, bf16[180,540]{1,0:T(8,128)(2,1)}, u32[]{:S(2)}) %copy-start.4) | copy-done | bytes 194424
  8.5 0.0 copy-start.7
  8.5 0.9 %copy-done.7 = bf16[180,180]{1,0:T(8,128)(2,1)S(1)} copy-done((bf16[180,180]{1,0:T(8,128)(2,1)S(1)}, bf16[180,180]{1,0:T(8,128)(2,1)}, u32[]{:S(2)}) %copy-start.7) | copy-done | bytes 64824
  9.4 0.0 copy-start.8
  9.4 0.8 %copy-done.8 = f32[1521,6]{0,1:T(8,128)S(1)} copy-done((f32[1521,6]{0,1:T(8,128)S(1)}, f32[1521,6]{0,1:T(8,128)}, u32[]{:S(2)}) %copy-start.8) | copy-done | bytes 36528
  10.2 0.0 copy-start
  10.2 0.0 copy-start.5
  10.2 0.0 copy-start.6
  10.2 0.0 copy-start.9
  10.2 0.0 copy-start.10
  10.2 4.2 %shard_map.109 = (bf16[3,6,576,128]{3,2,1,0:T(8,128)(2,1)S(1)}, bf16[180,384]{1,0:T(8,128)(2,1)S(1)}, bf16[384,180]{1,0:T(8,128)(2,1)S(1)}, bf16[192,180]{1,0:T(8,128)(2,1)S(1)}) custom-call(f32[6,1521]{1,0:T(8,128)S(1)} %bitcast.9, bf16[180,540]{1,0:T(8,128)(2,1)S(1)} %copy-done.4, bf16[180,180]{1,0:T(8,128)(2,1)S(1)} %copy-done.7), custom_call_target="tpu_custom_call" | custom-call | flops 4000000000 | bytes 4000000 | tf_op jit(solution)/shard_map/pallas_call | solution.py:113
  14.4 0.0 collective-permute-done.1.row_two_ref
  14.4 0.0 collective-permute-done.row_one_ref
  14.4 0.0 copy-done
  14.4 0.2 shard_map.111
  14.7 0.7 %collective-permute-start.2 = (bf16[720,128]{1,0:T(8,128)(2,1)S(1)}, bf16[720,128]{1,0:T(8,128)(2,1)S(1)}, u32[]{:S(2)}, u32[]{:S(2)}) collective-permute-start(bf16[720,128]{1,0:T(8,128)(2,1)S(1)} %get-tuple-element.33), channel_id=1, source_target_pairs={{1,2},{3,4},{5,6},{2,1},{4,3},{6,5},{9,10},{11,12},{13,14},{10,9},... | collective-permute-start | bytes 552968 | tf_op jit(solution)/shard_map/ppermute | solution.py:865
  15.3 2.9 %collective-permute-start.3 = (bf16[720,128]{1,0:T(8,128)(2,1)S(1)}, bf16[720,128]{1,0:T(8,128)(2,1)S(1)}, u32[]{:S(2)}, u32[]{:S(2)}) collective-permute-start(bf16[720,128]{1,0:T(8,128)(2,1)S(1)} %get-tuple-element.34), channel_id=1, source_target_pairs={{0,1},{2,3},{4,5},{6,7},{1,0},{3,2},{5,4},{7,6},{8,9},{10,11},{12,... | collective-permute-start | bytes 552968 | tf_op jit(solution)/shard_map/ppermute | solution.py:865
  18.2 0.0 copy-done.5
  18.2 0.0 copy-done.6
  18.2 0.0 copy-done.9
  18.2 0.0 copy-done.10
  18.3 4.5 %shard_map.110 = (f32[24,64,180]{2,1,0:T(8,128)S(1)}, bf16[2,576,384]{2,1,0:T(8,128)(2,1)S(1)}, bf16[2,192,576]{2,1,0:T(8,128)(2,1)S(1)}, f32[8,32,180]{2,1,0:T(8,128)S(1)}, f32[8,16,180]{2,1,0:T(8,128)S(1)}) custom-call(bf16[16,64,180]{2,1,0:T(8,128)(2,1)S(1)} %copy-done, bf16[4,64,180]{2,1,0:T(8,128)(2,1)S(1)} %collective-permute-done.row_one_ref, ...), custom_call_target="tpu_custom_call" | custom-call | flops 5000000000 | bytes 4000000 | tf_op jit(solution)/shard_map/pallas_call | solution.py:651
  22.8 0.0 collective-permute-done.2.col_two_ref
  22.8 0.0 collective-permute-done.3.col_one_ref
  22.8 0.0 copy-start.1
  22.8 0.0 copy-start.2
  22.8 0.0 copy-start.3
  22.8 5.7 %shard_map.112 = (bf16[368,128]{1,0:T(8,128)(2,1)S(1)}, bf16[368,128]{1,0:T(8,128)(2,1)S(1)}, f32[8,80,180]{2,1,0:T(8,128)S(1)}, f32[8,16,180]{2,1,0:T(8,128)S(1...) custom-call(bf16[16,64,180]{2,1,0:T(8,128)(2,1)S(1)} %copy-done, ...), custom_call_target="tpu_custom_call" | custom-call | flops 5000000000 | bytes 4000000 | tf_op jit(solution)/shard_map/pallas_call | solution.py:669
  28.6 0.8 %collective-permute-start.4 = (bf16[368,128]{1,0:T(8,128)(2,1)S(1)}, bf16[368,128]{1,0:T(8,128)(2,1)S(1)}, u32[]{:S(2)}, u32[]{:S(2)}) collective-permute-start(bf16[368,128]{1,0:T(8,128)(2,1)S(1)} %get-tuple-element.46), channel_id=1, source_target_pairs={{8,16},{16,8},{9,17},{17,9},{10,18},{18,10},{11,19},{19,11},{12,20... | collective-permute-start | bytes 282632 | tf_op jit(solution)/shard_map/ppermute | solution.py:865
  29.4 1.8 %collective-permute-start.5 = (bf16[368,128]{1,0:T(8,128)(2,1)S(1)}, bf16[368,128]{1,0:T(8,128)(2,1)S(1)}, u32[]{:S(2)}, u32[]{:S(2)}) collective-permute-start(bf16[368,128]{1,0:T(8,128)(2,1)S(1)} %get-tuple-element.47), channel_id=1, source_target_pairs={{0,8},{16,24},{8,0},{24,16},{1,9},{17,25},{9,1},{25,17},{2,10},{18... | collective-permute-start | bytes 282632 | tf_op jit(solution)/shard_map/ppermute | solution.py:865
  31.2 0.0 copy-done.1
  31.2 0.0 copy-done.2
  31.2 0.0 copy-done.3
  31.2 4.3 %shard_map.113 = (bf16[16,80,768]{2,1,0:T(8,128)(2,1)S(1)}, f32[20,88,180]{2,1,0:T(8,128)S(1)}, bf16[2304,180]{1,0:T(8,128)(2,1)S(1)}, bf16[768,192]{1,0:T(8,128)(2,1)S(1)}, bf16[768,256]{1,0:T(8,128)(2,1)S(1)}) custom-call(bf16[16,64,180]{2,1,0:T(8,128)(2,1)S(1)} %copy-done, f32[24,64,180]{2,1,0:T(8,128)S(1)} %get-tuple-element.32.nrm_ref, ...), custom_call_target="tpu_custom_call" | custom-call | flops 5000000000 | bytes 4000000 | tf_op jit(solution)/shard_map/pallas_call | solution.py:699
  35.5 0.0 collective-permute-done.4.back_two_ref
  35.5 0.0 collective-permute-done.5.back_one_ref
  35.6 6.0 %shard_map.114 = bf16[64,32,128]{2,1,0:T(8,128)(2,1)} custom-call(bf16[16,80,768]{2,1,0:T(8,128)(2,1)S(1)} %get-tuple-element.44.taps_ref, f32[20,88,180]{2,1,0:T(8,128)S(1)} %get-tuple-element.45.base, bf16[368,128]{1,0:T(8,128)(2,1)S(1)} %collective-permute-done.4.back_two_ref, bf16[368,128]{1,0:T(8,128)(2,1)S(1)} %collective-permute-done.5.back_one_ref, ...), custom_call_target="tpu_custom_call" | custom-call | flops 8000000000 | bytes 4000000 | tf_op jit(solution)/shard_map/pallas_call | solution.py:842
Async XLA Ops:
  1.0 13.4 %collective-permute-start.1 = (bf16[4,64,180]{2,1,0:T(8,128)(2,1)S(1)}, bf16[4,64,180]{2,1,0:T(8,128)(2,1)S(1)}, u32[]{:S(2)}, u32[]{:S(2)}) collective-permute-start(bf16[4,64,180]{2,1,0:T(8,128)(2,1)S(1)} %get-tuple-element.51), channel_id=1, source_target_pairs={{8,16},{16,8},{9,17},{17,9},{10,18},{18,10},{11,19},{19,11},{12,20... | collective-permute-start | bytes 276488 | tf_op jit(solution)/shard_map/ppermute | solution.py:865
  1.7 12.7 %collective-permute-start = (bf16[4,64,180]{2,1,0:T(8,128)(2,1)S(1)}, bf16[4,64,180]{2,1,0:T(8,128)(2,1)S(1)}, u32[]{:S(2)}, u32[]{:S(2)}) collective-permute-start(bf16[4,64,180]{2,1,0:T(8,128)(2,1)S(1)} %get-tuple-element.52), channel_id=1, source_target_pairs={{0,8},{16,24},{8,0},{24,16},{1,9},{17,25},{9,1},{25,17},{2,10},{18... | collective-permute-start | bytes 276488 | tf_op jit(solution)/shard_map/ppermute | solution.py:865
  7.6 0.9 %copy-start.4 = (bf16[180,540]{1,0:T(8,128)(2,1)S(1)}, bf16[180,540]{1,0:T(8,128)(2,1)}, u32[]{:S(2)}) copy-start(bf16[180,540]{1,0:T(8,128)(2,1)} %qkv_ref.1) | copy-start | bytes 583204
  8.5 0.9 %copy-start.7 = (bf16[180,180]{1,0:T(8,128)(2,1)S(1)}, bf16[180,180]{1,0:T(8,128)(2,1)}, u32[]{:S(2)}) copy-start(bf16[180,180]{1,0:T(8,128)(2,1)} %proj_ref.1) | copy-start | bytes 194404
  9.4 0.8 %copy-start.8 = (f32[1521,6]{0,1:T(8,128)S(1)}, f32[1521,6]{0,1:T(8,128)}, u32[]{:S(2)}) copy-start(f32[1521,6]{0,1:T(8,128)} %param.14) | copy-start | bytes 109516
  10.2 4.2 %copy-start = (bf16[16,64,180]{2,1,0:T(8,128)(2,1)S(1)}, bf16[16,64,180]{2,1,0:T(8,128)(2,1)}, u32[]{:S(2)}) copy-start(bf16[16,64,180]{2,1,0:T(8,128)(2,1)} %own_ref.7) | copy-start | bytes 1105924
  10.2 8.0 %copy-start.5 = (bf16[180,360]{1,0:T(8,128)(2,1)S(1)}, bf16[180,360]{1,0:T(8,128)(2,1)}, u32[]{:S(2)}) copy-start(bf16[180,360]{1,0:T(8,128)(2,1)} %hidden_ref.5) | copy-start | bytes 388804
  10.2 8.0 %copy-start.6 = (bf16[360,180]{0,1:T(8,128)(2,1)S(1)}, bf16[360,180]{0,1:T(8,128)(2,1)}, u32[]{:S(2)}) copy-start(bf16[360,180]{0,1:T(8,128)(2,1)} %param.18) | copy-start | bytes 388804
  10.2 8.0 %copy-start.9 = (f32[180]{0:T(256)S(1)}, f32[180]{0:T(256)}, u32[]{:S(2)}) copy-start(f32[180]{0:T(256)} %param.12) | copy-start | bytes 2164
  10.2 8.0 %copy-start.10 = (f32[180]{0:T(256)S(1)}, f32[180]{0:T(256)}, u32[]{:S(2)}) copy-start(f32[180]{0:T(256)} %param.16) | copy-start | bytes 2164
  14.7 8.1 %collective-permute-start.2 = (bf16[720,128]{1,0:T(8,128)(2,1)S(1)}, bf16[720,128]{1,0:T(8,128)(2,1)S(1)}, u32[]{:S(2)}, u32[]{:S(2)}) collective-permute-start(bf16[720,128]{1,0:T(8,128)(2,1)S(1)} %get-tuple-element.33), channel_id=1, source_target_pairs={{1,2},{3,4},{5,6},{2,1},{4,3},{6,5},{9,10},{11,12},{13,14},{10,9},... | collective-permute-start | bytes 552968 | tf_op jit(solution)/shard_map/ppermute | solution.py:865
  15.3 7.5 %collective-permute-start.3 = (bf16[720,128]{1,0:T(8,128)(2,1)S(1)}, bf16[720,128]{1,0:T(8,128)(2,1)S(1)}, u32[]{:S(2)}, u32[]{:S(2)}) collective-permute-start(bf16[720,128]{1,0:T(8,128)(2,1)S(1)} %get-tuple-element.34), channel_id=1, source_target_pairs={{0,1},{2,3},{4,5},{6,7},{1,0},{3,2},{5,4},{7,6},{8,9},{10,11},{12,... | collective-permute-start | bytes 552968 | tf_op jit(solution)/shard_map/ppermute | solution.py:865
  22.8 8.4 %copy-start.1 = (bf16[3,3,180,180]{3,2,1,0:T(8,128)(2,1)S(1)}, bf16[3,3,180,180]{3,2,1,0:T(8,128)(2,1)}, u32[]{:S(2)}) copy-start(bf16[3,3,180,180]{3,2,1,0:T(8,128)(2,1)} %group_ref.1) | copy-start | bytes 1749604
  22.8 8.4 %copy-start.2 = (bf16[3,3,180,64]{2,3,1,0:T(8,128)(2,1)S(1)}, bf16[3,3,180,64]{2,3,1,0:T(8,128)(2,1)}, u32[]{:S(2)}) copy-start(bf16[3,3,180,64]{2,3,1,0:T(8,128)(2,1)} %param.20) | copy-start | bytes 622084
  22.8 8.4 %copy-start.3 = (bf16[3,3,64,256]{3,2,1,0:T(8,128)(2,1)S(1)}, bf16[3,3,64,256]{3,2,1,0:T(8,128)(2,1)}, u32[]{:S(2)}) copy-start(bf16[3,3,64,256]{3,2,1,0:T(8,128)(2,1)} %upsample_ref.1) | copy-start | bytes 884740
  28.6 7.0 %collective-permute-start.4 = (bf16[368,128]{1,0:T(8,128)(2,1)S(1)}, bf16[368,128]{1,0:T(8,128)(2,1)S(1)}, u32[]{:S(2)}, u32[]{:S(2)}) collective-permute-start(bf16[368,128]{1,0:T(8,128)(2,1)S(1)} %get-tuple-element.46), channel_id=1, source_target_pairs={{8,16},{16,8},{9,17},{17,9},{10,18},{18,10},{11,19},{19,11},{12,20... | collective-permute-start | bytes 282632 | tf_op jit(solution)/shard_map/ppermute | solution.py:865
  29.4 6.1 %collective-permute-start.5 = (bf16[368,128]{1,0:T(8,128)(2,1)S(1)}, bf16[368,128]{1,0:T(8,128)(2,1)S(1)}, u32[]{:S(2)}, u32[]{:S(2)}) collective-permute-start(bf16[368,128]{1,0:T(8,128)(2,1)S(1)} %get-tuple-element.47), channel_id=1, source_target_pairs={{0,8},{16,24},{8,0},{24,16},{1,9},{17,25},{9,1},{25,17},{2,10},{18... | collective-permute-start | bytes 282632 | tf_op jit(solution)/shard_map/ppermute | solution.py:865

commit v12 on v10

--- a/solution.py
+++ b/solution.py
@@ -819,14 +819,13 @@
                         a * feats : (a + 1) * feats, 128 * r : 128 * (r + 1)
                     ]
 
-    half, third = (height + 4) // 2, (height + 2) // 3
-    group(0, half)
-    group(half, half)
-    narrow(0, third)
-    narrow(third, third)
-    narrow(2 * third, third)
-    expand(0, height // 2)
-    expand(height // 2, height // 2)
+    quarter, third = (height + 4) // 4, (height + 2) // 3
+    for step in range(4):
+        group(quarter * step, quarter)
+    for step in range(3):
+        narrow(third * step, third)
+    for step in range(4):
+        expand(height // 4 * step, height // 4)
     out_ref[...] = out_scr[...].reshape(feats, 2 * height, 128).astype(BF16)
 
 

time: 39.4 us -> 40 us (1.015)
  Pallas kernels: 23.9 us -> 24.5 us
    pallas_call x1, Pallas kernels: 5.5 us -> 6.12 us  [convs(): call(conv_kernel, jax.ShapeDtypeStruct((feats, 2 * height, 2 * cols), BF1...]
  transfers between devices with their start and end apart: 6 -> 6, of which waited for: 0 -> 0; matrix products, arithmetic and copies ran while one was open for 0% -> 0% of each run, Pallas kernels for 32% -> 31%
where the time goes in v12:
time: 40 us; the launch traced here: 39.8 us
  Pallas kernels  24.5 us (61%)
  starting transfers between devices  13.2 us (33%)
  other arithmetic  0.99 us (2%)
  local copies, waits for them, and re-layouts  0.85 us (2%)
    ppermute x6, starting transfers between devices, swapped(): out.append(lax.ppermute(payload, axis, pairs))  13.2 us
    pallas_call x1, Pallas kernels, convs(): call(conv_kernel, jax.ShapeDtypeStruct((feats, 2 * height, 2 * cols), BF1...  6.12 us
    pallas_call x1, Pallas kernels, outer_block(): call(outer_kernel, (jax.ShapeDtypeStruct((3 * span + 128, 128), BF16), ja...  5.72 us
    pallas_call x1, Pallas kernels, inner_block(): call(inner_kernel, (jax.ShapeDtypeStruct((height + 2 * RIM, cols, chans),...  4.53 us
    pallas_call x1, Pallas kernels, middle_block(): call(middle_kernel, (jax.ShapeDtypeStruct((height, span, 768), BF16), jax...  4.32 us
    pallas_call x1, Pallas kernels, build_bias(): call(bias_kernel, jax.ShapeDtypeStruct((3, HEADS, KEYS, 128), BF16), [plt...  3.63 us
    select_n x1, other arithmetic, on_device(): jnp.where(even_row, low, high)  0.99 us
    unnamed x22, local copies, waits for them, and re-layouts  0.85 us
  transfers between devices with their start and end apart: 6, of which 0 were waited for; matrix products, arithmetic and copies ran while one was open for 0% of the time, Pallas kernels for 31%

profile of v12, /device:TPU:0, one launch (start us, length us, event | category | flops | bytes accessed | tf_op | source)
XLA Modules:
  0.0 39.8 jit_solution(366774458489972198)
XLA Ops:
  0.0 1.0 %broadcast_select_fusion = (bf16[4,64,180]{2,1,0:T(8,128)(2,1)S(1)}, bf16[4,64,180]{2,1,0:T(8,128)(2,1)S(1)}) fusion(pred[]{:T(512)S(6)} %eq.5, bf16[16,64,180]{2,1,0:T(8,128)(2,1)} %own_ref.7), kind=kLoop, calls=%fused_computation | loop fusion | flops 92160 | bytes 368641 | tf_op jit(solution)/shard_map/jit(_where)/select_n | solution.py:881
  1.0 0.7 %collective-permute-start.1 = (bf16[4,64,180]{2,1,0:T(8,128)(2,1)S(1)}, bf16[4,64,180]{2,1,0:T(8,128)(2,1)S(1)}, u32[]{:S(2)}, u32[]{:S(2)}) collective-permute-start(bf16[4,64,180]{2,1,0:T(8,128)(2,1)S(1)} %get-tuple-element.49), channel_id=1, source_target_pairs={{8,16},{16,8},{9,17},{17,9},{10,18},{18,10},{11,19},{19,11},{12,20... | collective-permute-start | bytes 276488 | tf_op jit(solution)/shard_map/ppermute | solution.py:860
  1.7 5.9 %collective-permute-start = (bf16[4,64,180]{2,1,0:T(8,128)(2,1)S(1)}, bf16[4,64,180]{2,1,0:T(8,128)(2,1)S(1)}, u32[]{:S(2)}, u32[]{:S(2)}) collective-permute-start(bf16[4,64,180]{2,1,0:T(8,128)(2,1)S(1)} %get-tuple-element.50), channel_id=1, source_target_pairs={{0,8},{16,24},{8,0},{24,16},{1,9},{17,25},{9,1},{25,17},{2,10},{18... | collective-permute-start | bytes 276488 | tf_op jit(solution)/shard_map/ppermute | solution.py:860
  7.6 0.0 copy-start.8
  7.6 0.8 %copy-done.8 = f32[1521,6]{0,1:T(8,128)S(1)} copy-done((f32[1521,6]{0,1:T(8,128)S(1)}, f32[1521,6]{0,1:T(8,128)}, u32[]{:S(2)}) %copy-start.8) | copy-done | bytes 36528
  8.4 0.0 copy-start
  8.4 0.0 copy-start.4
  8.4 0.0 copy-start.5
  8.4 0.0 copy-start.6
  8.4 0.0 copy-start.7
  8.4 0.0 copy-start.9
  8.4 0.0 copy-start.10
  8.4 3.6 %shard_map.109.bias_ref = bf16[3,6,576,128]{3,2,1,0:T(8,128)(2,1)S(1)} custom-call(f32[6,1521]{1,0:T(8,128)S(1)} %bitcast.9), custom_call_target="tpu_custom_call" | custom-call | flops 4000000000 | bytes 4000000 | tf_op jit(solution)/shard_map/pallas_call | solution.py:108
  12.1 0.0 collective-permute-done.1.row_two_ref
  12.1 0.0 collective-permute-done.row_one_ref
  12.1 0.0 copy-done
  12.1 0.2 shard_map.111
  12.3 0.7 %collective-permute-start.2 = (bf16[720,128]{1,0:T(8,128)(2,1)S(1)}, bf16[720,128]{1,0:T(8,128)(2,1)S(1)}, u32[]{:S(2)}, u32[]{:S(2)}) collective-permute-start(bf16[720,128]{1,0:T(8,128)(2,1)S(1)} %get-tuple-element.28), channel_id=1, source_target_pairs={{1,2},{3,4},{5,6},{2,1},{4,3},{6,5},{9,10},{11,12},{13,14},{10,9},... | collective-permute-start | bytes 552968 | tf_op jit(solution)/shard_map/ppermute | solution.py:860
  13.0 2.9 %collective-permute-start.3 = (bf16[720,128]{1,0:T(8,128)(2,1)S(1)}, bf16[720,128]{1,0:T(8,128)(2,1)S(1)}, u32[]{:S(2)}, u32[]{:S(2)}) collective-permute-start(bf16[720,128]{1,0:T(8,128)(2,1)S(1)} %get-tuple-element.29), channel_id=1, source_target_pairs={{0,1},{2,3},{4,5},{6,7},{1,0},{3,2},{5,4},{7,6},{8,9},{10,11},{12,... | collective-permute-start | bytes 552968 | tf_op jit(solution)/shard_map/ppermute | solution.py:860
  15.9 0.0 copy-done.4
  15.9 0.0 copy-done.5
  15.9 0.0 copy-done.6
  15.9 0.0 copy-done.7
  15.9 0.0 copy-done.9
  15.9 0.0 copy-done.10
  15.9 4.5 %shard_map.110 = (f32[24,64,180]{2,1,0:T(8,128)S(1)}, bf16[180,384]{1,0:T(8,128)(2,1)S(1)}, bf16[384,180]{1,0:T(8,128)(2,1)S(1)}, bf16[192,180]{1,0:T(8,128)(2,1...) custom-call(bf16[16,64,180]{2,1,0:T(8,128)(2,1)S(1)} %copy-done, ...), custom_call_target="tpu_custom_call" | custom-call | flops 5000000000 | bytes 4000000 | tf_op jit(solution)/shard_map/pallas_call | solution.py:644
  20.5 0.0 collective-permute-done.2.col_two_ref
  20.5 0.0 collective-permute-done.3.col_one_ref
  20.5 0.0 copy-start.1
  20.5 0.0 copy-start.2
  20.5 0.0 copy-start.3
  20.5 5.7 %shard_map.112 = (bf16[368,128]{1,0:T(8,128)(2,1)S(1)}, bf16[368,128]{1,0:T(8,128)(2,1)S(1)}, f32[8,80,180]{2,1,0:T(8,128)S(1)}, f32[8,16,180]{2,1,0:T(8,128)S(1...) custom-call(bf16[16,64,180]{2,1,0:T(8,128)(2,1)S(1)} %copy-done, ...), custom_call_target="tpu_custom_call" | custom-call | flops 5000000000 | bytes 4000000 | tf_op jit(solution)/shard_map/pallas_call | solution.py:665
  26.3 0.8 %collective-permute-start.4 = (bf16[368,128]{1,0:T(8,128)(2,1)S(1)}, bf16[368,128]{1,0:T(8,128)(2,1)S(1)}, u32[]{:S(2)}, u32[]{:S(2)}) collective-permute-start(bf16[368,128]{1,0:T(8,128)(2,1)S(1)} %get-tuple-element.44), channel_id=1, source_target_pairs={{8,16},{16,8},{9,17},{17,9},{10,18},{18,10},{11,19},{19,11},{12,20... | collective-permute-start | bytes 282632 | tf_op jit(solution)/shard_map/ppermute | solution.py:860
  27.1 2.2 %collective-permute-start.5 = (bf16[368,128]{1,0:T(8,128)(2,1)S(1)}, bf16[368,128]{1,0:T(8,128)(2,1)S(1)}, u32[]{:S(2)}, u32[]{:S(2)}) collective-permute-start(bf16[368,128]{1,0:T(8,128)(2,1)S(1)} %get-tuple-element.45), channel_id=1, source_target_pairs={{0,8},{16,24},{8,0},{24,16},{1,9},{17,25},{9,1},{25,17},{2,10},{18... | collective-permute-start | bytes 282632 | tf_op jit(solution)/shard_map/ppermute | solution.py:860
  29.3 0.0 copy-done.1
  29.3 0.0 copy-done.2
  29.3 0.0 copy-done.3
  29.3 4.3 %shard_map.113 = (bf16[16,80,768]{2,1,0:T(8,128)(2,1)S(1)}, f32[20,88,180]{2,1,0:T(8,128)S(1)}, bf16[2304,180]{1,0:T(8,128)(2,1)S(1)}, bf16[768,192]{1,0:T(8,128)(2,1)S(1)}, bf16[768,256]{1,0:T(8,128)(2,1)S(1)}) custom-call(bf16[16,64,180]{2,1,0:T(8,128)(2,1)S(1)} %copy-done, f32[24,64,180]{2,1,0:T(8,128)S(1)} %get-tuple-element.27.nrm_ref, ...), custom_call_target="tpu_custom_call" | custom-call | flops 5000000000 | bytes 4000000 | tf_op jit(solution)/shard_map/pallas_call | solution.py:695
  33.7 0.0 collective-permute-done.4.back_two_ref
  33.7 0.0 collective-permute-done.5.back_one_ref
  33.7 6.1 %shard_map.114 = bf16[64,32,128]{2,1,0:T(8,128)(2,1)} custom-call(bf16[16,80,768]{2,1,0:T(8,128)(2,1)S(1)} %get-tuple-element.42.taps_ref, f32[20,88,180]{2,1,0:T(8,128)S(1)} %get-tuple-element.43.base, bf16[368,128]{1,0:T(8,128)(2,1)S(1)} %collective-permute-done.4.back_two_ref, bf16[368,128]{1,0:T(8,128)(2,1)S(1)} %collective-permute-done.5.back_one_ref, ...), custom_call_target="tpu_custom_call" | custom-call | flops 8000000000 | bytes 4000000 | tf_op jit(solution)/shard_map/pallas_call | solution.py:837
Async XLA Ops:
  1.0 11.1 %collective-permute-start.1 = (bf16[4,64,180]{2,1,0:T(8,128)(2,1)S(1)}, bf16[4,64,180]{2,1,0:T(8,128)(2,1)S(1)}, u32[]{:S(2)}, u32[]{:S(2)}) collective-permute-start(bf16[4,64,180]{2,1,0:T(8,128)(2,1)S(1)} %get-tuple-element.49), channel_id=1, source_target_pairs={{8,16},{16,8},{9,17},{17,9},{10,18},{18,10},{11,19},{19,11},{12,20... | collective-permute-start | bytes 276488 | tf_op jit(solution)/shard_map/ppermute | solution.py:860
  1.7 10.4 %collective-permute-start = (bf16[4,64,180]{2,1,0:T(8,128)(2,1)S(1)}, bf16[4,64,180]{2,1,0:T(8,128)(2,1)S(1)}, u32[]{:S(2)}, u32[]{:S(2)}) collective-permute-start(bf16[4,64,180]{2,1,0:T(8,128)(2,1)S(1)} %get-tuple-element.50), channel_id=1, source_target_pairs={{0,8},{16,24},{8,0},{24,16},{1,9},{17,25},{9,1},{25,17},{2,10},{18... | collective-permute-start | bytes 276488 | tf_op jit(solution)/shard_map/ppermute | solution.py:860
  7.6 0.8 %copy-start.8 = (f32[1521,6]{0,1:T(8,128)S(1)}, f32[1521,6]{0,1:T(8,128)}, u32[]{:S(2)}) copy-start(f32[1521,6]{0,1:T(8,128)} %param.14) | copy-start | bytes 109516
  8.4 3.7 %copy-start = (bf16[16,64,180]{2,1,0:T(8,128)(2,1)S(1)}, bf16[16,64,180]{2,1,0:T(8,128)(2,1)}, u32[]{:S(2)}) copy-start(bf16[16,64,180]{2,1,0:T(8,128)(2,1)} %own_ref.7) | copy-start | bytes 1105924
  8.4 7.5 %copy-start.4 = (bf16[180,540]{1,0:T(8,128)(2,1)S(1)}, bf16[180,540]{1,0:T(8,128)(2,1)}, u32[]{:S(2)}) copy-start(bf16[180,540]{1,0:T(8,128)(2,1)} %qkv_ref.1) | copy-start | bytes 583204
  8.4 7.5 %copy-start.5 = (bf16[180,360]{1,0:T(8,128)(2,1)S(1)}, bf16[180,360]{1,0:T(8,128)(2,1)}, u32[]{:S(2)}) copy-start(bf16[180,360]{1,0:T(8,128)(2,1)} %hidden_ref.5) | copy-start | bytes 388804
  8.4 7.5 %copy-start.6 = (bf16[360,180]{0,1:T(8,128)(2,1)S(1)}, bf16[360,180]{0,1:T(8,128)(2,1)}, u32[]{:S(2)}) copy-start(bf16[360,180]{0,1:T(8,128)(2,1)} %param.18) | copy-start | bytes 388804
  8.4 7.5 %copy-start.7 = (bf16[180,180]{1,0:T(8,128)(2,1)S(1)}, bf16[180,180]{1,0:T(8,128)(2,1)}, u32[]{:S(2)}) copy-start(bf16[180,180]{1,0:T(8,128)(2,1)} %proj_ref.1) | copy-start | bytes 194404
  8.4 7.5 %copy-start.9 = (f32[180]{0:T(256)S(1)}, f32[180]{0:T(256)}, u32[]{:S(2)}) copy-start(f32[180]{0:T(256)} %param.12) | copy-start | bytes 2164
  8.4 7.5 %copy-start.10 = (f32[180]{0:T(256)S(1)}, f32[180]{0:T(256)}, u32[]{:S(2)}) copy-start(f32[180]{0:T(256)} %param.16) | copy-start | bytes 2164
  12.3 8.2 %collective-permute-start.2 = (bf16[720,128]{1,0:T(8,128)(2,1)S(1)}, bf16[720,128]{1,0:T(8,128)(2,1)S(1)}, u32[]{:S(2)}, u32[]{:S(2)}) collective-permute-start(bf16[720,128]{1,0:T(8,128)(2,1)S(1)} %get-tuple-element.28), channel_id=1, source_target_pairs={{1,2},{3,4},{5,6},{2,1},{4,3},{6,5},{9,10},{11,12},{13,14},{10,9},... | collective-permute-start | bytes 552968 | tf_op jit(solution)/shard_map/ppermute | solution.py:860
  13.0 7.5 %collective-permute-start.3 = (bf16[720,128]{1,0:T(8,128)(2,1)S(1)}, bf16[720,128]{1,0:T(8,128)(2,1)S(1)}, u32[]{:S(2)}, u32[]{:S(2)}) collective-permute-start(bf16[720,128]{1,0:T(8,128)(2,1)S(1)} %get-tuple-element.29), channel_id=1, source_target_pairs={{0,1},{2,3},{4,5},{6,7},{1,0},{3,2},{5,4},{7,6},{8,9},{10,11},{12,... | collective-permute-start | bytes 552968 | tf_op jit(solution)/shard_map/ppermute | solution.py:860
  20.5 8.8 %copy-start.1 = (bf16[3,3,180,180]{3,2,1,0:T(8,128)(2,1)S(1)}, bf16[3,3,180,180]{3,2,1,0:T(8,128)(2,1)}, u32[]{:S(2)}) copy-start(bf16[3,3,180,180]{3,2,1,0:T(8,128)(2,1)} %group_ref.1) | copy-start | bytes 1749604
  20.5 8.8 %copy-start.2 = (bf16[3,3,180,64]{2,3,1,0:T(8,128)(2,1)S(1)}, bf16[3,3,180,64]{2,3,1,0:T(8,128)(2,1)}, u32[]{:S(2)}) copy-start(bf16[3,3,180,64]{2,3,1,0:T(8,128)(2,1)} %param.20) | copy-start | bytes 622084
  20.5 8.8 %copy-start.3 = (bf16[3,3,64,256]{3,2,1,0:T(8,128)(2,1)S(1)}, bf16[3,3,64,256]{3,2,1,0:T(8,128)(2,1)}, u32[]{:S(2)}) copy-start(bf16[3,3,64,256]{3,2,1,0:T(8,128)(2,1)} %upsample_ref.1) | copy-start | bytes 884740
  26.3 7.4 %collective-permute-start.4 = (bf16[368,128]{1,0:T(8,128)(2,1)S(1)}, bf16[368,128]{1,0:T(8,128)(2,1)S(1)}, u32[]{:S(2)}, u32[]{:S(2)}) collective-permute-start(bf16[368,128]{1,0:T(8,128)(2,1)S(1)} %get-tuple-element.44), channel_id=1, source_target_pairs={{8,16},{16,8},{9,17},{17,9},{10,18},{18,10},{11,19},{19,11},{12,20... | collective-permute-start | bytes 282632 | tf_op jit(solution)/shard_map/ppermute | solution.py:860
  27.1 6.6 %collective-permute-start.5 = (bf16[368,128]{1,0:T(8,128)(2,1)S(1)}, bf16[368,128]{1,0:T(8,128)(2,1)S(1)}, u32[]{:S(2)}, u32[]{:S(2)}) collective-permute-start(bf16[368,128]{1,0:T(8,128)(2,1)S(1)} %get-tuple-element.45), channel_id=1, source_target_pairs={{0,8},{16,24},{8,0},{24,16},{1,9},{17,25},{9,1},{25,17},{2,10},{18... | collective-permute-start | bytes 282632 | tf_op jit(solution)/shard_map/ppermute | solution.py:860

commit v13 on v10

--- a/solution.py
+++ b/solution.py
@@ -819,12 +819,11 @@
                         a * feats : (a + 1) * feats, 128 * r : 128 * (r + 1)
                     ]
 
-    half, third = (height + 4) // 2, (height + 2) // 3
-    group(0, half)
-    group(half, half)
-    narrow(0, third)
-    narrow(third, third)
-    narrow(2 * third, third)
+    group_part, narrow_part = (height + 4) // 2, (height + 2) // 2
+    group(0, group_part)
+    group(group_part, group_part)
+    narrow(0, narrow_part)
+    narrow(narrow_part, narrow_part)
     expand(0, height // 2)
     expand(height // 2, height // 2)
     out_ref[...] = out_scr[...].reshape(feats, 2 * height, 128).astype(BF16)
@@ -842,7 +841,7 @@
             pltpu.VMEM((6, span + STRIP, chans), F32),
             pltpu.VMEM((6, span, 768), BF16),
             pltpu.VMEM((height + 4, span, 256), BF16),
-            pltpu.VMEM((2, 6, span, 256), F32),
+            pltpu.VMEM((2, 9, span, 256), F32),
             pltpu.VMEM((height + 2, cols + 8, 128), F32),
             pltpu.VMEM((height + 2, cols, 256), BF16),
             pltpu.VMEM((feats * 2 * height, 128), F32),

time: 39.4 us -> 39.7 us (level)
  no operation moved by 1% of the time
where the time goes in v13:
time: 39.7 us; the launch traced here: 39.5 us
  Pallas kernels  24.2 us (61%)
  starting transfers between devices  13.2 us (33%)
  other arithmetic  0.99 us (2%)
  local copies, waits for them, and re-layouts  0.85 us (2%)
    ppermute x6, starting transfers between devices, swapped(): out.append(lax.ppermute(payload, axis, pairs))  13.2 us
    pallas_call x1, Pallas kernels, convs(): call(conv_kernel, jax.ShapeDtypeStruct((feats, 2 * height, 2 * cols), BF1...  5.78 us
    pallas_call x1, Pallas kernels, outer_block(): call(outer_kernel, (jax.ShapeDtypeStruct((3 * span + 128, 128), BF16), ja...  5.72 us
    pallas_call x1, Pallas kernels, inner_block(): call(inner_kernel, (jax.ShapeDtypeStruct((height + 2 * RIM, cols, chans),...  4.53 us
    pallas_call x1, Pallas kernels, middle_block(): call(middle_kernel, (jax.ShapeDtypeStruct((height, span, 768), BF16), jax...  4.32 us
    pallas_call x1, Pallas kernels, build_bias(): call(bias_kernel, jax.ShapeDtypeStruct((3, HEADS, KEYS, 128), BF16), [plt...  3.63 us
    select_n x1, other arithmetic, on_device(): jnp.where(even_row, low, high)  0.99 us
    unnamed x22, local copies, waits for them, and re-layouts  0.85 us
  transfers between devices with their start and end apart: 6, of which 0 were waited for; matrix products, arithmetic and copies ran while one was open for 0% of the time, Pallas kernels for 32%

profile of v13, /device:TPU:0, one launch (start us, length us, event | category | flops | bytes accessed | tf_op | source)
XLA Modules:
  0.0 39.5 jit_solution(15772805000308569064)
XLA Ops:
  0.0 1.0 %broadcast_select_fusion = (bf16[4,64,180]{2,1,0:T(8,128)(2,1)S(1)}, bf16[4,64,180]{2,1,0:T(8,128)(2,1)S(1)}) fusion(pred[]{:T(512)S(6)} %eq.5, bf16[16,64,180]{2,1,0:T(8,128)(2,1)} %own_ref.7), kind=kLoop, calls=%fused_computation | loop fusion | flops 92160 | bytes 368641 | tf_op jit(solution)/shard_map/jit(_where)/select_n | solution.py:881
  1.0 0.7 %collective-permute-start.1 = (bf16[4,64,180]{2,1,0:T(8,128)(2,1)S(1)}, bf16[4,64,180]{2,1,0:T(8,128)(2,1)S(1)}, u32[]{:S(2)}, u32[]{:S(2)}) collective-permute-start(bf16[4,64,180]{2,1,0:T(8,128)(2,1)S(1)} %get-tuple-element.49), channel_id=1, source_target_pairs={{8,16},{16,8},{9,17},{17,9},{10,18},{18,10},{11,19},{19,11},{12,20... | collective-permute-start | bytes 276488 | tf_op jit(solution)/shard_map/ppermute | solution.py:860
  1.7 5.9 %collective-permute-start = (bf16[4,64,180]{2,1,0:T(8,128)(2,1)S(1)}, bf16[4,64,180]{2,1,0:T(8,128)(2,1)S(1)}, u32[]{:S(2)}, u32[]{:S(2)}) collective-permute-start(bf16[4,64,180]{2,1,0:T(8,128)(2,1)S(1)} %get-tuple-element.50), channel_id=1, source_target_pairs={{0,8},{16,24},{8,0},{24,16},{1,9},{17,25},{9,1},{25,17},{2,10},{18... | collective-permute-start | bytes 276488 | tf_op jit(solution)/shard_map/ppermute | solution.py:860
  7.6 0.0 copy-start.8
  7.6 0.8 %copy-done.8 = f32[1521,6]{0,1:T(8,128)S(1)} copy-done((f32[1521,6]{0,1:T(8,128)S(1)}, f32[1521,6]{0,1:T(8,128)}, u32[]{:S(2)}) %copy-start.8) | copy-done | bytes 36528
  8.4 0.0 copy-start
  8.4 0.0 copy-start.4
  8.4 0.0 copy-start.5
  8.4 0.0 copy-start.6
  8.4 0.0 copy-start.7
  8.4 0.0 copy-start.9
  8.4 0.0 copy-start.10
  8.4 3.6 %shard_map.109.bias_ref = bf16[3,6,576,128]{3,2,1,0:T(8,128)(2,1)S(1)} custom-call(f32[6,1521]{1,0:T(8,128)S(1)} %bitcast.9), custom_call_target="tpu_custom_call" | custom-call | flops 4000000000 | bytes 4000000 | tf_op jit(solution)/shard_map/pallas_call | solution.py:108
  12.1 0.0 collective-permute-done.1.row_two_ref
  12.1 0.0 collective-permute-done.row_one_ref
  12.1 0.0 copy-done
  12.1 0.2 shard_map.111
  12.3 0.7 %collective-permute-start.2 = (bf16[720,128]{1,0:T(8,128)(2,1)S(1)}, bf16[720,128]{1,0:T(8,128)(2,1)S(1)}, u32[]{:S(2)}, u32[]{:S(2)}) collective-permute-start(bf16[720,128]{1,0:T(8,128)(2,1)S(1)} %get-tuple-element.28), channel_id=1, source_target_pairs={{1,2},{3,4},{5,6},{2,1},{4,3},{6,5},{9,10},{11,12},{13,14},{10,9},... | collective-permute-start | bytes 552968 | tf_op jit(solution)/shard_map/ppermute | solution.py:860
  13.0 2.9 %collective-permute-start.3 = (bf16[720,128]{1,0:T(8,128)(2,1)S(1)}, bf16[720,128]{1,0:T(8,128)(2,1)S(1)}, u32[]{:S(2)}, u32[]{:S(2)}) collective-permute-start(bf16[720,128]{1,0:T(8,128)(2,1)S(1)} %get-tuple-element.29), channel_id=1, source_target_pairs={{0,1},{2,3},{4,5},{6,7},{1,0},{3,2},{5,4},{7,6},{8,9},{10,11},{12,... | collective-permute-start | bytes 552968 | tf_op jit(solution)/shard_map/ppermute | solution.py:860
  15.9 0.0 copy-done.4
  15.9 0.0 copy-done.5
  15.9 0.0 copy-done.6
  15.9 0.0 copy-done.7
  15.9 0.0 copy-done.9
  15.9 0.0 copy-done.10
  15.9 4.5 %shard_map.110 = (f32[24,64,180]{2,1,0:T(8,128)S(1)}, bf16[180,384]{1,0:T(8,128)(2,1)S(1)}, bf16[384,180]{1,0:T(8,128)(2,1)S(1)}, bf16[192,180]{1,0:T(8,128)(2,1...) custom-call(bf16[16,64,180]{2,1,0:T(8,128)(2,1)S(1)} %copy-done, ...), custom_call_target="tpu_custom_call" | custom-call | flops 5000000000 | bytes 4000000 | tf_op jit(solution)/shard_map/pallas_call | solution.py:644
  20.5 0.0 collective-permute-done.2.col_two_ref
  20.5 0.0 collective-permute-done.3.col_one_ref
  20.5 0.0 copy-start.1
  20.5 0.0 copy-start.2
  20.5 0.0 copy-start.3
  20.5 5.7 %shard_map.112 = (bf16[368,128]{1,0:T(8,128)(2,1)S(1)}, bf16[368,128]{1,0:T(8,128)(2,1)S(1)}, f32[8,80,180]{2,1,0:T(8,128)S(1)}, f32[8,16,180]{2,1,0:T(8,128)S(1...) custom-call(bf16[16,64,180]{2,1,0:T(8,128)(2,1)S(1)} %copy-done, ...), custom_call_target="tpu_custom_call" | custom-call | flops 5000000000 | bytes 4000000 | tf_op jit(solution)/shard_map/pallas_call | solution.py:665
  26.3 0.8 %collective-permute-start.4 = (bf16[368,128]{1,0:T(8,128)(2,1)S(1)}, bf16[368,128]{1,0:T(8,128)(2,1)S(1)}, u32[]{:S(2)}, u32[]{:S(2)}) collective-permute-start(bf16[368,128]{1,0:T(8,128)(2,1)S(1)} %get-tuple-element.44), channel_id=1, source_target_pairs={{8,16},{16,8},{9,17},{17,9},{10,18},{18,10},{11,19},{19,11},{12,20... | collective-permute-start | bytes 282632 | tf_op jit(solution)/shard_map/ppermute | solution.py:860
  27.1 2.2 %collective-permute-start.5 = (bf16[368,128]{1,0:T(8,128)(2,1)S(1)}, bf16[368,128]{1,0:T(8,128)(2,1)S(1)}, u32[]{:S(2)}, u32[]{:S(2)}) collective-permute-start(bf16[368,128]{1,0:T(8,128)(2,1)S(1)} %get-tuple-element.45), channel_id=1, source_target_pairs={{0,8},{16,24},{8,0},{24,16},{1,9},{17,25},{9,1},{25,17},{2,10},{18... | collective-permute-start | bytes 282632 | tf_op jit(solution)/shard_map/ppermute | solution.py:860
  29.3 0.0 copy-done.1
  29.3 0.0 copy-done.2
  29.3 0.0 copy-done.3
  29.3 4.3 %shard_map.113 = (bf16[16,80,768]{2,1,0:T(8,128)(2,1)S(1)}, f32[20,88,180]{2,1,0:T(8,128)S(1)}, bf16[2304,180]{1,0:T(8,128)(2,1)S(1)}, bf16[768,192]{1,0:T(8,128)(2,1)S(1)}, bf16[768,256]{1,0:T(8,128)(2,1)S(1)}) custom-call(bf16[16,64,180]{2,1,0:T(8,128)(2,1)S(1)} %copy-done, f32[24,64,180]{2,1,0:T(8,128)S(1)} %get-tuple-element.27.nrm_ref, ...), custom_call_target="tpu_custom_call" | custom-call | flops 5000000000 | bytes 4000000 | tf_op jit(solution)/shard_map/pallas_call | solution.py:695
  33.7 0.0 collective-permute-done.4.back_two_ref
  33.7 0.0 collective-permute-done.5.back_one_ref
  33.7 5.8 %shard_map.114 = bf16[64,32,128]{2,1,0:T(8,128)(2,1)} custom-call(bf16[16,80,768]{2,1,0:T(8,128)(2,1)S(1)} %get-tuple-element.42.taps_ref, f32[20,88,180]{2,1,0:T(8,128)S(1)} %get-tuple-element.43.base, bf16[368,128]{1,0:T(8,128)(2,1)S(1)} %collective-permute-done.4.back_two_ref, bf16[368,128]{1,0:T(8,128)(2,1)S(1)} %collective-permute-done.5.back_one_ref, ...), custom_call_target="tpu_custom_call" | custom-call | flops 8000000000 | bytes 4000000 | tf_op jit(solution)/shard_map/pallas_call | solution.py:837
Async XLA Ops:
  1.0 11.1 %collective-permute-start.1 = (bf16[4,64,180]{2,1,0:T(8,128)(2,1)S(1)}, bf16[4,64,180]{2,1,0:T(8,128)(2,1)S(1)}, u32[]{:S(2)}, u32[]{:S(2)}) collective-permute-start(bf16[4,64,180]{2,1,0:T(8,128)(2,1)S(1)} %get-tuple-element.49), channel_id=1, source_target_pairs={{8,16},{16,8},{9,17},{17,9},{10,18},{18,10},{11,19},{19,11},{12,20... | collective-permute-start | bytes 276488 | tf_op jit(solution)/shard_map/ppermute | solution.py:860
  1.7 10.4 %collective-permute-start = (bf16[4,64,180]{2,1,0:T(8,128)(2,1)S(1)}, bf16[4,64,180]{2,1,0:T(8,128)(2,1)S(1)}, u32[]{:S(2)}, u32[]{:S(2)}) collective-permute-start(bf16[4,64,180]{2,1,0:T(8,128)(2,1)S(1)} %get-tuple-element.50), channel_id=1, source_target_pairs={{0,8},{16,24},{8,0},{24,16},{1,9},{17,25},{9,1},{25,17},{2,10},{18... | collective-permute-start | bytes 276488 | tf_op jit(solution)/shard_map/ppermute | solution.py:860
  7.6 0.8 %copy-start.8 = (f32[1521,6]{0,1:T(8,128)S(1)}, f32[1521,6]{0,1:T(8,128)}, u32[]{:S(2)}) copy-start(f32[1521,6]{0,1:T(8,128)} %param.14) | copy-start | bytes 109516
  8.4 3.7 %copy-start = (bf16[16,64,180]{2,1,0:T(8,128)(2,1)S(1)}, bf16[16,64,180]{2,1,0:T(8,128)(2,1)}, u32[]{:S(2)}) copy-start(bf16[16,64,180]{2,1,0:T(8,128)(2,1)} %own_ref.7) | copy-start | bytes 1105924
  8.4 7.5 %copy-start.4 = (bf16[180,540]{1,0:T(8,128)(2,1)S(1)}, bf16[180,540]{1,0:T(8,128)(2,1)}, u32[]{:S(2)}) copy-start(bf16[180,540]{1,0:T(8,128)(2,1)} %qkv_ref.1) | copy-start | bytes 583204
  8.4 7.5 %copy-start.5 = (bf16[180,360]{1,0:T(8,128)(2,1)S(1)}, bf16[180,360]{1,0:T(8,128)(2,1)}, u32[]{:S(2)}) copy-start(bf16[180,360]{1,0:T(8,128)(2,1)} %hidden_ref.5) | copy-start | bytes 388804
  8.4 7.5 %copy-start.6 = (bf16[360,180]{0,1:T(8,128)(2,1)S(1)}, bf16[360,180]{0,1:T(8,128)(2,1)}, u32[]{:S(2)}) copy-start(bf16[360,180]{0,1:T(8,128)(2,1)} %param.18) | copy-start | bytes 388804
  8.4 7.5 %copy-start.7 = (bf16[180,180]{1,0:T(8,128)(2,1)S(1)}, bf16[180,180]{1,0:T(8,128)(2,1)}, u32[]{:S(2)}) copy-start(bf16[180,180]{1,0:T(8,128)(2,1)} %proj_ref.1) | copy-start | bytes 194404
  8.4 7.5 %copy-start.9 = (f32[180]{0:T(256)S(1)}, f32[180]{0:T(256)}, u32[]{:S(2)}) copy-start(f32[180]{0:T(256)} %param.12) | copy-start | bytes 2164
  8.4 7.5 %copy-start.10 = (f32[180]{0:T(256)S(1)}, f32[180]{0:T(256)}, u32[]{:S(2)}) copy-start(f32[180]{0:T(256)} %param.16) | copy-start | bytes 2164
  12.3 8.2 %collective-permute-start.2 = (bf16[720,128]{1,0:T(8,128)(2,1)S(1)}, bf16[720,128]{1,0:T(8,128)(2,1)S(1)}, u32[]{:S(2)}, u32[]{:S(2)}) collective-permute-start(bf16[720,128]{1,0:T(8,128)(2,1)S(1)} %get-tuple-element.28), channel_id=1, source_target_pairs={{1,2},{3,4},{5,6},{2,1},{4,3},{6,5},{9,10},{11,12},{13,14},{10,9},... | collective-permute-start | bytes 552968 | tf_op jit(solution)/shard_map/ppermute | solution.py:860
  13.0 7.5 %collective-permute-start.3 = (bf16[720,128]{1,0:T(8,128)(2,1)S(1)}, bf16[720,128]{1,0:T(8,128)(2,1)S(1)}, u32[]{:S(2)}, u32[]{:S(2)}) collective-permute-start(bf16[720,128]{1,0:T(8,128)(2,1)S(1)} %get-tuple-element.29), channel_id=1, source_target_pairs={{0,1},{2,3},{4,5},{6,7},{1,0},{3,2},{5,4},{7,6},{8,9},{10,11},{12,... | collective-permute-start | bytes 552968 | tf_op jit(solution)/shard_map/ppermute | solution.py:860
  20.5 8.8 %copy-start.1 = (bf16[3,3,180,180]{3,2,1,0:T(8,128)(2,1)S(1)}, bf16[3,3,180,180]{3,2,1,0:T(8,128)(2,1)}, u32[]{:S(2)}) copy-start(bf16[3,3,180,180]{3,2,1,0:T(8,128)(2,1)} %group_ref.1) | copy-start | bytes 1749604
  20.5 8.8 %copy-start.2 = (bf16[3,3,180,64]{2,3,1,0:T(8,128)(2,1)S(1)}, bf16[3,3,180,64]{2,3,1,0:T(8,128)(2,1)}, u32[]{:S(2)}) copy-start(bf16[3,3,180,64]{2,3,1,0:T(8,128)(2,1)} %param.20) | copy-start | bytes 622084
  20.5 8.8 %copy-start.3 = (bf16[3,3,64,256]{3,2,1,0:T(8,128)(2,1)S(1)}, bf16[3,3,64,256]{3,2,1,0:T(8,128)(2,1)}, u32[]{:S(2)}) copy-start(bf16[3,3,64,256]{3,2,1,0:T(8,128)(2,1)} %upsample_ref.1) | copy-start | bytes 884740
  26.3 7.4 %collective-permute-start.4 = (bf16[368,128]{1,0:T(8,128)(2,1)S(1)}, bf16[368,128]{1,0:T(8,128)(2,1)S(1)}, u32[]{:S(2)}, u32[]{:S(2)}) collective-permute-start(bf16[368,128]{1,0:T(8,128)(2,1)S(1)} %get-tuple-element.44), channel_id=1, source_target_pairs={{8,16},{16,8},{9,17},{17,9},{10,18},{18,10},{11,19},{19,11},{12,20... | collective-permute-start | bytes 282632 | tf_op jit(solution)/shard_map/ppermute | solution.py:860
  27.1 6.6 %collective-permute-start.5 = (bf16[368,128]{1,0:T(8,128)(2,1)S(1)}, bf16[368,128]{1,0:T(8,128)(2,1)S(1)}, u32[]{:S(2)}, u32[]{:S(2)}) collective-permute-start(bf16[368,128]{1,0:T(8,128)(2,1)S(1)} %get-tuple-element.45), channel_id=1, source_target_pairs={{0,8},{16,24},{8,0},{24,16},{1,9},{17,25},{9,1},{25,17},{2,10},{18... | collective-permute-start | bytes 282632 | tf_op jit(solution)/shard_map/ppermute | solution.py:860
